TPU v7x, 32 devices: a whole 2x2x4 slice. The times are simulated.
32 devices in a mesh: ctx: 8 (over z, y), fsdp: 4 (over x, core).
Axes of the slice: x: 2, y: 2, z: 4, core: 2. Of those that a mesh axis runs over, the one named last changes fastest.
Arguments:
- tokens: bfloat16 [4, 2, 512, 2048], P('fsdp', None, 'ctx'), may hold values from -6 to 6
- segments: int32 [4, 2, 512], P('fsdp'), may hold values from 0 to 9, as said below
- routes: int32 [4, 2, 512, 4], P('fsdp', None, 'ctx'), may hold values from 0 to 7, all different within a row
- cotangent: bfloat16 [4, 2, 512, 2048], P('fsdp', None, 'ctx'), may hold values from -6 to 6
- w_qkv: bfloat16 [2048, 6144], P(('ctx', 'fsdp')), may hold values from -0.125 to 0.125
- b_qkv: bfloat16 [6144], P(('ctx', 'fsdp')), may hold values from -1.1953125 to 1.1953125
- w_out: bfloat16 [2048, 2048], P(('ctx', 'fsdp')), may hold values from -0.375 to 0.375
- gain_attn: bfloat16 [2048], P(('ctx', 'fsdp')), may hold values from 0.5 to 1.5
- gain_ffn: bfloat16 [2048], P(('ctx', 'fsdp')), may hold values from 0.5 to 1.5
- w_router: bfloat16 [2048, 8], P(('ctx', 'fsdp')), may hold values from -0.0625 to 0.0625
- w_shared_gate: bfloat16 [2048], P(('ctx', 'fsdp')), may hold values from -0.125 to 0.125
- w_shared_in: bfloat16 [2048, 11264], P(('ctx', 'fsdp')), may hold values from -0.125 to 0.125
- w_shared_out: bfloat16 [5632, 2048], P(('ctx', 'fsdp')), may hold values from -0.15625 to 0.15625
- w_expert_in: bfloat16 [8, 2048, 2816], P('ctx', 'fsdp'), may hold values from -0.125 to 0.125
- w_expert_out: bfloat16 [8, 1408, 2048], P('ctx', 'fsdp'), may hold values from -0.875 to 0.875
Outputs:
- output: bfloat16 [4, 2, 512, 2048], P('fsdp', None, 'ctx')
- grad_tokens: float32 [4, 2, 512, 2048], P('fsdp', None, 'ctx')
- grad_w_qkv: float32 [2048, 6144], P(('ctx', 'fsdp'))
- grad_b_qkv: float32 [6144], P(('ctx', 'fsdp'))
- grad_w_out: float32 [2048, 2048], P(('ctx', 'fsdp'))
- grad_gain_attn: float32 [2048], P(('ctx', 'fsdp'))
- grad_gain_ffn: float32 [2048], P(('ctx', 'fsdp'))
- grad_w_router: float32 [2048, 8], P(('ctx', 'fsdp'))
- grad_w_shared_gate: float32 [2048], P(('ctx', 'fsdp'))
- grad_w_shared_in: float32 [2048, 11264], P(('ctx', 'fsdp'))
- grad_w_shared_out: float32 [5632, 2048], P(('ctx', 'fsdp'))
- grad_w_expert_in: float32 [8, 2048, 2816], P('ctx', 'fsdp')
- grad_w_expert_out: float32 [8, 1408, 2048], P('ctx', 'fsdp')
Inputs may be any that keep to these rules, and one draw needn't show every extreme that they name: `segments`: along each sequence in order of position, segment numbers never fall; each sequence's last position has the number 1024 // 200 + 4. `routes`: each token names 4 different experts.
All inputs are finite; a program needn't handle non-finite values.
Results may differ from a plain program's by a relative error of at most 0.018.
Values may be sent and summed in bfloat16 or wider, within the bound.
No kernel may reach another device: no remote copies, remote signals or barrier semaphores. Data moves between devices by JAX's collectives and lax.ppermute only.
A program may use at most 448 MiB of HBM per device.

v0:
```python
import jax
import jax.numpy as jnp
from jax import lax
from jax.sharding import PartitionSpec as P

HD = 128
FS = 5632
FE = 1408


RMS_EPS = 1e-06
ROPE_THETA = 1000000.0
MASK_FILL = -1e30
HIGHEST = lax.Precision.HIGHEST


def rope_tables(positions, head_dim):
    half_dim = head_dim // 2
    inv_freq = ROPE_THETA ** (-(jnp.arange(half_dim, dtype=jnp.float32) * 2.0 / head_dim))
    angles = positions.astype(jnp.float32)[:, None] * inv_freq[None, :]
    cos_tab = jnp.concatenate([jnp.cos(angles), jnp.cos(angles)], axis=-1)
    sine_tab = jnp.concatenate([jnp.sin(angles), jnp.sin(angles)], axis=-1)
    return (cos_tab, sine_tab)


def rotate(values, cos_tab, sine_tab):
    half_dim = values.shape[-1] // 2
    turned = jnp.concatenate([-values[..., half_dim:], values[..., :half_dim]], axis=-1)
    return values * cos_tab[:, None, :] + turned * sine_tab[:, None, :]


def rotate_back(upstream, cos_tab, sine_tab):
    half_dim = upstream.shape[-1] // 2
    scaled = upstream * sine_tab[:, None, :]
    return upstream * cos_tab[:, None, :] + jnp.concatenate(
        [scaled[..., half_dim:], -scaled[..., :half_dim]], axis=-1
    )


def rms_norm(values, gain_vec):
    inv_rms = lax.rsqrt(jnp.mean(values * values, axis=-1, keepdims=True) + RMS_EPS)
    return (values * inv_rms * gain_vec, inv_rms)


def rms_back(values, inv_rms, gain_vec, upstream):
    weighted = upstream * gain_vec
    inner_mean = jnp.mean(weighted * values, axis=-1, keepdims=True)
    return (
        inv_rms * weighted - values * inv_rms * inv_rms * inv_rms * inner_mean,
        jnp.sum(upstream * values * inv_rms, axis=0),
    )


def swiglu(pre_act, split_at):
    return jax.nn.silu(pre_act[..., :split_at]) * pre_act[..., split_at:]


def swiglu_back(pre_act, split_at, upstream):
    gate_part = pre_act[..., :split_at]
    up_part = pre_act[..., split_at:]
    sigmoid_g = jax.nn.sigmoid(gate_part)
    d_gate = upstream * up_part * sigmoid_g * (1.0 + gate_part * (1.0 - sigmoid_g))
    d_up = upstream * gate_part * sigmoid_g
    return jnp.concatenate([d_gate, d_up], axis=-1)


def local(
    tokens,
    segments,
    routes,
    cotangent,
    w_qkv,
    b_qkv,
    w_out,
    gain_attn,
    gain_ffn,
    w_router,
    w_shared_gate,
    w_shared_in,
    w_shared_out,
    w_expert_in,
    w_expert_out,
):
    block_len = tokens.shape[2]
    model_width = tokens.shape[3]
    token_count = 2 * block_len
    top_count = routes.shape[3]
    half_len = segments.shape[2]
    seq_len = 2 * half_len
    ctx_index = lax.axis_index("ctx")
    head_count = model_width // HD
    expert_count = w_router.shape[1]
    capacity = token_count * top_count // expert_count
    slot_count = expert_count * capacity
    key_rows = min(512, seq_len)
    key_blocks = seq_len // key_rows
    score_scale = HD ** (-0.5)
    head_shape = (token_count, head_count, HD)
    attn_set = (
        lax.all_gather(w_qkv, ("ctx", "fsdp"), axis=0, tiled=True),
        lax.all_gather(b_qkv, ("ctx", "fsdp"), axis=0, tiled=True),
        lax.all_gather(w_out, ("ctx", "fsdp"), axis=0, tiled=True),
        lax.all_gather(gain_attn, ("ctx", "fsdp"), axis=0, tiled=True),
    )
    qkv_weight, qkv_bias, out_weight, attn_gain = attn_set
    inputs = tokens.reshape(token_count, model_width).astype(jnp.float32)
    normed, inv_one = rms_norm(inputs, attn_gain.astype(jnp.float32))
    normed_low = normed.astype(jnp.bfloat16)
    projected = jnp.dot(
        normed_low, qkv_weight, preferred_element_type=jnp.float32
    ) + qkv_bias.astype(jnp.float32)
    local_index = jnp.arange(block_len, dtype=jnp.int32)
    query_pos = jnp.concatenate(
        [ctx_index * block_len + local_index, seq_len - (ctx_index + 1) * block_len + local_index]
    )
    half_index = jnp.arange(half_len, dtype=jnp.int32)
    key_pos = jnp.concatenate(
        [half_index, seq_len - block_len * (half_index // block_len + 1) + half_index % block_len]
    ).reshape(key_blocks, key_rows)
    key_seg = segments.reshape(key_blocks, key_rows)
    query_seg = lax.dynamic_slice_in_dim(segments[0], ctx_index * block_len, block_len, 1).reshape(
        token_count
    )
    cos_tab, sine_tab = rope_tables(query_pos, HD)
    queries = rotate(projected[:, :model_width].reshape(head_shape), cos_tab, sine_tab).astype(
        jnp.bfloat16
    )
    keys_own = rotate(
        projected[:, model_width : 2 * model_width].reshape(head_shape), cos_tab, sine_tab
    ).astype(jnp.bfloat16)
    values_own = projected[:, 2 * model_width :].astype(jnp.bfloat16)
    keys_all, values_all = (
        lax.all_gather(keys_own.reshape(2, block_len, model_width), "ctx", axis=1, tiled=True),
        lax.all_gather(values_own.reshape(2, block_len, model_width), "ctx", axis=1, tiled=True),
    )
    keys_all = keys_all.reshape(key_blocks, key_rows, head_count, HD)
    values_all = values_all.reshape(key_blocks, key_rows, head_count, HD)

    def score_block(key_blk, pos_blk, seg_blk):
        raw_scores = (
            jnp.einsum("qhd,khd->hqk", queries, key_blk, preferred_element_type=jnp.float32)
            * score_scale
        )
        allowed = (pos_blk[None, :] <= query_pos[:, None]) & (
            seg_blk[None, :] == query_seg[:, None]
        )
        return (jnp.where(allowed[None], raw_scores, MASK_FILL), allowed)

    def total_step(running, key_part):
        run_max, run_sum = running
        scores = score_block(key_part[0], key_part[1], key_part[2])[0]
        new_max = jnp.maximum(run_max, jnp.max(scores, axis=-1))
        run_sum = run_sum * jnp.exp(run_max - new_max) + jnp.sum(
            jnp.exp(scores - new_max[..., None]), axis=-1
        )
        return ((new_max, run_sum), None)

    start_max = jnp.full((head_count, token_count), MASK_FILL, jnp.float32)
    start_sum = jnp.zeros((head_count, token_count), jnp.float32)
    (run_max, run_sum), unused = lax.scan(
        total_step, (start_max, start_sum), (keys_all, key_pos, key_seg)
    )
    log_total = run_max + jnp.log(run_sum)

    def attend_step(summed, key_part):
        key_blk, value_blk, pos_blk, seg_blk = key_part
        scores = score_block(key_blk, pos_blk, seg_blk)[0]
        weights = jnp.exp(scores - log_total[..., None]).astype(jnp.bfloat16)
        return (
            summed
            + jnp.einsum("hqk,khd->qhd", weights, value_blk, preferred_element_type=jnp.float32),
            None,
        )

    key_stack = (keys_all, values_all, key_pos, key_seg)
    attended, unused = lax.scan(attend_step, jnp.zeros(head_shape, jnp.float32), key_stack)
    attn_low = attended.reshape(token_count, model_width).astype(jnp.bfloat16)
    residual = inputs + jnp.dot(attn_low, out_weight, preferred_element_type=jnp.float32)
    ffn_set = (
        lax.all_gather(gain_ffn, ("ctx", "fsdp"), axis=0, tiled=True),
        lax.all_gather(w_router, ("ctx", "fsdp"), axis=0, tiled=True),
        lax.all_gather(w_shared_gate, ("ctx", "fsdp"), axis=0, tiled=True),
        lax.all_gather(w_shared_in, ("ctx", "fsdp"), axis=0, tiled=True),
        lax.all_gather(w_shared_out, ("ctx", "fsdp"), axis=0, tiled=True),
    )
    ffn_gain, router_weight, gate_vector, shared_in, shared_out = ffn_set
    normed_two, inv_two = rms_norm(residual, ffn_gain.astype(jnp.float32))
    low_two = normed_two.astype(jnp.bfloat16)
    logits = jnp.dot(low_two, router_weight, preferred_element_type=jnp.float32)
    router_probs = jax.nn.softmax(logits, axis=-1)
    chosen = routes.reshape(token_count, top_count)
    chosen_mask = chosen[..., None] == jnp.arange(expert_count, dtype=jnp.int32)
    gate_vals = jnp.sum(jnp.where(chosen_mask, router_probs[:, None, :], 0.0), axis=-1)
    shared_scale = jax.nn.sigmoid(jnp.dot(low_two, gate_vector, preferred_element_type=jnp.float32))
    shared_pre = jnp.dot(low_two, shared_in, preferred_element_type=jnp.float32)
    shared_hid = swiglu(shared_pre, FS).astype(jnp.bfloat16)
    shared_res = jnp.dot(shared_hid, shared_out, preferred_element_type=jnp.float32)
    pair_routes = chosen.reshape(token_count * top_count)
    expert_marks = (
        pair_routes[:, None] == jnp.arange(expert_count, dtype=jnp.int32)[None, :]
    ).astype(jnp.int32)
    pair_ranks = jnp.sum((jnp.cumsum(expert_marks, axis=0) - expert_marks) * expert_marks, axis=1)
    pair_target = jnp.where(pair_ranks < capacity, pair_routes * capacity + pair_ranks, -1)
    pair_map = pair_target[:, None] == jnp.arange(slot_count, dtype=jnp.int32)[None, :]
    pair_low = pair_map.astype(jnp.bfloat16)
    token_map = jnp.sum(
        pair_map.reshape(token_count, top_count, slot_count).astype(jnp.int32), axis=1
    ).astype(jnp.bfloat16)
    outgoing = jnp.einsum(
        "tc,td->cd", token_map, low_two, preferred_element_type=jnp.float32
    ).astype(jnp.bfloat16)
    incoming = lax.all_to_all(
        outgoing.reshape(expert_count, capacity, model_width),
        "ctx",
        split_axis=0,
        concat_axis=1,
        tiled=True,
    )
    expert_in, expert_out = (
        lax.all_gather(w_expert_in, "fsdp", axis=1, tiled=True),
        lax.all_gather(w_expert_out, "fsdp", axis=1, tiled=True),
    )
    expert_pre = jnp.einsum("erd,edf->erf", incoming, expert_in, preferred_element_type=jnp.float32)
    expert_hid = swiglu(expert_pre, FE).astype(jnp.bfloat16)
    expert_res = jnp.einsum(
        "erf,efd->erd", expert_hid, expert_out, preferred_element_type=jnp.float32
    ).astype(jnp.bfloat16)
    returned = lax.all_to_all(expert_res, "ctx", split_axis=1, concat_axis=0, tiled=True).reshape(
        slot_count, model_width
    )
    pair_vals = jnp.dot(pair_low, returned, preferred_element_type=jnp.float32).reshape(
        token_count, top_count, model_width
    )
    routed = jnp.sum(gate_vals[..., None] * pair_vals, axis=1)
    output = (
        (residual + shared_scale[:, None] * shared_res + routed)
        .astype(jnp.bfloat16)
        .reshape(tokens.shape)
    )
    grad_out = cotangent.reshape(token_count, model_width).astype(jnp.float32)
    pair_grads = gate_vals[..., None] * grad_out[:, None, :]
    grad_gates = jnp.sum(grad_out[:, None, :] * pair_vals, axis=-1)
    grad_returned = jnp.einsum(
        "pc,pd->cd",
        pair_map.astype(jnp.float32),
        pair_grads.reshape(token_count * top_count, model_width),
        precision=HIGHEST,
    ).astype(jnp.bfloat16)
    grad_res = lax.all_to_all(
        grad_returned.reshape(expert_count, capacity, model_width),
        "ctx",
        split_axis=0,
        concat_axis=1,
        tiled=True,
    )
    grad_expert_out = jnp.einsum(
        "erf,erd->efd", expert_hid, grad_res, preferred_element_type=jnp.float32
    )
    grad_hid = jnp.einsum("erd,efd->erf", grad_res, expert_out, preferred_element_type=jnp.float32)
    grad_pre = swiglu_back(expert_pre, FE, grad_hid).astype(jnp.bfloat16)
    grad_expert_in = jnp.einsum(
        "erd,erf->edf", incoming, grad_pre, preferred_element_type=jnp.float32
    )
    grad_incoming = jnp.einsum(
        "erf,edf->erd", grad_pre, expert_in, preferred_element_type=jnp.float32
    ).astype(jnp.bfloat16)
    grad_outgoing = lax.all_to_all(
        grad_incoming, "ctx", split_axis=1, concat_axis=0, tiled=True
    ).reshape(slot_count, model_width)
    expert_grads = (
        lax.psum_scatter(
            grad_expert_in.astype(jnp.bfloat16), "fsdp", scatter_dimension=1, tiled=True
        ).astype(jnp.float32),
        lax.psum_scatter(
            grad_expert_out.astype(jnp.bfloat16), "fsdp", scatter_dimension=1, tiled=True
        ).astype(jnp.float32),
    )
    grad_two = jnp.einsum("tc,cd->td", token_map, grad_outgoing, preferred_element_type=jnp.float32)
    grad_probs = jnp.sum(jnp.where(chosen_mask, grad_gates[..., None], 0.0), axis=1)
    grad_logits = (
        router_probs * (grad_probs - jnp.sum(router_probs * grad_probs, axis=-1, keepdims=True))
    ).astype(jnp.bfloat16)
    grad_router = jnp.einsum("td,te->de", low_two, grad_logits, preferred_element_type=jnp.float32)
    grad_shared_res = (shared_scale[:, None] * grad_out).astype(jnp.bfloat16)
    grad_gate_pre = (
        jnp.sum(grad_out * shared_res, axis=-1) * shared_scale * (1.0 - shared_scale)
    ).astype(jnp.bfloat16)
    grad_shared_out = jnp.einsum(
        "tf,td->fd", shared_hid, grad_shared_res, preferred_element_type=jnp.float32
    )
    grad_shared_hid = jnp.einsum(
        "td,fd->tf", grad_shared_res, shared_out, preferred_element_type=jnp.float32
    )
    grad_shared_pre = swiglu_back(shared_pre, FS, grad_shared_hid).astype(jnp.bfloat16)
    grad_shared_in = jnp.einsum(
        "td,tf->df", low_two, grad_shared_pre, preferred_element_type=jnp.float32
    )
    grad_gate_vector = jnp.einsum(
        "td,t->d", low_two, grad_gate_pre, preferred_element_type=jnp.float32
    )
    grad_two = grad_two + jnp.einsum(
        "te,de->td", grad_logits, router_weight, preferred_element_type=jnp.float32
    )
    grad_two = grad_two + jnp.einsum(
        "tf,df->td", grad_shared_pre, shared_in, preferred_element_type=jnp.float32
    )
    grad_two = (
        grad_two
        + grad_gate_pre.astype(jnp.float32)[:, None] * gate_vector.astype(jnp.float32)[None, :]
    )
    grad_resid_norm, grad_gain_two = rms_back(
        residual, inv_two, ffn_gain.astype(jnp.float32), grad_two
    )
    grad_resid = grad_out + grad_resid_norm
    ffn_grads = (
        lax.psum_scatter(grad_gain_two, ("ctx", "fsdp"), scatter_dimension=0, tiled=True),
        lax.psum_scatter(grad_router, ("ctx", "fsdp"), scatter_dimension=0, tiled=True),
        lax.psum_scatter(grad_gate_vector, ("ctx", "fsdp"), scatter_dimension=0, tiled=True),
        lax.psum_scatter(grad_shared_in, ("ctx", "fsdp"), scatter_dimension=0, tiled=True),
        lax.psum_scatter(grad_shared_out, ("ctx", "fsdp"), scatter_dimension=0, tiled=True),
    )
    grad_mixed = grad_resid.astype(jnp.bfloat16)
    grad_out_weight = jnp.einsum(
        "tc,td->cd", attn_low, grad_mixed, preferred_element_type=jnp.float32
    )
    grad_attn = (
        jnp.einsum("td,cd->tc", grad_mixed, out_weight, preferred_element_type=jnp.float32)
        .astype(jnp.bfloat16)
        .reshape(head_shape)
    )

    def delta_step(summed, key_part):
        key_blk, value_blk, pos_blk, seg_blk = key_part
        weights = jnp.exp(score_block(key_blk, pos_blk, seg_blk)[0] - log_total[..., None])
        grad_weights = jnp.einsum(
            "qhd,khd->hqk", grad_attn, value_blk, preferred_element_type=jnp.float32
        )
        return (summed + jnp.sum(weights * grad_weights, axis=-1), None)

    delta_sum, unused = lax.scan(
        delta_step, jnp.zeros((head_count, token_count), jnp.float32), key_stack
    )

    def grad_step(summed, key_part):
        key_blk, value_blk, pos_blk, seg_blk = key_part
        scores, allowed = score_block(key_blk, pos_blk, seg_blk)
        weights = jnp.exp(scores - log_total[..., None])
        grad_weights = jnp.einsum(
            "qhd,khd->hqk", grad_attn, value_blk, preferred_element_type=jnp.float32
        )
        grad_scores = jnp.where(
            allowed[None], weights * (grad_weights - delta_sum[..., None]), 0.0
        ).astype(jnp.bfloat16)
        summed = (
            summed
            + jnp.einsum("hqk,khd->qhd", grad_scores, key_blk, preferred_element_type=jnp.float32)
            * score_scale
        )
        grad_key = (
            jnp.einsum("hqk,qhd->khd", grad_scores, queries, preferred_element_type=jnp.float32)
            * score_scale
        )
        grad_value = jnp.einsum(
            "hqk,qhd->khd",
            weights.astype(jnp.bfloat16),
            grad_attn,
            preferred_element_type=jnp.float32,
        )
        return (summed, (grad_key, grad_value))

    grad_query, (grad_keys, grad_values) = lax.scan(
        grad_step, jnp.zeros(head_shape, jnp.float32), key_stack
    )
    grad_keys_own, grad_values_own = (
        lax.psum_scatter(
            grad_keys.reshape(2, half_len, model_width).astype(jnp.bfloat16),
            "ctx",
            scatter_dimension=1,
            tiled=True,
        ).astype(jnp.float32),
        lax.psum_scatter(
            grad_values.reshape(2, half_len, model_width).astype(jnp.bfloat16),
            "ctx",
            scatter_dimension=1,
            tiled=True,
        ).astype(jnp.float32),
    )
    grad_q_rows = rotate_back(grad_query, cos_tab, sine_tab).reshape(token_count, model_width)
    grad_k_rows = rotate_back(grad_keys_own.reshape(head_shape), cos_tab, sine_tab).reshape(
        token_count, model_width
    )
    grad_projected = jnp.concatenate(
        [grad_q_rows, grad_k_rows, grad_values_own.reshape(token_count, model_width)], axis=-1
    ).astype(jnp.bfloat16)
    grad_qkv_weight = jnp.einsum(
        "td,te->de", normed_low, grad_projected, preferred_element_type=jnp.float32
    )
    grad_qkv_bias = jnp.sum(grad_projected.astype(jnp.float32), axis=0)
    grad_normed = jnp.einsum(
        "te,de->td", grad_projected, qkv_weight, preferred_element_type=jnp.float32
    )
    grad_inputs_norm, grad_gain_one = rms_back(
        inputs, inv_one, attn_gain.astype(jnp.float32), grad_normed
    )
    grad_tokens = (grad_resid + grad_inputs_norm).reshape(tokens.shape)
    attn_grads = (
        lax.psum_scatter(grad_qkv_weight, ("ctx", "fsdp"), scatter_dimension=0, tiled=True),
        lax.psum_scatter(grad_qkv_bias, ("ctx", "fsdp"), scatter_dimension=0, tiled=True),
        lax.psum_scatter(grad_out_weight, ("ctx", "fsdp"), scatter_dimension=0, tiled=True),
        lax.psum_scatter(grad_gain_one, ("ctx", "fsdp"), scatter_dimension=0, tiled=True),
    )
    return (
        output,
        grad_tokens,
        attn_grads[0],
        attn_grads[1],
        attn_grads[2],
        attn_grads[3],
        ffn_grads[0],
        ffn_grads[1],
        ffn_grads[2],
        ffn_grads[3],
        ffn_grads[4],
        expert_grads[0],
        expert_grads[1],
    )


def solution(mesh):
    in_specs = (
        P("fsdp", None, "ctx", None),
        P("fsdp", None, None),
        P("fsdp", None, "ctx", None),
        P("fsdp", None, "ctx", None),
        P(("ctx", "fsdp"), None),
        P(("ctx", "fsdp")),
        P(("ctx", "fsdp"), None),
        P(("ctx", "fsdp")),
        P(("ctx", "fsdp")),
        P(("ctx", "fsdp"), None),
        P(("ctx", "fsdp")),
        P(("ctx", "fsdp"), None),
        P(("ctx", "fsdp"), None),
        P("ctx", "fsdp", None),
        P("ctx", "fsdp", None),
    )
    out_specs = (
        P("fsdp", None, "ctx", None),
        P("fsdp", None, "ctx", None),
        P(("ctx", "fsdp"), None),
        P(("ctx", "fsdp")),
        P(("ctx", "fsdp"), None),
        P(("ctx", "fsdp")),
        P(("ctx", "fsdp")),
        P(("ctx", "fsdp"), None),
        P(("ctx", "fsdp")),
        P(("ctx", "fsdp"), None),
        P(("ctx", "fsdp"), None),
        P("ctx", "fsdp", None),
        P("ctx", "fsdp", None),
    )
    return jax.shard_map(local, mesh=mesh, in_specs=in_specs, out_specs=out_specs, check_vma=False)
```

profile of v0, /device:TPU:8, one launch (start us, length us, event | category | flops | bytes accessed | tf_op | source)
XLA Modules:
  0.0 3815.4 jit_solution(16514937621037915840)
XLA Ops:
  11.4 42.7 %all-reduce.11 = (bf16[2048]{0:T(1024)(128)(2,1)S(1)}, bf16[6144]{0:T(1024)(128)(2,1)S(1)}, bf16[2048]{0:T(1024)(128)(2,1)S(1)}, bf16[2048]{0:T(1024)(128)(2,1)S(1)}) all-reduce(bf16[2048]{0:T(1024)(128)(2,1)S(1)} %dynamic-update-slice, bf16[6144]{0:T(1024)(128)(2,1)S(1)} %dynamic-update-slice.1, ...), channel_id=1, replica_groups=mesh['ctx'=8,'fsdp'=4] {'ctx','fsdp'}, use_global_device_ids=true, to_apply=%add | all-reduce | flops 12288 | bytes 49152
  58.3 108.0 %all-gather.10.cloned.1.call-done = bf16[2048,6144]{1,0:T(8,128)(2,1)} async-done(((bf16[64,6144]{1,0:T(8,128)(2,1)}), bf16[2048,6144]{1,0:T(8,128)(2,1)}) %all-gather.10.cloned.1.call-update) | async-done | bytes 25165840 | tf_op jit(solution)/shard_map/all_gather | solution.py:100
  193.5 65.3 %all-gather.14.cloned.1.call-done = bf16[2,512,2048]{2,1,0:T(8,128)(2,1)} async-done(((bf16[2,64,2048]{2,1,0:T(8,128)(2,1)}), bf16[2,512,2048]{2,1,0:T(8,128)(2,1)}) %all-gather.14.cloned.1.call-update) | async-done | bytes 4194320 | tf_op jit(solution)/shard_map/all_gather | solution.py:133
  271.3 61.9 %all-gather.12.cloned.1.call-done = bf16[2,512,2048]{2,0,1:T(2,128)(2,1)} async-done(((bf16[2,64,2048]{2,0,1:T(2,128)(2,1)}), bf16[2,512,2048]{2,0,1:T(2,128)(2,1)}) %all-gather.12.cloned.1.call-update) | async-done | bytes 4194320 | tf_op jit(solution)/shard_map/all_gather | solution.py:134
  344.4 15.4 while.54
  373.8 38.6 %all-gather.16.cloned.1.call-done = bf16[2048,2048]{1,0:T(8,128)(2,1)} async-done(((bf16[64,2048]{1,0:T(8,128)(2,1)}), bf16[2048,2048]{1,0:T(8,128)(2,1)}) %all-gather.16.cloned.1.call-update) | async-done | bytes 8388624 | tf_op jit(solution)/shard_map/all_gather | solution.py:102
  432.7 63.3 %all-gather = bf16[32,64,8]{1,2,0:T(8,128)(2,1)S(1)} all-gather(bf16[1,64,8]{1,2,0:T(8,128)(2,1)S(1)} %bitcast.483), channel_id=1, replica_groups=mesh['ctx'=8,'fsdp'=4] {'ctx','fsdp'}, dimensions={0}, use_global_device_ids=true | all-gather | bytes 33792 | tf_op jit(solution)/shard_map/all_gather | solution.py:181
  511.7 12.6 fusion.77
  534.2 48.5 %all-to-all-done.2 = bf16[8,64,2048]{2,1,0:T(8,128)(2,1)} async-done(((bf16[8,64,2048]{2,1,0:T(8,128)(2,1)}), bf16[8,64,2048]{2,1,0:T(8,128)(2,1)}, u32[]{:S(2)}, u32[]{:S(2)}) %all-to-all-start.2) | async-done | bytes 2097184 | tf_op jit(solution)/shard_map/all_to_all | solution.py:249
  605.3 14.5 reduce.3
  647.8 14.5 reduce.4
  668.5 40.4 %all-to-all-done.3 = bf16[8,2,65536]{2,1,0:T(2,128)(2,1)} async-done(((bf16[8,2,65536]{2,1,0:T(2,128)(2,1)}), bf16[8,2,65536]{2,1,0:T(2,128)(2,1)}, u32[]{:S(2)}, u32[]{:S(2)}) %all-to-all-start.3) | async-done | bytes 2097184 | tf_op jit(solution)/shard_map/all_to_all | solution.py:267
  733.9 81.3 %all-to-all-done.1 = bf16[8,2,65536]{2,1,0:T(2,128)(2,1)} async-done(((bf16[8,2,65536]{2,1,0:T(2,128)(2,1)}), bf16[8,2,65536]{2,1,0:T(2,128)(2,1)}, u32[]{:S(2)}, u32[]{:S(2)}) %all-to-all-start.1) | async-done | bytes 2097184 | tf_op jit(solution)/shard_map/all_to_all | solution.py:228
  830.9 40.4 %all-gather.18.cloned.1.call-done = bf16[2048,11264]{1,0:T(8,128)(2,1)} async-done(((bf16[64,11264]{1,0:T(8,128)(2,1)}), bf16[2048,11264]{1,0:T(8,128)(2,1)}) %all-gather.18.cloned.1.call-update) | async-done | bytes 46137360 | tf_op jit(solution)/shard_map/all_gather | solution.py:183
  871.2 19.9 fusion.177
  891.1 132.3 %all-gather.20.cloned.1.call-done = bf16[5632,2048]{1,0:T(8,128)(2,1)} async-done(((bf16[176,2048]{1,0:T(8,128)(2,1)}), bf16[5632,2048]{1,0:T(8,128)(2,1)}) %all-gather.20.cloned.1.call-update) | async-done | bytes 23068688 | tf_op jit(solution)/shard_map/all_gather | solution.py:184
  1023.5 15.1 multiply_convert_fusion.1
  1050.9 21.4 fusion.110
  1091.2 49.2 %while.57 = (s32[]{:T(128)}, f32[128,16,128]{0,2,1:T(8,128)}, bf16[2,512,16,128]{1,3,2,0:T(8,128)(2,1)}, bf16[2,512,16,128]{1,3,2,0:T(8,128)(2,1)}, bf16[2,512,1...) while((s32[]{:T(128)}, f32[128,16,128]{0,2,1:T(8,128)}, ...), condition=%wide.wide.region_25.26_spmd.clone, body=%wide.wide.region_24.25_spmd.clone.sunk | while | flops 1356791808 | bytes 109286720 | solution.py:371
  1197.9 234.6 %all-reduce.15.cloned.1.call-done = (bf16[2,512,2048]{2,0,1:T(2,128)(2,1)}, bf16[2,512,2048]{2,0,1:T(2,128)(2,1)}) async-done(((bf16[2,512,2048]{2,0,1:T(2,128)(2,1)}, bf16[2,512,2048]{2,0,1:T(2,128)(2,1)}), (bf16[2,512,2048]{2,0,1:T(2,128)(2,1)}, bf16[2,512,2048]{2,0,1:T(2,128)(2,1)})) %all-reduce.15.cloned.1.call-update) | async-done | bytes 8388624
  1439.5 20.8 fusion.169
  1461.4 19.3 fusion.142
  1480.8 34.0 fusion.109
  1514.8 37.3 reduce-scatter.22.cloned.1.call-done
  1553.6 71.4 %reduce-scatter.20.cloned.1.call-done = bf16[1,352,2048]{2,1,0:T(8,128)(2,1)} async-done(((bf16[1,1408,2048]{2,1,0:T(8,128)(2,1)}), bf16[1,352,2048]{2,1,0:T(8,128)(2,1)}) %reduce-scatter.20.cloned.1.call-update) | async-done | bytes 1441808 | tf_op jit(solution)/shard_map/reduce_scatter | solution.py:274
  1628.2 91.4 %reduce-scatter.18.cloned.1.call-done = bf16[1,512,2816]{2,1,0:T(8,128)(2,1)} async-done(((bf16[1,2048,2816]{2,1,0:T(8,128)(2,1)}), bf16[1,512,2816]{2,1,0:T(8,128)(2,1)}) %reduce-scatter.18.cloned.1.call-update) | async-done | bytes 2883600 | tf_op jit(solution)/shard_map/reduce_scatter | solution.py:271
  1724.9 14.5 fusion.126
  1739.4 42.5 %all-reduce.10 = (f32[6144]{0:T(1024)S(1)}, f32[2048]{0:T(1024)S(1)}, f32[2048]{0:T(1024)S(1)}, f32[2048]{0:T(1024)S(1)}) all-reduce(f32[6144]{0:T(1024)S(1)} %convert_reduce_fusion, f32[2048]{0:T(1024)S(1)} %get-tuple-element.619, f32[2048]{0:T(1024)S(1)} %copy-done.47, ...), channel_id=5, replica_groups=mesh['ctx'=8,'fsdp'=4] {'ctx','fsdp'}, use_global_device_ids=true, to_apply=%region_31.32.clone | all-reduce | flops 12288 | bytes 98304
  1786.9 116.3 %reduce-scatter.12.cloned.1.call-done = f32[64,2048]{1,0:T(8,128)} async-done(((f32[2048,2048]{1,0:T(8,128)}), f32[64,2048]{1,0:T(8,128)}) %reduce-scatter.12.cloned.1.call-update) | async-done | bytes 524304 | tf_op jit(solution)/shard_map/reduce_scatter | solution.py:409
  1903.2 442.1 %reduce-scatter.10.cloned.1.call-done = f32[64,6144]{1,0:T(8,128)} async-done(((f32[2048,6144]{1,0:T(8,128)}), f32[64,6144]{1,0:T(8,128)}) %reduce-scatter.10.cloned.1.call-update) | async-done | bytes 1572880 | tf_op jit(solution)/shard_map/reduce_scatter | solution.py:407
  2345.3 488.4 %reduce-scatter.16.cloned.1.call-done = f32[176,2048]{1,0:T(8,128)} async-done(((f32[5632,2048]{1,0:T(8,128)}), f32[176,2048]{1,0:T(8,128)}) %reduce-scatter.16.cloned.1.call-update) | async-done | bytes 1441808 | tf_op jit(solution)/shard_map/reduce_scatter | solution.py:320
  2833.6 974.8 %reduce-scatter.14.cloned.1.call-done = f32[64,11264]{1,0:T(8,128)} async-done(((f32[2048,11264]{1,0:T(8,128)}), f32[64,11264]{1,0:T(8,128)}) %reduce-scatter.14.cloned.1.call-update) | async-done | bytes 2883600 | tf_op jit(solution)/shard_map/reduce_scatter | solution.py:319
  (385 shorter events, 409.5 us)
Async XLA Ops:
  7.2 159.2 %all-gather.10.cloned.1.call-start = ((), (), s32[]{:S(2)}) async-start(), calls=%async_computation.11 | async-start | bytes 25952256 | tf_op jit(solution)/shard_map/all_gather | solution.py:100
  7.9 250.9 %all-gather.14.cloned.1.call-start = ((), (), s32[]{:S(2)}) async-start(), calls=%async_computation.13 | async-start | bytes 4718592 | tf_op jit(solution)/shard_map/all_gather | solution.py:133
  55.4 121.1 %copy-start.56 = (f32[128]{0:T(128)}, f32[128]{0:T(128)S(1)}, u32[]{:S(2)}) copy-start(f32[128]{0:T(128)S(1)} %rsqrt.20) | copy-start | bytes 1540
  55.9 123.0 %copy-start.28 = (f32[128,128]{1,0:T(8,128)}, f32[128,128]{1,0:T(8,128)S(1)}, u32[]{:S(2)}) copy-start(f32[128,128]{1,0:T(8,128)S(1)} %pad_maximum_fusion.8) | copy-start | bytes 196612
  57.4 121.6 %copy-start.31 = (f32[128,128]{1,0:T(8,128)}, f32[128,128]{1,0:T(8,128)S(1)}, u32[]{:S(2)}) copy-start(f32[128,128]{1,0:T(8,128)S(1)} %pad_maximum_fusion.9) | copy-start | bytes 196612
  185.9 147.3 %all-gather.12.cloned.1.call-start = ((), (), s32[]{:S(2)}) async-start(), calls=%async_computation.12 | async-start | bytes 4718592 | tf_op jit(solution)/shard_map/all_gather | solution.py:134
  187.4 225.0 %all-gather.16.cloned.1.call-start = ((), (), s32[]{:S(2)}) async-start(), calls=%async_computation.14 | async-start | bytes 8650752 | tf_op jit(solution)/shard_map/all_gather | solution.py:102
  188.0 323.7 %all-gather.22.cloned.1.call-start = ((), (), s32[]{:S(2)}) async-start(), calls=%async_computation.17 | async-start | bytes 14417920 | tf_op jit(solution)/shard_map/all_gather | solution.py:220
  188.6 345.6 %all-gather.24.cloned.1.call-start = ((), (), s32[]{:S(2)}) async-start(), calls=%async_computation.18 | async-start | bytes 7208960 | tf_op jit(solution)/shard_map/all_gather | solution.py:221
  189.2 682.1 %all-gather.18.cloned.1.call-start = ((), (), s32[]{:S(2)}) async-start(), calls=%async_computation.15 | async-start | bytes 47579136 | tf_op jit(solution)/shard_map/all_gather | solution.py:183
  189.9 833.5 %all-gather.20.cloned.1.call-start = ((), (), s32[]{:S(2)}) async-start(), calls=%async_computation.16 | async-start | bytes 23789568 | tf_op jit(solution)/shard_map/all_gather | solution.py:184
  190.8 74.3 %copy-start.61 = (s32[2,64]{1,0:T(2,128)}, s32[2,64]{1,0:T(2,128)S(1)}, u32[]{:S(2)}) copy-start(s32[2,64]{1,0:T(2,128)S(1)} %dynamic-slice_bitcast_fusion) | copy-start | bytes 1540
  417.4 453.9 %copy-start.6 = (bf16[128,2048]{1,0:T(8,128)(2,1)}, bf16[128,2048]{1,0:T(8,128)(2,1)S(1)}, u32[]{:S(2)}) copy-start(bf16[128,2048]{1,0:T(8,128)(2,1)S(1)} %multiply_convert_fusion.7) | copy-start | bytes 1572868
  419.4 86.1 %all-to-all-start = ((bf16[8,64,2048]{2,1,0:T(8,128)(2,1)}), bf16[8,64,2048]{2,1,0:T(8,128)(2,1)}, u32[]{:S(2)}, u32[]{:S(2)}) async-start(bf16[8,64,2048]{2,1,0:T(8,128)(2,1)} %bitcast.453), calls=%async_computation | async-start | bytes 4194304 | tf_op jit(solution)/shard_map/all_to_all | solution.py:212
  505.6 77.0 %all-to-all-start.2 = ((bf16[8,64,2048]{2,1,0:T(8,128)(2,1)}), bf16[8,64,2048]{2,1,0:T(8,128)(2,1)}, u32[]{:S(2)}, u32[]{:S(2)}) async-start(bf16[8,64,2048]{2,1,0:T(8,128)(2,1)} %bitcast.469), calls=%async_computation.2 | async-start | bytes 4194304 | tf_op jit(solution)/shard_map/all_to_all | solution.py:249
  626.1 82.9 %all-to-all-start.3 = ((bf16[8,2,65536]{2,1,0:T(2,128)(2,1)}), bf16[8,2,65536]{2,1,0:T(2,128)(2,1)}, u32[]{:S(2)}, u32[]{:S(2)}) async-start(bf16[8,2,65536]{2,1,0:T(2,128)(2,1)} %reshape.603), calls=%async_computation.3 | async-start | bytes 4194304 | tf_op jit(solution)/shard_map/all_to_all | solution.py:267
  662.2 56.5 %copy-start.62 = (s32[2,64]{1,0:T(2,128)S(1)}, s32[2,64]{1,0:T(2,128)}, u32[]{:S(2)}) copy-start(s32[2,64]{1,0:T(2,128)} %get-tuple-element.1525) | copy-start | bytes 1540
  709.0 106.3 %all-to-all-start.1 = ((bf16[8,2,65536]{2,1,0:T(2,128)(2,1)}), bf16[8,2,65536]{2,1,0:T(2,128)(2,1)}, u32[]{:S(2)}, u32[]{:S(2)}) async-start(bf16[8,2,65536]{2,1,0:T(2,128)(2,1)} %reshape.601), calls=%async_computation.1 | async-start | bytes 4194304 | tf_op jit(solution)/shard_map/all_to_all | solution.py:228
  717.1 715.5 %all-reduce.15.cloned.1.call-start = ((), (), s32[]{:S(2)}) async-start(), calls=%async_computation.26 | async-start | bytes 16777216
  1163.2 388.9 %reduce-scatter.22.cloned.1.call-start = ((), (), s32[]{:S(2)}) async-start(), calls=%async_computation.25 | async-start | bytes 1081344
  1165.5 459.4 %reduce-scatter.20.cloned.1.call-start = ((), (), s32[]{:S(2)}) async-start(), calls=%async_computation.24 | async-start | bytes 7208960 | tf_op jit(solution)/shard_map/reduce_scatter | solution.py:274
  1172.9 546.6 %reduce-scatter.18.cloned.1.call-start = ((), (), s32[]{:S(2)}) async-start(), calls=%async_computation.23 | async-start | bytes 14417920 | tf_op jit(solution)/shard_map/reduce_scatter | solution.py:271
  1185.1 718.1 %reduce-scatter.12.cloned.1.call-start = ((), (), s32[]{:S(2)}) async-start(), calls=%async_computation.20 | async-start | bytes 17301504 | tf_op jit(solution)/shard_map/reduce_scatter | solution.py:409
  1194.6 1150.6 %reduce-scatter.10.cloned.1.call-start = ((), (), s32[]{:S(2)}) async-start(), calls=%async_computation.19 | async-start | bytes 51904512 | tf_op jit(solution)/shard_map/reduce_scatter | solution.py:407
  1196.5 239.4 %copy-start.32 = (f32[128,128]{1,0:T(8,128)S(1)}, f32[128,128]{1,0:T(8,128)}, u32[]{:S(2)}) copy-start(f32[128,128]{1,0:T(8,128)} %copy-done.31) | copy-start | bytes 196612
  1197.9 238.0 %copy-start.16 = (f32[128,16,128]{2,1,0:T(8,128)S(1)}, f32[128,16,128]{2,1,0:T(8,128)}, u32[]{:S(2)}) copy-start(f32[128,16,128]{2,1,0:T(8,128)} %copy.189) | copy-start | bytes 3145732
  1460.3 1373.3 %reduce-scatter.16.cloned.1.call-start = ((), (), s32[]{:S(2)}) async-start(), calls=%async_computation.22 | async-start | bytes 47579136 | tf_op jit(solution)/shard_map/reduce_scatter | solution.py:320
  1480.7 2327.7 %reduce-scatter.14.cloned.1.call-start = ((), (), s32[]{:S(2)}) async-start(), calls=%async_computation.21 | async-start | bytes 95158272 | tf_op jit(solution)/shard_map/reduce_scatter | solution.py:319
  1628.2 96.2 %copy-start.60 = (f32[128]{0:T(128)S(1)}, f32[128]{0:T(128)}, u32[]{:S(2)}) copy-start(f32[128]{0:T(128)} %copy-done.59) | copy-start | bytes 1540
  1628.2 96.7 %copy-start.19 = (bf16[1,2,64,2048]{3,2,1,0:T(8,128)(2,1)S(1)}, bf16[1,2,64,2048]{3,2,1,0:T(8,128)(2,1)}, u32[]{:S(2)}) copy-start(bf16[1,2,64,2048]{3,2,1,0:T(8,128)(2,1)} %param.23) | copy-start | bytes 1572868
  1628.2 96.7 %copy-start.45 = (f32[2048]{0:T(1024)S(1)}, f32[2048]{0:T(1024)}, u32[]{:S(2)}) copy-start(f32[2048]{0:T(1024)} %copy-done.44) | copy-start | bytes 24580
  1628.2 96.7 %copy-start.57 = (f32[128]{0:T(128)S(1)}, f32[128]{0:T(128)}, u32[]{:S(2)}) copy-start(f32[128]{0:T(128)} %copy-done.56) | copy-start | bytes 1540
  (62 other events, 572.6 us)
Sparse Core Ops, SparseCore 0:
  10.9 155.4 all-gather.9
  186.0 72.7 all-gather.13
  261.5 71.6 all-gather.11
  336.0 76.3 all-gather.15
  413.8 75.2 all-gather.21
  490.5 43.6 all-gather.23
  537.0 334.1 all-gather.17
  874.1 149.3 all-gather.19
  1163.3 269.1 all-reduce.14
  1435.2 116.8 reduce-scatter.21
  1555.4 69.4 reduce-scatter.19
  1627.4 92.1 reduce-scatter.17
  1722.4 180.7 reduce-scatter.11
  1910.1 435.1 reduce-scatter.9
  2348.0 485.5 reduce-scatter.15
  2836.4 971.9 reduce-scatter.13
where the time goes:
time: 3830 us; the launch traced here: 3820 us
  waiting for transfers between devices  3090 us (81%)
  matrix products  315 us (8%)
  local copies, waits for them, and re-layouts  154 us (4%)
  blocking collectives  149 us (4%)
  other arithmetic  64.8 us (2%)
    reduce_scatter x1, waiting for transfers between devices, local(): lax.psum_scatter(grad_shared_in, ('ctx', 'fsdp'), scatter_dimension=0, ti...  975 us
    reduce_scatter x1, waiting for transfers between devices, local(): lax.psum_scatter(grad_shared_out, ('ctx', 'fsdp'), scatter_dimension=0, t...  488 us
    reduce_scatter x1, waiting for transfers between devices, local(): lax.psum_scatter(grad_qkv_weight, ('ctx', 'fsdp'), scatter_dimension=0, t...  442 us
    unnamed x18, waiting for transfers between devices  276 us
    all_gather x1, waiting for transfers between devices, local(): lax.all_gather(w_shared_out, ('ctx', 'fsdp'), axis=0, tiled=True)  132 us
    reduce_scatter x1, waiting for transfers between devices, local(): lax.psum_scatter(grad_out_weight, ('ctx', 'fsdp'), scatter_dimension=0, t...  116 us
    all_gather x1, waiting for transfers between devices, local(): lax.all_gather(w_qkv, ('ctx', 'fsdp'), axis=0, tiled=True)  108 us
    reduce_scatter x1, waiting for transfers between devices, local(): lax.psum_scatter(grad_expert_in.astype(jnp.bfloat16), 'fsdp', scatter_dim...  91.4 us
  transfers between devices with their start and end apart: 20, of which 18 were waited for; matrix products, arithmetic and copies ran while one was open for 10% of the time, Pallas kernels for 0%

commit v1 on v0

--- a/solution.py
+++ b/solution.py
@@ -4,6 +4,7 @@
 from jax.sharding import PartitionSpec as P
 
 HD = 128
+HEADS = 16
 FS = 5632
 FE = 1408
 
@@ -64,7 +65,386 @@
     return jnp.concatenate([d_gate, d_up], axis=-1)
 
 
-def local(
+def ring_order(size):
+    return list(range(0, size, 2)) + list(range(size - 1, 0, -2))
+
+
+def ring_steps(size):
+    order = ring_order(size)
+    ahead = [(order[i], order[(i + 1) % size]) for i in range(size)]
+    back = [(dst, src) for src, dst in ahead]
+    return (ahead, back)
+
+
+def ring_peers(size, ctx_index):
+    order = ring_order(size)
+    place = {dev: i for i, dev in enumerate(order)}
+    table = jnp.array(
+        [[order[(place[dev] + k) % size] for k in range(size)] for dev in range(size)], jnp.int32
+    )
+    row = lax.dynamic_index_in_dim(table, ctx_index, 0, keepdims=False)
+    return [row[k] for k in range(size)]
+
+
+def ring_gather(block, size, ctx_index):
+    rows = block.shape[0] // 2
+    ahead, back = ring_steps(size)
+    peers = ring_peers(size, ctx_index)
+    half = size // 2
+    halves = (block[:rows], block[rows:])
+    out = jnp.zeros((size, 2, rows) + block.shape[1:], block.dtype)
+    zero = jnp.zeros((), jnp.int32)
+
+    def put(out, piece, peer, part):
+        start = (peer, jnp.full((), part, jnp.int32)) + (zero,) * block.ndim
+        return lax.dynamic_update_slice(out, piece[None, None], start)
+
+    for part in range(2):
+        out = put(out, halves[part], ctx_index, part)
+    fore, rear = list(halves), list(halves)
+    for k in range(1, half + 1):
+        for part in (0, 1):
+            if k < half or part == 0:
+                fore[part] = lax.ppermute(fore[part], "ctx", ahead)
+                out = put(out, fore[part], peers[(size - k) % size], part)
+            if k < half or part == 1:
+                rear[part] = lax.ppermute(rear[part], "ctx", back)
+                out = put(out, rear[part], peers[k], part)
+    return out.reshape((size,) + block.shape)
+
+
+def ring_scatter(parts, size, ctx_index):
+    rows = parts.shape[1] // 2
+    ahead, back = ring_steps(size)
+    peers = ring_peers(size, ctx_index)
+    half = size // 2
+
+    def own(k, part):
+        block = lax.dynamic_index_in_dim(parts, peers[k % size], 0, keepdims=False)
+        return block[part * rows : (part + 1) * rows]
+
+    sums = []
+    for part in (0, 1):
+        total = own(0, part).astype(jnp.float32)
+        for perm, sign, first in (
+            (ahead, 1, half if part == 0 else half - 1),
+            (back, -1, half if part == 1 else half - 1),
+        ):
+            moving = own(sign * first, part)
+            for k in range(first, 0, -1):
+                moving = lax.ppermute(moving, "ctx", perm)
+                if k > 1:
+                    moving = (
+                        moving.astype(jnp.float32)
+                        + own(sign * (k - 1), part).astype(jnp.float32)
+                    ).astype(jnp.bfloat16)
+            total = total + moving.astype(jnp.float32)
+        sums.append(total)
+    return jnp.concatenate(sums, axis=0)
+
+
+def split_columns(weight, groups, size):
+    rows = weight.shape[0]
+    width = weight.shape[1] // (groups * size)
+    pieces = weight.reshape(rows, groups, size, width).transpose(2, 0, 1, 3)
+    pieces = pieces.reshape(size, rows, groups * width)
+    pieces = lax.all_to_all(pieces, "ctx", split_axis=0, concat_axis=0, tiled=True)
+    whole = lax.all_gather(pieces, "fsdp", axis=0, tiled=False)
+    return whole.transpose(1, 0, 2, 3).reshape(-1, groups * width)
+
+
+def merge_columns(grad, groups, size, fsdp_size):
+    width = grad.shape[1] // groups
+    rows = grad.shape[0] // (size * fsdp_size)
+    pieces = grad.reshape(size, fsdp_size, rows, groups * width).transpose(1, 0, 2, 3)
+    pieces = pieces.astype(jnp.bfloat16).reshape(grad.shape)
+    pieces = lax.psum_scatter(pieces, "fsdp", scatter_dimension=0, tiled=True)
+    pieces = pieces.reshape(size, rows, groups * width)
+    pieces = lax.all_to_all(pieces, "ctx", split_axis=0, concat_axis=0, tiled=True)
+    pieces = pieces.reshape(size, rows, groups, width).transpose(1, 2, 0, 3)
+    return pieces.reshape(rows, groups * size * width).astype(jnp.float32)
+
+
+def local_split(
+    ctx_size,
+    fsdp_size,
+    tokens,
+    segments,
+    routes,
+    cotangent,
+    w_qkv,
+    b_qkv,
+    w_out,
+    gain_attn,
+    gain_ffn,
+    w_router,
+    w_shared_gate,
+    w_shared_in,
+    w_shared_out,
+    w_expert_in,
+    w_expert_out,
+):
+    bf16, f32, i32 = jnp.bfloat16, jnp.float32, jnp.int32
+    axes = ("ctx", "fsdp")
+    device_count = ctx_size * fsdp_size
+    block_len = tokens.shape[2]
+    width = tokens.shape[3]
+    token_count = 2 * block_len
+    top_count = routes.shape[3]
+    seq_len = token_count * ctx_size
+    ctx_index = lax.axis_index("ctx")
+    expert_count = w_router.shape[1]
+    capacity = token_count * top_count // expert_count
+    own_heads = HEADS // ctx_size
+    own_width = own_heads * HD
+    fs_own = FS // ctx_size
+    score_scale = HD ** (-0.5)
+
+    def dot(a, b):
+        return jnp.dot(a, b, preferred_element_type=f32)
+
+    def dot_t(a, b):
+        return lax.dot_general(a, b, (((1,), (1,)), ((), ())), preferred_element_type=f32)
+
+    def t_dot(a, b):
+        return lax.dot_general(a, b, (((0,), (0,)), ((), ())), preferred_element_type=f32)
+
+    def own_rows(values):
+        return lax.dynamic_index_in_dim(
+            values.reshape((ctx_size, token_count) + values.shape[1:]), ctx_index, 0, keepdims=False
+        )
+
+    small = jnp.concatenate(
+        [gain_attn, gain_ffn, w_shared_gate, w_router.reshape(-1), b_qkv], axis=0
+    )
+    small = lax.all_gather(small, axes, axis=0, tiled=False)
+    shard = width // device_count
+    attn_gain = small[:, :shard].reshape(width).astype(f32)
+    ffn_gain = small[:, shard : 2 * shard].reshape(width).astype(f32)
+    gate_vector = small[:, 2 * shard : 3 * shard].reshape(width)
+    router_end = 3 * shard + shard * expert_count
+    router_weight = small[:, 3 * shard : router_end].reshape(width, expert_count)
+    bias = small[:, router_end:].reshape(3, ctx_size, own_width).astype(f32)
+    bias = lax.dynamic_index_in_dim(bias, ctx_index, 1, keepdims=False).reshape(3 * own_width)
+
+    token_rows = ring_gather(tokens.reshape(token_count, width), ctx_size, ctx_index)
+    token_rows = token_rows.reshape(seq_len, width)
+    qkv_weight = split_columns(w_qkv, 3, ctx_size)
+    out_weight = lax.all_gather(w_out, axes, axis=0, tiled=True)
+    shared_in = split_columns(w_shared_in, 2, ctx_size)
+    shared_out = lax.all_gather(w_shared_out, "fsdp", axis=0, tiled=True)
+    expert_in = lax.all_gather(w_expert_in[0], "fsdp", axis=0, tiled=True)
+    expert_out = lax.all_gather(w_expert_out[0], "fsdp", axis=0, tiled=True)
+    route_rows = lax.all_gather(
+        routes.reshape(token_count, top_count), "ctx", axis=0, tiled=False
+    )
+    grad_rows = ring_gather(cotangent.reshape(token_count, width), ctx_size, ctx_index)
+    grad_rows = grad_rows.reshape(seq_len, width)
+
+    block_ids = jnp.arange(ctx_size, dtype=i32)[:, None]
+    local_index = jnp.arange(block_len, dtype=i32)[None, :]
+    positions = jnp.stack(
+        [
+            block_ids * block_len + local_index,
+            seq_len - (block_ids + 1) * block_len + local_index,
+        ],
+        axis=1,
+    ).reshape(seq_len)
+    seg_rows = (
+        segments.reshape(2, ctx_size, block_len).transpose(1, 0, 2).reshape(seq_len)
+    )
+    cos_tab, sine_tab = rope_tables(positions, HD)
+
+    inputs = token_rows.astype(f32)
+    normed, inv_one_all = rms_norm(inputs, attn_gain)
+    normed_low = normed.astype(bf16)
+    projected = dot(normed_low, qkv_weight) + bias
+    head_shape = (seq_len, own_heads, HD)
+    queries = rotate(projected[:, :own_width].reshape(head_shape), cos_tab, sine_tab).astype(bf16)
+    keys = rotate(
+        projected[:, own_width : 2 * own_width].reshape(head_shape), cos_tab, sine_tab
+    ).astype(bf16)
+    values = projected[:, 2 * own_width :].reshape(head_shape).astype(bf16)
+    allowed = (positions[None, :] <= positions[:, None]) & (seg_rows[None, :] == seg_rows[:, None])
+    scores = jnp.einsum("qhd,khd->hqk", queries, keys, preferred_element_type=f32) * score_scale
+    scores = jnp.where(allowed[None], scores, MASK_FILL)
+    top_score = jnp.max(scores, axis=-1, keepdims=True)
+    log_total = top_score + jnp.log(jnp.sum(jnp.exp(scores - top_score), axis=-1, keepdims=True))
+    weights = jnp.exp(scores - log_total)
+    weights_low = weights.astype(bf16)
+    attended = jnp.einsum("hqk,khd->qhd", weights_low, values, preferred_element_type=f32)
+    attn_own = attended.astype(bf16).reshape(seq_len, own_width)
+    attn_all = ring_gather(attn_own, ctx_size, ctx_index)
+    attn_rows = attn_all.transpose(1, 0, 2).reshape(seq_len, width)
+    residual = inputs + dot(attn_rows, out_weight)
+
+    normed_two, inv_two_all = rms_norm(residual, ffn_gain)
+    low_two = normed_two.astype(bf16)
+    mixed_weight = jnp.concatenate([router_weight, gate_vector[:, None]], axis=1)
+    logits = dot(low_two, mixed_weight)
+    probs_all = jax.nn.softmax(logits[:, :expert_count], axis=-1)
+    scale_all = jax.nn.sigmoid(logits[:, expert_count])
+    gate_all = lax.dynamic_index_in_dim(probs_all, ctx_index, 1, keepdims=False)
+    shared_pre = dot(low_two, shared_in)
+    shared_hid = swiglu(shared_pre, fs_own).astype(bf16)
+    shared_res = dot(shared_hid, shared_out)
+
+    named = jnp.any(route_rows == ctx_index, axis=-1)
+    before = jnp.arange(token_count)[:, None] < jnp.arange(token_count)[None, :]
+    rank = dot(named.astype(bf16), before.astype(bf16)).astype(i32)
+    slot_of = jnp.where(named & (rank < capacity), rank, -1)
+    slot_mask = slot_of[:, None, :] == jnp.arange(capacity, dtype=i32)[None, :, None]
+    slot_map = slot_mask.astype(bf16)
+    blocks_two = low_two.reshape(ctx_size, token_count, width)
+    blocks_grad = grad_rows.reshape(ctx_size, token_count, width)
+    gate_blocks = gate_all.reshape(ctx_size, token_count)
+
+    def to_slots(blocks):
+        picked = jnp.einsum("bmt,btd->bmd", slot_map, blocks, preferred_element_type=f32)
+        return picked.reshape(ctx_size * capacity, width)
+
+    def to_tokens(slots):
+        spread = jnp.einsum(
+            "bmt,bmd->btd",
+            slot_map,
+            slots.reshape(ctx_size, capacity, width),
+            preferred_element_type=f32,
+        )
+        return spread.reshape(seq_len, width)
+
+    buffer = to_slots(blocks_two).astype(bf16)
+    expert_pre = dot(buffer, expert_in)
+    expert_hid = swiglu(expert_pre, FE).astype(bf16)
+    expert_res = dot(expert_hid, expert_out).astype(bf16)
+    routed = gate_all[:, None] * to_tokens(expert_res)
+    out_parts = (scale_all[:, None] * shared_res + routed).astype(bf16)
+    out_sum = ring_scatter(
+        out_parts.reshape(ctx_size, token_count, width), ctx_size, ctx_index
+    )
+    own_residual = own_rows(residual)
+    output = (own_residual + out_sum).astype(bf16).reshape(tokens.shape)
+
+    grad_slots = to_slots(blocks_grad)
+    gate_slots = jnp.sum(jnp.where(slot_mask, gate_blocks[:, None, :], 0.0), axis=-1).reshape(-1, 1)
+    grad_res = (gate_slots * grad_slots).astype(bf16)
+    slot_dots = jnp.sum(grad_slots * expert_res.astype(f32), axis=-1).reshape(ctx_size, capacity, 1)
+    grad_gates = jnp.sum(jnp.where(slot_mask, slot_dots, 0.0), axis=1)
+    grad_expert_out = t_dot(expert_hid, grad_res)
+    grad_hid = dot_t(grad_res, expert_out)
+    grad_pre = swiglu_back(expert_pre, FE, grad_hid).astype(bf16)
+    grad_expert_in = t_dot(buffer, grad_pre)
+    grad_buffer = dot_t(grad_pre, expert_in).astype(bf16)
+
+    grad_f32 = grad_rows.astype(f32)
+    grad_shared_res = (scale_all[:, None] * grad_f32).astype(bf16)
+    gate_dots = jnp.sum(grad_f32 * shared_res, axis=-1).reshape(ctx_size, token_count)
+    grad_shared_out = t_dot(shared_hid, grad_shared_res)
+    grad_shared_hid = dot_t(grad_shared_res, shared_out)
+    grad_shared_pre = swiglu_back(shared_pre, fs_own, grad_shared_hid).astype(bf16)
+    grad_shared_in = t_dot(low_two, grad_shared_pre)
+    two_parts = (dot_t(grad_shared_pre, shared_in) + to_tokens(grad_buffer)).astype(bf16)
+    grad_two = ring_scatter(
+        two_parts.reshape(ctx_size, token_count, width), ctx_size, ctx_index
+    )
+
+    dots = jnp.stack([grad_gates, gate_dots], axis=1)
+    dots = lax.all_to_all(dots, "ctx", split_axis=0, concat_axis=0, tiled=True)
+    own_probs = own_rows(probs_all)
+    own_scale = own_rows(scale_all)
+    own_low = own_rows(low_two)
+    own_chosen = routes.reshape(token_count, top_count)
+    chosen_mask = jnp.any(
+        own_chosen[..., None] == jnp.arange(expert_count, dtype=i32), axis=1
+    )
+    grad_probs = jnp.where(chosen_mask, dots[:, 0].T, 0.0)
+    grad_logits = (
+        own_probs * (grad_probs - jnp.sum(own_probs * grad_probs, axis=-1, keepdims=True))
+    ).astype(bf16)
+    grad_gate_pre = (jnp.sum(dots[:, 1], axis=0) * own_scale * (1.0 - own_scale)).astype(bf16)
+    grad_router = t_dot(own_low, grad_logits)
+    grad_gate_vector = t_dot(own_low, grad_gate_pre[:, None])
+    grad_two = grad_two + dot_t(grad_logits, router_weight)
+    grad_two = grad_two + grad_gate_pre.astype(f32)[:, None] * gate_vector.astype(f32)[None, :]
+    grad_resid_norm, grad_gain_two = rms_back(
+        own_residual, own_rows(inv_two_all), ffn_gain, grad_two
+    )
+    grad_resid = cotangent.reshape(token_count, width).astype(f32) + grad_resid_norm
+
+    grad_mixed = grad_resid.astype(bf16)
+    grad_attn_rows = dot_t(grad_mixed, out_weight).astype(bf16)
+    grad_attn = lax.all_to_all(
+        grad_attn_rows.reshape(token_count, ctx_size, own_width).transpose(1, 0, 2),
+        "ctx",
+        split_axis=0,
+        concat_axis=0,
+        tiled=True,
+    ).reshape(head_shape)
+    mixed_all = ring_gather(grad_mixed, ctx_size, ctx_index).reshape(seq_len, width)
+    grad_out_weight = t_dot(attn_own, mixed_all)
+    grad_weights = jnp.einsum("qhd,khd->hqk", grad_attn, values, preferred_element_type=f32)
+    delta = jnp.sum(weights * grad_weights, axis=-1, keepdims=True)
+    grad_scores = jnp.where(allowed[None], weights * (grad_weights - delta), 0.0).astype(bf16)
+    grad_q = jnp.einsum("hqk,khd->qhd", grad_scores, keys, preferred_element_type=f32) * score_scale
+    grad_k = (
+        jnp.einsum("hqk,qhd->khd", grad_scores, queries, preferred_element_type=f32) * score_scale
+    )
+    grad_v = jnp.einsum("hqk,qhd->khd", weights_low, grad_attn, preferred_element_type=f32)
+    grad_projected = jnp.concatenate(
+        [
+            rotate_back(grad_q, cos_tab, sine_tab).reshape(seq_len, own_width),
+            rotate_back(grad_k, cos_tab, sine_tab).reshape(seq_len, own_width),
+            grad_v.reshape(seq_len, own_width),
+        ],
+        axis=-1,
+    ).astype(bf16)
+    one_parts = dot_t(grad_projected, qkv_weight).astype(bf16)
+    grad_normed = ring_scatter(
+        one_parts.reshape(ctx_size, token_count, width), ctx_size, ctx_index
+    )
+    grad_inputs_norm, grad_gain_one = rms_back(
+        tokens.reshape(token_count, width).astype(f32),
+        own_rows(inv_one_all),
+        attn_gain,
+        grad_normed,
+    )
+    grad_tokens = (grad_resid + grad_inputs_norm).reshape(tokens.shape)
+    grad_qkv_weight = t_dot(normed_low, grad_projected)
+    grad_bias = jnp.sum(grad_projected.astype(f32), axis=0).reshape(3, 1, own_width)
+    grad_bias = jnp.where(
+        jnp.arange(ctx_size, dtype=i32)[None, :, None] == ctx_index, grad_bias, 0.0
+    )
+
+    def sum_rows(grad):
+        return lax.psum_scatter(
+            grad.astype(bf16), "fsdp", scatter_dimension=0, tiled=True
+        ).astype(f32)
+
+    small_grads = jnp.concatenate(
+        [
+            piece.reshape(device_count, -1)
+            for piece in (grad_gain_one, grad_gain_two, grad_gate_vector, grad_router, grad_bias)
+        ],
+        axis=1,
+    )
+    small_grads = lax.psum_scatter(small_grads, axes, scatter_dimension=0, tiled=False)
+    return (
+        output,
+        grad_tokens,
+        merge_columns(grad_qkv_weight, 3, ctx_size, fsdp_size),
+        small_grads[router_end:],
+        sum_rows(grad_out_weight),
+        small_grads[:shard],
+        small_grads[shard : 2 * shard],
+        small_grads[3 * shard : router_end].reshape(shard, expert_count),
+        small_grads[2 * shard : 3 * shard],
+        merge_columns(grad_shared_in, 2, ctx_size, fsdp_size),
+        sum_rows(grad_shared_out),
+        sum_rows(grad_expert_in)[None],
+        sum_rows(grad_expert_out)[None],
+    )
+
+
+def local_wide(
     tokens,
     segments,
     routes,
@@ -459,4 +839,12 @@
         P("ctx", "fsdp", None),
         P("ctx", "fsdp", None),
     )
+    ctx_size = mesh.shape["ctx"]
+    fsdp_size = mesh.shape["fsdp"]
+
+    def local(*arrays):
+        if HEADS % ctx_size:
+            return local_wide(*arrays)
+        return local_split(ctx_size, fsdp_size, *arrays)
+
     return jax.shard_map(local, mesh=mesh, in_specs=in_specs, out_specs=out_specs, check_vma=False)

time: 3830 us -> 1090 us (0.28)
  waiting for transfers between devices: 3090 us -> 356 us
  matrix products: 315 us -> 211 us
  starting transfers between devices: 29.8 us -> 124 us
    reduce_scatter x6, waiting for transfers between devices: 2180 us -> 188 us  [the longest x4 188 us: sum_rows(): lax.psum_scatter(grad.astype(bf16), 'fsdp', scatter_dimension=0, tiled=True)]
    all_gather x8 -> x6, waiting for transfers between devices: 456 us -> 0.03 us  [the longest x1 0.02 us: local_split(): shared_out = lax.all_gather(w_shared_out, 'fsdp', axis=0, tiled=True)]
    unnamed x18 -> x14, waiting for transfers between devices: 276 us -> 19.8 us
    all_to_all x4, waiting for transfers between devices: 170 us -> 0.01 us  [the longest x2 0.01 us: merge_columns(): lax.all_to_all(pieces, 'ctx', split_axis=0, concat_axis=0, tiled=True)]
    ppermute x0 -> x98, waiting for transfers between devices: none -> 148 us  [the longest x42 88.3 us: ring_scatter(): moving = lax.ppermute(moving, 'ctx', perm)]
    dot_general x44 -> x33, matrix products: 314 us -> 211 us  [the longest x8 54.1 us: dot(): return jnp.dot(a, b, preferred_element_type=f32)]
    ppermute x0 -> x98, starting transfers between devices: none -> 101 us  [the longest x42 42.6 us: ring_scatter(): moving = lax.ppermute(moving, 'ctx', perm)]
    unnamed x2 -> x0, blocking collectives: 85.2 us -> none
  transfers between devices with their start and end apart: 20 -> 115, of which waited for: 18 -> 52; matrix products, arithmetic and copies ran while one was open for 10% -> 28% of each run, Pallas kernels for 0% -> 0%
where the time goes in v1:
time: 1090 us; the launch traced here: 1070 us
  waiting for transfers between devices  356 us (33%)
  matrix products  211 us (19%)
  local copies, waits for them, and re-layouts  144 us (13%)
  blocking collectives  128 us (12%)
  starting transfers between devices  124 us (11%)
  other arithmetic  78.1 us (7%)
  between operations  31.4 us (3%)
    reduce_scatter x4, waiting for transfers between devices, sum_rows(): lax.psum_scatter(grad.astype(bf16), 'fsdp', scatter_dimension=0, tiled=True)  188 us
    ppermute x42, waiting for transfers between devices, ring_scatter(): moving = lax.ppermute(moving, 'ctx', perm)  88.3 us
    all_to_all x2, blocking collectives, split_columns(): lax.all_to_all(pieces, 'ctx', split_axis=0, concat_axis=0, tiled=True)  62.9 us
    dot_general x8, matrix products, dot(): return jnp.dot(a, b, preferred_element_type=f32)  54.1 us
    dot_general x8, matrix products, t_dot(): lax.dot_general(a, b, (((0,), (0,)), ((), ())), preferred_element_type=f32)  50.1 us
    dot_general x7, matrix products, dot_t(): lax.dot_general(a, b, (((1,), (1,)), ((), ())), preferred_element_type=f32)  49.5 us
    dynamic_update_slice x62, local copies, waits for them, and re-layouts, put(): return lax.dynamic_update_slice(out, piece[None, None], start)  42.7 us
    ppermute x42, starting transfers between devices, ring_scatter(): moving = lax.ppermute(moving, 'ctx', perm)  42.6 us
  transfers between devices with their start and end apart: 115, of which 52 were waited for; matrix products, arithmetic and copies ran while one was open for 28% of the time, Pallas kernels for 0%

profile of v1, /device:TPU:8, one launch (start us, length us, event | category | flops | bytes accessed | tf_op | source)
XLA Modules:
  0.0 1073.0 jit_solution(7575889340493309068)
XLA Ops:
  9.9 25.4 %all_to_all.30 = bf16[8,64,768]{2,1,0:T(8,128)(2,1)} all-to-all(bf16[8,64,768]{2,1,0:T(8,128)(2,1)S(1)} %reshape.807), channel_id=1, replica_groups=mesh['ctx'=8,'fsdp'=4] {'ctx'}, dimensions={0} | all-to-all | bytes 1572864 | tf_op jit(solution)/shard_map/all_to_all | solution.py:151
  41.0 37.5 %all_to_all.31 = bf16[8,64,1408]{2,1,0:T(8,128)(2,1)} all-to-all(bf16[8,64,1408]{2,1,0:T(8,128)(2,1)S(1)} %reshape.817), channel_id=1, replica_groups=mesh['ctx'=8,'fsdp'=4] {'ctx'}, dimensions={0} | all-to-all | bytes 2883584 | tf_op jit(solution)/shard_map/all_to_all | solution.py:151
  93.7 35.6 %all-gather.5 = bf16[32,1,896]{2,1,0:T(2,128)(2,1)S(1)} all-gather(bf16[1,1,896]{2,1,0:T(2,128)(2,1)S(1)} %reshape.899), channel_id=2, replica_groups=mesh['ctx'=8,'fsdp'=4] {'ctx','fsdp'}, dimensions={0}, use_global_device_ids=true | all-gather | bytes 59136 | tf_op jit(solution)/shard_map/all_gather | solution.py:220
  131.9 29.6 %all_gather.41 = s32[8,128,4]{1,2,0:T(4,128)S(1)} all-gather(s32[1,128,4]{1,2,0:T(4,128)S(1)} %all_gather_reshape.3), channel_id=1, replica_groups=mesh['ctx'=8,'fsdp'=4] {'ctx'}, dimensions={0}, use_global_device_ids=true | all-gather | bytes 18432 | tf_op jit(solution)/shard_map/all_gather | solution.py:238
  199.2 9.3 collective-permute-done
  339.3 6.6 copy.217
  351.8 14.4 %multiply_reduce_fusion.1 = (f32[1024]{0:T(1024)S(1)}, f32[1024,2048]{1,0:T(8,128)S(1)}) fusion(bf16[1024,2048]{0,1:T(8,128)(2,1)} %bitcast.679, bf16[2048,2048]{1,0:T(8,128)(2,1)} %all-gather.13.cloned.1.call-done, bf16[8,2,64,2048]{3,2,1,0:T(8,128)(2,1)} %bitcast_dynamic-update-slice_fusion.44), kind=kOutput, calls=%fused_computation.28 | convolution fusion | flops 8598322176 | bytes 25169920 | tf_op jit(solution)/shard_map/dot_general | solution.py:204
  377.7 8.9 fusion.182
  386.6 11.2 %multiply_convert_fusion.2 = (bf16[1024,704]{1,0:T(8,128)(2,1)}, bf16[1024,704]{1,0:T(8,128)(2,1)}, bf16[1024,704]{1,0:T(8,128)(2,1)}) fusion(f32[1024,1408]{1,0:T(8,128)} %fusion.182, bf16[1024,2048]{1,0:T(8,128)(2,1)} %fusion.5, bf16[704,2048]{1,0:T(8,128)(2,1)} %all-gather.15.cloned.1.call-done), kind=kOutput, calls=%fused_computation.62 | convolution fusion | flops 2964324352 | bytes 17170432 | tf_op jit(solution)/shard_map/dot_general | solution.py:207
  397.9 9.5 fusion.3
  411.8 7.8 fusion.31
  423.9 7.6 multiply_convert_fusion.5
  431.5 10.1 fusion.50
  443.0 8.6 fusion.7
  469.7 7.9 fusion.9
  478.2 6.4 all-to-all-start.2
  508.8 6.3 convolution_convert_fusion.7
  527.6 6.4 copy.236
  536.5 7.0 convolution_convert_fusion.8
  549.5 15.9 %fusion.60 = f32[1024,2,128]{0,2,1:T(8,128)} fusion(bf16[1024,2,128]{0,2,1:T(8,128)(2,1)} %copy-done.30, f32[2,1024,1024]{1,2,0:T(8,128)} %fusion.183, f32[2,1024,1024]{1,2,0:T(8,128)} %copy-done.2, f32[2,1024]{1,0:T(2,128)S(1)} %copy-done.43, pred[1024,1024]{0,1:T(8,128)(4,1)} %copy-done.13), kind=kOutput, calls=%fused_computation.83 | convolution fusion | flops 559942656 | bytes 19406848 | tf_op jit(solution)/shard_map/hqk,qhd->khd/dot_general | solution.py:389
  565.3 17.0 %broadcast_multiply_fusion.1 = (f32[1024,2,128]{0,2,1:T(8,128)}, f32[1024,2,128]{0,2,1:T(8,128)}, f32[1024,2,128]{0,2,1:T(8,128)}) fusion(f32[1024,128]{0,1:T(8,128)} %get-tuple-element.163, f32[1024,2,128]{0,2,1:T(8,128)} %fusion.60, bf16[1024,2,128]{0,2,1:T(8,128)(2,1)} %copy-done.29, f32[2,1024,1024]{1,2,0:T(8,128)} %fusion.183, ...), kind=kOutput, calls=%fused_computation.204 | convolution fusion | flops 560466944 | bytes 23076864 | tf_op jit(solution)/shard_map/hqk,khd->qhd/dot_general | solution.py:387
  602.2 9.7 convolution_convert_fusion.2
  716.1 7.4 convolution_convert_fusion.4
  723.6 7.7 convolution_convert_fusion.1
  731.3 11.4 %convolution_convert_fusion = bf16[2048,2816]{1,0:T(8,128)(2,1)} fusion(bf16[512,2048]{1,0:T(8,128)(2,1)} %bitcast.698, bf16[512,1408]{1,0:T(8,128)(2,1)} %copy-done.62, bf16[512,1408]{1,0:T(8,128)(2,1)} %copy-done.61), kind=kOutput, calls=%fused_computation.5 | convolution fusion | flops 5917114368 | bytes 16515072 | tf_op jit(solution)/shard_map/dot_general | solution.py:210
  746.7 8.1 collective-permute-done.28
  788.9 12.5 %collective-permute-done.31 = bf16[64,2048]{1,0:T(8,128)(2,1)S(1)} collective-permute-done((bf16[64,2048]{1,0:T(8,128)(2,1)S(1)}, bf16[64,2048]{1,0:T(8,128)(2,1)S(1)}, u32[]{:S(2)}, u32[]{:S(2)}) %collective-permute-start.31) | collective-permute-done | bytes 262176 | tf_op jit(solution)/shard_map/ppermute | solution.py:135
  825.3 17.9 %all-reduce.3.cloned.1.call-done = f32[32,896]{1,0:T(8,128)} async-done(((f32[32,896]{1,0:T(8,128)}), f32[32,896]{1,0:T(8,128)}) %all-reduce.3.cloned.1.call-update) | async-done | bytes 114704
  847.5 21.9 %reduce-scatter.9.cloned.1.call-done = bf16[64,2048]{1,0:T(8,128)(2,1)} async-done(((bf16[256,2048]{1,0:T(8,128)(2,1)}), bf16[64,2048]{1,0:T(8,128)(2,1)}) %reduce-scatter.9.cloned.1.call-update) | async-done | bytes 262160 | tf_op jit(solution)/shard_map/reduce_scatter | solution.py:418
  871.2 37.9 %reduce-scatter.13.cloned.1.call-done = bf16[176,2048]{1,0:T(8,128)(2,1)} async-done(((bf16[704,2048]{1,0:T(8,128)(2,1)}), bf16[176,2048]{1,0:T(8,128)(2,1)}) %reduce-scatter.13.cloned.1.call-update) | async-done | bytes 720912 | tf_op jit(solution)/shard_map/reduce_scatter | solution.py:418
  916.5 49.9 %reduce-scatter.17.cloned.1.call-done = bf16[352,2048]{1,0:T(8,128)(2,1)} async-done(((bf16[1408,2048]{1,0:T(8,128)(2,1)}), bf16[352,2048]{1,0:T(8,128)(2,1)}) %reduce-scatter.17.cloned.1.call-update) | async-done | bytes 1441808 | tf_op jit(solution)/shard_map/reduce_scatter | solution.py:418
  982.5 78.8 %reduce-scatter.15.cloned.1.call-done = bf16[512,2816]{1,0:T(8,128)(2,1)} async-done(((bf16[2048,2816]{1,0:T(8,128)(2,1)}), bf16[512,2816]{1,0:T(8,128)(2,1)}) %reduce-scatter.15.cloned.1.call-update) | async-done | bytes 2883600 | tf_op jit(solution)/shard_map/reduce_scatter | solution.py:418
  (604 shorter events, 489.3 us)
Async XLA Ops:
  7.2 270.7 %all-gather.17.cloned.1.call-start = ((), (), s32[]{:S(2)}) async-start(), calls=%async_computation.20 | async-start | bytes 3932160 | tf_op jit(solution)/shard_map/all_gather | solution.py:152
  35.3 310.6 %all-gather.19.cloned.1.call-start = ((), (), s32[]{:S(2)}) async-start(), calls=%async_computation.21 | async-start | bytes 7208960 | tf_op jit(solution)/shard_map/all_gather | solution.py:152
  78.6 273.2 %all-gather.13.cloned.1.call-start = ((), (), s32[]{:S(2)}) async-start(), calls=%async_computation.12 | async-start | bytes 8650752 | tf_op jit(solution)/shard_map/all_gather | solution.py:233
  79.3 307.3 %all-gather.15.cloned.1.call-start = ((), (), s32[]{:S(2)}) async-start(), calls=%async_computation.13 | async-start | bytes 3604480 | tf_op jit(solution)/shard_map/all_gather | solution.py:235
  79.9 318.0 %all-gather.21.cloned.1.call-start = ((), (), s32[]{:S(2)}) async-start(), calls=%async_computation.22 | async-start | bytes 14417920 | tf_op jit(solution)/shard_map/all_gather | solution.py:236
  80.5 331.3 %all-gather.23.cloned.1.call-start = ((), (), s32[]{:S(2)}) async-start(), calls=%async_computation.23 | async-start | bytes 7208960 | tf_op jit(solution)/shard_map/all_gather | solution.py:237
  84.7 109.1 %collective-permute-start.45 = (bf16[64,2048]{1,0:T(8,128)(2,1)S(1)}, bf16[64,2048]{1,0:T(8,128)(2,1)}, u32[]{:S(2)}, u32[]{:S(2)}) collective-permute-start(bf16[64,2048]{1,0:T(8,128)(2,1)S(1)} %get-tuple-element.153), channel_id=1, source_target_pairs={{8,0},{16,8},{24,16},{28,24},{20,28},{12,20},{4,12},{0,4},{9,1},{1... | collective-permute-start | bytes 786440 | tf_op jit(solution)/shard_map/ppermute | solution.py:111
  85.8 108.3 %collective-permute-start.44 = (bf16[64,2048]{1,0:T(8,128)(2,1)S(1)}, bf16[64,2048]{1,0:T(8,128)(2,1)}, u32[]{:S(2)}, u32[]{:S(2)}) collective-permute-start(bf16[64,2048]{1,0:T(8,128)(2,1)S(1)} %get-tuple-element.153), channel_id=1, source_target_pairs={{0,8},{8,16},{16,24},{24,28},{28,20},{20,12},{12,4},{4,0},{1,9},{9... | collective-permute-start | bytes 786440 | tf_op jit(solution)/shard_map/ppermute | solution.py:108
  86.7 103.6 %collective-permute-start.43 = (bf16[64,2048]{1,0:T(8,128)(2,1)}, bf16[64,2048]{1,0:T(8,128)(2,1)}, u32[]{:S(2)}, u32[]{:S(2)}) collective-permute-start(bf16[64,2048]{1,0:T(8,128)(2,1)} %get-tuple-element.154), channel_id=1, source_target_pairs={{8,0},{16,8},{24,16},{28,24},{20,28},{12,20},{4,12},{0,4},{9,1},{1... | collective-permute-start | bytes 786440 | tf_op jit(solution)/shard_map/ppermute | solution.py:111
  87.9 100.5 %collective-permute-start.42 = (bf16[64,2048]{1,0:T(8,128)(2,1)}, bf16[64,2048]{1,0:T(8,128)(2,1)}, u32[]{:S(2)}, u32[]{:S(2)}) collective-permute-start(bf16[64,2048]{1,0:T(8,128)(2,1)} %get-tuple-element.154), channel_id=1, source_target_pairs={{0,8},{8,16},{16,24},{24,28},{28,20},{20,12},{12,4},{4,0},{1,9},{9... | collective-permute-start | bytes 786440 | tf_op jit(solution)/shard_map/ppermute | solution.py:108
  92.0 119.9 %collective-permute-start.3 = (bf16[64,2048]{1,0:T(8,128)(2,1)S(1)}, bf16[64,2048]{1,0:T(8,128)(2,1)}, u32[]{:S(2)}, u32[]{:S(2)}) collective-permute-start(bf16[64,2048]{1,0:T(8,128)(2,1)S(1)} %get-tuple-element.158), channel_id=1, source_target_pairs={{8,0},{16,8},{24,16},{28,24},{20,28},{12,20},{4,12},{0,4},{9,1},{1... | collective-permute-start | bytes 786440 | tf_op jit(solution)/shard_map/ppermute | solution.py:111
  188.4 24.2 %collective-permute-start.2 = (bf16[64,2048]{1,0:T(8,128)(2,1)S(1)}, bf16[64,2048]{1,0:T(8,128)(2,1)S(1)}, u32[]{:S(2)}, u32[]{:S(2)}) collective-permute-start(bf16[64,2048]{1,0:T(8,128)(2,1)S(1)} %get-tuple-element.158), channel_id=1, source_target_pairs={{0,8},{8,16},{16,24},{24,28},{28,20},{20,12},{12,4},{4,0},{1,9},{9... | collective-permute-start | bytes 786440 | tf_op jit(solution)/shard_map/ppermute | solution.py:108
  194.1 29.6 %collective-permute-start.49 = (bf16[64,2048]{1,0:T(8,128)(2,1)}, bf16[64,2048]{1,0:T(8,128)(2,1)S(1)}, u32[]{:S(2)}, u32[]{:S(2)}) collective-permute-start(bf16[64,2048]{1,0:T(8,128)(2,1)} %collective-permute-done.45), channel_id=1, source_target_pairs={{8,0},{16,8},{24,16},{28,24},{20,28},{12,20},{4,12},{0,4},{9,1},{1... | collective-permute-start | bytes 786440 | tf_op jit(solution)/shard_map/ppermute | solution.py:111
  212.6 23.1 %collective-permute-start.7 = (bf16[64,2048]{1,0:T(8,128)(2,1)}, bf16[64,2048]{1,0:T(8,128)(2,1)S(1)}, u32[]{:S(2)}, u32[]{:S(2)}) collective-permute-start(bf16[64,2048]{1,0:T(8,128)(2,1)} %collective-permute-done.3), channel_id=1, source_target_pairs={{8,0},{16,8},{24,16},{28,24},{20,28},{12,20},{4,12},{0,4},{9,1},{1... | collective-permute-start | bytes 786440 | tf_op jit(solution)/shard_map/ppermute | solution.py:111
  225.3 22.6 %collective-permute-start.53 = (bf16[64,2048]{1,0:T(8,128)(2,1)S(1)}, bf16[64,2048]{1,0:T(8,128)(2,1)S(1)}, u32[]{:S(2)}, u32[]{:S(2)}) collective-permute-start(bf16[64,2048]{1,0:T(8,128)(2,1)S(1)} %collective-permute-done.49), channel_id=1, source_target_pairs={{8,0},{16,8},{24,16},{28,24},{20,28},{12,20},{4,12},{0,4},{9,1},{1... | collective-permute-start | bytes 786440 | tf_op jit(solution)/shard_map/ppermute | solution.py:111
  237.3 20.9 %collective-permute-start.11 = (bf16[64,2048]{1,0:T(8,128)(2,1)S(1)}, bf16[64,2048]{1,0:T(8,128)(2,1)S(1)}, u32[]{:S(2)}, u32[]{:S(2)}) collective-permute-start(bf16[64,2048]{1,0:T(8,128)(2,1)S(1)} %collective-permute-done.7), channel_id=1, source_target_pairs={{8,0},{16,8},{24,16},{28,24},{20,28},{12,20},{4,12},{0,4},{9,1},{1... | collective-permute-start | bytes 786440 | tf_op jit(solution)/shard_map/ppermute | solution.py:111
  249.6 27.5 %collective-permute-start.55 = (bf16[64,2048]{1,0:T(8,128)(2,1)S(1)}, bf16[64,2048]{1,0:T(8,128)(2,1)S(1)}, u32[]{:S(2)}, u32[]{:S(2)}) collective-permute-start(bf16[64,2048]{1,0:T(8,128)(2,1)S(1)} %collective-permute-done.53), channel_id=1, source_target_pairs={{8,0},{16,8},{24,16},{28,24},{20,28},{12,20},{4,12},{0,4},{9,1},{1... | collective-permute-start | bytes 786440 | tf_op jit(solution)/shard_map/ppermute | solution.py:111
  454.4 30.3 %collective-permute-start.63 = (bf16[64,2048]{1,0:T(8,128)(2,1)S(1)}, bf16[64,2048]{1,0:T(8,128)(2,1)S(1)}, u32[]{:S(2)}, u32[]{:S(2)}) collective-permute-start(bf16[64,2048]{1,0:T(8,128)(2,1)S(1)} %get-tuple-element.133), channel_id=1, source_target_pairs={{0,8},{8,16},{16,24},{24,28},{28,20},{20,12},{12,4},{4,0},{1,9},{9... | collective-permute-start | bytes 786440 | tf_op jit(solution)/shard_map/ppermute | solution.py:135
  522.1 246.1 %reduce-scatter.7.cloned.1.call-start = ((), (), s32[]{:S(2)}) async-start(), calls=%async_computation.14 | async-start | bytes 3932160 | tf_op jit(solution)/shard_map/reduce_scatter | solution.py:161
  598.8 215.6 %reduce-scatter.11.cloned.1.call-start = ((), (), s32[]{:S(2)}) async-start(), calls=%async_computation.16 | async-start | bytes 7208960 | tf_op jit(solution)/shard_map/reduce_scatter | solution.py:161
  614.9 228.3 %all-reduce.3.cloned.1.call-start = ((), (), s32[]{:S(2)}) async-start(), calls=%async_computation.24 | async-start | bytes 229376
  636.9 22.0 %collective-permute-start.94 = (bf16[64,2048]{1,0:T(8,128)(2,1)S(1)}, bf16[64,2048]{1,0:T(8,128)(2,1)S(1)}, u32[]{:S(2)}, u32[]{:S(2)}) collective-permute-start(bf16[64,2048]{1,0:T(8,128)(2,1)S(1)} %collective-permute-done.90), channel_id=1, source_target_pairs={{0,8},{8,16},{16,24},{24,28},{28,20},{20,12},{12,4},{4,0},{1,9},{9... | collective-permute-start | bytes 786440 | tf_op jit(solution)/shard_map/ppermute | solution.py:108
  649.7 53.6 %collective-permute-start.97 = (bf16[64,2048]{1,0:T(8,128)(2,1)}, bf16[64,2048]{1,0:T(8,128)(2,1)}, u32[]{:S(2)}, u32[]{:S(2)}) collective-permute-start(bf16[64,2048]{1,0:T(8,128)(2,1)} %collective-permute-done.95), channel_id=1, source_target_pairs={{8,0},{16,8},{24,16},{28,24},{20,28},{12,20},{4,12},{0,4},{9,1},{1... | collective-permute-start | bytes 786440 | tf_op jit(solution)/shard_map/ppermute | solution.py:111
  711.4 158.1 %reduce-scatter.9.cloned.1.call-start = ((), (), s32[]{:S(2)}) async-start(), calls=%async_computation.15 | async-start | bytes 1310720 | tf_op jit(solution)/shard_map/reduce_scatter | solution.py:418
  716.0 193.0 %reduce-scatter.13.cloned.1.call-start = ((), (), s32[]{:S(2)}) async-start(), calls=%async_computation.17 | async-start | bytes 3604480 | tf_op jit(solution)/shard_map/reduce_scatter | solution.py:418
  723.5 242.8 %reduce-scatter.17.cloned.1.call-start = ((), (), s32[]{:S(2)}) async-start(), calls=%async_computation.19 | async-start | bytes 7208960 | tf_op jit(solution)/shard_map/reduce_scatter | solution.py:418
  731.3 330.1 %reduce-scatter.15.cloned.1.call-start = ((), (), s32[]{:S(2)}) async-start(), calls=%async_computation.18 | async-start | bytes 14417920 | tf_op jit(solution)/shard_map/reduce_scatter | solution.py:418
  768.2 46.2 %all-to-all-start.4 = ((bf16[8,64,768]{2,1,0:T(8,128)(2,1)}), bf16[8,64,768]{2,1,0:T(8,128)(2,1)}, u32[]{:S(2)}, u32[]{:S(2)}) async-start(bf16[8,64,768]{2,1,0:T(8,128)(2,1)} %bitcast.705), calls=%async_computation.5 | async-start | bytes 1572864 | tf_op jit(solution)/shard_map/all_to_all | solution.py:163
  784.8 22.4 %collective-permute-start.34 = (bf16[64,2048]{1,0:T(8,128)(2,1)S(1)}, bf16[64,2048]{1,0:T(8,128)(2,1)S(1)}, u32[]{:S(2)}, u32[]{:S(2)}) collective-permute-start(bf16[64,2048]{1,0:T(8,128)(2,1)S(1)} %get-tuple-element.111), channel_id=1, source_target_pairs={{8,0},{16,8},{24,16},{28,24},{20,28},{12,20},{4,12},{0,4},{9,1},{1... | collective-permute-start | bytes 786440 | tf_op jit(solution)/shard_map/ppermute | solution.py:135
  786.8 23.2 %collective-permute-start.40 = (bf16[64,2048]{1,0:T(8,128)(2,1)S(1)}, bf16[64,2048]{1,0:T(8,128)(2,1)S(1)}, u32[]{:S(2)}, u32[]{:S(2)}) collective-permute-start(bf16[64,2048]{1,0:T(8,128)(2,1)S(1)} %get-tuple-element.112), channel_id=1, source_target_pairs={{8,0},{16,8},{24,16},{28,24},{20,28},{12,20},{4,12},{0,4},{9,1},{1... | collective-permute-start | bytes 786440 | tf_op jit(solution)/shard_map/ppermute | solution.py:135
  786.9 23.2 %collective-permute-start.36 = (bf16[64,2048]{1,0:T(8,128)(2,1)S(1)}, bf16[64,2048]{1,0:T(8,128)(2,1)S(1)}, u32[]{:S(2)}, u32[]{:S(2)}) collective-permute-start(bf16[64,2048]{1,0:T(8,128)(2,1)S(1)} %get-tuple-element.113), channel_id=1, source_target_pairs={{0,8},{8,16},{16,24},{24,28},{28,20},{20,12},{12,4},{4,0},{1,9},{9... | collective-permute-start | bytes 786440 | tf_op jit(solution)/shard_map/ppermute | solution.py:135
  814.4 155.3 %all-to-all-start.5 = ((bf16[8,64,1408]{2,1,0:T(8,128)(2,1)}), bf16[8,64,1408]{2,1,0:T(8,128)(2,1)}, u32[]{:S(2)}, u32[]{:S(2)}) async-start(bf16[8,64,1408]{2,1,0:T(8,128)(2,1)} %bitcast.702), calls=%async_computation.8 | async-start | bytes 2883584 | tf_op jit(solution)/shard_map/all_to_all | solution.py:163
  (150 other events, 1970.8 us)
Sparse Core Ops, SparseCore 0:
  35.4 27.9 all-gather.16
  78.7 43.5 all-gather.18
  125.2 84.3 all-gather.12
  211.0 29.4 all-gather.14
  241.9 76.1 all-gather.20
  319.5 43.3 all-gather.22
  598.9 38.8 reduce-scatter.6
  641.1 54.8 reduce-scatter.10
  711.5 131.7 all-reduce.2
  846.2 23.1 reduce-scatter.8
  872.7 36.3 reduce-scatter.12
  911.5 54.8 reduce-scatter.16
  969.1 92.1 reduce-scatter.14

commit v2 on v1

--- a/solution.py
+++ b/solution.py
@@ -86,71 +86,140 @@
     return [row[k] for k in range(size)]
 
 
-def ring_gather(block, size, ctx_index):
-    rows = block.shape[0] // 2
+def ring_walk(block, size, ctx_index, out, put):
+    rows = block.shape[0]
     ahead, back = ring_steps(size)
     peers = ring_peers(size, ctx_index)
     half = size // 2
-    halves = (block[:rows], block[rows:])
-    out = jnp.zeros((size, 2, rows) + block.shape[1:], block.dtype)
-    zero = jnp.zeros((), jnp.int32)
-
-    def put(out, piece, peer, part):
-        start = (peer, jnp.full((), part, jnp.int32)) + (zero,) * block.ndim
-        return lax.dynamic_update_slice(out, piece[None, None], start)
-
-    for part in range(2):
-        out = put(out, halves[part], ctx_index, part)
-    fore, rear = list(halves), list(halves)
-    for k in range(1, half + 1):
-        for part in (0, 1):
-            if k < half or part == 0:
-                fore[part] = lax.ppermute(fore[part], "ctx", ahead)
-                out = put(out, fore[part], peers[(size - k) % size], part)
-            if k < half or part == 1:
-                rear[part] = lax.ppermute(rear[part], "ctx", back)
-                out = put(out, rear[part], peers[k], part)
-    return out.reshape((size,) + block.shape)
+    out = put(out, block, ctx_index, 0)
+    fore = rear = block
+    for k in range(1, half):
+        fore = lax.ppermute(fore, "ctx", ahead)
+        rear = lax.ppermute(rear, "ctx", back)
+        out = put(out, fore, peers[size - k], 0)
+        out = put(out, rear, peers[k], 0)
+    fore = lax.ppermute(fore[: rows // 2], "ctx", ahead)
+    rear = lax.ppermute(rear[rows // 2 :], "ctx", back)
+    out = put(out, fore, peers[half], 0)
+    return put(out, rear, peers[half], rows // 2)
+
+
+def ring_gather(block, size, ctx_index):
+    rows, width = block.shape
+
+    def put(out, piece, peer, offset):
+        return lax.dynamic_update_slice(out, piece, (peer * rows + offset, jnp.zeros_like(peer)))
+
+    return ring_walk(block, size, ctx_index, jnp.zeros((size * rows, width), block.dtype), put)
+
+
+def ring_gather_columns(block, size, ctx_index):
+    rows, width = block.shape
+
+    def put(out, piece, peer, offset):
+        return lax.dynamic_update_slice(out, piece, (jnp.full_like(peer, offset), peer * width))
+
+    return ring_walk(block, size, ctx_index, jnp.zeros((rows, size * width), block.dtype), put)
 
 
 def ring_scatter(parts, size, ctx_index):
-    rows = parts.shape[1] // 2
+    f32 = jnp.float32
+    rows = parts.shape[0] // size
     ahead, back = ring_steps(size)
     peers = ring_peers(size, ctx_index)
     half = size // 2
 
-    def own(k, part):
-        block = lax.dynamic_index_in_dim(parts, peers[k % size], 0, keepdims=False)
-        return block[part * rows : (part + 1) * rows]
-
-    sums = []
-    for part in (0, 1):
-        total = own(0, part).astype(jnp.float32)
-        for perm, sign, first in (
-            (ahead, 1, half if part == 0 else half - 1),
-            (back, -1, half if part == 1 else half - 1),
-        ):
-            moving = own(sign * first, part)
-            for k in range(first, 0, -1):
-                moving = lax.ppermute(moving, "ctx", perm)
-                if k > 1:
-                    moving = (
-                        moving.astype(jnp.float32)
-                        + own(sign * (k - 1), part).astype(jnp.float32)
-                    ).astype(jnp.bfloat16)
-            total = total + moving.astype(jnp.float32)
-        sums.append(total)
-    return jnp.concatenate(sums, axis=0)
-
-
-def split_columns(weight, groups, size):
+    def own(k, start, count):
+        first = (peers[k % size] * rows + start, jnp.zeros_like(peers[0]))
+        return lax.dynamic_slice(parts, first, (count, parts.shape[1])).astype(f32)
+
+    def low(values):
+        return values.astype(jnp.bfloat16)
+
+    cut = rows // 2
+    fore = lax.ppermute(low(own(half, 0, cut)), "ctx", ahead)
+    rear = lax.ppermute(low(own(half, cut, cut)), "ctx", back)
+    fore = jnp.concatenate(
+        [low(fore.astype(f32) + own(half - 1, 0, cut)), low(own(half - 1, cut, cut))], axis=0
+    )
+    rear = jnp.concatenate(
+        [low(own(1 - half, 0, cut)), low(rear.astype(f32) + own(1 - half, cut, cut))], axis=0
+    )
+    for k in range(half - 1, 0, -1):
+        fore = lax.ppermute(fore, "ctx", ahead)
+        rear = lax.ppermute(rear, "ctx", back)
+        if k > 1:
+            fore = low(fore.astype(f32) + own(k - 1, 0, rows))
+            rear = low(rear.astype(f32) + own(1 - k, 0, rows))
+    return own(0, 0, rows) + fore.astype(f32) + rear.astype(f32)
+
+
+def other_core(size):
+    return [(i, i ^ 1) for i in range(size)]
+
+
+def other_chip(size):
+    return [(i, i ^ 2) for i in range(size)]
+
+
+def fsdp_gather(shard, size):
+    index = lax.axis_index("fsdp")
+    far = lax.ppermute(shard, "fsdp", other_chip(size))
+    near = lax.ppermute(shard, "fsdp", other_core(size))
+    far_near = lax.ppermute(far, "fsdp", other_core(size))
+    out = jnp.zeros((size,) + shard.shape, shard.dtype)
+    for piece, peer in ((shard, index), (near, index ^ 1), (far, index ^ 2), (far_near, index ^ 3)):
+        out = lax.dynamic_update_index_in_dim(out, piece, peer, 0)
+    return out
+
+
+def small_scatter(parts, size, fsdp_size, ctx_index):
+    index = lax.axis_index("fsdp")
+
+    def pick(array, at, axis):
+        return lax.dynamic_index_in_dim(array, at, axis, keepdims=False)
+
+    halves = parts.reshape(size, fsdp_size // 2, 2, -1)
+    core, chip = index % 2, index // 2
+    kept = pick(halves, core, 2)
+    kept = kept + lax.ppermute(pick(halves, 1 - core, 2), "fsdp", other_core(fsdp_size))
+    mine = pick(kept, chip, 1)
+    mine = mine + lax.ppermute(pick(kept, 1 - chip, 1), "fsdp", other_chip(fsdp_size))
+    rows = mine.reshape(size // 2, 2, -1)
+    odd = ctx_index % 2
+    row = pick(rows, odd, 1)
+    row = row + lax.ppermute(pick(rows, 1 - odd, 1), "ctx", [(i, i ^ 1) for i in range(size)])
+    pairs = size // 2
+    total = pick(row, ctx_index // 2, 0)
+    for k in range(1, pairs):
+        total = total + lax.ppermute(
+            pick(row, (ctx_index // 2 + k) % pairs, 0),
+            "ctx",
+            [(i, (i + 2 * k) % size) for i in range(size)],
+        )
+    return total
+
+
+def split_columns(weight, groups, size, extra):
     rows = weight.shape[0]
     width = weight.shape[1] // (groups * size)
     pieces = weight.reshape(rows, groups, size, width).transpose(2, 0, 1, 3)
     pieces = pieces.reshape(size, rows, groups * width)
+    if extra is not None:
+        count = extra.shape[0]
+        more = -(-count // (groups * width * 16)) * 16
+        extra = jnp.pad(extra, (0, more * groups * width - count))
+        extra = jnp.broadcast_to(
+            extra.reshape(1, more, groups * width), (size, more, groups * width)
+        )
+        pieces = jnp.concatenate([pieces, extra], axis=1)
     pieces = lax.all_to_all(pieces, "ctx", split_axis=0, concat_axis=0, tiled=True)
     whole = lax.all_gather(pieces, "fsdp", axis=0, tiled=False)
-    return whole.transpose(1, 0, 2, 3).reshape(-1, groups * width)
+    whole = whole.transpose(1, 0, 2, 3)
+    taken = whole[:, :, :rows].reshape(-1, groups * width)
+    if extra is None:
+        return taken
+    return (taken, whole[:, :, rows:].reshape(-1, more * groups * width)[:, :count])
 
 
 def merge_columns(grad, groups, size, fsdp_size):
@@ -185,7 +254,6 @@
     w_expert_out,
 ):
     bf16, f32, i32 = jnp.bfloat16, jnp.float32, jnp.int32
-    axes = ("ctx", "fsdp")
     device_count = ctx_size * fsdp_size
     block_len = tokens.shape[2]
     width = tokens.shape[3]
@@ -214,32 +282,38 @@
             values.reshape((ctx_size, token_count) + values.shape[1:]), ctx_index, 0, keepdims=False
         )
 
-    small = jnp.concatenate(
-        [gain_attn, gain_ffn, w_shared_gate, w_router.reshape(-1), b_qkv], axis=0
-    )
-    small = lax.all_gather(small, axes, axis=0, tiled=False)
+    def sum_rows(grad):
+        return lax.psum_scatter(
+            grad.astype(bf16), "fsdp", scatter_dimension=0, tiled=True
+        ).astype(f32)
+
     shard = width // device_count
+    small = [gain_attn, gain_ffn, w_shared_gate, w_router.reshape(-1), b_qkv]
+    small_size = sum(piece.shape[0] for piece in small)
+    small = jnp.concatenate(small + [routes.astype(bf16).reshape(-1)], axis=0)
+    token_rows = ring_gather(tokens.reshape(token_count, width), ctx_size, ctx_index)
+    qkv_weight, small = split_columns(w_qkv, 3, ctx_size, small)
     attn_gain = small[:, :shard].reshape(width).astype(f32)
     ffn_gain = small[:, shard : 2 * shard].reshape(width).astype(f32)
     gate_vector = small[:, 2 * shard : 3 * shard].reshape(width)
     router_end = 3 * shard + shard * expert_count
     router_weight = small[:, 3 * shard : router_end].reshape(width, expert_count)
-    bias = small[:, router_end:].reshape(3, ctx_size, own_width).astype(f32)
+    bias = small[:, router_end:small_size].reshape(3, ctx_size, own_width).astype(f32)
     bias = lax.dynamic_index_in_dim(bias, ctx_index, 1, keepdims=False).reshape(3 * own_width)
-
-    token_rows = ring_gather(tokens.reshape(token_count, width), ctx_size, ctx_index)
-    token_rows = token_rows.reshape(seq_len, width)
-    qkv_weight = split_columns(w_qkv, 3, ctx_size)
-    out_weight = lax.all_gather(w_out, axes, axis=0, tiled=True)
-    shared_in = split_columns(w_shared_in, 2, ctx_size)
+    route_rows = small[:, small_size:].astype(i32)
+    route_rows = lax.dynamic_index_in_dim(
+        route_rows.reshape(ctx_size, fsdp_size, -1), lax.axis_index("fsdp"), 1, keepdims=False
+    ).reshape(ctx_size, token_count, top_count)
+
+    out_shard, token_rows = lax.optimization_barrier((w_out, token_rows))
+    out_weight = fsdp_gather(ring_gather(out_shard, ctx_size, ctx_index), fsdp_size)
+    out_weight = out_weight.reshape(fsdp_size, ctx_size, -1, width)
+    out_weight = out_weight.transpose(1, 0, 2, 3).reshape(width, width)
+    in_shard, token_rows = lax.optimization_barrier((w_shared_in, token_rows))
+    shared_in = split_columns(in_shard, 2, ctx_size, None)
     shared_out = lax.all_gather(w_shared_out, "fsdp", axis=0, tiled=True)
     expert_in = lax.all_gather(w_expert_in[0], "fsdp", axis=0, tiled=True)
     expert_out = lax.all_gather(w_expert_out[0], "fsdp", axis=0, tiled=True)
-    route_rows = lax.all_gather(
-        routes.reshape(token_count, top_count), "ctx", axis=0, tiled=False
-    )
-    grad_rows = ring_gather(cotangent.reshape(token_count, width), ctx_size, ctx_index)
-    grad_rows = grad_rows.reshape(seq_len, width)
 
     block_ids = jnp.arange(ctx_size, dtype=i32)[:, None]
     local_index = jnp.arange(block_len, dtype=i32)[None, :]
@@ -274,8 +348,9 @@
     weights_low = weights.astype(bf16)
     attended = jnp.einsum("hqk,khd->qhd", weights_low, values, preferred_element_type=f32)
     attn_own = attended.astype(bf16).reshape(seq_len, own_width)
-    attn_all = ring_gather(attn_own, ctx_size, ctx_index)
-    attn_rows = attn_all.transpose(1, 0, 2).reshape(seq_len, width)
+    attn_rows = ring_gather_columns(attn_own, ctx_size, ctx_index)
+    grad_block, attn_rows = lax.optimization_barrier((cotangent, attn_rows))
+    grad_rows = ring_gather(grad_block.reshape(token_count, width), ctx_size, ctx_index)
     residual = inputs + dot(attn_rows, out_weight)
 
     normed_two, inv_two_all = rms_norm(residual, ffn_gain)
@@ -285,9 +360,6 @@
     probs_all = jax.nn.softmax(logits[:, :expert_count], axis=-1)
     scale_all = jax.nn.sigmoid(logits[:, expert_count])
     gate_all = lax.dynamic_index_in_dim(probs_all, ctx_index, 1, keepdims=False)
-    shared_pre = dot(low_two, shared_in)
-    shared_hid = swiglu(shared_pre, fs_own).astype(bf16)
-    shared_res = dot(shared_hid, shared_out)
 
     named = jnp.any(route_rows == ctx_index, axis=-1)
     before = jnp.arange(token_count)[:, None] < jnp.arange(token_count)[None, :]
@@ -317,12 +389,6 @@
     expert_hid = swiglu(expert_pre, FE).astype(bf16)
     expert_res = dot(expert_hid, expert_out).astype(bf16)
     routed = gate_all[:, None] * to_tokens(expert_res)
-    out_parts = (scale_all[:, None] * shared_res + routed).astype(bf16)
-    out_sum = ring_scatter(
-        out_parts.reshape(ctx_size, token_count, width), ctx_size, ctx_index
-    )
-    own_residual = own_rows(residual)
-    output = (own_residual + out_sum).astype(bf16).reshape(tokens.shape)
 
     grad_slots = to_slots(blocks_grad)
     gate_slots = jnp.sum(jnp.where(slot_mask, gate_blocks[:, None, :], 0.0), axis=-1).reshape(-1, 1)
@@ -335,6 +401,19 @@
     grad_expert_in = t_dot(buffer, grad_pre)
     grad_buffer = dot_t(grad_pre, expert_in).astype(bf16)
 
+    grad_expert_in, grad_expert_out, low_shared = lax.optimization_barrier(
+        (grad_expert_in.astype(bf16), grad_expert_out.astype(bf16), low_two)
+    )
+    sum_expert_out = sum_rows(grad_expert_out)
+    sum_expert_in = sum_rows(grad_expert_in)
+
+    shared_pre = dot(low_shared, shared_in)
+    shared_hid = swiglu(shared_pre, fs_own).astype(bf16)
+    shared_res = dot(shared_hid, shared_out)
+    out_parts = (scale_all[:, None] * shared_res + routed).astype(bf16)
+    out_sum = ring_scatter(out_parts, ctx_size, ctx_index)
+    own_residual = own_rows(residual)
+    output = (own_residual + out_sum).astype(bf16).reshape(tokens.shape)
     grad_f32 = grad_rows.astype(f32)
     grad_shared_res = (scale_all[:, None] * grad_f32).astype(bf16)
     gate_dots = jnp.sum(grad_f32 * shared_res, axis=-1).reshape(ctx_size, token_count)
@@ -343,9 +422,7 @@
     grad_shared_pre = swiglu_back(shared_pre, fs_own, grad_shared_hid).astype(bf16)
     grad_shared_in = t_dot(low_two, grad_shared_pre)
     two_parts = (dot_t(grad_shared_pre, shared_in) + to_tokens(grad_buffer)).astype(bf16)
-    grad_two = ring_scatter(
-        two_parts.reshape(ctx_size, token_count, width), ctx_size, ctx_index
-    )
+    grad_two = ring_scatter(two_parts, ctx_size, ctx_index)
 
     dots = jnp.stack([grad_gates, gate_dots], axis=1)
     dots = lax.all_to_all(dots, "ctx", split_axis=0, concat_axis=0, tiled=True)
@@ -379,7 +456,7 @@
         concat_axis=0,
         tiled=True,
     ).reshape(head_shape)
-    mixed_all = ring_gather(grad_mixed, ctx_size, ctx_index).reshape(seq_len, width)
+    mixed_all = ring_gather(grad_mixed, ctx_size, ctx_index)
     grad_out_weight = t_dot(attn_own, mixed_all)
     grad_weights = jnp.einsum("qhd,khd->hqk", grad_attn, values, preferred_element_type=f32)
     delta = jnp.sum(weights * grad_weights, axis=-1, keepdims=True)
@@ -397,11 +474,11 @@
         ],
         axis=-1,
     ).astype(bf16)
-    one_parts = dot_t(grad_projected, qkv_weight).astype(bf16)
-    grad_normed = ring_scatter(
-        one_parts.reshape(ctx_size, token_count, width), ctx_size, ctx_index
-    )
-    grad_inputs_norm, grad_gain_one = rms_back(
+    one_sums = dot_t(grad_projected, qkv_weight)
+    grad_gain_one = jnp.sum(one_sums * inputs * inv_one_all, axis=0)
+    one_parts = one_sums.astype(bf16)
+    grad_normed = ring_scatter(one_parts, ctx_size, ctx_index)
+    grad_inputs_norm, unused = rms_back(
         tokens.reshape(token_count, width).astype(f32),
         own_rows(inv_one_all),
         attn_gain,
@@ -413,11 +490,6 @@
     grad_bias = jnp.where(
         jnp.arange(ctx_size, dtype=i32)[None, :, None] == ctx_index, grad_bias, 0.0
     )
-
-    def sum_rows(grad):
-        return lax.psum_scatter(
-            grad.astype(bf16), "fsdp", scatter_dimension=0, tiled=True
-        ).astype(f32)
 
     small_grads = jnp.concatenate(
         [
@@ -426,7 +498,8 @@
         ],
         axis=1,
     )
-    small_grads = lax.psum_scatter(small_grads, axes, scatter_dimension=0, tiled=False)
+    small_grads = small_grads.reshape(ctx_size, fsdp_size, small_size)
+    small_grads = small_scatter(small_grads, ctx_size, fsdp_size, ctx_index).reshape(small_size)
     return (
         output,
         grad_tokens,
@@ -439,8 +512,8 @@
         small_grads[2 * shard : 3 * shard],
         merge_columns(grad_shared_in, 2, ctx_size, fsdp_size),
         sum_rows(grad_shared_out),
-        sum_rows(grad_expert_in)[None],
-        sum_rows(grad_expert_out)[None],
+        sum_expert_in[None],
+        sum_expert_out[None],
     )
 
 

time: 1090 us -> 988 us (0.906)
  blocking collectives: 128 us -> 80.7 us
  starting transfers between devices: 124 us -> 99 us
  waiting for transfers between devices: 356 us -> 379 us
  other arithmetic: 78.1 us -> 55.4 us
  local copies, waits for them, and re-layouts: 144 us -> 126 us
    ppermute x98 -> x73, waiting for transfers between devices: 148 us -> 271 us  [the longest x9 66.7 us: ring_scatter(): fore = lax.ppermute(fore, 'ctx', ahead)]
    reduce_scatter x4, waiting for transfers between devices: 188 us -> 105 us  [sum_rows(): lax.psum_scatter(grad.astype(bf16), 'fsdp', scatter_dimension=0, tiled=True)]
    all_gather x2 -> x0, blocking collectives: 65.2 us -> none  [the longest x1 35.6 us: local_split(): small = lax.all_gather(small, axes, axis=0, tiled=False)]
    ppermute x98 -> x73, starting transfers between devices: 101 us -> 82.5 us  [the longest x15 16.4 us: ring_walk(): fore = lax.ppermute(fore, 'ctx', ahead)]
    unnamed x14 -> x11, waiting for transfers between devices: 19.8 us -> 3.05 us
    convert_element_type x15 -> x12, other arithmetic: 27.5 us -> 11.5 us  [the longest x9 10.7 us: low(): return values.astype(jnp.bfloat16)]
    all_to_all x0 -> x1, blocking collectives: none -> 15.5 us  [local_split(): lax.all_to_all(grad_attn_rows.reshape(token_count, ctx_size, own_width).t...]
    dynamic_update_slice x62 -> x48, local copies, waits for them, and re-layouts: 42.7 us -> 33.2 us  [the longest x35 14.6 us: put(): lax.dynamic_update_slice(out, piece, (peer * rows + offset, jnp.zeros_lik...]
  transfers between devices with their start and end apart: 115 -> 87, of which waited for: 52 -> 44; matrix products, arithmetic and copies ran while one was open for 28% -> 29% of each run, Pallas kernels for 0% -> 0%
where the time goes in v2:
time: 988 us; the launch traced here: 979 us
  waiting for transfers between devices  379 us (38%)
  matrix products  208 us (21%)
  local copies, waits for them, and re-layouts  126 us (13%)
  starting transfers between devices  99 us (10%)
  blocking collectives  80.7 us (8%)
  other arithmetic  55.4 us (6%)
  between operations  30.4 us (3%)
    reduce_scatter x4, waiting for transfers between devices, sum_rows(): lax.psum_scatter(grad.astype(bf16), 'fsdp', scatter_dimension=0, tiled=True)  105 us
    ppermute x9, waiting for transfers between devices, ring_scatter(): fore = lax.ppermute(fore, 'ctx', ahead)  66.7 us
    all_to_all x2, blocking collectives, split_columns(): lax.all_to_all(pieces, 'ctx', split_axis=0, concat_axis=0, tiled=True)  65.2 us
    ppermute x1, waiting for transfers between devices, fsdp_gather(): far = lax.ppermute(shard, 'fsdp', other_chip(size))  58.3 us
    dot_general x8, matrix products, dot(): return jnp.dot(a, b, preferred_element_type=f32)  55.1 us
    dot_general x7, matrix products, dot_t(): lax.dot_general(a, b, (((1,), (1,)), ((), ())), preferred_element_type=f32)  50.7 us
    ppermute x15, waiting for transfers between devices, ring_walk(): rear = lax.ppermute(rear, 'ctx', back)  46.9 us
    ppermute x15, waiting for transfers between devices, ring_walk(): fore = lax.ppermute(fore, 'ctx', ahead)  43.5 us
  transfers between devices with their start and end apart: 87, of which 44 were waited for; matrix products, arithmetic and copies ran while one was open for 29% of the time, Pallas kernels for 0%

profile of v2, /device:TPU:8, one launch (start us, length us, event | category | flops | bytes accessed | tf_op | source)
XLA Modules:
  0.0 979.0 jit_solution(2526309704437329071)
XLA Ops:
  14.6 29.7 %all_to_all.30 = bf16[8,80,768]{2,1,0:T(8,128)(2,1)} all-to-all(bf16[8,80,768]{2,1,0:T(8,128)(2,1)S(1)} %pad_maximum_fusion.7), channel_id=1, replica_groups=mesh['ctx'=8,'fsdp'=4] {'ctx'}, dimensions={0} | all-to-all | bytes 1966080 | tf_op jit(solution)/shard_map/all_to_all | solution.py:216
  47.2 9.8 %collective-permute-done.1 = bf16[128,2048]{1,0:T(8,128)(2,1)S(1)} collective-permute-done((bf16[128,2048]{1,0:T(8,128)(2,1)S(1)}, bf16[128,2048]{1,0:T(8,128)(2,1)S(1)}, u32[]{:S(2)}, u32[]{:S(2)}) %collective-permute-start.1) | collective-permute-done | bytes 524320 | tf_op jit(solution)/shard_map/ppermute | solution.py:98
  93.9 35.4 %all_to_all.31 = bf16[8,64,1408]{2,1,0:T(8,128)(2,1)} all-to-all(bf16[8,64,1408]{2,1,0:T(8,128)(2,1)S(1)} %reshape.778), channel_id=1, replica_groups=mesh['ctx'=8,'fsdp'=4] {'ctx'}, dimensions={0} | all-to-all | bytes 2883584 | tf_op jit(solution)/shard_map/all_to_all | solution.py:216
  182.0 58.3 %collective-permute-done.25 = bf16[512,2048]{1,0:T(8,128)(2,1)} collective-permute-done((bf16[512,2048]{1,0:T(8,128)(2,1)S(1)}, bf16[512,2048]{1,0:T(8,128)(2,1)}, u32[]{:S(2)}, u32[]{:S(2)}) %collective-permute-start.25) | collective-permute-done | bytes 2097184 | tf_op jit(solution)/shard_map/ppermute | solution.py:167
  272.6 8.2 copy.194
  284.3 10.8 %collective-permute-done.10 = bf16[1024,256]{1,0:T(8,128)(2,1)} collective-permute-done((bf16[1024,256]{1,0:T(8,128)(2,1)S(1)}, bf16[1024,256]{1,0:T(8,128)(2,1)}, u32[]{:S(2)}, u32[]{:S(2)}) %collective-permute-start.10) | collective-permute-done | bytes 524320 | tf_op jit(solution)/shard_map/ppermute | solution.py:97
  320.3 13.8 %multiply_reduce_fusion.1 = (f32[1024]{0:T(1024)S(1)}, f32[1024,2048]{1,0:T(8,128)S(1)}) fusion(bf16[1024,2048]{1,0:T(8,128)(2,1)} %constant_dynamic-update-slice_fusion.44, bf16[2048,2048]{1,0:T(8,128)(2,1)} %bitcast.297, bf16[1024,2048]{1,0:T(8,128)(2,1)} %constant_dynamic-update-slice_fusion.35), kind=kOutput, calls=%fused_computation.28 | convolution fusion | flops 8598322176 | bytes 25169920 | tf_op jit(solution)/shard_map/dot_general | solution.py:272
  342.2 9.3 collective-permute-done.30
  353.7 9.8 collective-permute-done.32
  381.2 9.6 fusion.3
  394.2 8.4 fusion.31
  410.8 8.1 multiply_convert_fusion.6
  420.4 9.0 convolution_convert_fusion
  429.4 10.2 %fusion.50 = bf16[512,2048]{1,0:T(8,128)(2,1)S(1)} fusion(bf16[1,2048,2816]{2,1,0:T(8,128)(2,1)} %all-gather.16.cloned.1.call-done, bf16[512,1408]{1,0:T(8,128)(2,1)} %copy-done.54, bf16[512,1408]{1,0:T(8,128)(2,1)} %copy-done.53), kind=kOutput, calls=%fused_computation.64 | convolution fusion | flops 5912395776 | bytes 16515072 | tf_op jit(solution)/shard_map/dot_general | solution.py:275
  448.7 8.4 fusion.152
  457.1 10.3 %multiply_convert_fusion.2 = (bf16[1024,704]{1,0:T(8,128)(2,1)S(1)}, bf16[1024,704]{1,0:T(8,128)(2,1)}, bf16[1024,704]{1,0:T(8,128)(2,1)S(1)}) fusion(f32[1024,1408]{1,0:T(8,128)} %fusion.152, bf16[704,2048]{1,0:T(8,128)(2,1)} %all-gather.10.cloned.1.call-done, bf16[1024,2048]{1,0:T(8,128)(2,1)} %copy-done.2, f32[1024]{0:T(1024)S(1)} %bitcast.374), kind=kOutput, calls=%fused_computation.61 | convolution fusion | flops 2970615808 | bytes 17174528 | tf_op jit(solution)/shard_map/dot_general | solution.py:275
  481.2 10.5 %fusion.12 = bf16[1024,2048]{1,0:T(8,128)(2,1)S(1)} fusion(f32[8,128,2048]{2,1,0:T(8,128)} %fusion.89, bf16[2048,1408]{1,0:T(8,128)(2,1)} %bitcast.315, bf16[1024,704]{1,0:T(8,128)(2,1)} %get-tuple-element.108, bf16[1024,704]{1,0:T(8,128)(2,1)S(1)} %get-tuple-element.107), kind=kOutput, calls=%fused_computation.20 | convolution fusion | flops 5915541504 | bytes 21233664 | tf_op jit(solution)/shard_map/dot_general | solution.py:275
  524.2 8.4 collective-permute-done.40
  535.1 8.7 collective-permute-done.45
  546.3 8.7 collective-permute-done.37
  580.5 15.5 %all_to_all.32 = bf16[8,128,256]{1,2,0:T(8,128)(2,1)S(1)} all-to-all(bf16[8,128,256]{1,2,0:T(8,128)(2,1)} %bitcast.336), channel_id=1, replica_groups=mesh['ctx'=8,'fsdp'=4] {'ctx'}, dimensions={0} | all-to-all | bytes 1048576 | tf_op jit(solution)/shard_map/all_to_all | solution.py:452
  609.8 15.0 %fusion.62 = f32[1024,2,128]{0,2,1:T(8,128)} fusion(bf16[1024,2,128]{0,2,1:T(8,128)(2,1)} %copy-done.36, f32[2,1024,1024]{1,2,0:T(8,128)} %fusion.154, f32[2,1024,1024]{1,2,0:T(8,128)} %copy-done.5, f32[2,1024]{1,0:T(2,128)S(1)} %copy-done.47, pred[1024,1024]{0,1:T(8,128)(4,1)S(1)} %copy-done.14), kind=kOutput, calls=%fused_computation.86 | convolution fusion | flops 559942656 | bytes 19406848 | tf_op jit(solution)/shard_map/hqk,qhd->khd/dot_general | solution.py:466
  624.9 16.0 %broadcast_multiply_fusion.1 = (f32[1024,2,128]{0,2,1:T(8,128)}, f32[1024,2,128]{0,2,1:T(8,128)}, f32[1024,2,128]{0,2,1:T(8,128)}) fusion(f32[1024,128]{0,1:T(8,128)} %get-tuple-element.172, f32[1024,2,128]{0,2,1:T(8,128)} %fusion.62, bf16[1024,2,128]{0,2,1:T(8,128)(2,1)S(1)} %copy-done.35, f32[2,1024,1024]{1,2,0:T(8,128)} %fusion.154, ...), kind=kOutput, calls=%fused_computation.155 | convolution fusion | flops 560466944 | bytes 23076864 | tf_op jit(solution)/shard_map/hqk,khd->qhd/dot_general | solution.py:464
  652.8 9.7 convolution_convert_fusion.1
  666.0 7.7 convolution_convert_fusion.4
  675.8 12.4 %collective-permute-done.65 = bf16[128,2048]{1,0:T(8,128)(2,1)S(1)} collective-permute-done((bf16[128,2048]{1,0:T(8,128)(2,1)S(1)}, bf16[128,2048]{1,0:T(8,128)(2,1)S(1)}, u32[]{:S(2)}, u32[]{:S(2)}) %collective-permute-start.65) | collective-permute-done | bytes 524320 | tf_op jit(solution)/shard_map/ppermute | solution.py:97
  691.1 10.9 %collective-permute-done.67 = bf16[128,2048]{1,0:T(8,128)(2,1)S(1)} collective-permute-done((bf16[128,2048]{1,0:T(8,128)(2,1)S(1)}, bf16[128,2048]{1,0:T(8,128)(2,1)S(1)}, u32[]{:S(2)}, u32[]{:S(2)}) %collective-permute-start.67) | collective-permute-done | bytes 524320 | tf_op jit(solution)/shard_map/ppermute | solution.py:97
  728.1 8.4 fusion.11
  772.0 9.6 collective-permute-start.64
  797.6 35.5 %collective-permute-done.54 = bf16[128,2048]{1,0:T(8,128)(2,1)S(1)} collective-permute-done((bf16[128,2048]{1,0:T(8,128)(2,1)}, bf16[128,2048]{1,0:T(8,128)(2,1)S(1)}, u32[]{:S(2)}, u32[]{:S(2)}) %collective-permute-start.54) | collective-permute-done | bytes 524320 | tf_op jit(solution)/shard_map/ppermute | solution.py:149
  846.3 26.2 %reduce-scatter.17.cloned.1.call-done = bf16[352,2048]{1,0:T(8,128)(2,1)} async-done(((bf16[1408,2048]{1,0:T(8,128)(2,1)}), bf16[352,2048]{1,0:T(8,128)(2,1)}) %reduce-scatter.17.cloned.1.call-update) | async-done | bytes 1441808 | tf_op jit(solution)/shard_map/reduce_scatter | solution.py:286
  888.6 78.9 %reduce-scatter.15.cloned.1.call-done = bf16[512,2816]{1,0:T(8,128)(2,1)} async-done(((bf16[2048,2816]{1,0:T(8,128)(2,1)}), bf16[512,2816]{1,0:T(8,128)(2,1)}) %reduce-scatter.15.cloned.1.call-update) | async-done | bytes 2883600 | tf_op jit(solution)/shard_map/reduce_scatter | solution.py:286
  (535 shorter events, 417.3 us)
Async XLA Ops:
  7.2 237.8 %all-gather.12.cloned.1.call-start = ((), (), s32[]{:S(2)}) async-start(), calls=%async_computation.19 | async-start | bytes 4915200 | tf_op jit(solution)/shard_map/all_gather | solution.py:217
  44.4 331.1 %all-gather.18.cloned.1.call-start = ((), (), s32[]{:S(2)}) async-start(), calls=%async_computation.22 | async-start | bytes 7208960 | tf_op jit(solution)/shard_map/all_gather | solution.py:217
  129.4 251.9 %all-gather.16.cloned.1.call-start = ((), (), s32[]{:S(2)}) async-start(), calls=%async_computation.21 | async-start | bytes 14417920 | tf_op jit(solution)/shard_map/all_gather | solution.py:315
  130.1 264.1 %all-gather.14.cloned.1.call-start = ((), (), s32[]{:S(2)}) async-start(), calls=%async_computation.20 | async-start | bytes 7208960 | tf_op jit(solution)/shard_map/all_gather | solution.py:316
  130.7 326.4 %all-gather.10.cloned.1.call-start = ((), (), s32[]{:S(2)}) async-start(), calls=%async_computation.12 | async-start | bytes 3604480 | tf_op jit(solution)/shard_map/all_gather | solution.py:314
  167.1 73.2 %collective-permute-start.25 = (bf16[512,2048]{1,0:T(8,128)(2,1)S(1)}, bf16[512,2048]{1,0:T(8,128)(2,1)}, u32[]{:S(2)}, u32[]{:S(2)}) collective-permute-start(bf16[512,2048]{1,0:T(8,128)(2,1)S(1)} %constant_dynamic-update-slice_fusion.17), channel_id=1, source_target_pairs={{0,2},{1,3},{2,0},{3,1},{4,6},{5,7},{6,4},{7,5},{8,10},{9,11},{10,... | collective-permute-start | bytes 6291464 | tf_op jit(solution)/shard_map/ppermute | solution.py:167
  168.7 71.6 %collective-permute-start.24 = (bf16[512,2048]{1,0:T(8,128)(2,1)S(1)}, bf16[512,2048]{1,0:T(8,128)(2,1)S(1)}, u32[]{:S(2)}, u32[]{:S(2)}) collective-permute-start(bf16[512,2048]{1,0:T(8,128)(2,1)S(1)} %constant_dynamic-update-slice_fusion.17), channel_id=1, source_target_pairs={{0,1},{1,0},{2,3},{3,2},{4,5},{5,4},{6,7},{7,6},{8,9},{9,8},{10,11... | collective-permute-start | bytes 6291464 | tf_op jit(solution)/shard_map/ppermute | solution.py:168
  240.3 29.0 %collective-permute-start.26 = (bf16[512,2048]{1,0:T(8,128)(2,1)}, bf16[512,2048]{1,0:T(8,128)(2,1)}, u32[]{:S(2)}, u32[]{:S(2)}) collective-permute-start(bf16[512,2048]{1,0:T(8,128)(2,1)} %collective-permute-done.25), channel_id=1, source_target_pairs={{0,1},{1,0},{2,3},{3,2},{4,5},{5,4},{6,7},{7,6},{8,9},{9,8},{10,11... | collective-permute-start | bytes 6291464 | tf_op jit(solution)/shard_map/ppermute | solution.py:169
  318.3 21.1 %collective-permute-start.28 = (bf16[128,2048]{1,0:T(8,128)(2,1)S(1)}, bf16[128,2048]{1,0:T(8,128)(2,1)S(1)}, u32[]{:S(2)}, u32[]{:S(2)}) collective-permute-start(bf16[128,2048]{1,0:T(8,128)(2,1)S(1)} %bitcast.345), channel_id=1, source_target_pairs={{8,0},{16,8},{24,16},{28,24},{20,28},{12,20},{4,12},{0,4},{9,1},{1... | collective-permute-start | bytes 1572872 | tf_op jit(solution)/shard_map/ppermute | solution.py:98
  319.0 21.2 %collective-permute-start.27 = (bf16[128,2048]{1,0:T(8,128)(2,1)S(1)}, bf16[128,2048]{1,0:T(8,128)(2,1)S(1)}, u32[]{:S(2)}, u32[]{:S(2)}) collective-permute-start(bf16[128,2048]{1,0:T(8,128)(2,1)S(1)} %bitcast.346), channel_id=1, source_target_pairs={{0,8},{8,16},{16,24},{24,28},{28,20},{20,12},{12,4},{4,0},{1,9},{9... | collective-permute-start | bytes 1572872 | tf_op jit(solution)/shard_map/ppermute | solution.py:97
  474.8 24.4 %all-to-all-start.2 = ((f32[8,2,128]{2,1,0:T(2,128)}), f32[8,2,128]{2,1,0:T(2,128)S(1)}, u32[]{:S(2)}, u32[]{:S(2)}) async-start(f32[8,2,128]{2,1,0:T(2,128)} %pad_maximum_fusion.16), calls=%async_computation.2 | async-start | bytes 16384 | tf_op jit(solution)/shard_map/all_to_all | solution.py:428
  481.1 271.3 %reduce-scatter.7.cloned.1.call-start = ((), (), s32[]{:S(2)}) async-start(), calls=%async_computation.13 | async-start | bytes 3932160 | tf_op jit(solution)/shard_map/reduce_scatter | solution.py:230
  511.5 21.1 %collective-permute-start.40 = (bf16[128,2048]{1,0:T(8,128)(2,1)S(1)}, bf16[128,2048]{1,0:T(8,128)(2,1)S(1)}, u32[]{:S(2)}, u32[]{:S(2)}) collective-permute-start(bf16[128,2048]{1,0:T(8,128)(2,1)S(1)} %pad_maximum_fusion.11), channel_id=1, source_target_pairs={{8,0},{16,8},{24,16},{28,24},{20,28},{12,20},{4,12},{0,4},{9,1},{1... | collective-permute-start | bytes 1572872 | tf_op jit(solution)/shard_map/ppermute | solution.py:150
  512.2 20.4 %collective-permute-start.36 = (bf16[128,2048]{1,0:T(8,128)(2,1)S(1)}, bf16[128,2048]{1,0:T(8,128)(2,1)S(1)}, u32[]{:S(2)}, u32[]{:S(2)}) collective-permute-start(bf16[128,2048]{1,0:T(8,128)(2,1)S(1)} %pad_maximum_fusion.10), channel_id=1, source_target_pairs={{0,8},{8,16},{16,24},{24,28},{28,20},{20,12},{12,4},{4,0},{1,9},{9... | collective-permute-start | bytes 1572872 | tf_op jit(solution)/shard_map/ppermute | solution.py:149
  521.7 22.0 %collective-permute-start.45 = (bf16[128,2048]{1,0:T(8,128)(2,1)S(1)}, bf16[128,2048]{1,0:T(8,128)(2,1)S(1)}, u32[]{:S(2)}, u32[]{:S(2)}) collective-permute-start(bf16[128,2048]{1,0:T(8,128)(2,1)S(1)} %get-tuple-element.130), channel_id=1, source_target_pairs={{0,8},{8,16},{16,24},{24,28},{28,20},{20,12},{12,4},{4,0},{1,9},{9... | collective-permute-start | bytes 1572872 | tf_op jit(solution)/shard_map/ppermute | solution.py:149
  523.3 20.6 %collective-permute-start.49 = (bf16[128,2048]{1,0:T(8,128)(2,1)S(1)}, bf16[128,2048]{1,0:T(8,128)(2,1)S(1)}, u32[]{:S(2)}, u32[]{:S(2)}) collective-permute-start(bf16[128,2048]{1,0:T(8,128)(2,1)S(1)} %get-tuple-element.131), channel_id=1, source_target_pairs={{8,0},{16,8},{24,16},{28,24},{20,28},{12,20},{4,12},{0,4},{9,1},{1... | collective-permute-start | bytes 1572872 | tf_op jit(solution)/shard_map/ppermute | solution.py:150
  533.0 22.0 %collective-permute-start.37 = (bf16[128,2048]{1,0:T(8,128)(2,1)S(1)}, bf16[128,2048]{1,0:T(8,128)(2,1)S(1)}, u32[]{:S(2)}, u32[]{:S(2)}) collective-permute-start(bf16[128,2048]{1,0:T(8,128)(2,1)S(1)} %get-tuple-element.140), channel_id=1, source_target_pairs={{0,8},{8,16},{16,24},{24,28},{28,20},{20,12},{12,4},{4,0},{1,9},{9... | collective-permute-start | bytes 1572872 | tf_op jit(solution)/shard_map/ppermute | solution.py:149
  534.6 20.5 %collective-permute-start.41 = (bf16[128,2048]{1,0:T(8,128)(2,1)S(1)}, bf16[128,2048]{1,0:T(8,128)(2,1)S(1)}, u32[]{:S(2)}, u32[]{:S(2)}) collective-permute-start(bf16[128,2048]{1,0:T(8,128)(2,1)S(1)} %get-tuple-element.141), channel_id=1, source_target_pairs={{8,0},{16,8},{24,16},{28,24},{20,28},{12,20},{4,12},{0,4},{9,1},{1... | collective-permute-start | bytes 1572872 | tf_op jit(solution)/shard_map/ppermute | solution.py:150
  544.2 20.5 %collective-permute-start.46 = (bf16[128,2048]{1,0:T(8,128)(2,1)S(1)}, bf16[128,2048]{1,0:T(8,128)(2,1)S(1)}, u32[]{:S(2)}, u32[]{:S(2)}) collective-permute-start(bf16[128,2048]{1,0:T(8,128)(2,1)S(1)} %get-tuple-element.128), channel_id=1, source_target_pairs={{0,8},{8,16},{16,24},{24,28},{28,20},{20,12},{12,4},{4,0},{1,9},{9... | collective-permute-start | bytes 1572872 | tf_op jit(solution)/shard_map/ppermute | solution.py:149
  652.7 133.8 %reduce-scatter.11.cloned.1.call-start = ((), (), s32[]{:S(2)}) async-start(), calls=%async_computation.15 | async-start | bytes 7208960 | tf_op jit(solution)/shard_map/reduce_scatter | solution.py:230
  665.5 173.1 %reduce-scatter.13.cloned.1.call-start = ((), (), s32[]{:S(2)}) async-start(), calls=%async_computation.16 | async-start | bytes 3604480 | tf_op jit(solution)/shard_map/reduce_scatter | solution.py:286
  673.7 167.5 %reduce-scatter.9.cloned.1.call-start = ((), (), s32[]{:S(2)}) async-start(), calls=%async_computation.14 | async-start | bytes 1310720 | tf_op jit(solution)/shard_map/reduce_scatter | solution.py:286
  724.4 148.1 %reduce-scatter.17.cloned.1.call-start = ((), (), s32[]{:S(2)}) async-start(), calls=%async_computation.18 | async-start | bytes 7208960 | tf_op jit(solution)/shard_map/reduce_scatter | solution.py:286
  725.0 242.5 %reduce-scatter.15.cloned.1.call-start = ((), (), s32[]{:S(2)}) async-start(), calls=%async_computation.17 | async-start | bytes 14417920 | tf_op jit(solution)/shard_map/reduce_scatter | solution.py:286
  752.4 34.1 %all-to-all-start.4 = ((bf16[8,64,768]{2,1,0:T(8,128)(2,1)}), bf16[8,64,768]{2,1,0:T(8,128)(2,1)S(1)}, u32[]{:S(2)}, u32[]{:S(2)}) async-start(bf16[8,64,768]{2,1,0:T(8,128)(2,1)} %bitcast.355), calls=%async_computation.5 | async-start | bytes 1572864 | tf_op jit(solution)/shard_map/all_to_all | solution.py:232
  764.3 26.5 %collective-permute-start.53 = (bf16[128,2048]{1,0:T(8,128)(2,1)}, bf16[128,2048]{1,0:T(8,128)(2,1)S(1)}, u32[]{:S(2)}, u32[]{:S(2)}) collective-permute-start(bf16[128,2048]{1,0:T(8,128)(2,1)} %get-tuple-element.120), channel_id=1, source_target_pairs={{0,8},{8,16},{16,24},{24,28},{28,20},{20,12},{12,4},{4,0},{1,9},{9... | collective-permute-start | bytes 1572872 | tf_op jit(solution)/shard_map/ppermute | solution.py:149
  764.3 26.5 %collective-permute-start.57 = (bf16[128,2048]{1,0:T(8,128)(2,1)S(1)}, bf16[128,2048]{1,0:T(8,128)(2,1)}, u32[]{:S(2)}, u32[]{:S(2)}) collective-permute-start(bf16[128,2048]{1,0:T(8,128)(2,1)S(1)} %get-tuple-element.121), channel_id=1, source_target_pairs={{8,0},{16,8},{24,16},{28,24},{20,28},{12,20},{4,12},{0,4},{9,1},{1... | collective-permute-start | bytes 1572872 | tf_op jit(solution)/shard_map/ppermute | solution.py:150
  772.0 23.6 %collective-permute-start.62 = (f32[896]{0:T(1024)S(1)}, f32[896]{0:T(1024)S(1)}, u32[]{:S(2)}, u32[]{:S(2)}) collective-permute-start(f32[896]{0:T(1024)S(1)} %get-tuple-element.98), channel_id=1, source_target_pairs={{0,8},{4,12},{8,16},{12,20},{16,24},{20,28},{24,0},{28,4},{1,9},{5... | collective-permute-start | bytes 10760 | tf_op jit(solution)/shard_map/ppermute | solution.py:195
  772.0 23.5 %collective-permute-start.64 = (f32[896]{0:T(1024)S(1)}, f32[896]{0:T(1024)S(1)}, u32[]{:S(2)}, u32[]{:S(2)}) collective-permute-start(f32[896]{0:T(1024)S(1)} %get-tuple-element.99), channel_id=1, source_target_pairs={{0,24},{4,28},{8,0},{12,4},{16,8},{20,12},{24,16},{28,20},{1,25},{... | collective-permute-start | bytes 10760 | tf_op jit(solution)/shard_map/ppermute | solution.py:195
  786.5 89.3 %all-to-all-start.5 = ((bf16[8,64,1408]{2,1,0:T(8,128)(2,1)}), bf16[8,64,1408]{2,1,0:T(8,128)(2,1)}, u32[]{:S(2)}, u32[]{:S(2)}) async-start(bf16[8,64,1408]{2,1,0:T(8,128)(2,1)} %bitcast.349), calls=%async_computation.8 | async-start | bytes 2883584 | tf_op jit(solution)/shard_map/all_to_all | solution.py:232
  793.5 39.6 %collective-permute-start.54 = (bf16[128,2048]{1,0:T(8,128)(2,1)}, bf16[128,2048]{1,0:T(8,128)(2,1)S(1)}, u32[]{:S(2)}, u32[]{:S(2)}) collective-permute-start(bf16[128,2048]{1,0:T(8,128)(2,1)} %get-tuple-element.118), channel_id=1, source_target_pairs={{0,8},{8,16},{16,24},{24,28},{28,20},{20,12},{12,4},{4,0},{1,9},{9... | collective-permute-start | bytes 1572872 | tf_op jit(solution)/shard_map/ppermute | solution.py:149
  794.9 39.8 %collective-permute-start.58 = (bf16[128,2048]{1,0:T(8,128)(2,1)}, bf16[128,2048]{1,0:T(8,128)(2,1)S(1)}, u32[]{:S(2)}, u32[]{:S(2)}) collective-permute-start(bf16[128,2048]{1,0:T(8,128)(2,1)} %get-tuple-element.119), channel_id=1, source_target_pairs={{8,0},{16,8},{24,16},{28,24},{20,28},{12,20},{4,12},{0,4},{9,1},{1... | collective-permute-start | bytes 1572872 | tf_op jit(solution)/shard_map/ppermute | solution.py:150
  (115 other events, 1554.0 us)
Sparse Core Ops, SparseCore 0:
  44.5 32.2 all-gather.11
  129.5 47.2 all-gather.17
  178.4 100.6 all-gather.15
  280.5 43.3 all-gather.13
  325.4 27.0 all-gather.9
  652.9 36.4 reduce-scatter.6
  692.6 54.8 reduce-scatter.10
  750.6 36.3 reduce-scatter.12
  790.3 24.8 reduce-scatter.8
  817.6 54.8 reduce-scatter.16
  875.3 92.1 reduce-scatter.14

commit v3 on v2

--- a/solution.py
+++ b/solution.py
@@ -162,14 +162,46 @@
     return [(i, i ^ 2) for i in range(size)]
 
 
-def fsdp_gather(shard, size):
-    index = lax.axis_index("fsdp")
+def fsdp_pieces(shard, size):
     far = lax.ppermute(shard, "fsdp", other_chip(size))
     near = lax.ppermute(shard, "fsdp", other_core(size))
+    return (far, near)
+
+
+def fsdp_join(shard, far, near, size):
+    index = lax.axis_index("fsdp")
     far_near = lax.ppermute(far, "fsdp", other_core(size))
     out = jnp.zeros((size,) + shard.shape, shard.dtype)
     for piece, peer in ((shard, index), (near, index ^ 1), (far, index ^ 2), (far_near, index ^ 3)):
         out = lax.dynamic_update_index_in_dim(out, piece, peer, 0)
+    return out
+
+
+def after(value, *deps):
+    return lax.optimization_barrier((value,) + deps)
+
+
+def fsdp_scatter(grad, size, axis):
+    index = lax.axis_index("fsdp")
+
+    def pick(peer):
+        return lax.dynamic_index_in_dim(grad, peer, axis, keepdims=False)
+
+    far_near = lax.ppermute(pick(index ^ 3), "fsdp", other_core(size))
+    near = lax.ppermute(pick(index ^ 1), "fsdp", other_core(size))
+    far = (pick(index ^ 2).astype(jnp.float32) + far_near.astype(jnp.float32)).astype(jnp.bfloat16)
+    far = lax.ppermute(far, "fsdp", other_chip(size))
+    return pick(index).astype(jnp.float32) + near.astype(jnp.float32) + far.astype(jnp.float32)
+
+
+def exchange(pieces, size, ctx_index):
+    out = jnp.zeros_like(pieces)
+    own = lax.dynamic_index_in_dim(pieces, ctx_index, 0, keepdims=False)
+    out = lax.dynamic_update_index_in_dim(out, own, ctx_index, 0)
+    for k in range(1, size):
+        piece = lax.dynamic_index_in_dim(pieces, (ctx_index + k) % size, 0, keepdims=False)
+        piece = lax.ppermute(piece, "ctx", [(i, (i + k) % size) for i in range(size)])
+        out = lax.dynamic_update_index_in_dim(out, piece, (ctx_index - k) % size, 0)
     return out
 
 
@@ -200,7 +232,7 @@
     return total
 
 
-def split_columns(weight, groups, size, extra):
+def column_pieces(weight, groups, size, ctx_index, extra):
     rows = weight.shape[0]
     width = weight.shape[1] // (groups * size)
     pieces = weight.reshape(rows, groups, size, width).transpose(2, 0, 1, 3)
@@ -213,22 +245,12 @@
             extra.reshape(1, more, groups * width), (size, more, groups * width)
         )
         pieces = jnp.concatenate([pieces, extra], axis=1)
-    pieces = lax.all_to_all(pieces, "ctx", split_axis=0, concat_axis=0, tiled=True)
-    whole = lax.all_gather(pieces, "fsdp", axis=0, tiled=False)
-    whole = whole.transpose(1, 0, 2, 3)
-    taken = whole[:, :, :rows].reshape(-1, groups * width)
-    if extra is None:
-        return taken
-    return (taken, whole[:, :, rows:].reshape(-1, more * groups * width)[:, :count])
-
-
-def merge_columns(grad, groups, size, fsdp_size):
-    width = grad.shape[1] // groups
-    rows = grad.shape[0] // (size * fsdp_size)
-    pieces = grad.reshape(size, fsdp_size, rows, groups * width).transpose(1, 0, 2, 3)
-    pieces = pieces.astype(jnp.bfloat16).reshape(grad.shape)
-    pieces = lax.psum_scatter(pieces, "fsdp", scatter_dimension=0, tiled=True)
-    pieces = pieces.reshape(size, rows, groups * width)
+    return exchange(pieces, size, ctx_index)
+
+
+def merge_columns(pieces, groups, size):
+    rows = pieces.shape[1]
+    width = pieces.shape[2] // groups
     pieces = lax.all_to_all(pieces, "ctx", split_axis=0, concat_axis=0, tiled=True)
     pieces = pieces.reshape(size, rows, groups, width).transpose(1, 2, 0, 3)
     return pieces.reshape(rows, groups * size * width).astype(jnp.float32)
@@ -291,8 +313,13 @@
     small = [gain_attn, gain_ffn, w_shared_gate, w_router.reshape(-1), b_qkv]
     small_size = sum(piece.shape[0] for piece in small)
     small = jnp.concatenate(small + [routes.astype(bf16).reshape(-1)], axis=0)
+    small_count = small.shape[0]
     token_rows = ring_gather(tokens.reshape(token_count, width), ctx_size, ctx_index)
-    qkv_weight, small = split_columns(w_qkv, 3, ctx_size, small)
+    pieces = column_pieces(w_qkv, 3, ctx_size, ctx_index, small)
+    pieces = fsdp_join(pieces, *fsdp_pieces(pieces, fsdp_size), fsdp_size)
+    pieces = pieces.transpose(1, 0, 2, 3)
+    qkv_weight = pieces[:, :, :shard].reshape(width, 3 * own_width)
+    small = pieces[:, :, shard:].reshape(device_count, -1)[:, :small_count]
     attn_gain = small[:, :shard].reshape(width).astype(f32)
     ffn_gain = small[:, shard : 2 * shard].reshape(width).astype(f32)
     gate_vector = small[:, 2 * shard : 3 * shard].reshape(width)
@@ -305,15 +332,14 @@
         route_rows.reshape(ctx_size, fsdp_size, -1), lax.axis_index("fsdp"), 1, keepdims=False
     ).reshape(ctx_size, token_count, top_count)
 
-    out_shard, token_rows = lax.optimization_barrier((w_out, token_rows))
-    out_weight = fsdp_gather(ring_gather(out_shard, ctx_size, ctx_index), fsdp_size)
-    out_weight = out_weight.reshape(fsdp_size, ctx_size, -1, width)
-    out_weight = out_weight.transpose(1, 0, 2, 3).reshape(width, width)
-    in_shard, token_rows = lax.optimization_barrier((w_shared_in, token_rows))
-    shared_in = split_columns(in_shard, 2, ctx_size, None)
-    shared_out = lax.all_gather(w_shared_out, "fsdp", axis=0, tiled=True)
     expert_in = lax.all_gather(w_expert_in[0], "fsdp", axis=0, tiled=True)
     expert_out = lax.all_gather(w_expert_out[0], "fsdp", axis=0, tiled=True)
+    out_shard, in_shard, token_rows = after(w_out, w_shared_in, token_rows)
+    out_rows = ring_gather(out_shard, ctx_size, ctx_index)
+    out_far, out_near = fsdp_pieces(out_rows, fsdp_size)
+    shared_in = column_pieces(in_shard, 2, ctx_size, ctx_index, None)
+    shared_in = lax.all_gather(shared_in, "fsdp", axis=0, tiled=False)
+    shared_out = lax.all_gather(w_shared_out, "fsdp", axis=0, tiled=True)
 
     block_ids = jnp.arange(ctx_size, dtype=i32)[:, None]
     local_index = jnp.arange(block_len, dtype=i32)[None, :]
@@ -348,8 +374,12 @@
     weights_low = weights.astype(bf16)
     attended = jnp.einsum("hqk,khd->qhd", weights_low, values, preferred_element_type=f32)
     attn_own = attended.astype(bf16).reshape(seq_len, own_width)
+    out_rows, out_far, out_near, attn_own = after(out_rows, out_far, out_near, attn_own)
+    out_weight = fsdp_join(out_rows, out_far, out_near, fsdp_size)
+    out_weight = out_weight.reshape(fsdp_size, ctx_size, -1, width)
+    out_weight = out_weight.transpose(1, 0, 2, 3).reshape(width, width)
     attn_rows = ring_gather_columns(attn_own, ctx_size, ctx_index)
-    grad_block, attn_rows = lax.optimization_barrier((cotangent, attn_rows))
+    grad_block, attn_rows = after(cotangent, attn_rows)
     grad_rows = ring_gather(grad_block.reshape(token_count, width), ctx_size, ctx_index)
     residual = inputs + dot(attn_rows, out_weight)
 
@@ -389,6 +419,14 @@
     expert_hid = swiglu(expert_pre, FE).astype(bf16)
     expert_res = dot(expert_hid, expert_out).astype(bf16)
     routed = gate_all[:, None] * to_tokens(expert_res)
+
+    shared_in, expert_res = after(shared_in, expert_res)
+    shared_in = shared_in.transpose(1, 0, 2, 3).reshape(width, 2 * fs_own)
+    shared_pre = dot(low_two, shared_in)
+    shared_hid = swiglu(shared_pre, fs_own).astype(bf16)
+    shared_res = dot(shared_hid, shared_out)
+    out_parts = (scale_all[:, None] * shared_res + routed).astype(bf16)
+    out_sum = ring_scatter(out_parts, ctx_size, ctx_index)
 
     grad_slots = to_slots(blocks_grad)
     gate_slots = jnp.sum(jnp.where(slot_mask, gate_blocks[:, None, :], 0.0), axis=-1).reshape(-1, 1)
@@ -401,21 +439,17 @@
     grad_expert_in = t_dot(buffer, grad_pre)
     grad_buffer = dot_t(grad_pre, expert_in).astype(bf16)
 
-    grad_expert_in, grad_expert_out, low_shared = lax.optimization_barrier(
-        (grad_expert_in.astype(bf16), grad_expert_out.astype(bf16), low_two)
-    )
-    sum_expert_out = sum_rows(grad_expert_out)
+    grad_expert_in, grad_expert_out, grad_shared_res = after(
+        grad_expert_in.astype(bf16),
+        grad_expert_out.astype(bf16),
+        (scale_all[:, None] * grad_rows.astype(f32)).astype(bf16),
+    )
+    sum_expert_out = fsdp_scatter(
+        grad_expert_out.reshape(fsdp_size, -1, width), fsdp_size, 0
+    )
     sum_expert_in = sum_rows(grad_expert_in)
 
-    shared_pre = dot(low_shared, shared_in)
-    shared_hid = swiglu(shared_pre, fs_own).astype(bf16)
-    shared_res = dot(shared_hid, shared_out)
-    out_parts = (scale_all[:, None] * shared_res + routed).astype(bf16)
-    out_sum = ring_scatter(out_parts, ctx_size, ctx_index)
-    own_residual = own_rows(residual)
-    output = (own_residual + out_sum).astype(bf16).reshape(tokens.shape)
     grad_f32 = grad_rows.astype(f32)
-    grad_shared_res = (scale_all[:, None] * grad_f32).astype(bf16)
     gate_dots = jnp.sum(grad_f32 * shared_res, axis=-1).reshape(ctx_size, token_count)
     grad_shared_out = t_dot(shared_hid, grad_shared_res)
     grad_shared_hid = dot_t(grad_shared_res, shared_out)
@@ -423,6 +457,9 @@
     grad_shared_in = t_dot(low_two, grad_shared_pre)
     two_parts = (dot_t(grad_shared_pre, shared_in) + to_tokens(grad_buffer)).astype(bf16)
     grad_two = ring_scatter(two_parts, ctx_size, ctx_index)
+    grad_two, out_sum = after(grad_two, out_sum)
+    own_residual = own_rows(residual)
+    output = (own_residual + out_sum).astype(bf16).reshape(tokens.shape)
 
     dots = jnp.stack([grad_gates, gate_dots], axis=1)
     dots = lax.all_to_all(dots, "ctx", split_axis=0, concat_axis=0, tiled=True)
@@ -456,8 +493,8 @@
         concat_axis=0,
         tiled=True,
     ).reshape(head_shape)
+    grad_attn, sum_expert_out = after(grad_attn, sum_expert_out)
     mixed_all = ring_gather(grad_mixed, ctx_size, ctx_index)
-    grad_out_weight = t_dot(attn_own, mixed_all)
     grad_weights = jnp.einsum("qhd,khd->hqk", grad_attn, values, preferred_element_type=f32)
     delta = jnp.sum(weights * grad_weights, axis=-1, keepdims=True)
     grad_scores = jnp.where(allowed[None], weights * (grad_weights - delta), 0.0).astype(bf16)
@@ -474,6 +511,7 @@
         ],
         axis=-1,
     ).astype(bf16)
+    grad_projected, mixed_all, sum_expert_in = after(grad_projected, mixed_all, sum_expert_in)
     one_sums = dot_t(grad_projected, qkv_weight)
     grad_gain_one = jnp.sum(one_sums * inputs * inv_one_all, axis=0)
     one_parts = one_sums.astype(bf16)
@@ -491,6 +529,19 @@
         jnp.arange(ctx_size, dtype=i32)[None, :, None] == ctx_index, grad_bias, 0.0
     )
 
+    grad_out_weight = t_dot(attn_own, mixed_all)
+    sum_qkv_weight = fsdp_scatter(
+        grad_qkv_weight.astype(bf16).reshape(ctx_size, fsdp_size, shard, 3 * own_width),
+        fsdp_size,
+        1,
+    ).astype(bf16)
+    sum_shared_in = grad_shared_in.astype(bf16).reshape(ctx_size, fsdp_size, shard, 2 * fs_own)
+    sum_shared_in = lax.psum_scatter(
+        sum_shared_in.transpose(1, 0, 2, 3).reshape(width, 2 * fs_own),
+        "fsdp",
+        scatter_dimension=0,
+        tiled=True,
+    ).reshape(ctx_size, shard, 2 * fs_own)
     small_grads = jnp.concatenate(
         [
             piece.reshape(device_count, -1)
@@ -503,14 +554,14 @@
     return (
         output,
         grad_tokens,
-        merge_columns(grad_qkv_weight, 3, ctx_size, fsdp_size),
+        merge_columns(sum_qkv_weight, 3, ctx_size),
         small_grads[router_end:],
         sum_rows(grad_out_weight),
         small_grads[:shard],
         small_grads[shard : 2 * shard],
         small_grads[3 * shard : router_end].reshape(shard, expert_count),
         small_grads[2 * shard : 3 * shard],
-        merge_columns(grad_shared_in, 2, ctx_size, fsdp_size),
+        merge_columns(sum_shared_in, 2, ctx_size),
         sum_rows(grad_shared_out),
         sum_expert_in[None],
         sum_expert_out[None],

time: 988 us -> 876 us (0.89)
  waiting for transfers between devices: 379 us -> 298 us
  blocking collectives: 80.7 us -> 0 us
  starting transfers between devices: 99 us -> 129 us
  other arithmetic: 55.4 us -> 78.2 us
  matrix products: 208 us -> 195 us
    reduce_scatter x4 -> x3, waiting for transfers between devices: 105 us -> 0.01 us  [sum_rows(): lax.psum_scatter(grad.astype(bf16), 'fsdp', scatter_dimension=0, tiled=True)]
    all_to_all x3 -> x0, blocking collectives: 80.7 us -> none  [the longest x2 65.2 us: split_columns(): lax.all_to_all(pieces, 'ctx', split_axis=0, concat_axis=0, tiled=True)]
    ppermute x3 -> x26, waiting for transfers between devices: 58.3 us -> 110 us  [the longest x2 64.5 us: fsdp_pieces(): far = lax.ppermute(shard, 'fsdp', other_chip(size))]
    ppermute x15, waiting for transfers between devices: 46.9 us -> 3.21 us  [ring_walk(): rear = lax.ppermute(rear, 'ctx', back)]
    ppermute x9, waiting for transfers between devices: 66.7 us -> 35.8 us  [ring_scatter(): fore = lax.ppermute(fore, 'ctx', ahead)]
    ppermute x3 -> x26, starting transfers between devices: 1.61 us -> 29.4 us  [the longest x14 25.7 us: exchange(): lax.ppermute(piece, 'ctx', [(i, (i + k) % size) for i in range(size)])]
    ppermute x15, waiting for transfers between devices: 43.5 us -> 66.4 us  [ring_walk(): fore = lax.ppermute(fore, 'ctx', ahead)]
    dynamic_update_slice x35, local copies, waits for them, and re-layouts: 14.6 us -> 28.9 us  [put(): lax.dynamic_update_slice(out, piece, (peer * rows + offset, jnp.zeros_lik...]
  transfers between devices with their start and end apart: 87 -> 108, of which waited for: 44 -> 53; matrix products, arithmetic and copies ran while one was open for 29% -> 40% of each run, Pallas kernels for 0% -> 0%
where the time goes in v3:
time: 876 us; the launch traced here: 863 us
  waiting for transfers between devices  298 us (34%)
  matrix products  195 us (22%)
  local copies, waits for them, and re-layouts  131 us (15%)
  starting transfers between devices  129 us (15%)
  other arithmetic  78.2 us (9%)
  between operations  31.3 us (4%)
    ppermute x15, waiting for transfers between devices, ring_walk(): fore = lax.ppermute(fore, 'ctx', ahead)  66.4 us
    ppermute x2, waiting for transfers between devices, fsdp_pieces(): far = lax.ppermute(shard, 'fsdp', other_chip(size))  64.5 us
    dot_general x8, matrix products, dot(): return jnp.dot(a, b, preferred_element_type=f32)  55.6 us
    dot_general x7, matrix products, dot_t(): lax.dot_general(a, b, (((1,), (1,)), ((), ())), preferred_element_type=f32)  46 us
    dot_general x8, matrix products, t_dot(): lax.dot_general(a, b, (((0,), (0,)), ((), ())), preferred_element_type=f32)  41 us
    ppermute x9, waiting for transfers between devices, ring_scatter(): fore = lax.ppermute(fore, 'ctx', ahead)  35.8 us
    ppermute x9, waiting for transfers between devices, ring_scatter(): rear = lax.ppermute(rear, 'ctx', back)  30.2 us
    dynamic_update_slice x35, local copies, waits for them, and re-layouts, put(): lax.dynamic_update_slice(out, piece, (peer * rows + offset, jnp.zeros_lik...  28.9 us
  transfers between devices with their start and end apart: 108, of which 53 were waited for; matrix products, arithmetic and copies ran while one was open for 40% of the time, Pallas kernels for 0%

profile of v3, /device:TPU:8, one launch (start us, length us, event | category | flops | bytes accessed | tf_op | source)
XLA Modules:
  0.0 862.9 jit_solution(15075464163327376908)
XLA Ops:
  11.5 10.9 %collective-permute-done = bf16[128,2048]{1,0:T(8,128)(2,1)S(1)} collective-permute-done((bf16[128,2048]{1,0:T(8,128)(2,1)S(1)}, bf16[128,2048]{1,0:T(8,128)(2,1)S(1)}, u32[]{:S(2)}, u32[]{:S(2)}) %collective-permute-start) | collective-permute-done | bytes 524320 | tf_op jit(solution)/shard_map/ppermute | solution.py:97
  39.8 7.5 collective-permute-done.4
  75.1 11.1 %collective-permute-done.47 = bf16[64,1408]{1,0:T(8,128)(2,1)S(1)} collective-permute-done((bf16[64,1408]{1,0:T(8,128)(2,1)S(1)}, bf16[64,1408]{1,0:T(8,128)(2,1)S(1)}, u32[]{:S(2)}, u32[]{:S(2)}) %collective-permute-start.47) | collective-permute-done | bytes 180256 | tf_op jit(solution)/shard_map/ppermute | solution.py:203
  106.9 8.8 %collective-permute-done.20 = bf16[80,768]{1,0:T(8,128)(2,1)S(1)} collective-permute-done((bf16[80,768]{1,0:T(8,128)(2,1)S(1)}, bf16[80,768]{1,0:T(8,128)(2,1)S(1)}, u32[]{:S(2)}, u32[]{:S(2)}) %collective-permute-start.20) | collective-permute-done | bytes 122912 | tf_op jit(solution)/shard_map/ppermute | solution.py:203
  134.0 17.4 %collective-permute-done.26 = bf16[8,80,768]{2,1,0:T(8,128)(2,1)} collective-permute-done((bf16[8,80,768]{2,1,0:T(8,128)(2,1)S(1)}, bf16[8,80,768]{2,1,0:T(8,128)(2,1)}, u32[]{:S(2)}, u32[]{:S(2)}) %collective-permute-start.26) | collective-permute-done | bytes 983072 | tf_op jit(solution)/shard_map/ppermute | solution.py:166
  212.0 47.1 %collective-permute-done.16 = bf16[512,2048]{1,0:T(8,128)(2,1)} collective-permute-done((bf16[512,2048]{1,0:T(8,128)(2,1)}, bf16[512,2048]{1,0:T(8,128)(2,1)}, u32[]{:S(2)}, u32[]{:S(2)}) %collective-permute-start.16) | collective-permute-done | bytes 2097184 | tf_op jit(solution)/shard_map/ppermute | solution.py:166
  277.2 6.9 collective-permute-done.30
  312.4 8.3 copy.170
  320.7 13.3 %multiply_reduce_fusion.1 = (f32[1024]{0:T(1024)S(1)}, f32[1024,2048]{1,0:T(8,128)S(1)}) fusion(bf16[1024,2048]{1,0:T(8,128)(2,1)} %copy-done.19, bf16[2048,2048]{1,0:T(8,128)(2,1)} %bitcast.388, bf16[1024,2048]{1,0:T(8,128)(2,1)} %constant_dynamic-update-slice_fusion.35), kind=kOutput, calls=%fused_computation.28 | convolution fusion | flops 8598322176 | bytes 25169920 | tf_op jit(solution)/shard_map/dot_general | solution.py:294
  343.4 11.4 %collective-permute-done.39 = bf16[128,2048]{1,0:T(8,128)(2,1)S(1)} collective-permute-done((bf16[128,2048]{1,0:T(8,128)(2,1)S(1)}, bf16[128,2048]{1,0:T(8,128)(2,1)S(1)}, u32[]{:S(2)}, u32[]{:S(2)}) %collective-permute-start.39) | collective-permute-done | bytes 524320 | tf_op jit(solution)/shard_map/ppermute | solution.py:97
  357.6 9.1 %collective-permute-done.41 = bf16[128,2048]{1,0:T(8,128)(2,1)S(1)} collective-permute-done((bf16[128,2048]{1,0:T(8,128)(2,1)S(1)}, bf16[128,2048]{1,0:T(8,128)(2,1)S(1)}, u32[]{:S(2)}, u32[]{:S(2)}) %collective-permute-start.41) | collective-permute-done | bytes 524320 | tf_op jit(solution)/shard_map/ppermute | solution.py:97
  381.4 9.5 %fusion.3 = f32[512,2816]{1,0:T(8,128)S(1)} fusion(bf16[512,2048]{1,0:T(8,128)(2,1)S(1)} %bitcast.435, bf16[1,2048,2816]{2,1,0:T(8,128)(2,1)} %all-gather.13.cloned.1.call-done), kind=kOutput, calls=%fused_computation.7 | convolution fusion | flops 5905580032 | bytes 19398656 | tf_op jit(solution)/shard_map/dot_general | solution.py:294
  421.1 9.3 %convolution_convert_fusion = bf16[2048,2816]{1,0:T(8,128)(2,1)} fusion(bf16[512,2048]{1,0:T(8,128)(2,1)S(1)} %bitcast.436, bf16[512,1408]{1,0:T(8,128)(2,1)S(1)} %get-tuple-element.121, bf16[512,1408]{1,0:T(8,128)(2,1)S(1)} %get-tuple-element.120), kind=kOutput, calls=%fused_computation.9 | convolution fusion | flops 5917114368 | bytes 16515072 | tf_op jit(solution)/shard_map/dot_general | solution.py:300
  430.4 11.3 %fusion.169 = f32[1024,1408]{0,1:T(8,128)} fusion(bf16[1024,2048]{1,0:T(8,128)(2,1)} %copy-done, bf16[2048,1408]{1,0:T(8,128)(2,1)} %bitcast.470), kind=kOutput, calls=%fused_computation.407 | convolution fusion | flops 5905580032 | bytes 15728640 | tf_op jit(solution)/shard_map/dot_general | solution.py:294
  441.7 9.1 %multiply_convert_fusion.3 = (bf16[1024,704]{0,1:T(8,128)(2,1)S(1)}, bf16[1024,704]{0,1:T(8,128)(2,1)S(1)}, bf16[1024,704]{0,1:T(8,128)(2,1)S(1)}) fusion(f32[1024,1408]{0,1:T(8,128)} %fusion.169, bf16[1024,2048]{1,0:T(8,128)(2,1)} %fusion.5, bf16[704,2048]{1,0:T(8,128)(2,1)} %all-gather.7.cloned.1.call-done), kind=kOutput, calls=%fused_computation.79 | convolution fusion | flops 2964324352 | bytes 17170432 | tf_op jit(solution)/shard_map/dot_general | solution.py:297
  450.8 7.2 convolution_convert_fusion.1
  475.2 7.1 fusion.6
  491.1 10.1 %fusion.50 = bf16[512,2048]{1,0:T(8,128)(2,1)S(1)} fusion(bf16[1,2048,2816]{2,1,0:T(8,128)(2,1)} %all-gather.13.cloned.1.call-done, bf16[512,1408]{1,0:T(8,128)(2,1)} %copy-done.67, bf16[512,1408]{1,0:T(8,128)(2,1)} %copy-done.66), kind=kOutput, calls=%fused_computation.68 | convolution fusion | flops 5912395776 | bytes 16515072 | tf_op jit(solution)/shard_map/dot_general | solution.py:297
  502.5 11.6 %fusion.14 = bf16[1024,2048]{1,0:T(8,128)(2,1)} fusion(f32[8,128,2048]{2,1,0:T(8,128)S(1)} %fusion.92, bf16[2048,1408]{1,0:T(8,128)(2,1)} %bitcast.471, bf16[1024,704]{0,1:T(8,128)(2,1)} %copy-done.69, bf16[1024,704]{0,1:T(8,128)(2,1)} %copy-done.68), kind=kOutput, calls=%fused_computation.23 | convolution fusion | flops 5915541504 | bytes 21233664 | tf_op jit(solution)/shard_map/dot_general | solution.py:297
  529.4 8.5 collective-permute-done.65
  540.5 8.5 collective-permute-done.57
  551.8 8.7 %collective-permute-done.62 = bf16[128,2048]{1,0:T(8,128)(2,1)S(1)} collective-permute-done((bf16[128,2048]{1,0:T(8,128)(2,1)S(1)}, bf16[128,2048]{1,0:T(8,128)(2,1)S(1)}, u32[]{:S(2)}, u32[]{:S(2)}) %collective-permute-start.62) | collective-permute-done | bytes 524320 | tf_op jit(solution)/shard_map/ppermute | solution.py:149
  562.9 8.7 %collective-permute-done.54 = bf16[128,2048]{1,0:T(8,128)(2,1)S(1)} collective-permute-done((bf16[128,2048]{1,0:T(8,128)(2,1)S(1)}, bf16[128,2048]{1,0:T(8,128)(2,1)S(1)}, u32[]{:S(2)}, u32[]{:S(2)}) %collective-permute-start.54) | collective-permute-done | bytes 524320 | tf_op jit(solution)/shard_map/ppermute | solution.py:149
  586.8 7.1 collective-permute-done.55
  629.7 17.5 %collective-permute-done.70 = bf16[352,2048]{1,0:T(8,128)(2,1)} collective-permute-done((bf16[352,2048]{1,0:T(8,128)(2,1)}, bf16[352,2048]{1,0:T(8,128)(2,1)}, u32[]{:S(2)}, u32[]{:S(2)}) %collective-permute-start.70) | collective-permute-done | bytes 1441824 | tf_op jit(solution)/shard_map/ppermute | solution.py:193
  660.0 14.2 %fusion.64 = f32[1024,2,128]{0,2,1:T(8,128)S(1)} fusion(bf16[1024,2,128]{0,2,1:T(8,128)(2,1)} %get-tuple-element.177, f32[2,1024,1024]{1,2,0:T(8,128)} %fusion.171, f32[2,1024,1024]{1,2,0:T(8,128)} %copy-done.7, f32[2,1024]{1,0:T(2,128)S(1)} %copy-done.54, pred[1024,1024]{0,1:T(8,128)(4,1)S(1)} %copy-done.18), kind=kOutput, calls=%fused_computation.102 | convolution fusion | flops 559942656 | bytes 19406848 | tf_op jit(solution)/shard_map/hqk,qhd->khd/dot_general | solution.py:503
  674.2 16.1 %broadcast_multiply_fusion.1 = (f32[1024,2,128]{0,2,1:T(8,128)}, f32[1024,2,128]{0,2,1:T(8,128)}, f32[1024,2,128]{0,2,1:T(8,128)}) fusion(f32[1024,128]{0,1:T(8,128)} %get-tuple-element.202, f32[1024,2,128]{0,2,1:T(8,128)S(1)} %fusion.64, bf16[1024,2,128]{0,2,1:T(8,128)(2,1)S(1)} %copy-done.39, f32[2,1024,1024]{1,2,0:T(8,128)} %fusion.171, ...), kind=kOutput, calls=%fused_computation.187 | convolution fusion | flops 560466944 | bytes 23076864 | tf_op jit(solution)/shard_map/hqk,khd->qhd/dot_general | solution.py:501
  721.7 12.9 %collective-permute-done.77 = bf16[64,2048]{1,0:T(8,128)(2,1)S(1)} collective-permute-done((bf16[64,2048]{1,0:T(8,128)(2,1)S(1)}, bf16[64,2048]{1,0:T(8,128)(2,1)S(1)}, u32[]{:S(2)}, u32[]{:S(2)}) %collective-permute-start.77) | collective-permute-done | bytes 262176 | tf_op jit(solution)/shard_map/ppermute | solution.py:101
  757.2 7.9 fusion.11
  765.4 7.7 convolution_convert_fusion.3
  794.8 7.3 collective-permute-done.84
  844.9 7.3 all-to-all-done.2
  (639 shorter events, 472.4 us)
Async XLA Ops:
  7.2 374.2 %all-gather.13.cloned.1.call-start = ((), (), s32[]{:S(2)}) async-start(), calls=%async_computation.15 | async-start | bytes 14417920 | tf_op jit(solution)/shard_map/all_gather | solution.py:335
  7.9 386.4 %all-gather.11.cloned.1.call-start = ((), (), s32[]{:S(2)}) async-start(), calls=%async_computation.14 | async-start | bytes 7208960 | tf_op jit(solution)/shard_map/all_gather | solution.py:336
  8.7 392.0 %all-gather.9.cloned.1.call-start = ((), (), s32[]{:S(2)}) async-start(), calls=%async_computation.9 | async-start | bytes 7208960 | tf_op jit(solution)/shard_map/all_gather | solution.py:341
  62.7 23.4 %collective-permute-start.47 = (bf16[64,1408]{1,0:T(8,128)(2,1)S(1)}, bf16[64,1408]{1,0:T(8,128)(2,1)S(1)}, u32[]{:S(2)}, u32[]{:S(2)}) collective-permute-start(bf16[64,1408]{1,0:T(8,128)(2,1)S(1)} %get-tuple-element.169), channel_id=1, source_target_pairs={{0,12},{4,16},{8,20},{12,24},{16,28},{20,0},{24,4},{28,8},{1,13},{... | collective-permute-start | bytes 540680 | tf_op jit(solution)/shard_map/ppermute | solution.py:203
  91.8 349.9 %all-gather.7.cloned.1.call-start = ((), (), s32[]{:S(2)}) async-start(), calls=%async_computation.8 | async-start | bytes 3604480 | tf_op jit(solution)/shard_map/all_gather | solution.py:342
  103.4 590.5 %reduce-scatter.9.cloned.1.call-start = ((), (), s32[]{:S(2)}) async-start(), calls=%async_computation.12 | async-start | bytes 7208960 | tf_op jit(solution)/shard_map/reduce_scatter | solution.py:539
  118.3 33.1 %collective-permute-start.25 = (bf16[8,80,768]{2,1,0:T(8,128)(2,1)S(1)}, bf16[8,80,768]{2,1,0:T(8,128)(2,1)}, u32[]{:S(2)}, u32[]{:S(2)}) collective-permute-start(bf16[8,80,768]{2,1,0:T(8,128)(2,1)S(1)} %bitcast_dynamic-update-slice_fusion.16), channel_id=1, source_target_pairs={{0,1},{1,0},{2,3},{3,2},{4,5},{5,4},{6,7},{7,6},{8,9},{9,8},{10,11... | collective-permute-start | bytes 2949128 | tf_op jit(solution)/shard_map/ppermute | solution.py:167
  118.4 33.0 %collective-permute-start.26 = (bf16[8,80,768]{2,1,0:T(8,128)(2,1)S(1)}, bf16[8,80,768]{2,1,0:T(8,128)(2,1)}, u32[]{:S(2)}, u32[]{:S(2)}) collective-permute-start(bf16[8,80,768]{2,1,0:T(8,128)(2,1)S(1)} %bitcast_dynamic-update-slice_fusion.16), channel_id=1, source_target_pairs={{0,2},{1,3},{2,0},{3,1},{4,6},{5,7},{6,4},{7,5},{8,10},{9,11},{10,... | collective-permute-start | bytes 2949128 | tf_op jit(solution)/shard_map/ppermute | solution.py:166
  154.4 25.8 %collective-permute-start.8 = (bf16[64,2048]{1,0:T(8,128)(2,1)}, bf16[64,2048]{1,0:T(8,128)(2,1)}, u32[]{:S(2)}, u32[]{:S(2)}) collective-permute-start(bf16[64,2048]{1,0:T(8,128)(2,1)} %param.29), channel_id=1, source_target_pairs={{0,8},{8,16},{16,24},{24,28},{28,20},{20,12},{12,4},{4,0},{1,9},{9... | collective-permute-start | bytes 786440 | tf_op jit(solution)/shard_map/ppermute | solution.py:97
  156.0 25.8 %collective-permute-start.9 = (bf16[64,2048]{1,0:T(8,128)(2,1)}, bf16[64,2048]{1,0:T(8,128)(2,1)}, u32[]{:S(2)}, u32[]{:S(2)}) collective-permute-start(bf16[64,2048]{1,0:T(8,128)(2,1)} %param.29), channel_id=1, source_target_pairs={{8,0},{16,8},{24,16},{28,24},{20,28},{12,20},{4,12},{0,4},{9,1},{1... | collective-permute-start | bytes 786440 | tf_op jit(solution)/shard_map/ppermute | solution.py:98
  203.5 55.5 %collective-permute-start.16 = (bf16[512,2048]{1,0:T(8,128)(2,1)}, bf16[512,2048]{1,0:T(8,128)(2,1)}, u32[]{:S(2)}, u32[]{:S(2)}) collective-permute-start(bf16[512,2048]{1,0:T(8,128)(2,1)} %constant_dynamic-update-slice_fusion.26), channel_id=1, source_target_pairs={{0,2},{1,3},{2,0},{3,1},{4,6},{5,7},{6,4},{7,5},{8,10},{9,11},{10,... | collective-permute-start | bytes 6291464 | tf_op jit(solution)/shard_map/ppermute | solution.py:166
  204.0 55.1 %collective-permute-start.17 = (bf16[512,2048]{1,0:T(8,128)(2,1)}, bf16[512,2048]{1,0:T(8,128)(2,1)}, u32[]{:S(2)}, u32[]{:S(2)}) collective-permute-start(bf16[512,2048]{1,0:T(8,128)(2,1)} %constant_dynamic-update-slice_fusion.26), channel_id=1, source_target_pairs={{0,1},{1,0},{2,3},{3,2},{4,5},{5,4},{6,7},{7,6},{8,9},{9,8},{10,11... | collective-permute-start | bytes 6291464 | tf_op jit(solution)/shard_map/ppermute | solution.py:167
  261.4 49.5 %collective-permute-start.36 = (bf16[512,2048]{1,0:T(8,128)(2,1)}, bf16[512,2048]{1,0:T(8,128)(2,1)S(1)}, u32[]{:S(2)}, u32[]{:S(2)}) collective-permute-start(bf16[512,2048]{1,0:T(8,128)(2,1)} %collective-permute-done.16), channel_id=1, source_target_pairs={{0,1},{1,0},{2,3},{3,2},{4,5},{5,4},{6,7},{7,6},{8,9},{9,8},{10,11... | collective-permute-start | bytes 6291464 | tf_op jit(solution)/shard_map/ppermute | solution.py:173
  308.1 32.6 %collective-permute-start.37 = (bf16[128,2048]{1,0:T(8,128)(2,1)S(1)}, bf16[128,2048]{1,0:T(8,128)(2,1)S(1)}, u32[]{:S(2)}, u32[]{:S(2)}) collective-permute-start(bf16[128,2048]{1,0:T(8,128)(2,1)S(1)} %bitcast.431), channel_id=1, source_target_pairs={{0,8},{8,16},{16,24},{24,28},{28,20},{20,12},{12,4},{4,0},{1,9},{9... | collective-permute-start | bytes 1572872 | tf_op jit(solution)/shard_map/ppermute | solution.py:97
  309.9 32.8 %collective-permute-start.38 = (bf16[128,2048]{1,0:T(8,128)(2,1)S(1)}, bf16[128,2048]{1,0:T(8,128)(2,1)S(1)}, u32[]{:S(2)}, u32[]{:S(2)}) collective-permute-start(bf16[128,2048]{1,0:T(8,128)(2,1)S(1)} %bitcast.432), channel_id=1, source_target_pairs={{8,0},{16,8},{24,16},{28,24},{20,28},{12,20},{4,12},{0,4},{9,1},{1... | collective-permute-start | bytes 1572872 | tf_op jit(solution)/shard_map/ppermute | solution.py:98
  461.0 276.6 %reduce-scatter.11.cloned.1.call-start = ((), (), s32[]{:S(2)}) async-start(), calls=%async_computation.13 | async-start | bytes 3604480 | tf_op jit(solution)/shard_map/reduce_scatter | solution.py:308
  467.8 284.5 %reduce-scatter.5.cloned.1.call-start = ((), (), s32[]{:S(2)}) async-start(), calls=%async_computation.10 | async-start | bytes 14417920 | tf_op jit(solution)/shard_map/reduce_scatter | solution.py:308
  482.9 37.2 %all-to-all-start = ((f32[8,2,128]{2,1,0:T(2,128)}), f32[8,2,128]{2,1,0:T(2,128)S(1)}, u32[]{:S(2)}, u32[]{:S(2)}) async-start(f32[8,2,128]{2,1,0:T(2,128)} %pad_maximum_fusion.15), calls=%async_computation | async-start | bytes 16384 | tf_op jit(solution)/shard_map/all_to_all | solution.py:465
  489.1 31.1 %collective-permute-start.60 = (bf16[64,2048]{1,0:T(8,128)(2,1)}, bf16[64,2048]{1,0:T(8,128)(2,1)}, u32[]{:S(2)}, u32[]{:S(2)}) collective-permute-start(bf16[64,2048]{1,0:T(8,128)(2,1)} %get-tuple-element.147), channel_id=1, source_target_pairs={{0,8},{8,16},{16,24},{24,28},{28,20},{20,12},{12,4},{4,0},{1,9},{9... | collective-permute-start | bytes 786440 | tf_op jit(solution)/shard_map/ppermute | solution.py:140
  490.5 29.7 %collective-permute-start.64 = (bf16[64,2048]{1,0:T(8,128)(2,1)}, bf16[64,2048]{1,0:T(8,128)(2,1)}, u32[]{:S(2)}, u32[]{:S(2)}) collective-permute-start(bf16[64,2048]{1,0:T(8,128)(2,1)} %get-tuple-element.148), channel_id=1, source_target_pairs={{8,0},{16,8},{24,16},{28,24},{20,28},{12,20},{4,12},{0,4},{9,1},{1... | collective-permute-start | bytes 786440 | tf_op jit(solution)/shard_map/ppermute | solution.py:141
  520.1 54.1 %collective-permute-start.69 = (bf16[352,2048]{1,0:T(8,128)(2,1)}, bf16[352,2048]{1,0:T(8,128)(2,1)}, u32[]{:S(2)}, u32[]{:S(2)}) collective-permute-start(bf16[352,2048]{1,0:T(8,128)(2,1)} %get-tuple-element.129), channel_id=1, source_target_pairs={{0,1},{1,0},{2,3},{3,2},{4,5},{5,4},{6,7},{7,6},{8,9},{9,8},{10,11... | collective-permute-start | bytes 4325384 | tf_op jit(solution)/shard_map/ppermute | solution.py:190
  560.4 69.3 %collective-permute-start.68 = (bf16[352,2048]{1,0:T(8,128)(2,1)}, bf16[352,2048]{1,0:T(8,128)(2,1)}, u32[]{:S(2)}, u32[]{:S(2)}) collective-permute-start(bf16[352,2048]{1,0:T(8,128)(2,1)} %get-tuple-element.128), channel_id=1, source_target_pairs={{0,1},{1,0},{2,3},{3,2},{4,5},{5,4},{6,7},{7,6},{8,9},{9,8},{10,11... | collective-permute-start | bytes 4325384 | tf_op jit(solution)/shard_map/ppermute | solution.py:191
  582.9 64.3 %collective-permute-start.70 = (bf16[352,2048]{1,0:T(8,128)(2,1)}, bf16[352,2048]{1,0:T(8,128)(2,1)}, u32[]{:S(2)}, u32[]{:S(2)}) collective-permute-start(bf16[352,2048]{1,0:T(8,128)(2,1)} %fusion.56), channel_id=1, source_target_pairs={{0,2},{1,3},{2,0},{3,1},{4,6},{5,7},{6,4},{7,5},{8,10},{9,11},{10,... | collective-permute-start | bytes 4325384 | tf_op jit(solution)/shard_map/ppermute | solution.py:193
  619.6 33.0 %collective-permute-start.73 = (bf16[128,2048]{1,0:T(8,128)(2,1)}, bf16[128,2048]{1,0:T(8,128)(2,1)}, u32[]{:S(2)}, u32[]{:S(2)}) collective-permute-start(bf16[128,2048]{1,0:T(8,128)(2,1)} %collective-permute-done.71), channel_id=1, source_target_pairs={{0,8},{8,16},{16,24},{24,28},{28,20},{20,12},{12,4},{4,0},{1,9},{9... | collective-permute-start | bytes 1572872 | tf_op jit(solution)/shard_map/ppermute | solution.py:97
  620.9 33.5 %collective-permute-start.74 = (bf16[128,2048]{1,0:T(8,128)(2,1)}, bf16[128,2048]{1,0:T(8,128)(2,1)}, u32[]{:S(2)}, u32[]{:S(2)}) collective-permute-start(bf16[128,2048]{1,0:T(8,128)(2,1)} %collective-permute-done.72), channel_id=1, source_target_pairs={{8,0},{16,8},{24,16},{28,24},{20,28},{12,20},{4,12},{0,4},{9,1},{1... | collective-permute-start | bytes 1572872 | tf_op jit(solution)/shard_map/ppermute | solution.py:98
  652.6 61.1 %collective-permute-start.75 = (bf16[128,2048]{1,0:T(8,128)(2,1)}, bf16[128,2048]{1,0:T(8,128)(2,1)}, u32[]{:S(2)}, u32[]{:S(2)}) collective-permute-start(bf16[128,2048]{1,0:T(8,128)(2,1)} %collective-permute-done.73), channel_id=1, source_target_pairs={{0,8},{8,16},{16,24},{24,28},{28,20},{20,12},{12,4},{4,0},{1,9},{9... | collective-permute-start | bytes 1572872 | tf_op jit(solution)/shard_map/ppermute | solution.py:97
  654.4 61.8 %collective-permute-start.76 = (bf16[128,2048]{1,0:T(8,128)(2,1)}, bf16[128,2048]{1,0:T(8,128)(2,1)}, u32[]{:S(2)}, u32[]{:S(2)}) collective-permute-start(bf16[128,2048]{1,0:T(8,128)(2,1)} %collective-permute-done.74), channel_id=1, source_target_pairs={{8,0},{16,8},{24,16},{28,24},{20,28},{12,20},{4,12},{0,4},{9,1},{1... | collective-permute-start | bytes 1572872 | tf_op jit(solution)/shard_map/ppermute | solution.py:98
  693.9 46.0 %all-to-all-start.3 = ((bf16[8,64,1408]{2,1,0:T(8,128)(2,1)}), bf16[8,64,1408]{2,1,0:T(8,128)(2,1)}, u32[]{:S(2)}, u32[]{:S(2)}) async-start(bf16[8,64,1408]{2,1,0:T(8,128)(2,1)} %bitcast.440), calls=%async_computation.6 | async-start | bytes 2883584 | tf_op jit(solution)/shard_map/all_to_all | solution.py:254
  700.3 142.9 %reduce-scatter.7.cloned.1.call-start = ((), (), s32[]{:S(2)}) async-start(), calls=%async_computation.11 | async-start | bytes 1310720 | tf_op jit(solution)/shard_map/reduce_scatter | solution.py:308
  776.8 47.1 %collective-permute-start.87 = (bf16[8,64,768]{2,1,0:T(8,128)(2,1)}, bf16[8,64,768]{2,1,0:T(8,128)(2,1)}, u32[]{:S(2)}, u32[]{:S(2)}) collective-permute-start(bf16[8,64,768]{2,1,0:T(8,128)(2,1)} %get-tuple-element.161), channel_id=1, source_target_pairs={{0,1},{1,0},{2,3},{3,2},{4,5},{5,4},{6,7},{7,6},{8,9},{9,8},{10,11... | collective-permute-start | bytes 2359304 | tf_op jit(solution)/shard_map/ppermute | solution.py:191
  794.5 30.4 %collective-permute-start.89 = (bf16[8,64,768]{2,1,0:T(8,128)(2,1)S(1)}, bf16[8,64,768]{2,1,0:T(8,128)(2,1)}, u32[]{:S(2)}, u32[]{:S(2)}) collective-permute-start(bf16[8,64,768]{2,1,0:T(8,128)(2,1)S(1)} %fusion.58), channel_id=1, source_target_pairs={{0,2},{1,3},{2,0},{3,1},{4,6},{5,7},{6,4},{7,5},{8,10},{9,11},{10,... | collective-permute-start | bytes 2359304 | tf_op jit(solution)/shard_map/ppermute | solution.py:193
  828.8 23.4 %all-to-all-start.2 = ((bf16[8,64,768]{2,1,0:T(8,128)(2,1)}), bf16[8,64,768]{2,1,0:T(8,128)(2,1)S(1)}, u32[]{:S(2)}, u32[]{:S(2)}) async-start(bf16[8,64,768]{2,1,0:T(8,128)(2,1)} %fusion.60), calls=%async_computation.3 | async-start | bytes 1572864 | tf_op jit(solution)/shard_map/all_to_all | solution.py:254
  (154 other events, 2081.1 us)
Sparse Core Ops, SparseCore 0:
  9.6 77.2 all-gather.12
  88.5 52.2 all-gather.10
  142.9 44.1 all-gather.8
  188.5 36.6 all-gather.6
  461.1 52.5 reduce-scatter.8
  516.9 36.3 reduce-scatter.10
  555.8 123.7 reduce-scatter.4
  813.2 23.5 reduce-scatter.6

commit v4 on v3

--- a/solution.py
+++ b/solution.py
@@ -122,7 +122,7 @@
     return ring_walk(block, size, ctx_index, jnp.zeros((rows, size * width), block.dtype), put)
 
 
-def ring_scatter(parts, size, ctx_index):
+def ring_sums(parts, size, ctx_index):
     f32 = jnp.float32
     rows = parts.shape[0] // size
     ahead, back = ring_steps(size)
@@ -151,7 +151,14 @@
         if k > 1:
             fore = low(fore.astype(f32) + own(k - 1, 0, rows))
             rear = low(rear.astype(f32) + own(1 - k, 0, rows))
-    return own(0, 0, rows) + fore.astype(f32) + rear.astype(f32)
+    return (fore, rear)
+
+
+def ring_scatter(parts, size, ctx_index, kept=None):
+    fore, rear = ring_sums(parts, size, ctx_index)
+    kept = (parts if kept is None else kept).reshape(size, -1, parts.shape[1])
+    kept = lax.dynamic_index_in_dim(kept, ctx_index, 0, keepdims=False)
+    return kept.astype(jnp.float32) + fore.astype(jnp.float32) + rear.astype(jnp.float32)
 
 
 def other_core(size):
@@ -162,14 +169,10 @@
     return [(i, i ^ 2) for i in range(size)]
 
 
-def fsdp_pieces(shard, size):
+def fsdp_join(shard, size):
+    index = lax.axis_index("fsdp")
     far = lax.ppermute(shard, "fsdp", other_chip(size))
     near = lax.ppermute(shard, "fsdp", other_core(size))
-    return (far, near)
-
-
-def fsdp_join(shard, far, near, size):
-    index = lax.axis_index("fsdp")
     far_near = lax.ppermute(far, "fsdp", other_core(size))
     out = jnp.zeros((size,) + shard.shape, shard.dtype)
     for piece, peer in ((shard, index), (near, index ^ 1), (far, index ^ 2), (far_near, index ^ 3)):
@@ -305,18 +308,18 @@
         )
 
     def sum_rows(grad):
-        return lax.psum_scatter(
-            grad.astype(bf16), "fsdp", scatter_dimension=0, tiled=True
-        ).astype(f32)
+        return lax.psum_scatter(grad.astype(bf16), "fsdp", scatter_dimension=0, tiled=True)
 
     shard = width // device_count
     small = [gain_attn, gain_ffn, w_shared_gate, w_router.reshape(-1), b_qkv]
     small_size = sum(piece.shape[0] for piece in small)
     small = jnp.concatenate(small + [routes.astype(bf16).reshape(-1)], axis=0)
     small_count = small.shape[0]
-    token_rows = ring_gather(tokens.reshape(token_count, width), ctx_size, ctx_index)
     pieces = column_pieces(w_qkv, 3, ctx_size, ctx_index, small)
-    pieces = fsdp_join(pieces, *fsdp_pieces(pieces, fsdp_size), fsdp_size)
+    pieces, token_block, out_shard = after(pieces, tokens.reshape(token_count, width), w_out)
+    token_rows = ring_gather(token_block, ctx_size, ctx_index)
+    out_far = lax.ppermute(out_shard, "fsdp", other_chip(fsdp_size))
+    pieces = fsdp_join(pieces, fsdp_size)
     pieces = pieces.transpose(1, 0, 2, 3)
     qkv_weight = pieces[:, :, :shard].reshape(width, 3 * own_width)
     small = pieces[:, :, shard:].reshape(device_count, -1)[:, :small_count]
@@ -334,9 +337,17 @@
 
     expert_in = lax.all_gather(w_expert_in[0], "fsdp", axis=0, tiled=True)
     expert_out = lax.all_gather(w_expert_out[0], "fsdp", axis=0, tiled=True)
-    out_shard, in_shard, token_rows = after(w_out, w_shared_in, token_rows)
-    out_rows = ring_gather(out_shard, ctx_size, ctx_index)
-    out_far, out_near = fsdp_pieces(out_rows, fsdp_size)
+    chip = lax.axis_index("fsdp") // 2
+    out_block = jnp.where(
+        chip == 0,
+        jnp.concatenate([out_shard, out_far], axis=0),
+        jnp.concatenate([out_far, out_shard], axis=0),
+    )
+    out_block, in_shard, token_rows, qkv_weight = after(
+        out_block, w_shared_in, token_rows, qkv_weight
+    )
+    out_rows = ring_gather(out_block, ctx_size, ctx_index)
+    out_near = lax.ppermute(out_rows, "fsdp", other_core(fsdp_size))
     shared_in = column_pieces(in_shard, 2, ctx_size, ctx_index, None)
     shared_in = lax.all_gather(shared_in, "fsdp", axis=0, tiled=False)
     shared_out = lax.all_gather(w_shared_out, "fsdp", axis=0, tiled=True)
@@ -374,10 +385,13 @@
     weights_low = weights.astype(bf16)
     attended = jnp.einsum("hqk,khd->qhd", weights_low, values, preferred_element_type=f32)
     attn_own = attended.astype(bf16).reshape(seq_len, own_width)
-    out_rows, out_far, out_near, attn_own = after(out_rows, out_far, out_near, attn_own)
-    out_weight = fsdp_join(out_rows, out_far, out_near, fsdp_size)
-    out_weight = out_weight.reshape(fsdp_size, ctx_size, -1, width)
-    out_weight = out_weight.transpose(1, 0, 2, 3).reshape(width, width)
+    out_rows, out_near, attn_own = after(out_rows, out_near, attn_own)
+    core = lax.axis_index("fsdp") % 2
+    out_weight = jnp.zeros((ctx_size * fsdp_size // 2, 2, shard, width), bf16)
+    for piece, place in ((out_rows, core), (out_near, 1 - core)):
+        piece = piece.reshape(-1, shard, width)
+        out_weight = lax.dynamic_update_index_in_dim(out_weight, piece, place, 1)
+    out_weight = out_weight.reshape(width, width)
     attn_rows = ring_gather_columns(attn_own, ctx_size, ctx_index)
     grad_block, attn_rows = after(cotangent, attn_rows)
     grad_rows = ring_gather(grad_block.reshape(token_count, width), ctx_size, ctx_index)
@@ -398,7 +412,6 @@
     slot_mask = slot_of[:, None, :] == jnp.arange(capacity, dtype=i32)[None, :, None]
     slot_map = slot_mask.astype(bf16)
     blocks_two = low_two.reshape(ctx_size, token_count, width)
-    blocks_grad = grad_rows.reshape(ctx_size, token_count, width)
     gate_blocks = gate_all.reshape(ctx_size, token_count)
 
     def to_slots(blocks):
@@ -420,7 +433,7 @@
     expert_res = dot(expert_hid, expert_out).astype(bf16)
     routed = gate_all[:, None] * to_tokens(expert_res)
 
-    shared_in, expert_res = after(shared_in, expert_res)
+    shared_in, grad_rows, expert_res = after(shared_in, grad_rows, expert_res)
     shared_in = shared_in.transpose(1, 0, 2, 3).reshape(width, 2 * fs_own)
     shared_pre = dot(low_two, shared_in)
     shared_hid = swiglu(shared_pre, fs_own).astype(bf16)
@@ -428,7 +441,7 @@
     out_parts = (scale_all[:, None] * shared_res + routed).astype(bf16)
     out_sum = ring_scatter(out_parts, ctx_size, ctx_index)
 
-    grad_slots = to_slots(blocks_grad)
+    grad_slots = to_slots(grad_rows.reshape(ctx_size, token_count, width))
     gate_slots = jnp.sum(jnp.where(slot_mask, gate_blocks[:, None, :], 0.0), axis=-1).reshape(-1, 1)
     grad_res = (gate_slots * grad_slots).astype(bf16)
     slot_dots = jnp.sum(grad_slots * expert_res.astype(f32), axis=-1).reshape(ctx_size, capacity, 1)
@@ -455,9 +468,20 @@
     grad_shared_hid = dot_t(grad_shared_res, shared_out)
     grad_shared_pre = swiglu_back(shared_pre, fs_own, grad_shared_hid).astype(bf16)
     grad_shared_in = t_dot(low_two, grad_shared_pre)
+    grad_shared_pre, out_sum = after(grad_shared_pre, out_sum)
     two_parts = (dot_t(grad_shared_pre, shared_in) + to_tokens(grad_buffer)).astype(bf16)
     grad_two = ring_scatter(two_parts, ctx_size, ctx_index)
-    grad_two, out_sum = after(grad_two, out_sum)
+    sum_expert_in, grad_shared_in, grad_shared_out = after(
+        sum_expert_in, grad_shared_in.astype(bf16), grad_shared_out.astype(bf16)
+    )
+    sum_shared_in = grad_shared_in.reshape(ctx_size, fsdp_size, shard, 2 * fs_own)
+    sum_shared_in = lax.psum_scatter(
+        sum_shared_in.transpose(1, 0, 2, 3).reshape(width, 2 * fs_own),
+        "fsdp",
+        scatter_dimension=0,
+        tiled=True,
+    ).reshape(ctx_size, shard, 2 * fs_own)
+    sum_shared_out = sum_rows(grad_shared_out)
     own_residual = own_rows(residual)
     output = (own_residual + out_sum).astype(bf16).reshape(tokens.shape)
 
@@ -511,11 +535,15 @@
         ],
         axis=-1,
     ).astype(bf16)
-    grad_projected, mixed_all, sum_expert_in = after(grad_projected, mixed_all, sum_expert_in)
+    grad_projected, mixed_all = after(grad_projected, mixed_all)
     one_sums = dot_t(grad_projected, qkv_weight)
     grad_gain_one = jnp.sum(one_sums * inputs * inv_one_all, axis=0)
     one_parts = one_sums.astype(bf16)
-    grad_normed = ring_scatter(one_parts, ctx_size, ctx_index)
+    one_kept, grad_projected = after(one_parts, grad_projected)
+    one_kept, sum_shared_in, sum_shared_out, sum_expert_in = after(
+        one_kept, sum_shared_in, sum_shared_out, sum_expert_in
+    )
+    grad_normed = ring_scatter(one_parts, ctx_size, ctx_index, one_kept)
     grad_inputs_norm, unused = rms_back(
         tokens.reshape(token_count, width).astype(f32),
         own_rows(inv_one_all),
@@ -535,13 +563,6 @@
         fsdp_size,
         1,
     ).astype(bf16)
-    sum_shared_in = grad_shared_in.astype(bf16).reshape(ctx_size, fsdp_size, shard, 2 * fs_own)
-    sum_shared_in = lax.psum_scatter(
-        sum_shared_in.transpose(1, 0, 2, 3).reshape(width, 2 * fs_own),
-        "fsdp",
-        scatter_dimension=0,
-        tiled=True,
-    ).reshape(ctx_size, shard, 2 * fs_own)
     small_grads = jnp.concatenate(
         [
             piece.reshape(device_count, -1)
@@ -556,14 +577,14 @@
         grad_tokens,
         merge_columns(sum_qkv_weight, 3, ctx_size),
         small_grads[router_end:],
-        sum_rows(grad_out_weight),
+        sum_rows(grad_out_weight).astype(f32),
         small_grads[:shard],
         small_grads[shard : 2 * shard],
         small_grads[3 * shard : router_end].reshape(shard, expert_count),
         small_grads[2 * shard : 3 * shard],
         merge_columns(sum_shared_in, 2, ctx_size),
-        sum_rows(grad_shared_out),
-        sum_expert_in[None],
+        sum_shared_out.astype(f32),
+        sum_expert_in.astype(f32)[None],
         sum_expert_out[None],
     )
 

time: 876 us -> 874 us (level)
  waiting for transfers between devices: 298 us -> 267 us
  starting transfers between devices: 129 us -> 147 us
  matrix products: 195 us -> 204 us
    ppermute x28, waiting for transfers between devices: 137 us -> 98.5 us  [the longest x1 48.9 us: local_split(): out_far = lax.ppermute(out_shard, 'fsdp', other_chip(fsdp_size))]
    ppermute x2, waiting for transfers between devices: 17.5 us -> 47.5 us  [fsdp_scatter(): far = lax.ppermute(far, 'fsdp', other_chip(size))]
    ppermute x15, starting transfers between devices: 8.33 us -> 20.8 us  [ring_walk(): rear = lax.ppermute(rear, 'ctx', back)]
    dynamic_update_slice x8 -> x4, local copies, waits for them, and re-layouts: 12.4 us -> 0.33 us  [fsdp_join(): out = lax.dynamic_update_index_in_dim(out, piece, peer, 0)]
    ppermute x15, waiting for transfers between devices: 66.4 us -> 76.8 us  [ring_walk(): fore = lax.ppermute(fore, 'ctx', ahead)]
    ppermute x15, starting transfers between devices: 24.7 us -> 14.4 us  [ring_walk(): fore = lax.ppermute(fore, 'ctx', ahead)]
    ppermute x3, starting transfers between devices: 3.39 us -> 13.3 us  [small_scatter(): lax.ppermute(pick(row, (ctx_index // 2 + k) % pairs, 0), 'ctx', [(i, (i +...]
    ppermute x5, waiting for transfers between devices: 21.1 us -> 12.1 us  [ring_walk(): fore = lax.ppermute(fore[:rows // 2], 'ctx', ahead)]
  transfers between devices with their start and end apart: 108 -> 107, of which waited for: 53 -> 41; matrix products, arithmetic and copies ran while one was open for 40% -> 45% of each run, Pallas kernels for 0% -> 0%
where the time goes in v4:
time: 874 us; the launch traced here: 862 us
  waiting for transfers between devices  267 us (31%)
  matrix products  204 us (23%)
  starting transfers between devices  147 us (17%)
  local copies, waits for them, and re-layouts  131 us (15%)
  other arithmetic  86.8 us (10%)
  between operations  25.8 us (3%)
    ppermute x15, waiting for transfers between devices, ring_walk(): fore = lax.ppermute(fore, 'ctx', ahead)  76.8 us
    dot_general x8, matrix products, dot(): return jnp.dot(a, b, preferred_element_type=f32)  52.6 us
    ppermute x1, waiting for transfers between devices, local_split(): out_far = lax.ppermute(out_shard, 'fsdp', other_chip(fsdp_size))  48.9 us
    ppermute x2, waiting for transfers between devices, fsdp_scatter(): far = lax.ppermute(far, 'fsdp', other_chip(size))  47.5 us
    dot_general x7, matrix products, dot_t(): lax.dot_general(a, b, (((1,), (1,)), ((), ())), preferred_element_type=f32)  46.8 us
    dot_general x8, matrix products, t_dot(): lax.dot_general(a, b, (((0,), (0,)), ((), ())), preferred_element_type=f32)  45.3 us
    dynamic_update_slice x35, local copies, waits for them, and re-layouts, put(): lax.dynamic_update_slice(out, piece, (peer * rows + offset, jnp.zeros_lik...  35.9 us
    ppermute x9, waiting for transfers between devices, ring_sums(): fore = lax.ppermute(fore, 'ctx', ahead)  35.9 us
  transfers between devices with their start and end apart: 107, of which 41 were waited for; matrix products, arithmetic and copies ran while one was open for 45% of the time, Pallas kernels for 0%

profile of v4, /device:TPU:8, one launch (start us, length us, event | category | flops | bytes accessed | tf_op | source)
XLA Modules:
  0.0 861.5 jit_solution(10648541780550554821)
XLA Ops:
  44.9 48.9 %collective-permute-done.7 = bf16[64,2048]{1,0:T(8,128)(2,1)S(1)} collective-permute-done((bf16[64,2048]{1,0:T(8,128)(2,1)S(1)}, bf16[64,2048]{1,0:T(8,128)(2,1)S(1)}, u32[]{:S(2)}, u32[]{:S(2)}) %collective-permute-start.7) | collective-permute-done | bytes 262176 | tf_op jit(solution)/shard_map/ppermute | solution.py:321
  98.5 9.7 %collective-permute-done.10 = bf16[128,2048]{1,0:T(8,128)(2,1)S(1)} collective-permute-done((bf16[128,2048]{1,0:T(8,128)(2,1)S(1)}, bf16[128,2048]{1,0:T(8,128)(2,1)S(1)}, u32[]{:S(2)}, u32[]{:S(2)}) %collective-permute-start.10) | collective-permute-done | bytes 524320 | tf_op jit(solution)/shard_map/ppermute | solution.py:97
  112.2 9.5 %collective-permute-done.12 = bf16[128,2048]{1,0:T(8,128)(2,1)S(1)} collective-permute-done((bf16[128,2048]{1,0:T(8,128)(2,1)S(1)}, bf16[128,2048]{1,0:T(8,128)(2,1)S(1)}, u32[]{:S(2)}, u32[]{:S(2)}) %collective-permute-start.12) | collective-permute-done | bytes 524320 | tf_op jit(solution)/shard_map/ppermute | solution.py:97
  154.2 11.4 %collective-permute-done.38 = bf16[64,1408]{1,0:T(8,128)(2,1)S(1)} collective-permute-done((bf16[64,1408]{1,0:T(8,128)(2,1)S(1)}, bf16[64,1408]{1,0:T(8,128)(2,1)S(1)}, u32[]{:S(2)}, u32[]{:S(2)}) %collective-permute-start.38) | collective-permute-done | bytes 180256 | tf_op jit(solution)/shard_map/ppermute | solution.py:206
  189.0 6.7 collective-permute-done.19
  202.7 6.0 collective-permute-done.21
  255.1 10.0 %collective-permute-done.28 = bf16[1024,256]{1,0:T(8,128)(2,1)S(1)} collective-permute-done((bf16[1024,256]{1,0:T(8,128)(2,1)S(1)}, bf16[1024,256]{1,0:T(8,128)(2,1)S(1)}, u32[]{:S(2)}, u32[]{:S(2)}) %collective-permute-start.28) | collective-permute-done | bytes 524320 | tf_op jit(solution)/shard_map/ppermute | solution.py:97
  272.6 6.1 collective-permute-done.30
  284.4 6.9 collective-permute-done.32
  303.0 11.0 %multiply_reduce_fusion.1 = (f32[1024]{0:T(1024)S(1)}, f32[1024,2048]{1,0:T(8,128)S(1)}) fusion(bf16[1024,2048]{1,0:T(8,128)(2,1)S(1)} %constant_dynamic-update-slice_fusion.46, bf16[2048,2048]{1,0:T(8,128)(2,1)S(1)} %bitcast.391, bf16[1024,2048]{1,0:T(8,128)(2,1)} %constant_dynamic-update-slice_fusion.37), kind=kOutput, calls=%fused_computation.28 | convolution fusion | flops 8598322176 | bytes 25169920 | tf_op jit(solution)/shard_map/dot_general | solution.py:297
  336.0 7.5 collective-permute-done.47
  352.2 9.5 %fusion.3 = f32[512,2816]{1,0:T(8,128)S(1)} fusion(bf16[512,2048]{1,0:T(8,128)(2,1)S(1)} %bitcast.441, bf16[1,2048,2816]{2,1,0:T(8,128)(2,1)} %all-gather.11.cloned.1.call-done), kind=kOutput, calls=%fused_computation.7 | convolution fusion | flops 5905580032 | bytes 19398656 | tf_op jit(solution)/shard_map/dot_general | solution.py:297
  365.1 6.3 fusion.53
  399.4 9.1 %convolution_convert_fusion = bf16[2048,2816]{1,0:T(8,128)(2,1)} fusion(bf16[512,2048]{1,0:T(8,128)(2,1)S(1)} %bitcast.442, bf16[512,1408]{1,0:T(8,128)(2,1)S(1)} %get-tuple-element.145, bf16[512,1408]{1,0:T(8,128)(2,1)S(1)} %get-tuple-element.144), kind=kOutput, calls=%fused_computation.9 | convolution fusion | flops 5917114368 | bytes 16515072 | tf_op jit(solution)/shard_map/dot_general | solution.py:303
  415.5 11.4 %fusion.174 = f32[1024,1408]{0,1:T(8,128)} fusion(bf16[1024,2048]{1,0:T(8,128)(2,1)S(1)} %copy-done.1, bf16[2048,1408]{1,0:T(8,128)(2,1)} %bitcast.476), kind=kOutput, calls=%fused_computation.410 | convolution fusion | flops 5905580032 | bytes 15728640 | tf_op jit(solution)/shard_map/dot_general | solution.py:297
  426.9 10.6 %multiply_convert_fusion.3 = (bf16[1024,704]{0,1:T(8,128)(2,1)S(1)}, bf16[1024,704]{0,1:T(8,128)(2,1)}, bf16[1024,704]{0,1:T(8,128)(2,1)S(1)}) fusion(f32[1024,1408]{0,1:T(8,128)} %fusion.174, bf16[1024,2048]{1,0:T(8,128)(2,1)} %fusion.5, bf16[704,2048]{1,0:T(8,128)(2,1)} %all-gather.9.cloned.1.call-done), kind=kOutput, calls=%fused_computation.80 | convolution fusion | flops 2964324352 | bytes 17170432 | tf_op jit(solution)/shard_map/dot_general | solution.py:300
  437.5 7.4 fusion.6
  451.4 6.4 all-to-all-start
  462.8 7.7 convolution_convert_fusion.4
  476.9 11.0 %convolution_convert_fusion.1 = bf16[2048,1408]{1,0:T(8,128)(2,1)} fusion(bf16[1024,2048]{1,0:T(8,128)(2,1)} %copy-done, bf16[1024,704]{0,1:T(8,128)(2,1)} %get-tuple-element.143, bf16[1024,704]{0,1:T(8,128)(2,1)S(1)} %get-tuple-element.142), kind=kOutput, calls=%fused_computation.32 | convolution fusion | flops 5914230784 | bytes 12845056 | tf_op jit(solution)/shard_map/dot_general | solution.py:303
  493.5 9.3 %fusion.50 = bf16[512,2048]{1,0:T(8,128)(2,1)S(1)} fusion(bf16[1,2048,2816]{2,1,0:T(8,128)(2,1)} %all-gather.11.cloned.1.call-done, bf16[512,1408]{1,0:T(8,128)(2,1)S(1)} %copy-done.74, bf16[512,1408]{1,0:T(8,128)(2,1)S(1)} %copy-done.72), kind=kOutput, calls=%fused_computation.68 | convolution fusion | flops 5912395776 | bytes 16515072 | tf_op jit(solution)/shard_map/dot_general | solution.py:300
  509.9 10.9 %fusion.12 = bf16[1024,2048]{1,0:T(8,128)(2,1)S(1)} fusion(f32[8,128,2048]{2,1,0:T(8,128)} %fusion.97, bf16[1024,1408]{0,1:T(8,128)(2,1)} %pad_maximum_fusion.1, bf16[2048,1408]{1,0:T(8,128)(2,1)} %bitcast.477), kind=kOutput, calls=%fused_computation.20 | convolution fusion | flops 5909774336 | bytes 21233664 | tf_op jit(solution)/shard_map/dot_general | solution.py:300
  535.6 9.5 %collective-permute-done.64 = bf16[128,2048]{1,0:T(8,128)(2,1)S(1)} collective-permute-done((bf16[128,2048]{1,0:T(8,128)(2,1)S(1)}, bf16[128,2048]{1,0:T(8,128)(2,1)S(1)}, u32[]{:S(2)}, u32[]{:S(2)}) %collective-permute-start.64) | collective-permute-done | bytes 524320 | tf_op jit(solution)/shard_map/ppermute | solution.py:150
  589.8 6.5 all-to-all-start.1
  596.3 32.0 %collective-permute-done.69 = bf16[352,2048]{1,0:T(8,128)(2,1)} collective-permute-done((bf16[352,2048]{1,0:T(8,128)(2,1)}, bf16[352,2048]{1,0:T(8,128)(2,1)}, u32[]{:S(2)}, u32[]{:S(2)}) %collective-permute-start.69) | collective-permute-done | bytes 1441824 | tf_op jit(solution)/shard_map/ppermute | solution.py:196
  645.6 15.0 %fusion.64 = f32[1024,2,128]{0,2,1:T(8,128)} fusion(bf16[1024,2,128]{0,2,1:T(8,128)(2,1)} %copy-done.45, f32[2,1024,1024]{1,2,0:T(8,128)} %fusion.176, f32[2,1024,1024]{1,2,0:T(8,128)} %copy-done.6, f32[2,1024]{1,0:T(2,128)S(1)} %copy-done.59, pred[1024,1024]{0,1:T(8,128)(4,1)S(1)} %copy-done.15), kind=kOutput, calls=%fused_computation.99 | convolution fusion | flops 559942656 | bytes 19406848 | tf_op jit(solution)/shard_map/hqk,qhd->khd/dot_general | solution.py:527
  660.7 15.9 %broadcast_multiply_fusion.1 = (f32[1024,2,128]{0,2,1:T(8,128)}, f32[1024,2,128]{0,2,1:T(8,128)}, f32[1024,2,128]{0,2,1:T(8,128)}) fusion(f32[1024,128]{0,1:T(8,128)} %get-tuple-element.226, f32[1024,2,128]{0,2,1:T(8,128)} %fusion.64, bf16[1024,2,128]{0,2,1:T(8,128)(2,1)S(1)} %copy-done.44, f32[2,1024,1024]{1,2,0:T(8,128)} %fusion.176, ...), kind=kOutput, calls=%fused_computation.190 | convolution fusion | flops 560466944 | bytes 23076864 | tf_op jit(solution)/shard_map/hqk,khd->qhd/dot_general | solution.py:525
  703.2 7.7 fusion.11
  738.8 15.5 %collective-permute-done.88 = bf16[8,64,768]{2,1,0:T(8,128)(2,1)S(1)} collective-permute-done((bf16[8,64,768]{2,1,0:T(8,128)(2,1)S(1)}, bf16[8,64,768]{2,1,0:T(8,128)(2,1)S(1)}, u32[]{:S(2)}, u32[]{:S(2)}) %collective-permute-start.88) | collective-permute-done | bytes 786464 | tf_op jit(solution)/shard_map/ppermute | solution.py:196
  756.9 6.8 all-to-all-start.2
  777.0 9.8 %collective-permute-start.93 = (f32[896]{0:T(1024)S(1)}, f32[896]{0:T(1024)S(1)}, u32[]{:S(2)}, u32[]{:S(2)}) collective-permute-start(f32[896]{0:T(1024)S(1)} %get-tuple-element.135), channel_id=1, source_target_pairs={{0,16},{4,20},{8,24},{12,28},{16,0},{20,4},{24,8},{28,12},{1,17},{... | collective-permute-start | bytes 10760 | tf_op jit(solution)/shard_map/ppermute | solution.py:230
  807.9 24.6 %collective-permute-done.81 = bf16[128,2048]{1,0:T(8,128)(2,1)} collective-permute-done((bf16[128,2048]{1,0:T(8,128)(2,1)}, bf16[128,2048]{1,0:T(8,128)(2,1)}, u32[]{:S(2)}, u32[]{:S(2)}) %collective-permute-start.81) | collective-permute-done | bytes 524320 | tf_op jit(solution)/shard_map/ppermute | solution.py:149
  (645 shorter events, 459.2 us)
Async XLA Ops:
  7.2 345.0 %all-gather.11.cloned.1.call-start = ((), (), s32[]{:S(2)}) async-start(), calls=%async_computation.14 | async-start | bytes 14417920 | tf_op jit(solution)/shard_map/all_gather | solution.py:338
  8.0 357.1 %all-gather.13.cloned.1.call-start = ((), (), s32[]{:S(2)}) async-start(), calls=%async_computation.15 | async-start | bytes 7208960 | tf_op jit(solution)/shard_map/all_gather | solution.py:339
  21.2 350.2 %all-gather.7.cloned.1.call-start = ((), (), s32[]{:S(2)}) async-start(), calls=%async_computation.8 | async-start | bytes 7208960 | tf_op jit(solution)/shard_map/all_gather | solution.py:352
  36.9 61.5 %collective-permute-start.16 = (bf16[8,80,768]{2,1,0:T(8,128)(2,1)S(1)}, bf16[8,80,768]{2,1,0:T(8,128)(2,1)S(1)}, u32[]{:S(2)}, u32[]{:S(2)}) collective-permute-start(bf16[8,80,768]{2,1,0:T(8,128)(2,1)S(1)} %bitcast_dynamic-update-slice_fusion.12), channel_id=1, source_target_pairs={{0,1},{1,0},{2,3},{3,2},{4,5},{5,4},{6,7},{7,6},{8,9},{9,8},{10,11... | collective-permute-start | bytes 2949128 | tf_op jit(solution)/shard_map/ppermute | solution.py:175
  37.0 61.4 %collective-permute-start.17 = (bf16[8,80,768]{2,1,0:T(8,128)(2,1)S(1)}, bf16[8,80,768]{2,1,0:T(8,128)(2,1)S(1)}, u32[]{:S(2)}, u32[]{:S(2)}) collective-permute-start(bf16[8,80,768]{2,1,0:T(8,128)(2,1)S(1)} %bitcast_dynamic-update-slice_fusion.12), channel_id=1, source_target_pairs={{0,2},{1,3},{2,0},{3,1},{4,6},{5,7},{6,4},{7,5},{8,10},{9,11},{10,... | collective-permute-start | bytes 2949128 | tf_op jit(solution)/shard_map/ppermute | solution.py:174
  38.5 56.1 %collective-permute-start.8 = (bf16[128,2048]{1,0:T(8,128)(2,1)S(1)}, bf16[128,2048]{1,0:T(8,128)(2,1)S(1)}, u32[]{:S(2)}, u32[]{:S(2)}) collective-permute-start(bf16[128,2048]{1,0:T(8,128)(2,1)S(1)} %bitcast.419), channel_id=1, source_target_pairs={{0,8},{8,16},{16,24},{24,28},{28,20},{20,12},{12,4},{4,0},{1,9},{9... | collective-permute-start | bytes 1572872 | tf_op jit(solution)/shard_map/ppermute | solution.py:97
  39.1 56.1 %collective-permute-start.9 = (bf16[128,2048]{1,0:T(8,128)(2,1)S(1)}, bf16[128,2048]{1,0:T(8,128)(2,1)S(1)}, u32[]{:S(2)}, u32[]{:S(2)}) collective-permute-start(bf16[128,2048]{1,0:T(8,128)(2,1)S(1)} %bitcast.420), channel_id=1, source_target_pairs={{8,0},{16,8},{24,16},{28,24},{20,28},{12,20},{4,12},{0,4},{9,1},{1... | collective-permute-start | bytes 1572872 | tf_op jit(solution)/shard_map/ppermute | solution.py:98
  40.6 53.2 %collective-permute-start.7 = (bf16[64,2048]{1,0:T(8,128)(2,1)S(1)}, bf16[64,2048]{1,0:T(8,128)(2,1)S(1)}, u32[]{:S(2)}, u32[]{:S(2)}) collective-permute-start(bf16[64,2048]{1,0:T(8,128)(2,1)S(1)} %copy-done.47), channel_id=1, source_target_pairs={{0,2},{1,3},{2,0},{3,1},{4,6},{5,7},{6,4},{7,5},{8,10},{9,11},{10,... | collective-permute-start | bytes 786440 | tf_op jit(solution)/shard_map/ppermute | solution.py:321
  98.4 31.7 %collective-permute-start.18 = (bf16[8,80,768]{2,1,0:T(8,128)(2,1)S(1)}, bf16[8,80,768]{2,1,0:T(8,128)(2,1)S(1)}, u32[]{:S(2)}, u32[]{:S(2)}) collective-permute-start(bf16[8,80,768]{2,1,0:T(8,128)(2,1)S(1)} %collective-permute-done.17), channel_id=1, source_target_pairs={{0,1},{1,0},{2,3},{3,2},{4,5},{5,4},{6,7},{7,6},{8,9},{9,8},{10,11... | collective-permute-start | bytes 2949128 | tf_op jit(solution)/shard_map/ppermute | solution.py:176
  141.3 24.3 %collective-permute-start.38 = (bf16[64,1408]{1,0:T(8,128)(2,1)S(1)}, bf16[64,1408]{1,0:T(8,128)(2,1)S(1)}, u32[]{:S(2)}, u32[]{:S(2)}) collective-permute-start(bf16[64,1408]{1,0:T(8,128)(2,1)S(1)} %get-tuple-element.193), channel_id=1, source_target_pairs={{0,12},{4,16},{8,20},{12,24},{16,28},{20,0},{24,4},{28,8},{1,13},{... | collective-permute-start | bytes 540680 | tf_op jit(solution)/shard_map/ppermute | solution.py:206
  144.7 25.2 %collective-permute-start.40 = (bf16[64,1408]{1,0:T(8,128)(2,1)S(1)}, bf16[64,1408]{1,0:T(8,128)(2,1)S(1)}, u32[]{:S(2)}, u32[]{:S(2)}) collective-permute-start(bf16[64,1408]{1,0:T(8,128)(2,1)S(1)} %get-tuple-element.191), channel_id=1, source_target_pairs={{0,20},{4,24},{8,28},{12,0},{16,4},{20,8},{24,12},{28,16},{1,21},{... | collective-permute-start | bytes 540680 | tf_op jit(solution)/shard_map/ppermute | solution.py:206
  171.5 255.4 %all-gather.9.cloned.1.call-start = ((), (), s32[]{:S(2)}) async-start(), calls=%async_computation.9 | async-start | bytes 3604480 | tf_op jit(solution)/shard_map/all_gather | solution.py:353
  172.1 337.7 %reduce-scatter.5.cloned.1.call-start = ((), (), s32[]{:S(2)}) async-start(), calls=%async_computation.10 | async-start | bytes 14417920 | tf_op jit(solution)/shard_map/reduce_scatter | solution.py:311
  451.4 76.9 %all-to-all-start = ((f32[8,2,128]{2,1,0:T(2,128)}), f32[8,2,128]{2,1,0:T(2,128)S(1)}, u32[]{:S(2)}, u32[]{:S(2)}) async-start(f32[8,2,128]{2,1,0:T(2,128)} %pad_maximum_fusion.13), calls=%async_computation | async-start | bytes 16384 | tf_op jit(solution)/shard_map/all_to_all | solution.py:489
  457.8 330.6 %reduce-scatter.9.cloned.1.call-start = ((), (), s32[]{:S(2)}) async-start(), calls=%async_computation.12 | async-start | bytes 3604480 | tf_op jit(solution)/shard_map/reduce_scatter | solution.py:311
  509.8 278.6 %reduce-scatter.7.cloned.1.call-start = ((), (), s32[]{:S(2)}) async-start(), calls=%async_computation.11 | async-start | bytes 7208960 | tf_op jit(solution)/shard_map/reduce_scatter | solution.py:478
  527.7 39.4 %collective-permute-start.68 = (bf16[352,2048]{1,0:T(8,128)(2,1)}, bf16[352,2048]{1,0:T(8,128)(2,1)}, u32[]{:S(2)}, u32[]{:S(2)}) collective-permute-start(bf16[352,2048]{1,0:T(8,128)(2,1)} %get-tuple-element.153), channel_id=1, source_target_pairs={{0,1},{1,0},{2,3},{3,2},{4,5},{5,4},{6,7},{7,6},{8,9},{9,8},{10,11... | collective-permute-start | bytes 4325384 | tf_op jit(solution)/shard_map/ppermute | solution.py:193
  527.7 68.6 %collective-permute-start.67 = (bf16[352,2048]{1,0:T(8,128)(2,1)}, bf16[352,2048]{1,0:T(8,128)(2,1)}, u32[]{:S(2)}, u32[]{:S(2)}) collective-permute-start(bf16[352,2048]{1,0:T(8,128)(2,1)} %get-tuple-element.152), channel_id=1, source_target_pairs={{0,1},{1,0},{2,3},{3,2},{4,5},{5,4},{6,7},{7,6},{8,9},{9,8},{10,11... | collective-permute-start | bytes 4325384 | tf_op jit(solution)/shard_map/ppermute | solution.py:194
  571.0 57.3 %collective-permute-start.69 = (bf16[352,2048]{1,0:T(8,128)(2,1)}, bf16[352,2048]{1,0:T(8,128)(2,1)}, u32[]{:S(2)}, u32[]{:S(2)}) collective-permute-start(bf16[352,2048]{1,0:T(8,128)(2,1)} %fusion.56), channel_id=1, source_target_pairs={{0,2},{1,3},{2,0},{3,1},{4,6},{5,7},{6,4},{7,5},{8,10},{9,11},{10,... | collective-permute-start | bytes 4325384 | tf_op jit(solution)/shard_map/ppermute | solution.py:196
  584.1 48.9 %collective-permute-start.70 = (bf16[128,2048]{1,0:T(8,128)(2,1)S(1)}, bf16[128,2048]{1,0:T(8,128)(2,1)}, u32[]{:S(2)}, u32[]{:S(2)}) collective-permute-start(bf16[128,2048]{1,0:T(8,128)(2,1)S(1)} %get-tuple-element.140), channel_id=1, source_target_pairs={{0,8},{8,16},{16,24},{24,28},{28,20},{20,12},{12,4},{4,0},{1,9},{9... | collective-permute-start | bytes 1572872 | tf_op jit(solution)/shard_map/ppermute | solution.py:97
  585.3 47.7 %collective-permute-start.71 = (bf16[128,2048]{1,0:T(8,128)(2,1)S(1)}, bf16[128,2048]{1,0:T(8,128)(2,1)}, u32[]{:S(2)}, u32[]{:S(2)}) collective-permute-start(bf16[128,2048]{1,0:T(8,128)(2,1)S(1)} %get-tuple-element.140), channel_id=1, source_target_pairs={{8,0},{16,8},{24,16},{28,24},{20,28},{12,20},{4,12},{0,4},{9,1},{1... | collective-permute-start | bytes 1572872 | tf_op jit(solution)/shard_map/ppermute | solution.py:98
  589.8 50.5 %all-to-all-start.1 = ((bf16[8,128,256]{2,1,0:T(8,128)(2,1)}), bf16[8,128,256]{2,1,0:T(8,128)(2,1)S(1)}, u32[]{:S(2)}, u32[]{:S(2)}) async-start(bf16[8,128,256]{2,1,0:T(8,128)(2,1)} %bitcast.384), calls=%async_computation.1 | async-start | bytes 1048576 | tf_op jit(solution)/shard_map/all_to_all | solution.py:513
  596.3 203.4 %reduce-scatter.11.cloned.1.call-start = ((), (), s32[]{:S(2)}) async-start(), calls=%async_computation.13 | async-start | bytes 1310720 | tf_op jit(solution)/shard_map/reduce_scatter | solution.py:311
  632.9 53.0 %collective-permute-start.72 = (bf16[128,2048]{1,0:T(8,128)(2,1)}, bf16[128,2048]{1,0:T(8,128)(2,1)}, u32[]{:S(2)}, u32[]{:S(2)}) collective-permute-start(bf16[128,2048]{1,0:T(8,128)(2,1)} %collective-permute-done.70), channel_id=1, source_target_pairs={{0,8},{8,16},{16,24},{24,28},{28,20},{20,12},{12,4},{4,0},{1,9},{9... | collective-permute-start | bytes 1572872 | tf_op jit(solution)/shard_map/ppermute | solution.py:97
  633.0 53.0 %collective-permute-start.73 = (bf16[128,2048]{1,0:T(8,128)(2,1)}, bf16[128,2048]{1,0:T(8,128)(2,1)}, u32[]{:S(2)}, u32[]{:S(2)}) collective-permute-start(bf16[128,2048]{1,0:T(8,128)(2,1)} %collective-permute-done.71), channel_id=1, source_target_pairs={{8,0},{16,8},{24,16},{28,24},{20,28},{12,20},{4,12},{0,4},{9,1},{1... | collective-permute-start | bytes 1572872 | tf_op jit(solution)/shard_map/ppermute | solution.py:98
  720.6 43.1 %collective-permute-start.89 = (f32[8,2,896]{2,1,0:T(2,128)S(1)}, f32[8,2,896]{2,1,0:T(2,128)}, u32[]{:S(2)}, u32[]{:S(2)}) collective-permute-start(f32[8,2,896]{2,1,0:T(2,128)S(1)} %bitcast.458), channel_id=1, source_target_pairs={{0,1},{1,0},{2,3},{3,2},{4,5},{5,4},{6,7},{7,6},{8,9},{9,8},{10,11... | collective-permute-start | bytes 172040 | tf_op jit(solution)/shard_map/ppermute | solution.py:220
  736.0 31.3 %collective-permute-start.83 = (bf16[128,2048]{1,0:T(8,128)(2,1)}, bf16[128,2048]{1,0:T(8,128)(2,1)}, u32[]{:S(2)}, u32[]{:S(2)}) collective-permute-start(bf16[128,2048]{1,0:T(8,128)(2,1)} %pad_maximum_fusion.12), channel_id=1, source_target_pairs={{8,0},{16,8},{24,16},{28,24},{20,28},{12,20},{4,12},{0,4},{9,1},{1... | collective-permute-start | bytes 1572872 | tf_op jit(solution)/shard_map/ppermute | solution.py:150
  738.7 28.5 %collective-permute-start.79 = (bf16[128,2048]{1,0:T(8,128)(2,1)}, bf16[128,2048]{1,0:T(8,128)(2,1)}, u32[]{:S(2)}, u32[]{:S(2)}) collective-permute-start(bf16[128,2048]{1,0:T(8,128)(2,1)} %pad_maximum_fusion.11), channel_id=1, source_target_pairs={{0,8},{8,16},{16,24},{24,28},{28,20},{20,12},{12,4},{4,0},{1,9},{9... | collective-permute-start | bytes 1572872 | tf_op jit(solution)/shard_map/ppermute | solution.py:149
  756.9 31.5 %all-to-all-start.2 = ((bf16[8,64,768]{2,1,0:T(8,128)(2,1)}), bf16[8,64,768]{2,1,0:T(8,128)(2,1)S(1)}, u32[]{:S(2)}, u32[]{:S(2)}) async-start(bf16[8,64,768]{2,1,0:T(8,128)(2,1)} %fusion.60), calls=%async_computation.5 | async-start | bytes 1572864 | tf_op jit(solution)/shard_map/all_to_all | solution.py:257
  788.4 53.6 %all-to-all-start.3 = ((bf16[8,64,1408]{2,1,0:T(8,128)(2,1)}), bf16[8,64,1408]{2,1,0:T(8,128)(2,1)}, u32[]{:S(2)}, u32[]{:S(2)}) async-start(bf16[8,64,1408]{2,1,0:T(8,128)(2,1)} %bitcast.446), calls=%async_computation.7 | async-start | bytes 2883584 | tf_op jit(solution)/shard_map/all_to_all | solution.py:257
  795.4 37.1 %collective-permute-start.81 = (bf16[128,2048]{1,0:T(8,128)(2,1)}, bf16[128,2048]{1,0:T(8,128)(2,1)}, u32[]{:S(2)}, u32[]{:S(2)}) collective-permute-start(bf16[128,2048]{1,0:T(8,128)(2,1)} %get-tuple-element.155), channel_id=1, source_target_pairs={{0,8},{8,16},{16,24},{24,28},{28,20},{20,12},{12,4},{4,0},{1,9},{9... | collective-permute-start | bytes 1572872 | tf_op jit(solution)/shard_map/ppermute | solution.py:149
  797.1 37.4 %collective-permute-start.85 = (bf16[128,2048]{1,0:T(8,128)(2,1)}, bf16[128,2048]{1,0:T(8,128)(2,1)}, u32[]{:S(2)}, u32[]{:S(2)}) collective-permute-start(bf16[128,2048]{1,0:T(8,128)(2,1)} %get-tuple-element.156), channel_id=1, source_target_pairs={{8,0},{16,8},{24,16},{28,24},{20,28},{12,20},{4,12},{0,4},{9,1},{1... | collective-permute-start | bytes 1572872 | tf_op jit(solution)/shard_map/ppermute | solution.py:150
  (158 other events, 1991.4 us)
Sparse Core Ops, SparseCore 0:
  9.6 103.9 all-gather.10
  115.2 43.3 all-gather.12
  171.6 44.9 all-gather.6
  218.1 27.0 all-gather.8
  408.6 93.6 reduce-scatter.4
  509.9 37.5 reduce-scatter.8
  556.8 77.3 reduce-scatter.6
  730.0 28.0 reduce-scatter.10

commit v5 on v4

--- a/solution.py
+++ b/solution.py
@@ -113,15 +113,6 @@
     return ring_walk(block, size, ctx_index, jnp.zeros((size * rows, width), block.dtype), put)
 
 
-def ring_gather_columns(block, size, ctx_index):
-    rows, width = block.shape
-
-    def put(out, piece, peer, offset):
-        return lax.dynamic_update_slice(out, piece, (jnp.full_like(peer, offset), peer * width))
-
-    return ring_walk(block, size, ctx_index, jnp.zeros((rows, size * width), block.dtype), put)
-
-
 def ring_sums(parts, size, ctx_index):
     f32 = jnp.float32
     rows = parts.shape[0] // size
@@ -169,17 +160,6 @@
     return [(i, i ^ 2) for i in range(size)]
 
 
-def fsdp_join(shard, size):
-    index = lax.axis_index("fsdp")
-    far = lax.ppermute(shard, "fsdp", other_chip(size))
-    near = lax.ppermute(shard, "fsdp", other_core(size))
-    far_near = lax.ppermute(far, "fsdp", other_core(size))
-    out = jnp.zeros((size,) + shard.shape, shard.dtype)
-    for piece, peer in ((shard, index), (near, index ^ 1), (far, index ^ 2), (far_near, index ^ 3)):
-        out = lax.dynamic_update_index_in_dim(out, piece, peer, 0)
-    return out
-
-
 def after(value, *deps):
     return lax.optimization_barrier((value,) + deps)
 
@@ -197,45 +177,7 @@
     return pick(index).astype(jnp.float32) + near.astype(jnp.float32) + far.astype(jnp.float32)
 
 
-def exchange(pieces, size, ctx_index):
-    out = jnp.zeros_like(pieces)
-    own = lax.dynamic_index_in_dim(pieces, ctx_index, 0, keepdims=False)
-    out = lax.dynamic_update_index_in_dim(out, own, ctx_index, 0)
-    for k in range(1, size):
-        piece = lax.dynamic_index_in_dim(pieces, (ctx_index + k) % size, 0, keepdims=False)
-        piece = lax.ppermute(piece, "ctx", [(i, (i + k) % size) for i in range(size)])
-        out = lax.dynamic_update_index_in_dim(out, piece, (ctx_index - k) % size, 0)
-    return out
-
-
-def small_scatter(parts, size, fsdp_size, ctx_index):
-    index = lax.axis_index("fsdp")
-
-    def pick(array, at, axis):
-        return lax.dynamic_index_in_dim(array, at, axis, keepdims=False)
-
-    halves = parts.reshape(size, fsdp_size // 2, 2, -1)
-    core, chip = index % 2, index // 2
-    kept = pick(halves, core, 2)
-    kept = kept + lax.ppermute(pick(halves, 1 - core, 2), "fsdp", other_core(fsdp_size))
-    mine = pick(kept, chip, 1)
-    mine = mine + lax.ppermute(pick(kept, 1 - chip, 1), "fsdp", other_chip(fsdp_size))
-    rows = mine.reshape(size // 2, 2, -1)
-    odd = ctx_index % 2
-    row = pick(rows, odd, 1)
-    row = row + lax.ppermute(pick(rows, 1 - odd, 1), "ctx", [(i, i ^ 1) for i in range(size)])
-    pairs = size // 2
-    total = pick(row, ctx_index // 2, 0)
-    for k in range(1, pairs):
-        total = total + lax.ppermute(
-            pick(row, (ctx_index // 2 + k) % pairs, 0),
-            "ctx",
-            [(i, (i + 2 * k) % size) for i in range(size)],
-        )
-    return total
-
-
-def column_pieces(weight, groups, size, ctx_index, extra):
+def column_pieces(weight, groups, size, extra):
     rows = weight.shape[0]
     width = weight.shape[1] // (groups * size)
     pieces = weight.reshape(rows, groups, size, width).transpose(2, 0, 1, 3)
@@ -248,15 +190,18 @@
             extra.reshape(1, more, groups * width), (size, more, groups * width)
         )
         pieces = jnp.concatenate([pieces, extra], axis=1)
-    return exchange(pieces, size, ctx_index)
+    return lax.all_to_all(pieces, "ctx", split_axis=0, concat_axis=0, tiled=True)
 
 
 def merge_columns(pieces, groups, size):
-    rows = pieces.shape[1]
     width = pieces.shape[2] // groups
     pieces = lax.all_to_all(pieces, "ctx", split_axis=0, concat_axis=0, tiled=True)
-    pieces = pieces.reshape(size, rows, groups, width).transpose(1, 2, 0, 3)
-    return pieces.reshape(rows, groups * size * width).astype(jnp.float32)
+    columns = [
+        pieces[peer, :, group * width : (group + 1) * width]
+        for group in range(groups)
+        for peer in range(size)
+    ]
+    return jnp.concatenate(columns, axis=1).astype(jnp.float32)
 
 
 def local_split(
@@ -315,12 +260,9 @@
     small_size = sum(piece.shape[0] for piece in small)
     small = jnp.concatenate(small + [routes.astype(bf16).reshape(-1)], axis=0)
     small_count = small.shape[0]
-    pieces = column_pieces(w_qkv, 3, ctx_size, ctx_index, small)
-    pieces, token_block, out_shard = after(pieces, tokens.reshape(token_count, width), w_out)
-    token_rows = ring_gather(token_block, ctx_size, ctx_index)
-    out_far = lax.ppermute(out_shard, "fsdp", other_chip(fsdp_size))
-    pieces = fsdp_join(pieces, fsdp_size)
-    pieces = pieces.transpose(1, 0, 2, 3)
+    token_rows = ring_gather(tokens.reshape(token_count, width), ctx_size, ctx_index)
+    pieces = column_pieces(w_qkv, 3, ctx_size, small)
+    pieces = lax.all_gather(pieces, "fsdp", axis=0, tiled=False).transpose(1, 0, 2, 3)
     qkv_weight = pieces[:, :, :shard].reshape(width, 3 * own_width)
     small = pieces[:, :, shard:].reshape(device_count, -1)[:, :small_count]
     attn_gain = small[:, :shard].reshape(width).astype(f32)
@@ -335,22 +277,10 @@
         route_rows.reshape(ctx_size, fsdp_size, -1), lax.axis_index("fsdp"), 1, keepdims=False
     ).reshape(ctx_size, token_count, top_count)
 
-    expert_in = lax.all_gather(w_expert_in[0], "fsdp", axis=0, tiled=True)
     expert_out = lax.all_gather(w_expert_out[0], "fsdp", axis=0, tiled=True)
-    chip = lax.axis_index("fsdp") // 2
-    out_block = jnp.where(
-        chip == 0,
-        jnp.concatenate([out_shard, out_far], axis=0),
-        jnp.concatenate([out_far, out_shard], axis=0),
-    )
-    out_block, in_shard, token_rows, qkv_weight = after(
-        out_block, w_shared_in, token_rows, qkv_weight
-    )
-    out_rows = ring_gather(out_block, ctx_size, ctx_index)
-    out_near = lax.ppermute(out_rows, "fsdp", other_core(fsdp_size))
-    shared_in = column_pieces(in_shard, 2, ctx_size, ctx_index, None)
-    shared_in = lax.all_gather(shared_in, "fsdp", axis=0, tiled=False)
-    shared_out = lax.all_gather(w_shared_out, "fsdp", axis=0, tiled=True)
+    expert_in, token_rows = after(w_expert_in[0], token_rows)
+    expert_in = lax.all_gather(expert_in, "fsdp", axis=0, tiled=True)
+    out_weight = lax.all_gather(w_out, "fsdp", axis=0, tiled=True)
 
     block_ids = jnp.arange(ctx_size, dtype=i32)[:, None]
     local_index = jnp.arange(block_len, dtype=i32)[None, :]
@@ -376,6 +306,10 @@
         projected[:, own_width : 2 * own_width].reshape(head_shape), cos_tab, sine_tab
     ).astype(bf16)
     values = projected[:, 2 * own_width :].reshape(head_shape).astype(bf16)
+    queries, in_shard, out_shard = after(queries, w_shared_in, w_shared_out)
+    shared_in = column_pieces(in_shard, 2, ctx_size, None)
+    shared_in = lax.all_gather(shared_in, "fsdp", axis=0, tiled=False)
+    shared_out = lax.all_gather(out_shard, "fsdp", axis=0, tiled=True)
     allowed = (positions[None, :] <= positions[:, None]) & (seg_rows[None, :] == seg_rows[:, None])
     scores = jnp.einsum("qhd,khd->hqk", queries, keys, preferred_element_type=f32) * score_scale
     scores = jnp.where(allowed[None], scores, MASK_FILL)
@@ -385,20 +319,15 @@
     weights_low = weights.astype(bf16)
     attended = jnp.einsum("hqk,khd->qhd", weights_low, values, preferred_element_type=f32)
     attn_own = attended.astype(bf16).reshape(seq_len, own_width)
-    out_rows, out_near, attn_own = after(out_rows, out_near, attn_own)
-    core = lax.axis_index("fsdp") % 2
-    out_weight = jnp.zeros((ctx_size * fsdp_size // 2, 2, shard, width), bf16)
-    for piece, place in ((out_rows, core), (out_near, 1 - core)):
-        piece = piece.reshape(-1, shard, width)
-        out_weight = lax.dynamic_update_index_in_dim(out_weight, piece, place, 1)
-    out_weight = out_weight.reshape(width, width)
-    attn_rows = ring_gather_columns(attn_own, ctx_size, ctx_index)
-    grad_block, attn_rows = after(cotangent, attn_rows)
-    grad_rows = ring_gather(grad_block.reshape(token_count, width), ctx_size, ctx_index)
-    residual = inputs + dot(attn_rows, out_weight)
-
-    normed_two, inv_two_all = rms_norm(residual, ffn_gain)
-    low_two = normed_two.astype(bf16)
+    attn_own, grad_block = after(attn_own, cotangent.reshape(token_count, width))
+    grad_rows = lax.all_gather(grad_block, "ctx", axis=0, tiled=True)
+    attn_parts = dot(attn_own, out_weight).astype(bf16)
+    own_tokens = tokens.reshape(token_count, width).astype(f32)
+    own_residual = own_tokens + ring_scatter(attn_parts, ctx_size, ctx_index)
+
+    normed_two, inv_two = rms_norm(own_residual, ffn_gain)
+    own_low = normed_two.astype(bf16)
+    low_two = ring_gather(own_low, ctx_size, ctx_index)
     mixed_weight = jnp.concatenate([router_weight, gate_vector[:, None]], axis=1)
     logits = dot(low_two, mixed_weight)
     probs_all = jax.nn.softmax(logits[:, :expert_count], axis=-1)
@@ -433,7 +362,6 @@
     expert_res = dot(expert_hid, expert_out).astype(bf16)
     routed = gate_all[:, None] * to_tokens(expert_res)
 
-    shared_in, grad_rows, expert_res = after(shared_in, grad_rows, expert_res)
     shared_in = shared_in.transpose(1, 0, 2, 3).reshape(width, 2 * fs_own)
     shared_pre = dot(low_two, shared_in)
     shared_hid = swiglu(shared_pre, fs_own).astype(bf16)
@@ -457,9 +385,7 @@
         grad_expert_out.astype(bf16),
         (scale_all[:, None] * grad_rows.astype(f32)).astype(bf16),
     )
-    sum_expert_out = fsdp_scatter(
-        grad_expert_out.reshape(fsdp_size, -1, width), fsdp_size, 0
-    )
+    sum_expert_out = sum_rows(grad_expert_out)
     sum_expert_in = sum_rows(grad_expert_in)
 
     grad_f32 = grad_rows.astype(f32)
@@ -482,14 +408,12 @@
         tiled=True,
     ).reshape(ctx_size, shard, 2 * fs_own)
     sum_shared_out = sum_rows(grad_shared_out)
-    own_residual = own_rows(residual)
     output = (own_residual + out_sum).astype(bf16).reshape(tokens.shape)
 
     dots = jnp.stack([grad_gates, gate_dots], axis=1)
     dots = lax.all_to_all(dots, "ctx", split_axis=0, concat_axis=0, tiled=True)
     own_probs = own_rows(probs_all)
     own_scale = own_rows(scale_all)
-    own_low = own_rows(low_two)
     own_chosen = routes.reshape(token_count, top_count)
     chosen_mask = jnp.any(
         own_chosen[..., None] == jnp.arange(expert_count, dtype=i32), axis=1
@@ -504,21 +428,13 @@
     grad_two = grad_two + dot_t(grad_logits, router_weight)
     grad_two = grad_two + grad_gate_pre.astype(f32)[:, None] * gate_vector.astype(f32)[None, :]
     grad_resid_norm, grad_gain_two = rms_back(
-        own_residual, own_rows(inv_two_all), ffn_gain, grad_two
+        own_residual, inv_two, ffn_gain, grad_two
     )
     grad_resid = cotangent.reshape(token_count, width).astype(f32) + grad_resid_norm
 
     grad_mixed = grad_resid.astype(bf16)
-    grad_attn_rows = dot_t(grad_mixed, out_weight).astype(bf16)
-    grad_attn = lax.all_to_all(
-        grad_attn_rows.reshape(token_count, ctx_size, own_width).transpose(1, 0, 2),
-        "ctx",
-        split_axis=0,
-        concat_axis=0,
-        tiled=True,
-    ).reshape(head_shape)
-    grad_attn, sum_expert_out = after(grad_attn, sum_expert_out)
     mixed_all = ring_gather(grad_mixed, ctx_size, ctx_index)
+    grad_attn = dot_t(mixed_all, out_weight).astype(bf16).reshape(head_shape)
     grad_weights = jnp.einsum("qhd,khd->hqk", grad_attn, values, preferred_element_type=f32)
     delta = jnp.sum(weights * grad_weights, axis=-1, keepdims=True)
     grad_scores = jnp.where(allowed[None], weights * (grad_weights - delta), 0.0).astype(bf16)
@@ -535,7 +451,6 @@
         ],
         axis=-1,
     ).astype(bf16)
-    grad_projected, mixed_all = after(grad_projected, mixed_all)
     one_sums = dot_t(grad_projected, qkv_weight)
     grad_gain_one = jnp.sum(one_sums * inputs * inv_one_all, axis=0)
     one_parts = one_sums.astype(bf16)
@@ -545,7 +460,7 @@
     )
     grad_normed = ring_scatter(one_parts, ctx_size, ctx_index, one_kept)
     grad_inputs_norm, unused = rms_back(
-        tokens.reshape(token_count, width).astype(f32),
+        own_tokens,
         own_rows(inv_one_all),
         attn_gain,
         grad_normed,
@@ -570,8 +485,9 @@
         ],
         axis=1,
     )
-    small_grads = small_grads.reshape(ctx_size, fsdp_size, small_size)
-    small_grads = small_scatter(small_grads, ctx_size, fsdp_size, ctx_index).reshape(small_size)
+    small_grads = lax.psum_scatter(
+        small_grads, ("ctx", "fsdp"), scatter_dimension=0, tiled=True
+    ).reshape(small_size)
     return (
         output,
         grad_tokens,
@@ -585,7 +501,7 @@
         merge_columns(sum_shared_in, 2, ctx_size),
         sum_shared_out.astype(f32),
         sum_expert_in.astype(f32)[None],
-        sum_expert_out[None],
+        sum_expert_out.astype(f32)[None],
     )
 
 

time: 874 us -> 1020 us (1.17)
  waiting for transfers between devices: 267 us -> 425 us
  blocking collectives: 0 us -> 83.1 us
  starting transfers between devices: 147 us -> 76.5 us
  local copies, waits for them, and re-layouts: 131 us -> 118 us
  other arithmetic: 86.8 us -> 73.9 us
    reduce_scatter x3 -> x4, waiting for transfers between devices: 0.01 us -> 87.6 us  [sum_rows(): lax.psum_scatter(grad.astype(bf16), 'fsdp', scatter_dimension=0, tiled=True)]
    all_to_all x0 -> x2, blocking collectives: none -> 83.1 us  [column_pieces(): lax.all_to_all(pieces, 'ctx', split_axis=0, concat_axis=0, tiled=True)]
    ppermute x25 -> x0, waiting for transfers between devices: 71.6 us -> none  [the longest x1 48.9 us: local_split(): out_far = lax.ppermute(out_shard, 'fsdp', other_chip(fsdp_size))]
    reduce_scatter x1, waiting for transfers between devices: 0.01 us -> 57.3 us  [local_split(): lax.psum_scatter(sum_shared_in.transpose(1, 0, 2, 3).reshape(width, 2 * f...]
    ppermute x25 -> x0, starting transfers between devices: 46.9 us -> none  [the longest x14 26.8 us: exchange(): lax.ppermute(piece, 'ctx', [(i, (i + k) % size) for i in range(size)])]
    unnamed x8 -> x14, waiting for transfers between devices: 1.3 us -> 47 us
    ppermute x2 -> x1, waiting for transfers between devices: 47.5 us -> 9.77 us  [fsdp_scatter(): far = lax.ppermute(far, 'fsdp', other_chip(size))]
    ppermute x15 -> x9, waiting for transfers between devices: 76.8 us -> 46 us  [ring_walk(): fore = lax.ppermute(fore, 'ctx', ahead)]
  transfers between devices with their start and end apart: 107 -> 75, of which waited for: 41 -> 44; matrix products, arithmetic and copies ran while one was open for 45% -> 37% of each run, Pallas kernels for 0% -> 0%
where the time goes in v5:
time: 1020 us; the launch traced here: 1010 us
  waiting for transfers between devices  425 us (42%)
  matrix products  208 us (20%)
  local copies, waits for them, and re-layouts  118 us (12%)
  blocking collectives  83.1 us (8%)
  starting transfers between devices  76.5 us (8%)
  other arithmetic  73.9 us (7%)
  between operations  20.4 us (2%)
    reduce_scatter x4, waiting for transfers between devices, sum_rows(): lax.psum_scatter(grad.astype(bf16), 'fsdp', scatter_dimension=0, tiled=True)  87.6 us
    all_to_all x2, blocking collectives, column_pieces(): lax.all_to_all(pieces, 'ctx', split_axis=0, concat_axis=0, tiled=True)  83.1 us
    reduce_scatter x1, waiting for transfers between devices, local_split(): lax.psum_scatter(sum_shared_in.transpose(1, 0, 2, 3).reshape(width, 2 * f...  57.3 us
    ppermute x12, waiting for transfers between devices, ring_sums(): fore = lax.ppermute(fore, 'ctx', ahead)  52.3 us
    dot_general x8, matrix products, dot(): return jnp.dot(a, b, preferred_element_type=f32)  50.5 us
    dot_general x7, matrix products, dot_t(): lax.dot_general(a, b, (((1,), (1,)), ((), ())), preferred_element_type=f32)  50.1 us
    dot_general x8, matrix products, t_dot(): lax.dot_general(a, b, (((0,), (0,)), ((), ())), preferred_element_type=f32)  47.5 us
    unnamed x14, waiting for transfers between devices  47 us
  transfers between devices with their start and end apart: 75, of which 44 were waited for; matrix products, arithmetic and copies ran while one was open for 37% of the time, Pallas kernels for 0%

profile of v5, /device:TPU:8, one launch (start us, length us, event | category | flops | bytes accessed | tf_op | source)
XLA Modules:
  0.0 1005.4 jit_solution(4568430421182728794)
XLA Ops:
  10.7 29.7 %all_to_all.25 = bf16[8,80,768]{2,1,0:T(8,128)(2,1)} all-to-all(bf16[8,80,768]{2,1,0:T(8,128)(2,1)S(1)} %pad_maximum_fusion.5), channel_id=1, replica_groups=mesh['ctx'=8,'fsdp'=4] {'ctx'}, dimensions={0} | all-to-all | bytes 1966080 | tf_op jit(solution)/shard_map/all_to_all | solution.py:193
  122.6 53.4 %all_to_all.26 = bf16[8,64,1408]{2,1,0:T(8,128)(2,1)} all-to-all(bf16[8,64,1408]{2,1,0:T(8,128)(2,1)} %reshape.698), channel_id=1, replica_groups=mesh['ctx'=8,'fsdp'=4] {'ctx'}, dimensions={0} | all-to-all | bytes 2883584 | tf_op jit(solution)/shard_map/all_to_all | solution.py:193
  184.0 17.5 %collective-permute-done.12 = bf16[64,2048]{1,0:T(8,128)(2,1)S(1)} collective-permute-done((bf16[64,2048]{1,0:T(8,128)(2,1)S(1)}, bf16[64,2048]{1,0:T(8,128)(2,1)S(1)}, u32[]{:S(2)}, u32[]{:S(2)}) %collective-permute-start.12) | collective-permute-done | bytes 262176 | tf_op jit(solution)/shard_map/ppermute | solution.py:132
  205.5 18.0 %collective-permute-done.13 = bf16[128,2048]{1,0:T(8,128)(2,1)S(1)} collective-permute-done((bf16[128,2048]{1,0:T(8,128)(2,1)S(1)}, bf16[128,2048]{1,0:T(8,128)(2,1)S(1)}, u32[]{:S(2)}, u32[]{:S(2)}) %collective-permute-start.13) | collective-permute-done | bytes 524320 | tf_op jit(solution)/shard_map/ppermute | solution.py:141
  228.5 10.4 %collective-permute-done.10 = bf16[128,2048]{1,0:T(8,128)(2,1)S(1)} collective-permute-done((bf16[128,2048]{1,0:T(8,128)(2,1)S(1)}, bf16[128,2048]{1,0:T(8,128)(2,1)S(1)}, u32[]{:S(2)}, u32[]{:S(2)}) %collective-permute-start.10) | collective-permute-done | bytes 524320 | tf_op jit(solution)/shard_map/ppermute | solution.py:140
  242.7 9.4 collective-permute-done.11
  260.2 8.9 collective-permute-done.16
  322.4 10.2 %fusion.137 = f32[1024,1408]{0,1:T(8,128)} fusion(bf16[1024,2048]{1,0:T(8,128)(2,1)} %constant_dynamic-update-slice_fusion.30, bf16[2048,1408]{1,0:T(8,128)(2,1)S(1)} %bitcast.388), kind=kOutput, calls=%fused_computation.372 | convolution fusion | flops 5905580032 | bytes 15728640 | tf_op jit(solution)/shard_map/dot_general | solution.py:242
  332.5 12.4 %all-gather.15.cloned.1.call-done = bf16[2048,2816]{1,0:T(8,128)(2,1)} async-done(((bf16[512,2816]{1,0:T(8,128)(2,1)}), bf16[2048,2816]{1,0:T(8,128)(2,1)}) %all-gather.15.cloned.1.call-update) | async-done | bytes 11534352 | tf_op jit(solution)/shard_map/all_gather | solution.py:282
  344.9 10.1 %fusion.136 = f32[512,2816]{1,0:T(8,128)S(1)} fusion(bf16[512,2048]{1,0:T(8,128)(2,1)} %bitcast.415, bf16[2048,2816]{1,0:T(8,128)(2,1)} %all-gather.15.cloned.1.call-done), kind=kOutput, calls=%fused_computation.371 | convolution fusion | flops 5905580032 | bytes 19398656 | tf_op jit(solution)/shard_map/dot_general | solution.py:242
  359.9 29.9 %all-gather.21.cloned.1.call-done = bf16[1,1408,2048]{2,1,0:T(8,128)(2,1)} async-done(((bf16[1,352,2048]{2,1,0:T(8,128)(2,1)}), bf16[1,1408,2048]{2,1,0:T(8,128)(2,1)}) %all-gather.21.cloned.1.call-update) | async-done | bytes 5767184 | tf_op jit(solution)/shard_map/all_gather | solution.py:280
  389.8 9.0 fusion.27
  410.0 9.3 multiply_convert_fusion.5
  420.9 8.9 convolution_convert_fusion
  429.9 10.8 %multiply_convert_fusion.2 = (bf16[1024,704]{0,1:T(8,128)(2,1)}, bf16[1024,704]{0,1:T(8,128)(2,1)}, bf16[1024,704]{0,1:T(8,128)(2,1)S(1)}) fusion(f32[1024,1408]{0,1:T(8,128)} %fusion.137, bf16[1024,2048]{1,0:T(8,128)(2,1)} %fusion.1, bf16[704,2048]{1,0:T(8,128)(2,1)} %all-gather.17.cloned.1.call-done), kind=kOutput, calls=%fused_computation.62 | convolution fusion | flops 2964324352 | bytes 17170432 | tf_op jit(solution)/shard_map/dot_general | solution.py:245
  444.4 8.2 fusion.2
  464.8 10.9 %collective-permute-done.29 = bf16[128,2048]{1,0:T(8,128)(2,1)S(1)} collective-permute-done((bf16[128,2048]{1,0:T(8,128)(2,1)S(1)}, bf16[128,2048]{1,0:T(8,128)(2,1)S(1)}, u32[]{:S(2)}, u32[]{:S(2)}) %collective-permute-start.29) | collective-permute-done | bytes 524320 | tf_op jit(solution)/shard_map/ppermute | solution.py:141
  478.5 9.3 convolution_convert_fusion.6
  503.5 8.5 fusion.8
  541.0 12.2 %collective-permute-done.34 = bf16[128,2048]{1,0:T(8,128)(2,1)S(1)} collective-permute-done((bf16[128,2048]{1,0:T(8,128)(2,1)}, bf16[128,2048]{1,0:T(8,128)(2,1)S(1)}, u32[]{:S(2)}, u32[]{:S(2)}) %collective-permute-start.34) | collective-permute-done | bytes 524320 | tf_op jit(solution)/shard_map/ppermute | solution.py:140
  559.8 9.1 collective-permute-done.35
  578.4 9.1 collective-permute-done.40
  625.9 15.9 %fusion.55 = f32[1024,2,128]{0,2,1:T(8,128)} fusion(bf16[1024,2,128]{0,2,1:T(8,128)(2,1)} %copy-done.37, f32[2,1024,1024]{1,2,0:T(8,128)} %fusion.139, f32[2,1024,1024]{1,2,0:T(8,128)} %copy-done.3, f32[2,1024]{1,0:T(2,128)S(1)} %copy-done.47, pred[1024,1024]{0,1:T(8,128)(4,1)} %copy-done.10), kind=kOutput, calls=%fused_computation.82 | convolution fusion | flops 559942656 | bytes 19406848 | tf_op jit(solution)/shard_map/hqk,qhd->khd/dot_general | solution.py:443
  641.9 16.4 %broadcast_multiply_fusion.1 = (f32[1024,2,128]{0,2,1:T(8,128)}, f32[1024,2,128]{0,2,1:T(8,128)}, f32[1024,2,128]{0,2,1:T(8,128)}) fusion(f32[1024,128]{0,1:T(8,128)} %get-tuple-element.209, f32[1024,2,128]{0,2,1:T(8,128)} %fusion.55, bf16[1024,2,128]{0,2,1:T(8,128)(2,1)S(1)} %copy-done.36, f32[2,1024,1024]{1,2,0:T(8,128)} %fusion.139, ...), kind=kOutput, calls=%fused_computation.158 | convolution fusion | flops 560466944 | bytes 23076864 | tf_op jit(solution)/shard_map/hqk,khd->qhd/dot_general | solution.py:441
  668.2 8.4 fusion.7
  689.8 11.0 %convolution_convert_fusion.1 = bf16[2048,1408]{1,0:T(8,128)(2,1)} fusion(bf16[1024,2048]{1,0:T(8,128)(2,1)} %constant_dynamic-update-slice_fusion.30, bf16[1024,704]{0,1:T(8,128)(2,1)} %get-tuple-element.117, bf16[1024,704]{0,1:T(8,128)(2,1)} %get-tuple-element.116), kind=kOutput, calls=%fused_computation.25 | convolution fusion | flops 5914230784 | bytes 12845056 | tf_op jit(solution)/shard_map/dot_general | solution.py:248
  731.7 9.8 collective-permute-done.58
  754.1 45.3 %all-reduce.4.cloned.1.call-done = f32[32,896]{1,0:T(8,128)} async-done(((f32[32,896]{1,0:T(8,128)}), f32[32,896]{1,0:T(8,128)}) %all-reduce.4.cloned.1.call-update) | async-done | bytes 114704
  808.4 17.9 %reduce-scatter.12.cloned.1.call-done = bf16[64,2048]{1,0:T(8,128)(2,1)} async-done(((bf16[256,2048]{1,0:T(8,128)(2,1)}), bf16[64,2048]{1,0:T(8,128)(2,1)}) %reduce-scatter.12.cloned.1.call-update) | async-done | bytes 262160 | tf_op jit(solution)/shard_map/reduce_scatter | solution.py:256
  847.6 18.3 %reduce-scatter.10.cloned.1.call-done = bf16[176,2048]{1,0:T(8,128)(2,1)} async-done(((bf16[704,2048]{1,0:T(8,128)(2,1)}), bf16[176,2048]{1,0:T(8,128)(2,1)}) %reduce-scatter.10.cloned.1.call-update) | async-done | bytes 720912 | tf_op jit(solution)/shard_map/reduce_scatter | solution.py:256
  865.9 57.3 %reduce-scatter.8.cloned.1.call-done = bf16[512,1408]{1,0:T(8,128)(2,1)} async-done(((bf16[2048,1408]{1,0:T(8,128)(2,1)}), bf16[512,1408]{1,0:T(8,128)(2,1)}) %reduce-scatter.8.cloned.1.call-update) | async-done | bytes 1441808 | tf_op jit(solution)/shard_map/reduce_scatter | solution.py:404
  929.4 51.4 %reduce-scatter.14.cloned.1.call-done = bf16[352,2048]{1,0:T(8,128)(2,1)} async-done(((bf16[1408,2048]{1,0:T(8,128)(2,1)}), bf16[352,2048]{1,0:T(8,128)(2,1)}) %reduce-scatter.14.cloned.1.call-update) | async-done | bytes 1441808 | tf_op jit(solution)/shard_map/reduce_scatter | solution.py:256
  (502 shorter events, 418.1 us)
Async XLA Ops:
  7.2 82.0 %all-gather.19.cloned.1.call-start = ((), (), s32[]{:S(2)}) async-start(), calls=%async_computation.19 | async-start | bytes 4915200 | tf_op jit(solution)/shard_map/all_gather | solution.py:265
  40.5 136.8 %all-gather.11.cloned.1.call-start = ((), (), s32[]{:S(2)}) async-start(), calls=%async_computation.10 | async-start | bytes 1310720 | tf_op jit(solution)/shard_map/all_gather | solution.py:283
  41.1 13.0 %collective-permute-start.1 = (bf16[128,2048]{1,0:T(8,128)(2,1)S(1)}, bf16[128,2048]{1,0:T(8,128)(2,1)S(1)}, u32[]{:S(2)}, u32[]{:S(2)}) collective-permute-start(bf16[128,2048]{1,0:T(8,128)(2,1)S(1)} %bitcast.384), channel_id=1, source_target_pairs={{8,0},{16,8},{24,16},{28,24},{20,28},{12,20},{4,12},{0,4},{9,1},{1... | collective-permute-start | bytes 1572872 | tf_op jit(solution)/shard_map/ppermute | solution.py:98
  42.6 266.3 %all-gather.13.cloned.1.call-start = ((), (), s32[]{:S(2)}) async-start(), calls=%async_computation.11 | async-start | bytes 4718592 | tf_op jit(solution)/shard_map/all_gather | solution.py:323
  113.5 203.3 %all-gather.23.cloned.1.call-start = ((), (), s32[]{:S(2)}) async-start(), calls=%async_computation.21 | async-start | bytes 7208960 | tf_op jit(solution)/shard_map/all_gather | solution.py:311
  176.0 168.9 %all-gather.15.cloned.1.call-start = ((), (), s32[]{:S(2)}) async-start(), calls=%async_computation.12 | async-start | bytes 14417920 | tf_op jit(solution)/shard_map/all_gather | solution.py:282
  176.6 213.2 %all-gather.21.cloned.1.call-start = ((), (), s32[]{:S(2)}) async-start(), calls=%async_computation.20 | async-start | bytes 7208960 | tf_op jit(solution)/shard_map/all_gather | solution.py:280
  177.2 252.7 %all-gather.17.cloned.1.call-start = ((), (), s32[]{:S(2)}) async-start(), calls=%async_computation.13 | async-start | bytes 3604480 | tf_op jit(solution)/shard_map/all_gather | solution.py:312
  181.9 19.6 %collective-permute-start.12 = (bf16[64,2048]{1,0:T(8,128)(2,1)S(1)}, bf16[64,2048]{1,0:T(8,128)(2,1)S(1)}, u32[]{:S(2)}, u32[]{:S(2)}) collective-permute-start(bf16[64,2048]{1,0:T(8,128)(2,1)S(1)} %get-tuple-element.162), channel_id=1, source_target_pairs={{8,0},{16,8},{24,16},{28,24},{20,28},{12,20},{4,12},{0,4},{9,1},{1... | collective-permute-start | bytes 786440 | tf_op jit(solution)/shard_map/ppermute | solution.py:132
  183.2 18.3 %collective-permute-start.8 = (bf16[64,2048]{1,0:T(8,128)(2,1)S(1)}, bf16[64,2048]{1,0:T(8,128)(2,1)S(1)}, u32[]{:S(2)}, u32[]{:S(2)}) collective-permute-start(bf16[64,2048]{1,0:T(8,128)(2,1)S(1)} %get-tuple-element.161), channel_id=1, source_target_pairs={{0,8},{8,16},{16,24},{24,28},{28,20},{20,12},{12,4},{4,0},{1,9},{9... | collective-permute-start | bytes 786440 | tf_op jit(solution)/shard_map/ppermute | solution.py:131
  202.7 20.8 %collective-permute-start.13 = (bf16[128,2048]{1,0:T(8,128)(2,1)S(1)}, bf16[128,2048]{1,0:T(8,128)(2,1)S(1)}, u32[]{:S(2)}, u32[]{:S(2)}) collective-permute-start(bf16[128,2048]{1,0:T(8,128)(2,1)S(1)} %pad_maximum_fusion.9), channel_id=1, source_target_pairs={{8,0},{16,8},{24,16},{28,24},{20,28},{12,20},{4,12},{0,4},{9,1},{1... | collective-permute-start | bytes 1572872 | tf_op jit(solution)/shard_map/ppermute | solution.py:141
  204.3 20.6 %collective-permute-start.9 = (bf16[128,2048]{1,0:T(8,128)(2,1)S(1)}, bf16[128,2048]{1,0:T(8,128)(2,1)S(1)}, u32[]{:S(2)}, u32[]{:S(2)}) collective-permute-start(bf16[128,2048]{1,0:T(8,128)(2,1)S(1)} %pad_maximum_fusion.8), channel_id=1, source_target_pairs={{0,8},{8,16},{16,24},{24,28},{28,20},{20,12},{12,4},{4,0},{1,9},{9... | collective-permute-start | bytes 1572872 | tf_op jit(solution)/shard_map/ppermute | solution.py:140
  272.4 428.4 %reduce-scatter.6.cloned.1.call-start = ((), (), s32[]{:S(2)}) async-start(), calls=%async_computation.14 | async-start | bytes 14417920 | tf_op jit(solution)/shard_map/reduce_scatter | solution.py:256
  462.6 13.1 %collective-permute-start.29 = (bf16[128,2048]{1,0:T(8,128)(2,1)S(1)}, bf16[128,2048]{1,0:T(8,128)(2,1)S(1)}, u32[]{:S(2)}, u32[]{:S(2)}) collective-permute-start(bf16[128,2048]{1,0:T(8,128)(2,1)S(1)} %pad_maximum_fusion.11), channel_id=1, source_target_pairs={{8,0},{16,8},{24,16},{28,24},{20,28},{12,20},{4,12},{0,4},{9,1},{1... | collective-permute-start | bytes 1572872 | tf_op jit(solution)/shard_map/ppermute | solution.py:141
  526.7 14.3 %all-to-all-start.2 = ((f32[8,2,128]{2,1,0:T(2,128)}), f32[8,2,128]{2,1,0:T(2,128)S(1)}, u32[]{:S(2)}, u32[]{:S(2)}) async-start(f32[8,2,128]{2,1,0:T(2,128)} %pad_maximum_fusion.16), calls=%async_computation.2 | async-start | bytes 16384 | tf_op jit(solution)/shard_map/all_to_all | solution.py:414
  530.4 269.0 %all-reduce.4.cloned.1.call-start = ((), (), s32[]{:S(2)}) async-start(), calls=%async_computation.22 | async-start | bytes 229376
  538.6 14.6 %collective-permute-start.34 = (bf16[128,2048]{1,0:T(8,128)(2,1)}, bf16[128,2048]{1,0:T(8,128)(2,1)S(1)}, u32[]{:S(2)}, u32[]{:S(2)}) collective-permute-start(bf16[128,2048]{1,0:T(8,128)(2,1)} %get-tuple-element.137), channel_id=1, source_target_pairs={{0,8},{8,16},{16,24},{24,28},{28,20},{20,12},{12,4},{4,0},{1,9},{9... | collective-permute-start | bytes 1572872 | tf_op jit(solution)/shard_map/ppermute | solution.py:140
  540.9 14.6 %collective-permute-start.38 = (bf16[128,2048]{1,0:T(8,128)(2,1)S(1)}, bf16[128,2048]{1,0:T(8,128)(2,1)}, u32[]{:S(2)}, u32[]{:S(2)}) collective-permute-start(bf16[128,2048]{1,0:T(8,128)(2,1)S(1)} %get-tuple-element.138), channel_id=1, source_target_pairs={{8,0},{16,8},{24,16},{28,24},{20,28},{12,20},{4,12},{0,4},{9,1},{1... | collective-permute-start | bytes 1572872 | tf_op jit(solution)/shard_map/ppermute | solution.py:141
  677.9 148.4 %reduce-scatter.12.cloned.1.call-start = ((), (), s32[]{:S(2)}) async-start(), calls=%async_computation.17 | async-start | bytes 1310720 | tf_op jit(solution)/shard_map/reduce_scatter | solution.py:256
  682.4 183.6 %reduce-scatter.10.cloned.1.call-start = ((), (), s32[]{:S(2)}) async-start(), calls=%async_computation.16 | async-start | bytes 3604480 | tf_op jit(solution)/shard_map/reduce_scatter | solution.py:256
  700.8 222.4 %reduce-scatter.8.cloned.1.call-start = ((), (), s32[]{:S(2)}) async-start(), calls=%async_computation.15 | async-start | bytes 7208960 | tf_op jit(solution)/shard_map/reduce_scatter | solution.py:404
  706.5 274.3 %reduce-scatter.14.cloned.1.call-start = ((), (), s32[]{:S(2)}) async-start(), calls=%async_computation.18 | async-start | bytes 7208960 | tf_op jit(solution)/shard_map/reduce_scatter | solution.py:256
  716.7 15.0 %collective-permute-start.56 = (bf16[8,64,768]{2,1,0:T(8,128)(2,1)}, bf16[8,64,768]{2,1,0:T(8,128)(2,1)S(1)}, u32[]{:S(2)}, u32[]{:S(2)}) collective-permute-start(bf16[8,64,768]{2,1,0:T(8,128)(2,1)} %get-tuple-element.165), channel_id=1, source_target_pairs={{0,1},{1,0},{2,3},{3,2},{4,5},{5,4},{6,7},{7,6},{8,9},{9,8},{10,11... | collective-permute-start | bytes 2359304 | tf_op jit(solution)/shard_map/ppermute | solution.py:174
  722.2 19.4 %collective-permute-start.58 = (bf16[8,64,768]{2,1,0:T(8,128)(2,1)S(1)}, bf16[8,64,768]{2,1,0:T(8,128)(2,1)S(1)}, u32[]{:S(2)}, u32[]{:S(2)}) collective-permute-start(bf16[8,64,768]{2,1,0:T(8,128)(2,1)S(1)} %fusion.49), channel_id=1, source_target_pairs={{0,2},{1,3},{2,0},{3,1},{4,6},{5,7},{6,4},{7,5},{8,10},{9,11},{10,... | collective-permute-start | bytes 2359304 | tf_op jit(solution)/shard_map/ppermute | solution.py:176
  728.9 20.4 %collective-permute-start.53 = (bf16[128,2048]{1,0:T(8,128)(2,1)}, bf16[128,2048]{1,0:T(8,128)(2,1)}, u32[]{:S(2)}, u32[]{:S(2)}) collective-permute-start(bf16[128,2048]{1,0:T(8,128)(2,1)} %pad_maximum_fusion.15), channel_id=1, source_target_pairs={{8,0},{16,8},{24,16},{28,24},{20,28},{12,20},{4,12},{0,4},{9,1},{1... | collective-permute-start | bytes 1572872 | tf_op jit(solution)/shard_map/ppermute | solution.py:141
  731.5 17.9 %collective-permute-start.49 = (bf16[128,2048]{1,0:T(8,128)(2,1)}, bf16[128,2048]{1,0:T(8,128)(2,1)S(1)}, u32[]{:S(2)}, u32[]{:S(2)}) collective-permute-start(bf16[128,2048]{1,0:T(8,128)(2,1)} %pad_maximum_fusion.14), channel_id=1, source_target_pairs={{0,8},{8,16},{16,24},{24,28},{28,20},{20,12},{12,4},{4,0},{1,9},{9... | collective-permute-start | bytes 1572872 | tf_op jit(solution)/shard_map/ppermute | solution.py:140
  743.8 84.2 %all-to-all-start.3 = ((bf16[8,64,768]{2,1,0:T(8,128)(2,1)}), bf16[8,64,768]{2,1,0:T(8,128)(2,1)}, u32[]{:S(2)}, u32[]{:S(2)}) async-start(bf16[8,64,768]{2,1,0:T(8,128)(2,1)} %fusion.51), calls=%async_computation.6 | async-start | bytes 1572864 | tf_op jit(solution)/shard_map/all_to_all | solution.py:198
  752.1 51.6 %collective-permute-start.50 = (bf16[128,2048]{1,0:T(8,128)(2,1)}, bf16[128,2048]{1,0:T(8,128)(2,1)S(1)}, u32[]{:S(2)}, u32[]{:S(2)}) collective-permute-start(bf16[128,2048]{1,0:T(8,128)(2,1)} %get-tuple-element.127), channel_id=1, source_target_pairs={{0,8},{8,16},{16,24},{24,28},{28,20},{20,12},{12,4},{4,0},{1,9},{9... | collective-permute-start | bytes 1572872 | tf_op jit(solution)/shard_map/ppermute | solution.py:140
  753.5 50.1 %collective-permute-start.54 = (bf16[128,2048]{1,0:T(8,128)(2,1)}, bf16[128,2048]{1,0:T(8,128)(2,1)}, u32[]{:S(2)}, u32[]{:S(2)}) collective-permute-start(bf16[128,2048]{1,0:T(8,128)(2,1)} %get-tuple-element.128), channel_id=1, source_target_pairs={{8,0},{16,8},{24,16},{28,24},{20,28},{12,20},{4,12},{0,4},{9,1},{1... | collective-permute-start | bytes 1572872 | tf_op jit(solution)/shard_map/ppermute | solution.py:141
  806.4 179.1 %collective-permute-start.51 = (bf16[128,2048]{1,0:T(8,128)(2,1)}, bf16[128,2048]{1,0:T(8,128)(2,1)}, u32[]{:S(2)}, u32[]{:S(2)}) collective-permute-start(bf16[128,2048]{1,0:T(8,128)(2,1)} %get-tuple-element.125), channel_id=1, source_target_pairs={{0,8},{8,16},{16,24},{24,28},{28,20},{20,12},{12,4},{4,0},{1,9},{9... | collective-permute-start | bytes 1572872 | tf_op jit(solution)/shard_map/ppermute | solution.py:140
  806.9 178.6 %collective-permute-start.55 = (bf16[128,2048]{1,0:T(8,128)(2,1)}, bf16[128,2048]{1,0:T(8,128)(2,1)}, u32[]{:S(2)}, u32[]{:S(2)}) collective-permute-start(bf16[128,2048]{1,0:T(8,128)(2,1)} %get-tuple-element.126), channel_id=1, source_target_pairs={{8,0},{16,8},{24,16},{28,24},{20,28},{12,20},{4,12},{0,4},{9,1},{1... | collective-permute-start | bytes 1572872 | tf_op jit(solution)/shard_map/ppermute | solution.py:141
  923.2 70.7 %all-to-all-start.4 = ((bf16[8,64,1408]{2,1,0:T(8,128)(2,1)}), bf16[8,64,1408]{2,1,0:T(8,128)(2,1)}, u32[]{:S(2)}, u32[]{:S(2)}) async-start(bf16[8,64,1408]{2,1,0:T(8,128)(2,1)} %bitcast.421), calls=%async_computation.8 | async-start | bytes 2883584 | tf_op jit(solution)/shard_map/all_to_all | solution.py:198
  (106 other events, 1068.3 us)
Sparse Core Ops, SparseCore 0:
  40.6 32.2 all-gather.18
  74.5 16.7 all-gather.10
  113.6 110.0 all-gather.12
  225.1 42.1 all-gather.22
  268.7 76.1 all-gather.14
  346.3 43.4 all-gather.20
  391.4 27.0 all-gather.16
  429.9 92.2 reduce-scatter.5
  678.0 121.3 all-reduce.3
  802.3 23.8 reduce-scatter.11
  829.5 36.3 reduce-scatter.9
  868.3 54.8 reduce-scatter.7
  925.9 54.8 reduce-scatter.13

commit v6 on v5

--- a/solution.py
+++ b/solution.py
@@ -164,6 +164,20 @@
     return lax.optimization_barrier((value,) + deps)
 
 
+def fsdp_gather(shard, size):
+    index = lax.axis_index("fsdp")
+    rows, width = shard.shape
+    far = lax.ppermute(shard, "fsdp", other_chip(size))
+    pair = jnp.where(
+        index < 2, jnp.stack([shard, far], axis=0), jnp.stack([far, shard], axis=0)
+    )
+    near = lax.ppermute(pair, "fsdp", other_core(size))
+    out = jnp.zeros((2, 2, rows, width), shard.dtype)
+    out = lax.dynamic_update_index_in_dim(out, pair, index % 2, 1)
+    out = lax.dynamic_update_index_in_dim(out, near, 1 - index % 2, 1)
+    return out.reshape(size * rows, width)
+
+
 def fsdp_scatter(grad, size, axis):
     index = lax.axis_index("fsdp")
 
@@ -195,7 +209,6 @@
 
 def merge_columns(pieces, groups, size):
     width = pieces.shape[2] // groups
-    pieces = lax.all_to_all(pieces, "ctx", split_axis=0, concat_axis=0, tiled=True)
     columns = [
         pieces[peer, :, group * width : (group + 1) * width]
         for group in range(groups)
@@ -261,7 +274,9 @@
     small = jnp.concatenate(small + [routes.astype(bf16).reshape(-1)], axis=0)
     small_count = small.shape[0]
     token_rows = ring_gather(tokens.reshape(token_count, width), ctx_size, ctx_index)
+    expert_out = lax.all_gather(w_expert_out[0], "fsdp", axis=0, tiled=True)
     pieces = column_pieces(w_qkv, 3, ctx_size, small)
+    pieces, expert_out = after(pieces, expert_out)
     pieces = lax.all_gather(pieces, "fsdp", axis=0, tiled=False).transpose(1, 0, 2, 3)
     qkv_weight = pieces[:, :, :shard].reshape(width, 3 * own_width)
     small = pieces[:, :, shard:].reshape(device_count, -1)[:, :small_count]
@@ -277,10 +292,8 @@
         route_rows.reshape(ctx_size, fsdp_size, -1), lax.axis_index("fsdp"), 1, keepdims=False
     ).reshape(ctx_size, token_count, top_count)
 
-    expert_out = lax.all_gather(w_expert_out[0], "fsdp", axis=0, tiled=True)
-    expert_in, token_rows = after(w_expert_in[0], token_rows)
-    expert_in = lax.all_gather(expert_in, "fsdp", axis=0, tiled=True)
-    out_weight = lax.all_gather(w_out, "fsdp", axis=0, tiled=True)
+    expert_in = lax.all_gather(w_expert_in[0], "fsdp", axis=0, tiled=True)
+    out_weight = fsdp_gather(w_out, fsdp_size)
 
     block_ids = jnp.arange(ctx_size, dtype=i32)[:, None]
     local_index = jnp.arange(block_len, dtype=i32)[None, :]
@@ -309,7 +322,7 @@
     queries, in_shard, out_shard = after(queries, w_shared_in, w_shared_out)
     shared_in = column_pieces(in_shard, 2, ctx_size, None)
     shared_in = lax.all_gather(shared_in, "fsdp", axis=0, tiled=False)
-    shared_out = lax.all_gather(out_shard, "fsdp", axis=0, tiled=True)
+    shared_out = fsdp_gather(out_shard, fsdp_size)
     allowed = (positions[None, :] <= positions[:, None]) & (seg_rows[None, :] == seg_rows[:, None])
     scores = jnp.einsum("qhd,khd->hqk", queries, keys, preferred_element_type=f32) * score_scale
     scores = jnp.where(allowed[None], scores, MASK_FILL)
@@ -362,10 +375,12 @@
     expert_res = dot(expert_hid, expert_out).astype(bf16)
     routed = gate_all[:, None] * to_tokens(expert_res)
 
+    shared_in, expert_res = after(shared_in, expert_res)
     shared_in = shared_in.transpose(1, 0, 2, 3).reshape(width, 2 * fs_own)
     shared_pre = dot(low_two, shared_in)
     shared_hid = swiglu(shared_pre, fs_own).astype(bf16)
     shared_res = dot(shared_hid, shared_out)
+    grad_rows, shared_res = after(grad_rows, shared_res)
     out_parts = (scale_all[:, None] * shared_res + routed).astype(bf16)
     out_sum = ring_scatter(out_parts, ctx_size, ctx_index)
 
@@ -380,12 +395,11 @@
     grad_expert_in = t_dot(buffer, grad_pre)
     grad_buffer = dot_t(grad_pre, expert_in).astype(bf16)
 
-    grad_expert_in, grad_expert_out, grad_shared_res = after(
+    grad_expert_out = grad_expert_out.astype(bf16)
+    grad_expert_in, grad_shared_res = after(
         grad_expert_in.astype(bf16),
-        grad_expert_out.astype(bf16),
         (scale_all[:, None] * grad_rows.astype(f32)).astype(bf16),
     )
-    sum_expert_out = sum_rows(grad_expert_out)
     sum_expert_in = sum_rows(grad_expert_in)
 
     grad_f32 = grad_rows.astype(f32)
@@ -397,8 +411,11 @@
     grad_shared_pre, out_sum = after(grad_shared_pre, out_sum)
     two_parts = (dot_t(grad_shared_pre, shared_in) + to_tokens(grad_buffer)).astype(bf16)
     grad_two = ring_scatter(two_parts, ctx_size, ctx_index)
+    grad_two, grad_shared_in, grad_shared_out, grad_expert_out = after(
+        grad_two, grad_shared_in.astype(bf16), grad_shared_out.astype(bf16), grad_expert_out
+    )
     sum_expert_in, grad_shared_in, grad_shared_out = after(
-        sum_expert_in, grad_shared_in.astype(bf16), grad_shared_out.astype(bf16)
+        sum_expert_in, grad_shared_in, grad_shared_out
     )
     sum_shared_in = grad_shared_in.reshape(ctx_size, fsdp_size, shard, 2 * fs_own)
     sum_shared_in = lax.psum_scatter(
@@ -408,6 +425,8 @@
         tiled=True,
     ).reshape(ctx_size, shard, 2 * fs_own)
     sum_shared_out = sum_rows(grad_shared_out)
+    sum_expert_in, grad_expert_out = after(sum_expert_in, grad_expert_out)
+    sum_expert_out = sum_rows(grad_expert_out)
     output = (own_residual + out_sum).astype(bf16).reshape(tokens.shape)
 
     dots = jnp.stack([grad_gates, gate_dots], axis=1)
@@ -435,6 +454,7 @@
     grad_mixed = grad_resid.astype(bf16)
     mixed_all = ring_gather(grad_mixed, ctx_size, ctx_index)
     grad_attn = dot_t(mixed_all, out_weight).astype(bf16).reshape(head_shape)
+    grad_attn, sum_expert_in = after(grad_attn, sum_expert_in)
     grad_weights = jnp.einsum("qhd,khd->hqk", grad_attn, values, preferred_element_type=f32)
     delta = jnp.sum(weights * grad_weights, axis=-1, keepdims=True)
     grad_scores = jnp.where(allowed[None], weights * (grad_weights - delta), 0.0).astype(bf16)
@@ -455,8 +475,11 @@
     grad_gain_one = jnp.sum(one_sums * inputs * inv_one_all, axis=0)
     one_parts = one_sums.astype(bf16)
     one_kept, grad_projected = after(one_parts, grad_projected)
-    one_kept, sum_shared_in, sum_shared_out, sum_expert_in = after(
-        one_kept, sum_shared_in, sum_shared_out, sum_expert_in
+    one_kept, sum_shared_in, sum_shared_out, sum_expert_out = after(
+        one_kept, sum_shared_in, sum_shared_out, sum_expert_out
+    )
+    sum_shared_in = lax.all_to_all(
+        sum_shared_in, "ctx", split_axis=0, concat_axis=0, tiled=True
     )
     grad_normed = ring_scatter(one_parts, ctx_size, ctx_index, one_kept)
     grad_inputs_norm, unused = rms_back(
@@ -473,26 +496,27 @@
     )
 
     grad_out_weight = t_dot(attn_own, mixed_all)
-    sum_qkv_weight = fsdp_scatter(
-        grad_qkv_weight.astype(bf16).reshape(ctx_size, fsdp_size, shard, 3 * own_width),
-        fsdp_size,
-        1,
-    ).astype(bf16)
+    small_grads = [grad_gain_one, grad_gain_two, grad_gate_vector, grad_router, grad_bias]
     small_grads = jnp.concatenate(
+        [piece.reshape(device_count, -1) for piece in small_grads], axis=1
+    )
+    more = -(-small_size // (3 * own_width * 16)) * 16
+    small_grads = jnp.pad(small_grads, ((0, 0), (0, more * 3 * own_width - small_size)))
+    pieces = jnp.concatenate(
         [
-            piece.reshape(device_count, -1)
-            for piece in (grad_gain_one, grad_gain_two, grad_gate_vector, grad_router, grad_bias)
+            grad_qkv_weight.astype(bf16).reshape(ctx_size, fsdp_size, shard, 3 * own_width),
+            small_grads.astype(bf16).reshape(ctx_size, fsdp_size, more, 3 * own_width),
         ],
-        axis=1,
-    )
-    small_grads = lax.psum_scatter(
-        small_grads, ("ctx", "fsdp"), scatter_dimension=0, tiled=True
-    ).reshape(small_size)
+        axis=2,
+    )
+    pieces = fsdp_scatter(pieces, fsdp_size, 1).astype(bf16)
+    pieces = lax.all_to_all(pieces, "ctx", split_axis=0, concat_axis=0, tiled=True)
+    small_grads = jnp.sum(pieces[:, shard:].reshape(ctx_size, -1).astype(f32), axis=0)
     return (
         output,
         grad_tokens,
-        merge_columns(sum_qkv_weight, 3, ctx_size),
-        small_grads[router_end:],
+        merge_columns(pieces[:, :shard], 3, ctx_size),
+        small_grads[router_end:small_size],
         sum_rows(grad_out_weight).astype(f32),
         small_grads[:shard],
         small_grads[shard : 2 * shard],

time: 1020 us -> 847 us (0.83)
  waiting for transfers between devices: 425 us -> 307 us
  blocking collectives: 83.1 us -> 29.9 us
  other arithmetic: 73.9 us -> 94.9 us
  local copies, waits for them, and re-layouts: 118 us -> 98.3 us
  starting transfers between devices: 76.5 us -> 92.8 us
  matrix products: 208 us -> 194 us
    reduce_scatter x4, waiting for transfers between devices: 87.6 us -> 0.02 us  [sum_rows(): lax.psum_scatter(grad.astype(bf16), 'fsdp', scatter_dimension=0, tiled=True)]
    all_to_all x2 -> x1, blocking collectives: 83.1 us -> 29.9 us  [column_pieces(): lax.all_to_all(pieces, 'ctx', split_axis=0, concat_axis=0, tiled=True)]
    reduce_scatter x1, waiting for transfers between devices: 57.3 us -> 11.1 us  [local_split(): lax.psum_scatter(sum_shared_in.transpose(1, 0, 2, 3).reshape(width, 2 * f...]
    unnamed x14 -> x10, waiting for transfers between devices: 47 us -> 2.82 us
    ppermute x9, waiting for transfers between devices: 0.02 us -> 43.2 us  [ring_walk(): rear = lax.ppermute(rear, 'ctx', back)]
    all_to_all x2 -> x3, waiting for transfers between devices: 0.01 us -> 24.8 us  [the longest x1 13.4 us: column_pieces(): lax.all_to_all(pieces, 'ctx', split_axis=0, concat_axis=0, tiled=True)]
    ppermute x1, waiting for transfers between devices: 9.77 us -> 31.1 us  [fsdp_scatter(): far = lax.ppermute(far, 'fsdp', other_chip(size))]
    dynamic_update_slice x25, local copies, waits for them, and re-layouts: 30.9 us -> 9.77 us  [put(): lax.dynamic_update_slice(out, piece, (peer * rows + offset, jnp.zeros_lik...]
  transfers between devices with their start and end apart: 75 -> 77, of which waited for: 44 -> 45; matrix products, arithmetic and copies ran while one was open for 37% -> 39% of each run, Pallas kernels for 0% -> 0%
where the time goes in v6:
time: 847 us; the launch traced here: 837 us
  waiting for transfers between devices  307 us (36%)
  matrix products  194 us (23%)
  local copies, waits for them, and re-layouts  98.3 us (12%)
  other arithmetic  94.9 us (11%)
  starting transfers between devices  92.8 us (11%)
  blocking collectives  29.9 us (4%)
  between operations  20.8 us (2%)
    ppermute x12, waiting for transfers between devices, ring_sums(): fore = lax.ppermute(fore, 'ctx', ahead)  57 us
    ppermute x9, waiting for transfers between devices, ring_walk(): fore = lax.ppermute(fore, 'ctx', ahead)  47.2 us
    dot_general x8, matrix products, dot(): return jnp.dot(a, b, preferred_element_type=f32)  45.3 us
    dot_general x8, matrix products, t_dot(): lax.dot_general(a, b, (((0,), (0,)), ((), ())), preferred_element_type=f32)  45 us
    dot_general x7, matrix products, dot_t(): lax.dot_general(a, b, (((1,), (1,)), ((), ())), preferred_element_type=f32)  44 us
    ppermute x9, waiting for transfers between devices, ring_walk(): rear = lax.ppermute(rear, 'ctx', back)  43.2 us
    unnamed x194, local copies, waits for them, and re-layouts  37.8 us
    ppermute x1, waiting for transfers between devices, fsdp_scatter(): far = lax.ppermute(far, 'fsdp', other_chip(size))  31.1 us
  transfers between devices with their start and end apart: 77, of which 45 were waited for; matrix products, arithmetic and copies ran while one was open for 39% of the time, Pallas kernels for 0%

profile of v6, /device:TPU:8, one launch (start us, length us, event | category | flops | bytes accessed | tf_op | source)
XLA Modules:
  0.0 837.1 jit_solution(1298728556343252925)
XLA Ops:
  15.4 29.9 %all_to_all.25 = bf16[8,80,768]{2,1,0:T(8,128)(2,1)} all-to-all(bf16[8,80,768]{2,1,0:T(8,128)(2,1)S(1)} %pad_maximum_fusion.5), channel_id=1, replica_groups=mesh['ctx'=8,'fsdp'=4] {'ctx'}, dimensions={0} | all-to-all | bytes 1966080 | tf_op jit(solution)/shard_map/all_to_all | solution.py:207
  45.2 9.0 %all-gather.12.cloned.1.call-done = bf16[1,1408,2048]{2,1,0:T(8,128)(2,1)} async-done(((bf16[1,352,2048]{2,1,0:T(8,128)(2,1)}), bf16[1,1408,2048]{2,1,0:T(8,128)(2,1)}) %all-gather.12.cloned.1.call-update) | async-done | bytes 5767184 | tf_op jit(solution)/shard_map/all_gather | solution.py:277
  60.7 8.3 collective-permute-done
  85.8 9.4 %collective-permute-done.4 = bf16[128,2048]{1,0:T(8,128)(2,1)S(1)} collective-permute-done((bf16[128,2048]{1,0:T(8,128)(2,1)}, bf16[128,2048]{1,0:T(8,128)(2,1)S(1)}, u32[]{:S(2)}, u32[]{:S(2)}) %collective-permute-start.4) | collective-permute-done | bytes 524320 | tf_op jit(solution)/shard_map/ppermute | solution.py:97
  137.1 12.6 %collective-permute-done.8 = bf16[64,2048]{1,0:T(8,128)(2,1)S(1)} collective-permute-done((bf16[64,2048]{1,0:T(8,128)(2,1)}, bf16[64,2048]{1,0:T(8,128)(2,1)S(1)}, u32[]{:S(2)}, u32[]{:S(2)}) %collective-permute-start.8) | collective-permute-done | bytes 262176 | tf_op jit(solution)/shard_map/ppermute | solution.py:170
  151.8 13.4 %all-to-all-done.1 = bf16[8,64,1408]{2,1,0:T(8,128)(2,1)S(1)} async-done(((bf16[8,64,1408]{2,1,0:T(8,128)(2,1)}), bf16[8,64,1408]{2,1,0:T(8,128)(2,1)S(1)}, u32[]{:S(2)}, u32[]{:S(2)}) %all-to-all-start.1) | async-done | bytes 1441824 | tf_op jit(solution)/shard_map/all_to_all | solution.py:207
  197.3 10.3 %collective-permute-done.15 = bf16[128,2048]{1,0:T(8,128)(2,1)S(1)} collective-permute-done((bf16[128,2048]{1,0:T(8,128)(2,1)S(1)}, bf16[128,2048]{1,0:T(8,128)(2,1)S(1)}, u32[]{:S(2)}, u32[]{:S(2)}) %collective-permute-start.15) | collective-permute-done | bytes 524320 | tf_op jit(solution)/shard_map/ppermute | solution.py:141
  213.4 7.3 collective-permute-done.12
  247.5 7.4 collective-permute-done.19
  260.8 23.0 %collective-permute-done.21 = bf16[128,2048]{1,0:T(8,128)(2,1)S(1)} collective-permute-done((bf16[128,2048]{1,0:T(8,128)(2,1)S(1)}, bf16[128,2048]{1,0:T(8,128)(2,1)S(1)}, u32[]{:S(2)}, u32[]{:S(2)}) %collective-permute-start.21) | collective-permute-done | bytes 524320 | tf_op jit(solution)/shard_map/ppermute | solution.py:98
  288.4 12.8 %collective-permute-done.23 = bf16[128,2048]{1,0:T(8,128)(2,1)S(1)} collective-permute-done((bf16[128,2048]{1,0:T(8,128)(2,1)S(1)}, bf16[128,2048]{1,0:T(8,128)(2,1)S(1)}, u32[]{:S(2)}, u32[]{:S(2)}) %collective-permute-start.23) | collective-permute-done | bytes 524320 | tf_op jit(solution)/shard_map/ppermute | solution.py:98
  308.8 12.5 %collective-permute-done.24 = bf16[64,2048]{1,0:T(8,128)(2,1)S(1)} collective-permute-done((bf16[64,2048]{1,0:T(8,128)(2,1)S(1)}, bf16[64,2048]{1,0:T(8,128)(2,1)S(1)}, u32[]{:S(2)}, u32[]{:S(2)}) %collective-permute-start.24) | collective-permute-done | bytes 262176 | tf_op jit(solution)/shard_map/ppermute | solution.py:101
  329.2 10.2 %fusion.3 = f32[512,2816]{1,0:T(8,128)S(1)} fusion(bf16[512,2048]{1,0:T(8,128)(2,1)S(1)} %bitcast.443, bf16[1,2048,2816]{2,1,0:T(8,128)(2,1)} %all-gather.18.cloned.1.call-done), kind=kOutput, calls=%fused_computation.6 | convolution fusion | flops 5905580032 | bytes 19398656 | tf_op jit(solution)/shard_map/dot_general | solution.py:255
  340.4 7.9 convolution_convert_fusion.7
  355.9 10.0 %fusion.144 = f32[1024,1408]{1,0:T(8,128)S(1)} fusion(bf16[1024,2048]{1,0:T(8,128)(2,1)} %constant_dynamic-update-slice_fusion.30, bf16[2048,1408]{1,0:T(8,128)(2,1)S(1)} %bitcast.414), kind=kOutput, calls=%fused_computation.391 | convolution fusion | flops 5905580032 | bytes 15728640 | tf_op jit(solution)/shard_map/dot_general | solution.py:255
  384.4 8.9 %multiply_convert_fusion.4 = (bf16[512,1408]{1,0:T(8,128)(2,1)S(1)}, bf16[512,1408]{1,0:T(8,128)(2,1)S(1)}) fusion(f32[512,2816]{1,0:T(8,128)} %copy-done.17, bf16[512,2048]{1,0:T(8,128)(2,1)S(1)} %fusion.26, bf16[1408,2048]{1,0:T(8,128)(2,1)} %bitcast.480), kind=kOutput, calls=%fused_computation.73 | convolution fusion | flops 2962161664 | bytes 16515072 | tf_op jit(solution)/shard_map/dot_general | solution.py:258
  395.0 8.9 %convolution_convert_fusion = bf16[2048,2816]{1,0:T(8,128)(2,1)} fusion(bf16[512,2048]{1,0:T(8,128)(2,1)S(1)} %bitcast.444, bf16[512,1408]{1,0:T(8,128)(2,1)S(1)} %get-tuple-element.141, bf16[512,1408]{1,0:T(8,128)(2,1)S(1)} %get-tuple-element.140), kind=kOutput, calls=%fused_computation.8 | convolution fusion | flops 5917114368 | bytes 16515072 | tf_op jit(solution)/shard_map/dot_general | solution.py:261
  403.8 11.9 %fusion.6 = (f32[1024]{0:T(1024)S(1)}, bf16[1024,2048]{1,0:T(8,128)(2,1)}, bf16[1024,2048]{1,0:T(8,128)(2,1)}) fusion(f32[1024,2048]{1,0:T(8,128)} %fusion.145, bf16[1024,2048]{1,0:T(8,128)(2,1)} %all-gather.10.cloned.1.call-done, f32[8,128,2048]{2,1,0:T(8,128)} %fusion.88, f32[1024]{0:T(1024)S(1)} %bitcast.469, f32[1024]{0:T(1024)S(1)} %bitcast.473), kind=kLoop, calls=%fused_computation.12 | loop fusion | flops 18873344 | bytes 29372416 | tf_op jit(solution)/shard_map/reduce_sum | solution.py:406
  437.8 12.9 %fusion.46 = bf16[512,2048]{1,0:T(8,128)(2,1)} fusion(bf16[1,2048,2816]{2,1,0:T(8,128)(2,1)} %all-gather.18.cloned.1.call-done, bf16[512,1408]{1,0:T(8,128)(2,1)} %copy-done.77, bf16[512,1408]{1,0:T(8,128)(2,1)} %copy-done.76), kind=kOutput, calls=%fused_computation.66 | convolution fusion | flops 5912395776 | bytes 16515072 | tf_op jit(solution)/shard_map/dot_general | solution.py:258
  466.9 9.7 %collective-permute-done.31 = bf16[128,2048]{1,0:T(8,128)(2,1)S(1)} collective-permute-done((bf16[128,2048]{1,0:T(8,128)(2,1)S(1)}, bf16[128,2048]{1,0:T(8,128)(2,1)S(1)}, u32[]{:S(2)}, u32[]{:S(2)}) %collective-permute-start.31) | collective-permute-done | bytes 524320 | tf_op jit(solution)/shard_map/ppermute | solution.py:140
  478.3 7.5 fusion.12
  488.4 10.8 %convolution_convert_fusion.2 = bf16[2048,1408]{1,0:T(8,128)(2,1)} fusion(bf16[1024,2048]{1,0:T(8,128)(2,1)} %constant_dynamic-update-slice_fusion.30, bf16[1024,1408]{1,0:T(8,128)(2,1)S(1)} %pad_maximum_fusion.1), kind=kOutput, calls=%fused_computation.30 | convolution fusion | flops 5908463616 | bytes 12845056 | tf_op jit(solution)/shard_map/dot_general | solution.py:261
  508.6 7.4 convolution_convert_fusion.5
  523.5 7.3 convolution_convert_fusion.1
  554.3 7.2 collective-permute-done.44
  563.6 7.1 collective-permute-done.46
  610.7 13.4 %fusion.56 = f32[1024,2,128]{0,2,1:T(8,128)S(1)} fusion(bf16[1024,2,128]{0,2,1:T(8,128)(2,1)S(1)} %copy-done.57, f32[2,1024,1024]{1,2,0:T(8,128)} %fusion.147, f32[2,1024,1024]{1,2,0:T(8,128)} %copy-done.11, f32[2,1024]{1,0:T(2,128)S(1)} %copy-done.69, pred[1024,1024]{0,1:T(8,128)(4,1)S(1)} %copy-done.26), kind=kOutput, calls=%fused_computation.95 | convolution fusion | flops 559942656 | bytes 19406848 | tf_op jit(solution)/shard_map/hqk,qhd->khd/dot_general | solution.py:463
  624.1 17.0 %broadcast_multiply_fusion.1 = (f32[1024,2,128]{0,2,1:T(8,128)S(1)}, f32[1024,2,128]{0,2,1:T(8,128)}, f32[1024,2,128]{0,2,1:T(8,128)}) fusion(f32[1024,128]{0,1:T(8,128)} %get-tuple-element.231, f32[1024,2,128]{0,2,1:T(8,128)S(1)} %fusion.56, bf16[1024,2,128]{0,2,1:T(8,128)(2,1)} %get-tuple-element.213, f32[2,1024,1024]{1,2,0:T(8,128)} %fusion.147, ...), kind=kOutput, calls=%fused_computation.180 | convolution fusion | flops 560466944 | bytes 23076864 | tf_op jit(solution)/shard_map/hqk,khd->qhd/dot_general | solution.py:461
  688.0 31.1 %collective-permute-done.62 = bf16[8,80,768]{2,1,0:T(8,128)(2,1)} collective-permute-done((bf16[8,80,768]{2,1,0:T(8,128)(2,1)}, bf16[8,80,768]{2,1,0:T(8,128)(2,1)}, u32[]{:S(2)}, u32[]{:S(2)}) %collective-permute-start.62) | collective-permute-done | bytes 983072 | tf_op jit(solution)/shard_map/ppermute | solution.py:190
  734.3 23.9 %collective-permute-done.54 = bf16[128,2048]{1,0:T(8,128)(2,1)S(1)} collective-permute-done((bf16[128,2048]{1,0:T(8,128)(2,1)S(1)}, bf16[128,2048]{1,0:T(8,128)(2,1)S(1)}, u32[]{:S(2)}, u32[]{:S(2)}) %collective-permute-start.54) | collective-permute-done | bytes 524320 | tf_op jit(solution)/shard_map/ppermute | solution.py:140
  778.3 11.1 %reduce-scatter.8.cloned.1.call-done = bf16[512,1408]{1,0:T(8,128)(2,1)} async-done(((bf16[2048,1408]{1,0:T(8,128)(2,1)}), bf16[512,1408]{1,0:T(8,128)(2,1)}) %reduce-scatter.8.cloned.1.call-update) | async-done | bytes 1441808 | tf_op jit(solution)/shard_map/reduce_scatter | solution.py:421
  815.4 11.4 %all-to-all-done.4 = bf16[8,64,1408]{2,1,0:T(8,128)(2,1)S(1)} async-done(((bf16[8,64,1408]{2,1,0:T(8,128)(2,1)}), bf16[8,64,1408]{2,1,0:T(8,128)(2,1)S(1)}, u32[]{:S(2)}, u32[]{:S(2)}) %all-to-all-start.4) | async-done | bytes 1441824 | tf_op jit(solution)/shard_map/all_to_all | solution.py:481
  (558 shorter events, 424.8 us)
Async XLA Ops:
  7.2 47.0 %all-gather.12.cloned.1.call-start = ((), (), s32[]{:S(2)}) async-start(), calls=%async_computation.16 | async-start | bytes 7208960 | tf_op jit(solution)/shard_map/all_gather | solution.py:277
  7.9 98.4 %all-gather.14.cloned.1.call-start = ((), (), s32[]{:S(2)}) async-start(), calls=%async_computation.17 | async-start | bytes 4915200 | tf_op jit(solution)/shard_map/all_gather | solution.py:280
  54.2 275.0 %all-gather.18.cloned.1.call-start = ((), (), s32[]{:S(2)}) async-start(), calls=%async_computation.19 | async-start | bytes 14417920 | tf_op jit(solution)/shard_map/all_gather | solution.py:295
  130.7 34.4 %all-to-all-start.1 = ((bf16[8,64,1408]{2,1,0:T(8,128)(2,1)}), bf16[8,64,1408]{2,1,0:T(8,128)(2,1)S(1)}, u32[]{:S(2)}, u32[]{:S(2)}) async-start(bf16[8,64,1408]{2,1,0:T(8,128)(2,1)} %reshape.823), calls=%async_computation.1 | async-start | bytes 2883584 | tf_op jit(solution)/shard_map/all_to_all | solution.py:207
  136.3 216.5 %all-gather.16.cloned.1.call-start = ((), (), s32[]{:S(2)}) async-start(), calls=%async_computation.18 | async-start | bytes 7208960 | tf_op jit(solution)/shard_map/all_gather | solution.py:324
  151.8 17.7 %collective-permute-start.9 = (bf16[2,64,2048]{2,1,0:T(8,128)(2,1)}, bf16[2,64,2048]{2,1,0:T(8,128)(2,1)}, u32[]{:S(2)}, u32[]{:S(2)}) collective-permute-start(bf16[2,64,2048]{2,1,0:T(8,128)(2,1)} %maximum_select_fusion.3), channel_id=1, source_target_pairs={{0,1},{1,0},{2,3},{3,2},{4,5},{5,4},{6,7},{7,6},{8,9},{9,8},{10,11... | collective-permute-start | bytes 1572872 | tf_op jit(solution)/shard_map/ppermute | solution.py:174
  166.3 209.9 %all-gather.10.cloned.1.call-start = ((), (), s32[]{:S(2)}) async-start(), calls=%async_computation.10 | async-start | bytes 4718592 | tf_op jit(solution)/shard_map/all_gather | solution.py:336
  212.3 19.1 %collective-permute-start.26 = (bf16[176,2048]{1,0:T(8,128)(2,1)S(1)}, bf16[176,2048]{1,0:T(8,128)(2,1)S(1)}, u32[]{:S(2)}, u32[]{:S(2)}) collective-permute-start(bf16[176,2048]{1,0:T(8,128)(2,1)S(1)} %copy-done.38), channel_id=1, source_target_pairs={{0,2},{1,3},{2,0},{3,1},{4,6},{5,7},{6,4},{7,5},{8,10},{9,11},{10,... | collective-permute-start | bytes 2162696 | tf_op jit(solution)/shard_map/ppermute | solution.py:170
  232.7 24.3 %collective-permute-start.27 = (bf16[2,176,2048]{2,1,0:T(8,128)(2,1)}, bf16[2,176,2048]{2,1,0:T(8,128)(2,1)}, u32[]{:S(2)}, u32[]{:S(2)}) collective-permute-start(bf16[2,176,2048]{2,1,0:T(8,128)(2,1)} %maximum_select_fusion.1), channel_id=1, source_target_pairs={{0,1},{1,0},{2,3},{3,2},{4,5},{5,4},{6,7},{7,6},{8,9},{9,8},{10,11... | collective-permute-start | bytes 4325384 | tf_op jit(solution)/shard_map/ppermute | solution.py:174
  246.1 346.2 %reduce-scatter.6.cloned.1.call-start = ((), (), s32[]{:S(2)}) async-start(), calls=%async_computation.11 | async-start | bytes 14417920 | tf_op jit(solution)/shard_map/reduce_scatter | solution.py:269
  254.9 28.9 %collective-permute-start.21 = (bf16[128,2048]{1,0:T(8,128)(2,1)S(1)}, bf16[128,2048]{1,0:T(8,128)(2,1)S(1)}, u32[]{:S(2)}, u32[]{:S(2)}) collective-permute-start(bf16[128,2048]{1,0:T(8,128)(2,1)S(1)} %collective-permute-done.19), channel_id=1, source_target_pairs={{8,0},{16,8},{24,16},{28,24},{20,28},{12,20},{4,12},{0,4},{9,1},{1... | collective-permute-start | bytes 1572872 | tf_op jit(solution)/shard_map/ppermute | solution.py:98
  255.1 29.4 %collective-permute-start.20 = (bf16[128,2048]{1,0:T(8,128)(2,1)}, bf16[128,2048]{1,0:T(8,128)(2,1)S(1)}, u32[]{:S(2)}, u32[]{:S(2)}) collective-permute-start(bf16[128,2048]{1,0:T(8,128)(2,1)} %collective-permute-done.18), channel_id=1, source_target_pairs={{0,8},{8,16},{16,24},{24,28},{28,20},{20,12},{12,4},{4,0},{1,9},{9... | collective-permute-start | bytes 1572872 | tf_op jit(solution)/shard_map/ppermute | solution.py:97
  283.8 17.3 %collective-permute-start.23 = (bf16[128,2048]{1,0:T(8,128)(2,1)S(1)}, bf16[128,2048]{1,0:T(8,128)(2,1)S(1)}, u32[]{:S(2)}, u32[]{:S(2)}) collective-permute-start(bf16[128,2048]{1,0:T(8,128)(2,1)S(1)} %collective-permute-done.21), channel_id=1, source_target_pairs={{8,0},{16,8},{24,16},{28,24},{20,28},{12,20},{4,12},{0,4},{9,1},{1... | collective-permute-start | bytes 1572872 | tf_op jit(solution)/shard_map/ppermute | solution.py:98
  284.4 19.4 %collective-permute-start.22 = (bf16[128,2048]{1,0:T(8,128)(2,1)S(1)}, bf16[128,2048]{1,0:T(8,128)(2,1)S(1)}, u32[]{:S(2)}, u32[]{:S(2)}) collective-permute-start(bf16[128,2048]{1,0:T(8,128)(2,1)S(1)} %collective-permute-done.20), channel_id=1, source_target_pairs={{0,8},{8,16},{16,24},{24,28},{28,20},{20,12},{12,4},{4,0},{1,9},{9... | collective-permute-start | bytes 1572872 | tf_op jit(solution)/shard_map/ppermute | solution.py:97
  301.2 20.8 %collective-permute-start.25 = (bf16[64,2048]{1,0:T(8,128)(2,1)S(1)}, bf16[64,2048]{1,0:T(8,128)(2,1)S(1)}, u32[]{:S(2)}, u32[]{:S(2)}) collective-permute-start(bf16[64,2048]{1,0:T(8,128)(2,1)S(1)} %slice.618), channel_id=1, source_target_pairs={{8,0},{16,8},{24,16},{28,24},{20,28},{12,20},{4,12},{0,4},{9,1},{1... | collective-permute-start | bytes 786440 | tf_op jit(solution)/shard_map/ppermute | solution.py:102
  303.9 17.4 %collective-permute-start.24 = (bf16[64,2048]{1,0:T(8,128)(2,1)S(1)}, bf16[64,2048]{1,0:T(8,128)(2,1)S(1)}, u32[]{:S(2)}, u32[]{:S(2)}) collective-permute-start(bf16[64,2048]{1,0:T(8,128)(2,1)S(1)} %slice.617), channel_id=1, source_target_pairs={{0,8},{8,16},{16,24},{24,28},{28,20},{20,12},{12,4},{4,0},{1,9},{9... | collective-permute-start | bytes 786440 | tf_op jit(solution)/shard_map/ppermute | solution.py:101
  485.9 19.2 %collective-permute-start.36 = (bf16[64,2048]{1,0:T(8,128)(2,1)S(1)}, bf16[64,2048]{1,0:T(8,128)(2,1)S(1)}, u32[]{:S(2)}, u32[]{:S(2)}) collective-permute-start(bf16[64,2048]{1,0:T(8,128)(2,1)S(1)} %get-tuple-element.163), channel_id=1, source_target_pairs={{0,8},{8,16},{16,24},{24,28},{28,20},{20,12},{12,4},{4,0},{1,9},{9... | collective-permute-start | bytes 786440 | tf_op jit(solution)/shard_map/ppermute | solution.py:131
  486.0 19.1 %collective-permute-start.40 = (bf16[64,2048]{1,0:T(8,128)(2,1)S(1)}, bf16[64,2048]{1,0:T(8,128)(2,1)}, u32[]{:S(2)}, u32[]{:S(2)}) collective-permute-start(bf16[64,2048]{1,0:T(8,128)(2,1)S(1)} %get-tuple-element.164), channel_id=1, source_target_pairs={{8,0},{16,8},{24,16},{28,24},{20,28},{12,20},{4,12},{0,4},{9,1},{1... | collective-permute-start | bytes 786440 | tf_op jit(solution)/shard_map/ppermute | solution.py:132
  499.8 30.9 %all-to-all-start.2 = ((f32[8,2,128]{2,1,0:T(2,128)}), f32[8,2,128]{2,1,0:T(2,128)}, u32[]{:S(2)}, u32[]{:S(2)}) async-start(f32[8,2,128]{2,1,0:T(2,128)} %pad_maximum_fusion.16), calls=%async_computation.2 | async-start | bytes 16384 | tf_op jit(solution)/shard_map/all_to_all | solution.py:433
  505.1 181.1 %reduce-scatter.14.cloned.1.call-start = ((), (), s32[]{:S(2)}) async-start(), calls=%async_computation.15 | async-start | bytes 1310720 | tf_op jit(solution)/shard_map/reduce_scatter | solution.py:269
  592.2 186.0 %reduce-scatter.10.cloned.1.call-start = ((), (), s32[]{:S(2)}) async-start(), calls=%async_computation.13 | async-start | bytes 3604480 | tf_op jit(solution)/shard_map/reduce_scatter | solution.py:269
  593.0 185.3 %reduce-scatter.12.cloned.1.call-start = ((), (), s32[]{:S(2)}) async-start(), calls=%async_computation.14 | async-start | bytes 7208960 | tf_op jit(solution)/shard_map/reduce_scatter | solution.py:269
  593.7 195.7 %reduce-scatter.8.cloned.1.call-start = ((), (), s32[]{:S(2)}) async-start(), calls=%async_computation.12 | async-start | bytes 7208960 | tf_op jit(solution)/shard_map/reduce_scatter | solution.py:421
  675.9 43.3 %collective-permute-start.62 = (bf16[8,80,768]{2,1,0:T(8,128)(2,1)}, bf16[8,80,768]{2,1,0:T(8,128)(2,1)}, u32[]{:S(2)}, u32[]{:S(2)}) collective-permute-start(bf16[8,80,768]{2,1,0:T(8,128)(2,1)} %fusion.49), channel_id=1, source_target_pairs={{0,2},{1,3},{2,0},{3,1},{4,6},{5,7},{6,4},{7,5},{8,10},{9,11},{10,... | collective-permute-start | bytes 2949128 | tf_op jit(solution)/shard_map/ppermute | solution.py:190
  683.4 43.8 %collective-permute-start.57 = (bf16[128,2048]{1,0:T(8,128)(2,1)}, bf16[128,2048]{1,0:T(8,128)(2,1)}, u32[]{:S(2)}, u32[]{:S(2)}) collective-permute-start(bf16[128,2048]{1,0:T(8,128)(2,1)} %pad_maximum_fusion.15), channel_id=1, source_target_pairs={{8,0},{16,8},{24,16},{28,24},{20,28},{12,20},{4,12},{0,4},{9,1},{1... | collective-permute-start | bytes 1572872 | tf_op jit(solution)/shard_map/ppermute | solution.py:141
  684.8 42.5 %collective-permute-start.53 = (bf16[128,2048]{1,0:T(8,128)(2,1)}, bf16[128,2048]{1,0:T(8,128)(2,1)}, u32[]{:S(2)}, u32[]{:S(2)}) collective-permute-start(bf16[128,2048]{1,0:T(8,128)(2,1)} %pad_maximum_fusion.14), channel_id=1, source_target_pairs={{0,8},{8,16},{16,24},{24,28},{28,20},{20,12},{12,4},{4,0},{1,9},{9... | collective-permute-start | bytes 1572872 | tf_op jit(solution)/shard_map/ppermute | solution.py:140
  722.0 43.3 %all-to-all-start.3 = ((bf16[8,80,768]{2,1,0:T(8,128)(2,1)}), bf16[8,80,768]{2,1,0:T(8,128)(2,1)S(1)}, u32[]{:S(2)}, u32[]{:S(2)}) async-start(bf16[8,80,768]{2,1,0:T(8,128)(2,1)} %fusion.51), calls=%async_computation.7 | async-start | bytes 1966080 | tf_op jit(solution)/shard_map/all_to_all | solution.py:513
  729.3 29.0 %collective-permute-start.54 = (bf16[128,2048]{1,0:T(8,128)(2,1)S(1)}, bf16[128,2048]{1,0:T(8,128)(2,1)S(1)}, u32[]{:S(2)}, u32[]{:S(2)}) collective-permute-start(bf16[128,2048]{1,0:T(8,128)(2,1)S(1)} %get-tuple-element.149), channel_id=1, source_target_pairs={{0,8},{8,16},{16,24},{24,28},{28,20},{20,12},{12,4},{4,0},{1,9},{9... | collective-permute-start | bytes 1572872 | tf_op jit(solution)/shard_map/ppermute | solution.py:140
  730.8 29.9 %collective-permute-start.58 = (bf16[128,2048]{1,0:T(8,128)(2,1)S(1)}, bf16[128,2048]{1,0:T(8,128)(2,1)S(1)}, u32[]{:S(2)}, u32[]{:S(2)}) collective-permute-start(bf16[128,2048]{1,0:T(8,128)(2,1)S(1)} %get-tuple-element.150), channel_id=1, source_target_pairs={{8,0},{16,8},{24,16},{28,24},{20,28},{12,20},{4,12},{0,4},{9,1},{1... | collective-permute-start | bytes 1572872 | tf_op jit(solution)/shard_map/ppermute | solution.py:141
  763.3 45.2 %collective-permute-start.55 = (bf16[128,2048]{1,0:T(8,128)(2,1)}, bf16[128,2048]{1,0:T(8,128)(2,1)S(1)}, u32[]{:S(2)}, u32[]{:S(2)}) collective-permute-start(bf16[128,2048]{1,0:T(8,128)(2,1)} %get-tuple-element.147), channel_id=1, source_target_pairs={{0,8},{8,16},{16,24},{24,28},{28,20},{20,12},{12,4},{4,0},{1,9},{9... | collective-permute-start | bytes 1572872 | tf_op jit(solution)/shard_map/ppermute | solution.py:140
  763.3 45.1 %collective-permute-start.59 = (bf16[128,2048]{1,0:T(8,128)(2,1)}, bf16[128,2048]{1,0:T(8,128)(2,1)}, u32[]{:S(2)}, u32[]{:S(2)}) collective-permute-start(bf16[128,2048]{1,0:T(8,128)(2,1)} %get-tuple-element.148), channel_id=1, source_target_pairs={{8,0},{16,8},{24,16},{28,24},{20,28},{12,20},{4,12},{0,4},{9,1},{1... | collective-permute-start | bytes 1572872 | tf_op jit(solution)/shard_map/ppermute | solution.py:141
  789.4 37.5 %all-to-all-start.4 = ((bf16[8,64,1408]{2,1,0:T(8,128)(2,1)}), bf16[8,64,1408]{2,1,0:T(8,128)(2,1)S(1)}, u32[]{:S(2)}, u32[]{:S(2)}) async-start(bf16[8,64,1408]{2,1,0:T(8,128)(2,1)} %bitcast.449), calls=%async_computation.9 | async-start | bytes 2883584 | tf_op jit(solution)/shard_map/all_to_all | solution.py:481
  (127 other events, 1358.0 us)
Sparse Core Ops, SparseCore 0:
  9.6 44.5 all-gather.11
  55.7 32.9 all-gather.13
  90.3 81.7 all-gather.17
  174.1 45.8 all-gather.15
  246.2 89.6 all-gather.9
  415.9 99.0 reduce-scatter.5
  592.3 24.1 reduce-scatter.13
  619.8 36.3 reduce-scatter.9
  658.7 74.0 reduce-scatter.11
  735.3 54.0 reduce-scatter.7

commit v7 on v6

--- a/solution.py
+++ b/solution.py
@@ -164,10 +164,11 @@
     return lax.optimization_barrier((value,) + deps)
 
 
-def fsdp_gather(shard, size):
+def fsdp_gather(shard, size, hold):
     index = lax.axis_index("fsdp")
     rows, width = shard.shape
     far = lax.ppermute(shard, "fsdp", other_chip(size))
+    far, hold = after(far, hold)
     pair = jnp.where(
         index < 2, jnp.stack([shard, far], axis=0), jnp.stack([far, shard], axis=0)
     )
@@ -175,20 +176,7 @@
     out = jnp.zeros((2, 2, rows, width), shard.dtype)
     out = lax.dynamic_update_index_in_dim(out, pair, index % 2, 1)
     out = lax.dynamic_update_index_in_dim(out, near, 1 - index % 2, 1)
-    return out.reshape(size * rows, width)
-
-
-def fsdp_scatter(grad, size, axis):
-    index = lax.axis_index("fsdp")
-
-    def pick(peer):
-        return lax.dynamic_index_in_dim(grad, peer, axis, keepdims=False)
-
-    far_near = lax.ppermute(pick(index ^ 3), "fsdp", other_core(size))
-    near = lax.ppermute(pick(index ^ 1), "fsdp", other_core(size))
-    far = (pick(index ^ 2).astype(jnp.float32) + far_near.astype(jnp.float32)).astype(jnp.bfloat16)
-    far = lax.ppermute(far, "fsdp", other_chip(size))
-    return pick(index).astype(jnp.float32) + near.astype(jnp.float32) + far.astype(jnp.float32)
+    return (out.reshape(size * rows, width), hold)
 
 
 def column_pieces(weight, groups, size, extra):
@@ -293,7 +281,9 @@
     ).reshape(ctx_size, token_count, top_count)
 
     expert_in = lax.all_gather(w_expert_in[0], "fsdp", axis=0, tiled=True)
-    out_weight = fsdp_gather(w_out, fsdp_size)
+    grad_rows = lax.all_gather(
+        cotangent.reshape(token_count, width), "ctx", axis=0, tiled=True
+    )
 
     block_ids = jnp.arange(ctx_size, dtype=i32)[:, None]
     local_index = jnp.arange(block_len, dtype=i32)[None, :]
@@ -319,10 +309,9 @@
         projected[:, own_width : 2 * own_width].reshape(head_shape), cos_tab, sine_tab
     ).astype(bf16)
     values = projected[:, 2 * own_width :].reshape(head_shape).astype(bf16)
-    queries, in_shard, out_shard = after(queries, w_shared_in, w_shared_out)
+    queries, in_shard = after(queries, w_shared_in)
     shared_in = column_pieces(in_shard, 2, ctx_size, None)
-    shared_in = lax.all_gather(shared_in, "fsdp", axis=0, tiled=False)
-    shared_out = fsdp_gather(out_shard, fsdp_size)
+    out_weight, queries = fsdp_gather(w_out, fsdp_size, queries)
     allowed = (positions[None, :] <= positions[:, None]) & (seg_rows[None, :] == seg_rows[:, None])
     scores = jnp.einsum("qhd,khd->hqk", queries, keys, preferred_element_type=f32) * score_scale
     scores = jnp.where(allowed[None], scores, MASK_FILL)
@@ -332,8 +321,9 @@
     weights_low = weights.astype(bf16)
     attended = jnp.einsum("hqk,khd->qhd", weights_low, values, preferred_element_type=f32)
     attn_own = attended.astype(bf16).reshape(seq_len, own_width)
-    attn_own, grad_block = after(attn_own, cotangent.reshape(token_count, width))
-    grad_rows = lax.all_gather(grad_block, "ctx", axis=0, tiled=True)
+    shared_in, attn_own = after(shared_in, attn_own)
+    shared_in = lax.all_gather(shared_in, "fsdp", axis=0, tiled=False)
+    shared_out, attn_own = fsdp_gather(w_shared_out, fsdp_size, attn_own)
     attn_parts = dot(attn_own, out_weight).astype(bf16)
     own_tokens = tokens.reshape(token_count, width).astype(f32)
     own_residual = own_tokens + ring_scatter(attn_parts, ctx_size, ctx_index)
@@ -370,6 +360,7 @@
         return spread.reshape(seq_len, width)
 
     buffer = to_slots(blocks_two).astype(bf16)
+    buffer, grad_rows = after(buffer, grad_rows)
     expert_pre = dot(buffer, expert_in)
     expert_hid = swiglu(expert_pre, FE).astype(bf16)
     expert_res = dot(expert_hid, expert_out).astype(bf16)
@@ -414,9 +405,6 @@
     grad_two, grad_shared_in, grad_shared_out, grad_expert_out = after(
         grad_two, grad_shared_in.astype(bf16), grad_shared_out.astype(bf16), grad_expert_out
     )
-    sum_expert_in, grad_shared_in, grad_shared_out = after(
-        sum_expert_in, grad_shared_in, grad_shared_out
-    )
     sum_shared_in = grad_shared_in.reshape(ctx_size, fsdp_size, shard, 2 * fs_own)
     sum_shared_in = lax.psum_scatter(
         sum_shared_in.transpose(1, 0, 2, 3).reshape(width, 2 * fs_own),
@@ -425,7 +413,6 @@
         tiled=True,
     ).reshape(ctx_size, shard, 2 * fs_own)
     sum_shared_out = sum_rows(grad_shared_out)
-    sum_expert_in, grad_expert_out = after(sum_expert_in, grad_expert_out)
     sum_expert_out = sum_rows(grad_expert_out)
     output = (own_residual + out_sum).astype(bf16).reshape(tokens.shape)
 
@@ -451,10 +438,10 @@
     )
     grad_resid = cotangent.reshape(token_count, width).astype(f32) + grad_resid_norm
 
-    grad_mixed = grad_resid.astype(bf16)
+    grad_mixed, sum_expert_in = after(grad_resid.astype(bf16), sum_expert_in)
     mixed_all = ring_gather(grad_mixed, ctx_size, ctx_index)
     grad_attn = dot_t(mixed_all, out_weight).astype(bf16).reshape(head_shape)
-    grad_attn, sum_expert_in = after(grad_attn, sum_expert_in)
+    grad_attn, sum_shared_in, sum_shared_out = after(grad_attn, sum_shared_in, sum_shared_out)
     grad_weights = jnp.einsum("qhd,khd->hqk", grad_attn, values, preferred_element_type=f32)
     delta = jnp.sum(weights * grad_weights, axis=-1, keepdims=True)
     grad_scores = jnp.where(allowed[None], weights * (grad_weights - delta), 0.0).astype(bf16)
@@ -471,13 +458,12 @@
         ],
         axis=-1,
     ).astype(bf16)
+    grad_projected, sum_expert_out = after(grad_projected, sum_expert_out)
     one_sums = dot_t(grad_projected, qkv_weight)
     grad_gain_one = jnp.sum(one_sums * inputs * inv_one_all, axis=0)
     one_parts = one_sums.astype(bf16)
     one_kept, grad_projected = after(one_parts, grad_projected)
-    one_kept, sum_shared_in, sum_shared_out, sum_expert_out = after(
-        one_kept, sum_shared_in, sum_shared_out, sum_expert_out
-    )
+    one_kept, sum_shared_in = after(one_kept, sum_shared_in)
     sum_shared_in = lax.all_to_all(
         sum_shared_in, "ctx", split_axis=0, concat_axis=0, tiled=True
     )
@@ -509,7 +495,9 @@
         ],
         axis=2,
     )
-    pieces = fsdp_scatter(pieces, fsdp_size, 1).astype(bf16)
+    pieces = pieces.transpose(1, 0, 2, 3).reshape(-1, 3 * own_width)
+    pieces = lax.psum_scatter(pieces, "fsdp", scatter_dimension=0, tiled=True)
+    pieces = pieces.reshape(ctx_size, shard + more, 3 * own_width)
     pieces = lax.all_to_all(pieces, "ctx", split_axis=0, concat_axis=0, tiled=True)
     small_grads = jnp.sum(pieces[:, shard:].reshape(ctx_size, -1).astype(f32), axis=0)
     return (

time: 847 us -> 836 us (0.987)
  starting transfers between devices: 92.8 us -> 83.6 us
    all_to_all x1, waiting for transfers between devices: 13.4 us -> 51.3 us  [column_pieces(): lax.all_to_all(pieces, 'ctx', split_axis=0, concat_axis=0, tiled=True)]
    ppermute x3 -> x0, waiting for transfers between devices: 31.1 us -> none  [the longest x1 31.1 us: fsdp_scatter(): far = lax.ppermute(far, 'fsdp', other_chip(size))]
    ppermute x9, waiting for transfers between devices: 47.2 us -> 19.4 us  [ring_walk(): fore = lax.ppermute(fore, 'ctx', ahead)]
    ppermute x12, waiting for transfers between devices: 57 us -> 72.3 us  [ring_sums(): fore = lax.ppermute(fore, 'ctx', ahead)]
    ppermute x2, waiting for transfers between devices: 15.3 us -> 0.01 us  [fsdp_gather(): far = lax.ppermute(shard, 'fsdp', other_chip(size))]
    reduce_scatter x1, waiting for transfers between devices: 11.1 us -> 24.9 us  [local_split(): lax.psum_scatter(sum_shared_in.transpose(1, 0, 2, 3).reshape(width, 2 * f...]
    ppermute x4, waiting for transfers between devices: 10.9 us -> 23.2 us  [ring_sums(): fore = lax.ppermute(low(own(half, 0, cut)), 'ctx', ahead)]
    all_to_all x1, waiting for transfers between devices: 11.4 us -> 0.01 us  [local_split(): lax.all_to_all(sum_shared_in, 'ctx', split_axis=0, concat_axis=0, tiled=T...]
  transfers between devices with their start and end apart: 77 -> 75, of which waited for: 45 -> 51; matrix products, arithmetic and copies ran while one was open for 39% -> 34% of each run, Pallas kernels for 0% -> 0%
where the time goes in v7:
time: 836 us; the launch traced here: 825 us
  waiting for transfers between devices  299 us (36%)
  matrix products  198 us (24%)
  local copies, waits for them, and re-layouts  101 us (12%)
  other arithmetic  93.5 us (11%)
  starting transfers between devices  83.6 us (10%)
  blocking collectives  29.9 us (4%)
  between operations  20.4 us (2%)
    ppermute x12, waiting for transfers between devices, ring_sums(): fore = lax.ppermute(fore, 'ctx', ahead)  72.3 us
    all_to_all x1, waiting for transfers between devices, column_pieces(): lax.all_to_all(pieces, 'ctx', split_axis=0, concat_axis=0, tiled=True)  51.3 us
    dot_general x8, matrix products, dot(): return jnp.dot(a, b, preferred_element_type=f32)  47 us
    dot_general x7, matrix products, dot_t(): lax.dot_general(a, b, (((1,), (1,)), ((), ())), preferred_element_type=f32)  46.3 us
    dot_general x8, matrix products, t_dot(): lax.dot_general(a, b, (((0,), (0,)), ((), ())), preferred_element_type=f32)  41.2 us
    ppermute x9, waiting for transfers between devices, ring_walk(): rear = lax.ppermute(rear, 'ctx', back)  38.9 us
    unnamed x202, local copies, waits for them, and re-layouts  36.3 us
    all_to_all x1, blocking collectives, column_pieces(): lax.all_to_all(pieces, 'ctx', split_axis=0, concat_axis=0, tiled=True)  29.9 us
  transfers between devices with their start and end apart: 75, of which 51 were waited for; matrix products, arithmetic and copies ran while one was open for 34% of the time, Pallas kernels for 0%

profile of v7, /device:TPU:8, one launch (start us, length us, event | category | flops | bytes accessed | tf_op | source)
XLA Modules:
  0.0 824.9 jit_solution(16281109184581357768)
XLA Ops:
  15.4 29.9 %all_to_all.25 = bf16[8,80,768]{2,1,0:T(8,128)(2,1)} all-to-all(bf16[8,80,768]{2,1,0:T(8,128)(2,1)S(1)} %pad_maximum_fusion.6), channel_id=1, replica_groups=mesh['ctx'=8,'fsdp'=4] {'ctx'}, dimensions={0} | all-to-all | bytes 1966080 | tf_op jit(solution)/shard_map/all_to_all | solution.py:195
  45.2 8.9 %all-gather.12.cloned.1.call-done = bf16[1,1408,2048]{2,1,0:T(8,128)(2,1)} async-done(((bf16[1,352,2048]{2,1,0:T(8,128)(2,1)}), bf16[1,1408,2048]{2,1,0:T(8,128)(2,1)}) %all-gather.12.cloned.1.call-update) | async-done | bytes 5767184 | tf_op jit(solution)/shard_map/all_gather | solution.py:265
  87.4 8.4 %collective-permute-done.5 = bf16[128,2048]{1,0:T(8,128)(2,1)S(1)} collective-permute-done((bf16[128,2048]{1,0:T(8,128)(2,1)}, bf16[128,2048]{1,0:T(8,128)(2,1)S(1)}, u32[]{:S(2)}, u32[]{:S(2)}) %collective-permute-start.5) | collective-permute-done | bytes 524320 | tf_op jit(solution)/shard_map/ppermute | solution.py:97
  113.9 6.9 convolution_add_fusion
  149.5 51.3 %all-to-all-done.1 = bf16[8,64,1408]{2,1,0:T(8,128)(2,1)S(1)} async-done(((bf16[8,64,1408]{2,1,0:T(8,128)(2,1)}), bf16[8,64,1408]{2,1,0:T(8,128)(2,1)S(1)}, u32[]{:S(2)}, u32[]{:S(2)}) %all-to-all-start.1) | async-done | bytes 1441824 | tf_op jit(solution)/shard_map/all_to_all | solution.py:195
  220.1 11.0 %collective-permute-done.16 = bf16[128,2048]{1,0:T(8,128)(2,1)S(1)} collective-permute-done((bf16[128,2048]{1,0:T(8,128)(2,1)S(1)}, bf16[128,2048]{1,0:T(8,128)(2,1)S(1)}, u32[]{:S(2)}, u32[]{:S(2)}) %collective-permute-start.16) | collective-permute-done | bytes 524320 | tf_op jit(solution)/shard_map/ppermute | solution.py:141
  234.9 10.2 %collective-permute-done.13 = bf16[128,2048]{1,0:T(8,128)(2,1)S(1)} collective-permute-done((bf16[128,2048]{1,0:T(8,128)(2,1)S(1)}, bf16[128,2048]{1,0:T(8,128)(2,1)S(1)}, u32[]{:S(2)}, u32[]{:S(2)}) %collective-permute-start.13) | collective-permute-done | bytes 524320 | tf_op jit(solution)/shard_map/ppermute | solution.py:140
  281.9 7.9 collective-permute-done.22
  294.9 7.0 collective-permute-done.24
  319.2 9.7 %fusion.3 = f32[512,2816]{1,0:T(8,128)S(1)} fusion(bf16[512,2048]{1,0:T(8,128)(2,1)S(1)} %bitcast.417, bf16[1,2048,2816]{2,1,0:T(8,128)(2,1)} %all-gather.18.cloned.1.call-done), kind=kOutput, calls=%fused_computation.6 | convolution fusion | flops 5905580032 | bytes 19398656 | tf_op jit(solution)/shard_map/dot_general | solution.py:243
  329.7 7.9 convolution_convert_fusion.7
  345.3 10.0 %fusion.132 = f32[1024,1408]{1,0:T(8,128)S(1)} fusion(bf16[1024,2048]{1,0:T(8,128)(2,1)} %constant_dynamic-update-slice_fusion.31, bf16[2048,1408]{1,0:T(8,128)(2,1)S(1)} %bitcast.389), kind=kOutput, calls=%fused_computation.370 | convolution fusion | flops 5905580032 | bytes 15728640 | tf_op jit(solution)/shard_map/dot_general | solution.py:243
  371.0 9.0 %multiply_convert_fusion.4 = (bf16[512,1408]{1,0:T(8,128)(2,1)S(1)}, bf16[512,1408]{1,0:T(8,128)(2,1)S(1)}) fusion(f32[512,2816]{1,0:T(8,128)} %copy-done.14, bf16[512,2048]{1,0:T(8,128)(2,1)S(1)} %fusion.26, bf16[1408,2048]{1,0:T(8,128)(2,1)} %bitcast.452), kind=kOutput, calls=%fused_computation.66 | convolution fusion | flops 2962161664 | bytes 16515072 | tf_op jit(solution)/shard_map/dot_general | solution.py:246
  381.6 8.9 %convolution_convert_fusion = bf16[2048,2816]{1,0:T(8,128)(2,1)} fusion(bf16[512,2048]{1,0:T(8,128)(2,1)S(1)} %bitcast.418, bf16[512,1408]{1,0:T(8,128)(2,1)S(1)} %get-tuple-element.147, bf16[512,1408]{1,0:T(8,128)(2,1)S(1)} %get-tuple-element.146), kind=kOutput, calls=%fused_computation.8 | convolution fusion | flops 5917114368 | bytes 16515072 | tf_op jit(solution)/shard_map/dot_general | solution.py:249
  390.5 11.8 %fusion.6 = (f32[1024]{0:T(1024)S(1)}, bf16[1024,2048]{1,0:T(8,128)(2,1)}, bf16[1024,2048]{1,0:T(8,128)(2,1)}) fusion(f32[1024,2048]{1,0:T(8,128)} %fusion.133, bf16[1024,2048]{1,0:T(8,128)(2,1)} %all-gather.10.cloned.1.call-done, f32[8,128,2048]{2,1,0:T(8,128)} %fusion.77, f32[1024]{0:T(1024)S(1)} %bitcast.441, f32[1024]{0:T(1024)S(1)} %bitcast.445), kind=kLoop, calls=%fused_computation.12 | loop fusion | flops 18873344 | bytes 29372416 | tf_op jit(solution)/shard_map/reduce_sum | solution.py:397
  405.9 7.1 collective-permute-done.28
  417.5 11.7 %fusion.46 = bf16[512,2048]{1,0:T(8,128)(2,1)} fusion(bf16[1,2048,2816]{2,1,0:T(8,128)(2,1)} %all-gather.18.cloned.1.call-done, bf16[512,1408]{1,0:T(8,128)(2,1)S(1)} %copy-done.81, bf16[512,1408]{1,0:T(8,128)(2,1)S(1)} %copy-done.79), kind=kOutput, calls=%fused_computation.59 | convolution fusion | flops 5912395776 | bytes 16515072 | tf_op jit(solution)/shard_map/dot_general | solution.py:246
  437.2 7.2 collective-permute-done.30
  457.8 8.4 %fusion.12 = bf16[1024,2048]{1,0:T(8,128)(2,1)S(1)} fusion(f32[8,128,2048]{2,1,0:T(8,128)S(1)} %fusion.76, bf16[1024,1408]{1,0:T(8,128)(2,1)} %pad_maximum_fusion.2, bf16[2048,1408]{1,0:T(8,128)(2,1)S(1)} %bitcast.392), kind=kOutput, calls=%fused_computation.19 | convolution fusion | flops 5909774336 | bytes 21233664 | tf_op jit(solution)/shard_map/dot_general | solution.py:246
  476.0 10.8 %convolution_convert_fusion.2 = bf16[2048,1408]{1,0:T(8,128)(2,1)} fusion(bf16[1024,2048]{1,0:T(8,128)(2,1)} %constant_dynamic-update-slice_fusion.31, bf16[1024,1408]{1,0:T(8,128)(2,1)S(1)} %copy-done.31), kind=kOutput, calls=%fused_computation.30 | convolution fusion | flops 5908463616 | bytes 12845056 | tf_op jit(solution)/shard_map/dot_general | solution.py:249
  497.0 7.6 collective-permute-done.38
  509.6 7.7 convolution_convert_fusion.1
  543.5 9.4 %collective-permute-done.45 = bf16[128,2048]{1,0:T(8,128)(2,1)} collective-permute-done((bf16[128,2048]{1,0:T(8,128)(2,1)}, bf16[128,2048]{1,0:T(8,128)(2,1)}, u32[]{:S(2)}, u32[]{:S(2)}) %collective-permute-start.45) | collective-permute-done | bytes 524320 | tf_op jit(solution)/shard_map/ppermute | solution.py:98
  587.1 24.9 %reduce-scatter.9.cloned.1.call-done = bf16[512,1408]{1,0:T(8,128)(2,1)} async-done(((bf16[2048,1408]{1,0:T(8,128)(2,1)}), bf16[512,1408]{1,0:T(8,128)(2,1)}) %reduce-scatter.9.cloned.1.call-update) | async-done | bytes 1441808 | tf_op jit(solution)/shard_map/reduce_scatter | solution.py:409
  617.7 18.4 %fusion.53 = f32[1024,2,128]{0,2,1:T(8,128)} fusion(bf16[1024,2,128]{0,2,1:T(8,128)(2,1)} %get-tuple-element.51, f32[2,1024,1024]{1,2,0:T(8,128)} %fusion.135, f32[2,1024,1024]{1,2,0:T(8,128)} %copy-done.8, f32[2,1024]{1,0:T(2,128)S(1)} %copy-done.72, pred[1024,1024]{0,1:T(8,128)(4,1)} %compare_and_fusion), kind=kOutput, calls=%fused_computation.83 | convolution fusion | flops 559942656 | bytes 19406848 | tf_op jit(solution)/shard_map/hqk,qhd->khd/dot_general | solution.py:450
  636.0 16.9 %broadcast_multiply_fusion.1 = (f32[1024,2,128]{0,2,1:T(8,128)}, f32[1024,2,128]{0,2,1:T(8,128)}, f32[1024,2,128]{0,2,1:T(8,128)}) fusion(f32[1024,128]{0,1:T(8,128)} %get-tuple-element.235, f32[1024,2,128]{0,2,1:T(8,128)} %fusion.53, bf16[1024,2,128]{0,2,1:T(8,128)(2,1)S(1)} %copy-done.58, f32[2,1024,1024]{1,2,0:T(8,128)} %fusion.135, ...), kind=kOutput, calls=%fused_computation.160 | convolution fusion | flops 560466944 | bytes 23076864 | tf_op jit(solution)/shard_map/hqk,khd->qhd/dot_general | solution.py:448
  656.6 6.0 convolution_convert_fusion.10
  669.4 10.5 %fusion.11 = (bf16[2048]{0:T(1024)(128)(2,1)S(1)}, bf16[1024,2048]{1,0:T(8,128)(2,1)}) fusion(bf16[1024,2048]{1,0:T(8,128)(2,1)} %copy-done.5, f32[1024]{0:T(1024)S(1)} %copy-done.77, bf16[1024,768]{0,1:T(8,128)(2,1)} %pad_maximum_fusion.5, bf16[2048,768]{1,0:T(8,128)(2,1)} %bitcast.406), kind=kOutput, calls=%fused_computation.17 | convolution fusion | flops 3231709184 | bytes 13115392 | tf_op jit(solution)/shard_map/dot_general | solution.py:246
  693.9 6.0 collective-permute-done.52
  711.4 7.0 collective-permute-done.57
  736.3 22.0 %collective-permute-done.54 = bf16[128,2048]{1,0:T(8,128)(2,1)} collective-permute-done((bf16[128,2048]{1,0:T(8,128)(2,1)}, bf16[128,2048]{1,0:T(8,128)(2,1)}, u32[]{:S(2)}, u32[]{:S(2)}) %collective-permute-start.54) | collective-permute-done | bytes 524320 | tf_op jit(solution)/shard_map/ppermute | solution.py:140
  771.9 9.0 %collective-permute-done.55 = bf16[128,2048]{1,0:T(8,128)(2,1)} collective-permute-done((bf16[128,2048]{1,0:T(8,128)(2,1)}, bf16[128,2048]{1,0:T(8,128)(2,1)}, u32[]{:S(2)}, u32[]{:S(2)}) %collective-permute-start.55) | collective-permute-done | bytes 524320 | tf_op jit(solution)/shard_map/ppermute | solution.py:140
  (563 shorter events, 415.3 us)
Async XLA Ops:
  7.2 47.0 %all-gather.12.cloned.1.call-start = ((), (), s32[]{:S(2)}) async-start(), calls=%async_computation.18 | async-start | bytes 7208960 | tf_op jit(solution)/shard_map/all_gather | solution.py:265
  7.9 99.1 %all-gather.14.cloned.1.call-start = ((), (), s32[]{:S(2)}) async-start(), calls=%async_computation.19 | async-start | bytes 4915200 | tf_op jit(solution)/shard_map/all_gather | solution.py:268
  54.2 260.1 %all-gather.10.cloned.1.call-start = ((), (), s32[]{:S(2)}) async-start(), calls=%async_computation.11 | async-start | bytes 4718592 | tf_op jit(solution)/shard_map/all_gather | solution.py:284
  54.9 264.2 %all-gather.18.cloned.1.call-start = ((), (), s32[]{:S(2)}) async-start(), calls=%async_computation.21 | async-start | bytes 14417920 | tf_op jit(solution)/shard_map/all_gather | solution.py:283
  55.5 14.1 %collective-permute-start.1 = (bf16[128,2048]{1,0:T(8,128)(2,1)S(1)}, bf16[128,2048]{1,0:T(8,128)(2,1)S(1)}, u32[]{:S(2)}, u32[]{:S(2)}) collective-permute-start(bf16[128,2048]{1,0:T(8,128)(2,1)S(1)} %bitcast.382), channel_id=1, source_target_pairs={{0,8},{8,16},{16,24},{24,28},{28,20},{20,12},{12,4},{4,0},{1,9},{9... | collective-permute-start | bytes 1572872 | tf_op jit(solution)/shard_map/ppermute | solution.py:97
  57.1 14.1 %collective-permute-start.2 = (bf16[128,2048]{1,0:T(8,128)(2,1)S(1)}, bf16[128,2048]{1,0:T(8,128)(2,1)S(1)}, u32[]{:S(2)}, u32[]{:S(2)}) collective-permute-start(bf16[128,2048]{1,0:T(8,128)(2,1)S(1)} %bitcast.383), channel_id=1, source_target_pairs={{8,0},{16,8},{24,16},{28,24},{20,28},{12,20},{4,12},{0,4},{9,1},{1... | collective-permute-start | bytes 1572872 | tf_op jit(solution)/shard_map/ppermute | solution.py:98
  57.6 66.1 %collective-permute-start.9 = (bf16[64,2048]{1,0:T(8,128)(2,1)S(1)}, bf16[64,2048]{1,0:T(8,128)(2,1)S(1)}, u32[]{:S(2)}, u32[]{:S(2)}) collective-permute-start(bf16[64,2048]{1,0:T(8,128)(2,1)S(1)} %copy-done.48), channel_id=1, source_target_pairs={{0,2},{1,3},{2,0},{3,1},{4,6},{5,7},{6,4},{7,5},{8,10},{9,11},{10,... | collective-permute-start | bytes 786440 | tf_op jit(solution)/shard_map/ppermute | solution.py:170
  58.2 142.7 %collective-permute-start = (bf16[176,2048]{1,0:T(8,128)(2,1)}, bf16[176,2048]{1,0:T(8,128)(2,1)}, u32[]{:S(2)}, u32[]{:S(2)}) collective-permute-start(bf16[176,2048]{1,0:T(8,128)(2,1)} %param.34), channel_id=1, source_target_pairs={{0,2},{1,3},{2,0},{3,1},{4,6},{5,7},{6,4},{7,5},{8,10},{9,11},{10,... | collective-permute-start | bytes 2162696 | tf_op jit(solution)/shard_map/ppermute | solution.py:170
  124.6 23.8 %collective-permute-start.10 = (bf16[2,64,2048]{2,1,0:T(8,128)(2,1)}, bf16[2,64,2048]{2,1,0:T(8,128)(2,1)}, u32[]{:S(2)}, u32[]{:S(2)}) collective-permute-start(bf16[2,64,2048]{2,1,0:T(8,128)(2,1)} %maximum_select_fusion.3), channel_id=1, source_target_pairs={{0,1},{1,0},{2,3},{3,2},{4,5},{5,4},{6,7},{7,6},{8,9},{9,8},{10,11... | collective-permute-start | bytes 1572872 | tf_op jit(solution)/shard_map/ppermute | solution.py:175
  132.1 68.7 %all-to-all-start.1 = ((bf16[8,64,1408]{2,1,0:T(8,128)(2,1)}), bf16[8,64,1408]{2,1,0:T(8,128)(2,1)S(1)}, u32[]{:S(2)}, u32[]{:S(2)}) async-start(bf16[8,64,1408]{2,1,0:T(8,128)(2,1)} %reshape.818), calls=%async_computation.1 | async-start | bytes 2883584 | tf_op jit(solution)/shard_map/all_to_all | solution.py:195
  137.3 204.9 %all-gather.16.cloned.1.call-start = ((), (), s32[]{:S(2)}) async-start(), calls=%async_computation.20 | async-start | bytes 7208960 | tf_op jit(solution)/shard_map/all_gather | solution.py:325
  255.0 24.5 %collective-permute-start.27 = (bf16[2,176,2048]{2,1,0:T(8,128)(2,1)}, bf16[2,176,2048]{2,1,0:T(8,128)(2,1)S(1)}, u32[]{:S(2)}, u32[]{:S(2)}) collective-permute-start(bf16[2,176,2048]{2,1,0:T(8,128)(2,1)} %maximum_select_fusion.1), channel_id=1, source_target_pairs={{0,1},{1,0},{2,3},{3,2},{4,5},{5,4},{6,7},{7,6},{8,9},{9,8},{10,11... | collective-permute-start | bytes 4325384 | tf_op jit(solution)/shard_map/ppermute | solution.py:175
  255.0 285.3 %reduce-scatter.7.cloned.1.call-start = ((), (), s32[]{:S(2)}) async-start(), calls=%async_computation.12 | async-start | bytes 14417920 | tf_op jit(solution)/shard_map/reduce_scatter | solution.py:257
  402.3 184.7 %reduce-scatter.11.cloned.1.call-start = ((), (), s32[]{:S(2)}) async-start(), calls=%async_computation.14 | async-start | bytes 3604480 | tf_op jit(solution)/shard_map/reduce_scatter | solution.py:257
  415.3 13.9 %collective-permute-start.33 = (bf16[128,2048]{1,0:T(8,128)(2,1)S(1)}, bf16[128,2048]{1,0:T(8,128)(2,1)S(1)}, u32[]{:S(2)}, u32[]{:S(2)}) collective-permute-start(bf16[128,2048]{1,0:T(8,128)(2,1)S(1)} %pad_maximum_fusion.12), channel_id=1, source_target_pairs={{8,0},{16,8},{24,16},{28,24},{20,28},{12,20},{4,12},{0,4},{9,1},{1... | collective-permute-start | bytes 1572872 | tf_op jit(solution)/shard_map/ppermute | solution.py:141
  430.4 14.0 %collective-permute-start.30 = (bf16[128,2048]{1,0:T(8,128)(2,1)S(1)}, bf16[128,2048]{1,0:T(8,128)(2,1)S(1)}, u32[]{:S(2)}, u32[]{:S(2)}) collective-permute-start(bf16[128,2048]{1,0:T(8,128)(2,1)S(1)} %get-tuple-element.175), channel_id=1, source_target_pairs={{0,8},{8,16},{16,24},{24,28},{28,20},{20,12},{12,4},{4,0},{1,9},{9... | collective-permute-start | bytes 1572872 | tf_op jit(solution)/shard_map/ppermute | solution.py:140
  430.9 14.3 %collective-permute-start.34 = (bf16[128,2048]{1,0:T(8,128)(2,1)S(1)}, bf16[128,2048]{1,0:T(8,128)(2,1)S(1)}, u32[]{:S(2)}, u32[]{:S(2)}) collective-permute-start(bf16[128,2048]{1,0:T(8,128)(2,1)S(1)} %get-tuple-element.176), channel_id=1, source_target_pairs={{8,0},{16,8},{24,16},{28,24},{20,28},{12,20},{4,12},{0,4},{9,1},{1... | collective-permute-start | bytes 1572872 | tf_op jit(solution)/shard_map/ppermute | solution.py:141
  475.1 14.0 %collective-permute-start.37 = (bf16[128,2048]{1,0:T(8,128)(2,1)S(1)}, bf16[128,2048]{1,0:T(8,128)(2,1)S(1)}, u32[]{:S(2)}, u32[]{:S(2)}) collective-permute-start(bf16[128,2048]{1,0:T(8,128)(2,1)S(1)} %pad_maximum_fusion.13), channel_id=1, source_target_pairs={{0,8},{8,16},{16,24},{24,28},{28,20},{20,12},{12,4},{4,0},{1,9},{9... | collective-permute-start | bytes 1572872 | tf_op jit(solution)/shard_map/ppermute | solution.py:140
  490.5 14.2 %collective-permute-start.38 = (bf16[128,2048]{1,0:T(8,128)(2,1)}, bf16[128,2048]{1,0:T(8,128)(2,1)}, u32[]{:S(2)}, u32[]{:S(2)}) collective-permute-start(bf16[128,2048]{1,0:T(8,128)(2,1)} %get-tuple-element.165), channel_id=1, source_target_pairs={{0,8},{8,16},{16,24},{24,28},{28,20},{20,12},{12,4},{4,0},{1,9},{9... | collective-permute-start | bytes 1572872 | tf_op jit(solution)/shard_map/ppermute | solution.py:140
  491.6 14.0 %collective-permute-start.42 = (bf16[128,2048]{1,0:T(8,128)(2,1)}, bf16[128,2048]{1,0:T(8,128)(2,1)}, u32[]{:S(2)}, u32[]{:S(2)}) collective-permute-start(bf16[128,2048]{1,0:T(8,128)(2,1)} %get-tuple-element.166), channel_id=1, source_target_pairs={{8,0},{16,8},{24,16},{28,24},{20,28},{12,20},{4,12},{0,4},{9,1},{1... | collective-permute-start | bytes 1572872 | tf_op jit(solution)/shard_map/ppermute | solution.py:141
  519.9 92.0 %reduce-scatter.9.cloned.1.call-start = ((), (), s32[]{:S(2)}) async-start(), calls=%async_computation.13 | async-start | bytes 7208960 | tf_op jit(solution)/shard_map/reduce_scatter | solution.py:409
  525.7 143.6 %reduce-scatter.13.cloned.1.call-start = ((), (), s32[]{:S(2)}) async-start(), calls=%async_computation.15 | async-start | bytes 7208960 | tf_op jit(solution)/shard_map/reduce_scatter | solution.py:257
  531.8 231.8 %reduce-scatter.15.cloned.1.call-start = ((), (), s32[]{:S(2)}) async-start(), calls=%async_computation.16 | async-start | bytes 4915200 | tf_op jit(solution)/shard_map/reduce_scatter | solution.py:499
  703.2 15.2 %collective-permute-start.57 = (bf16[128,2048]{1,0:T(8,128)(2,1)}, bf16[128,2048]{1,0:T(8,128)(2,1)}, u32[]{:S(2)}, u32[]{:S(2)}) collective-permute-start(bf16[128,2048]{1,0:T(8,128)(2,1)} %pad_maximum_fusion.16), channel_id=1, source_target_pairs={{8,0},{16,8},{24,16},{28,24},{20,28},{12,20},{4,12},{0,4},{9,1},{1... | collective-permute-start | bytes 1572872 | tf_op jit(solution)/shard_map/ppermute | solution.py:141
  704.6 18.8 %collective-permute-start.53 = (bf16[128,2048]{1,0:T(8,128)(2,1)}, bf16[128,2048]{1,0:T(8,128)(2,1)S(1)}, u32[]{:S(2)}, u32[]{:S(2)}) collective-permute-start(bf16[128,2048]{1,0:T(8,128)(2,1)} %pad_maximum_fusion.15), channel_id=1, source_target_pairs={{0,8},{8,16},{16,24},{24,28},{28,20},{20,12},{12,4},{4,0},{1,9},{9... | collective-permute-start | bytes 1572872 | tf_op jit(solution)/shard_map/ppermute | solution.py:140
  706.0 57.6 %all-to-all-start.4 = ((bf16[8,64,1408]{2,1,0:T(8,128)(2,1)}), bf16[8,64,1408]{2,1,0:T(8,128)(2,1)}, u32[]{:S(2)}, u32[]{:S(2)}) async-start(bf16[8,64,1408]{2,1,0:T(8,128)(2,1)} %bitcast.421), calls=%async_computation.10 | async-start | bytes 2883584 | tf_op jit(solution)/shard_map/all_to_all | solution.py:467
  711.3 77.7 %reduce-scatter.17.cloned.1.call-start = ((), (), s32[]{:S(2)}) async-start(), calls=%async_computation.17 | async-start | bytes 1310720 | tf_op jit(solution)/shard_map/reduce_scatter | solution.py:257
  726.1 32.1 %collective-permute-start.54 = (bf16[128,2048]{1,0:T(8,128)(2,1)}, bf16[128,2048]{1,0:T(8,128)(2,1)}, u32[]{:S(2)}, u32[]{:S(2)}) collective-permute-start(bf16[128,2048]{1,0:T(8,128)(2,1)} %get-tuple-element.155), channel_id=1, source_target_pairs={{0,8},{8,16},{16,24},{24,28},{28,20},{20,12},{12,4},{4,0},{1,9},{9... | collective-permute-start | bytes 1572872 | tf_op jit(solution)/shard_map/ppermute | solution.py:140
  729.0 29.2 %collective-permute-start.58 = (bf16[128,2048]{1,0:T(8,128)(2,1)}, bf16[128,2048]{1,0:T(8,128)(2,1)}, u32[]{:S(2)}, u32[]{:S(2)}) collective-permute-start(bf16[128,2048]{1,0:T(8,128)(2,1)} %get-tuple-element.156), channel_id=1, source_target_pairs={{8,0},{16,8},{24,16},{28,24},{20,28},{12,20},{4,12},{0,4},{9,1},{1... | collective-permute-start | bytes 1572872 | tf_op jit(solution)/shard_map/ppermute | solution.py:141
  761.2 19.7 %collective-permute-start.55 = (bf16[128,2048]{1,0:T(8,128)(2,1)}, bf16[128,2048]{1,0:T(8,128)(2,1)}, u32[]{:S(2)}, u32[]{:S(2)}) collective-permute-start(bf16[128,2048]{1,0:T(8,128)(2,1)} %get-tuple-element.153), channel_id=1, source_target_pairs={{0,8},{8,16},{16,24},{24,28},{28,20},{20,12},{12,4},{4,0},{1,9},{9... | collective-permute-start | bytes 1572872 | tf_op jit(solution)/shard_map/ppermute | solution.py:140
  763.6 20.1 %collective-permute-start.59 = (bf16[128,2048]{1,0:T(8,128)(2,1)}, bf16[128,2048]{1,0:T(8,128)(2,1)}, u32[]{:S(2)}, u32[]{:S(2)}) collective-permute-start(bf16[128,2048]{1,0:T(8,128)(2,1)} %get-tuple-element.154), channel_id=1, source_target_pairs={{8,0},{16,8},{24,16},{28,24},{20,28},{12,20},{4,12},{0,4},{9,1},{1... | collective-permute-start | bytes 1572872 | tf_op jit(solution)/shard_map/ppermute | solution.py:141
  763.6 31.8 %all-to-all-start.3 = ((bf16[8,80,768]{2,1,0:T(8,128)(2,1)}), bf16[8,80,768]{2,1,0:T(8,128)(2,1)}, u32[]{:S(2)}, u32[]{:S(2)}) async-start(bf16[8,80,768]{2,1,0:T(8,128)(2,1)} %bitcast.432), calls=%async_computation.8 | async-start | bytes 1966080 | tf_op jit(solution)/shard_map/all_to_all | solution.py:501
  (129 other events, 1414.7 us)
Sparse Core Ops, SparseCore 0:
  9.6 44.5 all-gather.11
  55.7 47.8 all-gather.13
  105.8 96.4 all-gather.9
  203.7 77.7 all-gather.17
  283.5 43.3 all-gather.15
  402.4 91.4 reduce-scatter.6
  520.1 34.1 reduce-scatter.10
  557.0 54.8 reduce-scatter.8
  614.5 54.8 reduce-scatter.12
  690.7 42.8 reduce-scatter.14
  736.7 25.1 reduce-scatter.16

commit v8 on v7

--- a/solution.py
+++ b/solution.py
@@ -321,8 +321,6 @@
     weights_low = weights.astype(bf16)
     attended = jnp.einsum("hqk,khd->qhd", weights_low, values, preferred_element_type=f32)
     attn_own = attended.astype(bf16).reshape(seq_len, own_width)
-    shared_in, attn_own = after(shared_in, attn_own)
-    shared_in = lax.all_gather(shared_in, "fsdp", axis=0, tiled=False)
     shared_out, attn_own = fsdp_gather(w_shared_out, fsdp_size, attn_own)
     attn_parts = dot(attn_own, out_weight).astype(bf16)
     own_tokens = tokens.reshape(token_count, width).astype(f32)
@@ -330,6 +328,8 @@
 
     normed_two, inv_two = rms_norm(own_residual, ffn_gain)
     own_low = normed_two.astype(bf16)
+    shared_in, own_low = after(shared_in, own_low)
+    shared_in = lax.all_gather(shared_in, "fsdp", axis=0, tiled=False)
     low_two = ring_gather(own_low, ctx_size, ctx_index)
     mixed_weight = jnp.concatenate([router_weight, gate_vector[:, None]], axis=1)
     logits = dot(low_two, mixed_weight)
@@ -366,44 +366,41 @@
     expert_res = dot(expert_hid, expert_out).astype(bf16)
     routed = gate_all[:, None] * to_tokens(expert_res)
 
-    shared_in, expert_res = after(shared_in, expert_res)
-    shared_in = shared_in.transpose(1, 0, 2, 3).reshape(width, 2 * fs_own)
-    shared_pre = dot(low_two, shared_in)
-    shared_hid = swiglu(shared_pre, fs_own).astype(bf16)
-    shared_res = dot(shared_hid, shared_out)
-    grad_rows, shared_res = after(grad_rows, shared_res)
-    out_parts = (scale_all[:, None] * shared_res + routed).astype(bf16)
-    out_sum = ring_scatter(out_parts, ctx_size, ctx_index)
-
     grad_slots = to_slots(grad_rows.reshape(ctx_size, token_count, width))
     gate_slots = jnp.sum(jnp.where(slot_mask, gate_blocks[:, None, :], 0.0), axis=-1).reshape(-1, 1)
     grad_res = (gate_slots * grad_slots).astype(bf16)
     slot_dots = jnp.sum(grad_slots * expert_res.astype(f32), axis=-1).reshape(ctx_size, capacity, 1)
     grad_gates = jnp.sum(jnp.where(slot_mask, slot_dots, 0.0), axis=1)
-    grad_expert_out = t_dot(expert_hid, grad_res)
     grad_hid = dot_t(grad_res, expert_out)
     grad_pre = swiglu_back(expert_pre, FE, grad_hid).astype(bf16)
+    grad_pre, shared_in = after(grad_pre, shared_in)
     grad_expert_in = t_dot(buffer, grad_pre)
     grad_buffer = dot_t(grad_pre, expert_in).astype(bf16)
 
-    grad_expert_out = grad_expert_out.astype(bf16)
-    grad_expert_in, grad_shared_res = after(
-        grad_expert_in.astype(bf16),
-        (scale_all[:, None] * grad_rows.astype(f32)).astype(bf16),
-    )
+    grad_expert_in, low_shared = after(grad_expert_in.astype(bf16), low_two)
     sum_expert_in = sum_rows(grad_expert_in)
+
+    shared_in = shared_in.transpose(1, 0, 2, 3).reshape(width, 2 * fs_own)
+    shared_pre = dot(low_shared, shared_in)
+    shared_hid = swiglu(shared_pre, fs_own).astype(bf16)
+    shared_res = dot(shared_hid, shared_out)
+    out_parts = (scale_all[:, None] * shared_res + routed).astype(bf16)
 
     grad_f32 = grad_rows.astype(f32)
     gate_dots = jnp.sum(grad_f32 * shared_res, axis=-1).reshape(ctx_size, token_count)
-    grad_shared_out = t_dot(shared_hid, grad_shared_res)
+    grad_shared_res = (scale_all[:, None] * grad_f32).astype(bf16)
     grad_shared_hid = dot_t(grad_shared_res, shared_out)
     grad_shared_pre = swiglu_back(shared_pre, fs_own, grad_shared_hid).astype(bf16)
-    grad_shared_in = t_dot(low_two, grad_shared_pre)
-    grad_shared_pre, out_sum = after(grad_shared_pre, out_sum)
     two_parts = (dot_t(grad_shared_pre, shared_in) + to_tokens(grad_buffer)).astype(bf16)
+    two_parts, expert_hid, shared_hid, grad_shared_pre = after(
+        two_parts, expert_hid, shared_hid, grad_shared_pre
+    )
+    grad_expert_out = t_dot(expert_hid, grad_res).astype(bf16)
+    grad_shared_out = t_dot(shared_hid, grad_shared_res).astype(bf16)
+    grad_shared_in = t_dot(low_two, grad_shared_pre).astype(bf16)
     grad_two = ring_scatter(two_parts, ctx_size, ctx_index)
     grad_two, grad_shared_in, grad_shared_out, grad_expert_out = after(
-        grad_two, grad_shared_in.astype(bf16), grad_shared_out.astype(bf16), grad_expert_out
+        grad_two, grad_shared_in, grad_shared_out, grad_expert_out
     )
     sum_shared_in = grad_shared_in.reshape(ctx_size, fsdp_size, shard, 2 * fs_own)
     sum_shared_in = lax.psum_scatter(
@@ -414,8 +411,6 @@
     ).reshape(ctx_size, shard, 2 * fs_own)
     sum_shared_out = sum_rows(grad_shared_out)
     sum_expert_out = sum_rows(grad_expert_out)
-    output = (own_residual + out_sum).astype(bf16).reshape(tokens.shape)
-
     dots = jnp.stack([grad_gates, gate_dots], axis=1)
     dots = lax.all_to_all(dots, "ctx", split_axis=0, concat_axis=0, tiled=True)
     own_probs = own_rows(probs_all)
@@ -442,6 +437,9 @@
     mixed_all = ring_gather(grad_mixed, ctx_size, ctx_index)
     grad_attn = dot_t(mixed_all, out_weight).astype(bf16).reshape(head_shape)
     grad_attn, sum_shared_in, sum_shared_out = after(grad_attn, sum_shared_in, sum_shared_out)
+    sum_shared_in = lax.all_to_all(
+        sum_shared_in, "ctx", split_axis=0, concat_axis=0, tiled=True
+    )
     grad_weights = jnp.einsum("qhd,khd->hqk", grad_attn, values, preferred_element_type=f32)
     delta = jnp.sum(weights * grad_weights, axis=-1, keepdims=True)
     grad_scores = jnp.where(allowed[None], weights * (grad_weights - delta), 0.0).astype(bf16)
@@ -458,15 +456,16 @@
         ],
         axis=-1,
     ).astype(bf16)
-    grad_projected, sum_expert_out = after(grad_projected, sum_expert_out)
+    grad_projected, sum_expert_out, sum_shared_in = after(
+        grad_projected, sum_expert_out, sum_shared_in
+    )
     one_sums = dot_t(grad_projected, qkv_weight)
     grad_gain_one = jnp.sum(one_sums * inputs * inv_one_all, axis=0)
     one_parts = one_sums.astype(bf16)
     one_kept, grad_projected = after(one_parts, grad_projected)
-    one_kept, sum_shared_in = after(one_kept, sum_shared_in)
-    sum_shared_in = lax.all_to_all(
-        sum_shared_in, "ctx", split_axis=0, concat_axis=0, tiled=True
-    )
+    one_kept, out_parts = after(one_kept, out_parts)
+    output = own_residual + ring_scatter(out_parts, ctx_size, ctx_index)
+    output = output.astype(bf16).reshape(tokens.shape)
     grad_normed = ring_scatter(one_parts, ctx_size, ctx_index, one_kept)
     grad_inputs_norm, unused = rms_back(
         own_tokens,

time: 836 us -> 812 us (0.971)
  waiting for transfers between devices: 299 us -> 270 us
  local copies, waits for them, and re-layouts: 101 us -> 122 us
  other arithmetic: 93.5 us -> 82.4 us
    all_to_all x1, waiting for transfers between devices: 51.3 us -> 0.01 us  [column_pieces(): lax.all_to_all(pieces, 'ctx', split_axis=0, concat_axis=0, tiled=True)]
    ppermute x12, waiting for transfers between devices: 26.5 us -> 49.3 us  [ring_sums(): rear = lax.ppermute(rear, 'ctx', back)]
    reduce_scatter x1, waiting for transfers between devices: 24.9 us -> 7.72 us  [local_split(): lax.psum_scatter(sum_shared_in.transpose(1, 0, 2, 3).reshape(width, 2 * f...]
    unnamed x202 -> x218, local copies, waits for them, and re-layouts: 36.3 us -> 51.1 us
    reduce_sum x2 -> x0, other arithmetic: 12.3 us -> none  [the longest x1 11.8 us: local_split(): jnp.sum(grad_f32 * shared_res, axis=-1).reshape(ctx_size, token_count)]
    ppermute x9, waiting for transfers between devices: 38.9 us -> 47.9 us  [ring_walk(): rear = lax.ppermute(rear, 'ctx', back)]
    convert_element_type x12 -> x11, other arithmetic: 17.4 us -> 24.7 us  [low(): return values.astype(jnp.bfloat16)]
  transfers between devices with their start and end apart: 75 -> 75, of which waited for: 51 -> 43; matrix products, arithmetic and copies ran while one was open for 34% -> 42% of each run, Pallas kernels for 0% -> 0%
where the time goes in v8:
time: 812 us; the launch traced here: 802 us
  waiting for transfers between devices  270 us (33%)
  matrix products  194 us (24%)
  local copies, waits for them, and re-layouts  122 us (15%)
  other arithmetic  82.4 us (10%)
  starting transfers between devices  81.8 us (10%)
  blocking collectives  29.9 us (4%)
  between operations  20.8 us (3%)
    ppermute x12, waiting for transfers between devices, ring_sums(): fore = lax.ppermute(fore, 'ctx', ahead)  78.2 us
    unnamed x218, local copies, waits for them, and re-layouts  51.1 us
    dot_general x7, matrix products, dot_t(): lax.dot_general(a, b, (((1,), (1,)), ((), ())), preferred_element_type=f32)  49.4 us
    ppermute x12, waiting for transfers between devices, ring_sums(): rear = lax.ppermute(rear, 'ctx', back)  49.3 us
    ppermute x9, waiting for transfers between devices, ring_walk(): rear = lax.ppermute(rear, 'ctx', back)  47.9 us
    dot_general x8, matrix products, dot(): return jnp.dot(a, b, preferred_element_type=f32)  44.8 us
    dot_general x8, matrix products, t_dot(): lax.dot_general(a, b, (((0,), (0,)), ((), ())), preferred_element_type=f32)  40 us
    all_to_all x1, blocking collectives, column_pieces(): lax.all_to_all(pieces, 'ctx', split_axis=0, concat_axis=0, tiled=True)  29.9 us
  transfers between devices with their start and end apart: 75, of which 43 were waited for; matrix products, arithmetic and copies ran while one was open for 42% of the time, Pallas kernels for 0%

profile of v8, /device:TPU:8, one launch (start us, length us, event | category | flops | bytes accessed | tf_op | source)
XLA Modules:
  0.0 801.6 jit_solution(16194038261832768408)
XLA Ops:
  15.4 29.9 %all_to_all.25 = bf16[8,80,768]{2,1,0:T(8,128)(2,1)} all-to-all(bf16[8,80,768]{2,1,0:T(8,128)(2,1)S(1)} %pad_maximum_fusion.4), channel_id=1, replica_groups=mesh['ctx'=8,'fsdp'=4] {'ctx'}, dimensions={0} | all-to-all | bytes 1966080 | tf_op jit(solution)/shard_map/all_to_all | solution.py:195
  45.2 8.9 %all-gather.12.cloned.1.call-done = bf16[1,1408,2048]{2,1,0:T(8,128)(2,1)} async-done(((bf16[1,352,2048]{2,1,0:T(8,128)(2,1)}), bf16[1,1408,2048]{2,1,0:T(8,128)(2,1)}) %all-gather.12.cloned.1.call-update) | async-done | bytes 5767184 | tf_op jit(solution)/shard_map/all_gather | solution.py:265
  88.6 7.3 collective-permute-done.5
  118.7 6.8 convolution_add_fusion
  142.3 17.0 %collective-permute-done.11 = bf16[64,2048]{1,0:T(8,128)(2,1)S(1)} collective-permute-done((bf16[64,2048]{1,0:T(8,128)(2,1)}, bf16[64,2048]{1,0:T(8,128)(2,1)S(1)}, u32[]{:S(2)}, u32[]{:S(2)}) %collective-permute-start.11) | collective-permute-done | bytes 262176 | tf_op jit(solution)/shard_map/ppermute | solution.py:131
  165.2 26.9 %collective-permute-done.16 = bf16[128,2048]{1,0:T(8,128)(2,1)S(1)} collective-permute-done((bf16[128,2048]{1,0:T(8,128)(2,1)S(1)}, bf16[128,2048]{1,0:T(8,128)(2,1)S(1)}, u32[]{:S(2)}, u32[]{:S(2)}) %collective-permute-start.16) | collective-permute-done | bytes 524320 | tf_op jit(solution)/shard_map/ppermute | solution.py:141
  214.1 36.6 %collective-permute-done.14 = bf16[128,2048]{1,0:T(8,128)(2,1)S(1)} collective-permute-done((bf16[128,2048]{1,0:T(8,128)(2,1)}, bf16[128,2048]{1,0:T(8,128)(2,1)S(1)}, u32[]{:S(2)}, u32[]{:S(2)}) %collective-permute-start.14) | collective-permute-done | bytes 524320 | tf_op jit(solution)/shard_map/ppermute | solution.py:140
  259.7 8.3 %collective-permute-done.20 = bf16[128,2048]{1,0:T(8,128)(2,1)S(1)} collective-permute-done((bf16[128,2048]{1,0:T(8,128)(2,1)S(1)}, bf16[128,2048]{1,0:T(8,128)(2,1)S(1)}, u32[]{:S(2)}, u32[]{:S(2)}) %collective-permute-start.20) | collective-permute-done | bytes 524320 | tf_op jit(solution)/shard_map/ppermute | solution.py:98
  274.0 7.4 collective-permute-done.22
  285.9 8.0 %collective-permute-done.24 = bf16[128,2048]{1,0:T(8,128)(2,1)S(1)} collective-permute-done((bf16[128,2048]{1,0:T(8,128)(2,1)}, bf16[128,2048]{1,0:T(8,128)(2,1)S(1)}, u32[]{:S(2)}, u32[]{:S(2)}) %collective-permute-start.24) | collective-permute-done | bytes 524320 | tf_op jit(solution)/shard_map/ppermute | solution.py:98
  309.2 9.9 %fusion.3 = f32[512,2816]{1,0:T(8,128)S(1)} fusion(bf16[512,2048]{1,0:T(8,128)(2,1)S(1)} %bitcast.419, bf16[1,2048,2816]{2,1,0:T(8,128)(2,1)} %all-gather.16.cloned.1.call-done), kind=kOutput, calls=%fused_computation.6 | convolution fusion | flops 5905580032 | bytes 19398656 | tf_op jit(solution)/shard_map/dot_general | solution.py:243
  323.3 8.0 %fusion.27 = (f32[512]{0:T(512)S(1)}, bf16[512,2048]{1,0:T(8,128)(2,1)}) fusion(f32[8,64,2048]{2,1,0:T(8,128)S(1)} %copy-done.6, bf16[512,1408]{1,0:T(8,128)(2,1)S(1)} %multiply_convert_fusion.1, bf16[1408,2048]{1,0:T(8,128)(2,1)} %bitcast.455), kind=kOutput, calls=%fused_computation.38 | convolution fusion | flops 2956983808 | bytes 13502464 | tf_op jit(solution)/shard_map/dot_general | solution.py:243
  339.7 7.5 multiply_convert_fusion.5
  347.5 12.0 %convolution_convert_fusion = bf16[2048,2816]{1,0:T(8,128)(2,1)} fusion(bf16[512,2048]{1,0:T(8,128)(2,1)} %bitcast.420, bf16[512,2816]{1,0:T(8,128)(2,1)S(1)} %pad_maximum_fusion.1), kind=kOutput, calls=%fused_computation.8 | convolution fusion | flops 5911347200 | bytes 16515072 | tf_op jit(solution)/shard_map/dot_general | solution.py:249
  371.1 8.1 %fusion.136 = f32[1024,1408]{0,1:T(8,128)} fusion(bf16[1024,2048]{1,0:T(8,128)(2,1)S(1)} %copy-done.1, bf16[2048,1408]{1,0:T(8,128)(2,1)S(1)} %bitcast.388), kind=kOutput, calls=%fused_computation.371 | convolution fusion | flops 5905580032 | bytes 15728640 | tf_op jit(solution)/shard_map/dot_general | solution.py:243
  379.3 7.8 multiply_convert_fusion.3
  390.2 9.0 %fusion.46 = bf16[512,2048]{1,0:T(8,128)(2,1)S(1)} fusion(bf16[512,2816]{1,0:T(8,128)(2,1)S(1)} %copy-done.32, bf16[1,2048,2816]{2,1,0:T(8,128)(2,1)} %all-gather.16.cloned.1.call-done), kind=kOutput, calls=%fused_computation.55 | convolution fusion | flops 5906628608 | bytes 16515072 | tf_op jit(solution)/shard_map/dot_general | solution.py:246
  400.5 11.7 %fusion.14 = bf16[1024,2048]{1,0:T(8,128)(2,1)} fusion(f32[8,128,2048]{2,1,0:T(8,128)S(1)} %fusion.82, bf16[2048,1408]{1,0:T(8,128)(2,1)} %bitcast.389, bf16[1024,704]{0,1:T(8,128)(2,1)} %copy-done.54, bf16[1024,704]{0,1:T(8,128)(2,1)} %copy-done.53), kind=kOutput, calls=%fused_computation.22 | convolution fusion | flops 5915541504 | bytes 21233664 | tf_op jit(solution)/shard_map/dot_general | solution.py:246
  415.6 6.3 collective-permute-done.28
  426.7 8.5 %convolution_convert_fusion.2 = bf16[2048,1408]{1,0:T(8,128)(2,1)} fusion(bf16[1024,2048]{1,0:T(8,128)(2,1)S(1)} %copy-done.1, bf16[1024,1408]{0,1:T(8,128)(2,1)S(1)} %pad_maximum_fusion.2), kind=kOutput, calls=%fused_computation.30 | convolution fusion | flops 5908463616 | bytes 12845056 | tf_op jit(solution)/shard_map/dot_general | solution.py:249
  483.5 7.2 fusion.13
  508.0 10.9 %collective-permute-done.37 = bf16[128,2048]{1,0:T(8,128)(2,1)} collective-permute-done((bf16[128,2048]{1,0:T(8,128)(2,1)}, bf16[128,2048]{1,0:T(8,128)(2,1)}, u32[]{:S(2)}, u32[]{:S(2)}) %collective-permute-start.37) | collective-permute-done | bytes 524320 | tf_op jit(solution)/shard_map/ppermute | solution.py:98
  526.4 7.3 collective-permute-done.39
  557.5 7.7 reduce-scatter.9.cloned.1.call-done
  571.5 7.0 fusion.138
  580.8 16.4 %fusion.56 = f32[1024,2,128]{0,2,1:T(8,128)} fusion(bf16[1024,2,128]{0,2,1:T(8,128)(2,1)} %copy-done.65, f32[2,1024,1024]{1,2,0:T(8,128)} %fusion.138, f32[2,1024,1024]{1,2,0:T(8,128)} %copy-done.7, f32[2,1024]{1,0:T(2,128)S(1)} %copy-done.82, pred[1024,1024]{0,1:T(8,128)(4,1)} %copy-done.21), kind=kOutput, calls=%fused_computation.84 | convolution fusion | flops 559942656 | bytes 19406848 | tf_op jit(solution)/shard_map/hqk,qhd->khd/dot_general | solution.py:448
  597.3 16.9 %broadcast_multiply_fusion.1 = (f32[1024,2,128]{0,2,1:T(8,128)}, f32[1024,2,128]{0,2,1:T(8,128)}, f32[1024,2,128]{0,2,1:T(8,128)}) fusion(f32[1024,128]{0,1:T(8,128)} %get-tuple-element.235, f32[1024,2,128]{0,2,1:T(8,128)} %fusion.56, bf16[1024,2,128]{0,2,1:T(8,128)(2,1)} %copy-done.64, f32[2,1024,1024]{1,2,0:T(8,128)} %fusion.138, ...), kind=kOutput, calls=%fused_computation.164 | convolution fusion | flops 560466944 | bytes 23076864 | tf_op jit(solution)/shard_map/hqk,khd->qhd/dot_general | solution.py:446
  625.1 11.0 %fusion.11 = (bf16[2048]{0:T(1024)(128)(2,1)}, bf16[1024,2048]{1,0:T(8,128)(2,1)}) fusion(bf16[1024,2048]{1,0:T(8,128)(2,1)} %copy-done.5, f32[1024]{0:T(1024)} %copy-done.86, bf16[1024,768]{0,1:T(8,128)(2,1)} %pad_maximum_fusion.3, bf16[2048,768]{1,0:T(8,128)(2,1)} %bitcast.403), kind=kOutput, calls=%fused_computation.17 | convolution fusion | flops 3231709184 | bytes 13115392 | tf_op jit(solution)/shard_map/dot_general | solution.py:246
  644.9 6.8 convolution_convert_fusion.4
  694.9 6.3 collective-permute-done.57
  707.2 11.2 %collective-permute-done.54 = bf16[128,2048]{1,0:T(8,128)(2,1)S(1)} collective-permute-done((bf16[128,2048]{1,0:T(8,128)(2,1)S(1)}, bf16[128,2048]{1,0:T(8,128)(2,1)S(1)}, u32[]{:S(2)}, u32[]{:S(2)}) %collective-permute-start.54) | collective-permute-done | bytes 524320 | tf_op jit(solution)/shard_map/ppermute | solution.py:140
  747.4 18.1 %collective-permute-done.47 = bf16[128,2048]{1,0:T(8,128)(2,1)} collective-permute-done((bf16[128,2048]{1,0:T(8,128)(2,1)}, bf16[128,2048]{1,0:T(8,128)(2,1)}, u32[]{:S(2)}, u32[]{:S(2)}) %collective-permute-start.47) | collective-permute-done | bytes 524320 | tf_op jit(solution)/shard_map/ppermute | solution.py:140
  (577 shorter events, 407.8 us)
Async XLA Ops:
  7.2 47.0 %all-gather.12.cloned.1.call-start = ((), (), s32[]{:S(2)}) async-start(), calls=%async_computation.18 | async-start | bytes 7208960 | tf_op jit(solution)/shard_map/all_gather | solution.py:265
  7.9 98.9 %all-gather.14.cloned.1.call-start = ((), (), s32[]{:S(2)}) async-start(), calls=%async_computation.19 | async-start | bytes 4915200 | tf_op jit(solution)/shard_map/all_gather | solution.py:268
  54.2 249.2 %all-gather.10.cloned.1.call-start = ((), (), s32[]{:S(2)}) async-start(), calls=%async_computation.11 | async-start | bytes 4718592 | tf_op jit(solution)/shard_map/all_gather | solution.py:284
  54.9 254.3 %all-gather.16.cloned.1.call-start = ((), (), s32[]{:S(2)}) async-start(), calls=%async_computation.20 | async-start | bytes 14417920 | tf_op jit(solution)/shard_map/all_gather | solution.py:283
  57.6 70.1 %collective-permute-start.9 = (bf16[64,2048]{1,0:T(8,128)(2,1)S(1)}, bf16[64,2048]{1,0:T(8,128)(2,1)S(1)}, u32[]{:S(2)}, u32[]{:S(2)}) collective-permute-start(bf16[64,2048]{1,0:T(8,128)(2,1)S(1)} %copy-done.57), channel_id=1, source_target_pairs={{0,2},{1,3},{2,0},{3,1},{4,6},{5,7},{6,4},{7,5},{8,10},{9,11},{10,... | collective-permute-start | bytes 786440 | tf_op jit(solution)/shard_map/ppermute | solution.py:170
  58.2 77.7 %collective-permute-start = (bf16[176,2048]{1,0:T(8,128)(2,1)S(1)}, bf16[176,2048]{1,0:T(8,128)(2,1)S(1)}, u32[]{:S(2)}, u32[]{:S(2)}) collective-permute-start(bf16[176,2048]{1,0:T(8,128)(2,1)S(1)} %copy-done.36), channel_id=1, source_target_pairs={{0,2},{1,3},{2,0},{3,1},{4,6},{5,7},{6,4},{7,5},{8,10},{9,11},{10,... | collective-permute-start | bytes 2162696 | tf_op jit(solution)/shard_map/ppermute | solution.py:170
  140.3 19.0 %collective-permute-start.11 = (bf16[64,2048]{1,0:T(8,128)(2,1)}, bf16[64,2048]{1,0:T(8,128)(2,1)S(1)}, u32[]{:S(2)}, u32[]{:S(2)}) collective-permute-start(bf16[64,2048]{1,0:T(8,128)(2,1)} %get-tuple-element.189), channel_id=1, source_target_pairs={{0,8},{8,16},{16,24},{24,28},{28,20},{20,12},{12,4},{4,0},{1,9},{9... | collective-permute-start | bytes 786440 | tf_op jit(solution)/shard_map/ppermute | solution.py:131
  141.8 20.0 %collective-permute-start.15 = (bf16[64,2048]{1,0:T(8,128)(2,1)S(1)}, bf16[64,2048]{1,0:T(8,128)(2,1)S(1)}, u32[]{:S(2)}, u32[]{:S(2)}) collective-permute-start(bf16[64,2048]{1,0:T(8,128)(2,1)S(1)} %get-tuple-element.190), channel_id=1, source_target_pairs={{8,0},{16,8},{24,16},{28,24},{20,28},{12,20},{4,12},{0,4},{9,1},{1... | collective-permute-start | bytes 786440 | tf_op jit(solution)/shard_map/ppermute | solution.py:132
  163.1 29.1 %collective-permute-start.16 = (bf16[128,2048]{1,0:T(8,128)(2,1)S(1)}, bf16[128,2048]{1,0:T(8,128)(2,1)S(1)}, u32[]{:S(2)}, u32[]{:S(2)}) collective-permute-start(bf16[128,2048]{1,0:T(8,128)(2,1)S(1)} %pad_maximum_fusion.8), channel_id=1, source_target_pairs={{8,0},{16,8},{24,16},{28,24},{20,28},{12,20},{4,12},{0,4},{9,1},{1... | collective-permute-start | bytes 1572872 | tf_op jit(solution)/shard_map/ppermute | solution.py:141
  164.4 27.8 %collective-permute-start.12 = (bf16[128,2048]{1,0:T(8,128)(2,1)S(1)}, bf16[128,2048]{1,0:T(8,128)(2,1)S(1)}, u32[]{:S(2)}, u32[]{:S(2)}) collective-permute-start(bf16[128,2048]{1,0:T(8,128)(2,1)S(1)} %pad_maximum_fusion.7), channel_id=1, source_target_pairs={{0,8},{8,16},{16,24},{24,28},{28,20},{20,12},{12,4},{4,0},{1,9},{9... | collective-permute-start | bytes 1572872 | tf_op jit(solution)/shard_map/ppermute | solution.py:140
  204.4 51.2 %all-to-all-start.1 = ((bf16[8,64,1408]{2,1,0:T(8,128)(2,1)}), bf16[8,64,1408]{2,1,0:T(8,128)(2,1)S(1)}, u32[]{:S(2)}, u32[]{:S(2)}) async-start(bf16[8,64,1408]{2,1,0:T(8,128)(2,1)} %reshape.821), calls=%async_computation.1 | async-start | bytes 2883584 | tf_op jit(solution)/shard_map/all_to_all | solution.py:195
  209.3 138.2 %all-gather.18.cloned.1.call-start = ((), (), s32[]{:S(2)}) async-start(), calls=%async_computation.21 | async-start | bytes 7208960 | tf_op jit(solution)/shard_map/all_gather | solution.py:332
  212.0 38.7 %collective-permute-start.14 = (bf16[128,2048]{1,0:T(8,128)(2,1)}, bf16[128,2048]{1,0:T(8,128)(2,1)S(1)}, u32[]{:S(2)}, u32[]{:S(2)}) collective-permute-start(bf16[128,2048]{1,0:T(8,128)(2,1)} %get-tuple-element.183), channel_id=1, source_target_pairs={{0,8},{8,16},{16,24},{24,28},{28,20},{20,12},{12,4},{4,0},{1,9},{9... | collective-permute-start | bytes 1572872 | tf_op jit(solution)/shard_map/ppermute | solution.py:140
  213.4 39.5 %collective-permute-start.18 = (bf16[128,2048]{1,0:T(8,128)(2,1)S(1)}, bf16[128,2048]{1,0:T(8,128)(2,1)}, u32[]{:S(2)}, u32[]{:S(2)}) collective-permute-start(bf16[128,2048]{1,0:T(8,128)(2,1)S(1)} %get-tuple-element.184), channel_id=1, source_target_pairs={{8,0},{16,8},{24,16},{28,24},{20,28},{12,20},{4,12},{0,4},{9,1},{1... | collective-permute-start | bytes 1572872 | tf_op jit(solution)/shard_map/ppermute | solution.py:141
  273.3 231.7 %reduce-scatter.7.cloned.1.call-start = ((), (), s32[]{:S(2)}) async-start(), calls=%async_computation.12 | async-start | bytes 14417920 | tf_op jit(solution)/shard_map/reduce_scatter | solution.py:257
  359.5 198.0 %reduce-scatter.11.cloned.1.call-start = ((), (), s32[]{:S(2)}) async-start(), calls=%async_computation.14 | async-start | bytes 3604480 | tf_op jit(solution)/shard_map/reduce_scatter | solution.py:257
  471.7 93.5 %reduce-scatter.9.cloned.1.call-start = ((), (), s32[]{:S(2)}) async-start(), calls=%async_computation.13 | async-start | bytes 7208960 | tf_op jit(solution)/shard_map/reduce_scatter | solution.py:406
  477.8 147.3 %reduce-scatter.13.cloned.1.call-start = ((), (), s32[]{:S(2)}) async-start(), calls=%async_computation.15 | async-start | bytes 7208960 | tf_op jit(solution)/shard_map/reduce_scatter | solution.py:257
  565.2 59.8 %all-to-all-start.3 = ((bf16[8,64,1408]{2,1,0:T(8,128)(2,1)}), bf16[8,64,1408]{2,1,0:T(8,128)(2,1)S(1)}, u32[]{:S(2)}, u32[]{:S(2)}) async-start(bf16[8,64,1408]{2,1,0:T(8,128)(2,1)} %bitcast.423), calls=%async_computation.7 | async-start | bytes 2883584 | tf_op jit(solution)/shard_map/all_to_all | solution.py:440
  571.3 112.0 %reduce-scatter.17.cloned.1.call-start = ((), (), s32[]{:S(2)}) async-start(), calls=%async_computation.17 | async-start | bytes 1310720 | tf_op jit(solution)/shard_map/reduce_scatter | solution.py:257
  580.8 144.3 %reduce-scatter.15.cloned.1.call-start = ((), (), s32[]{:S(2)}) async-start(), calls=%async_computation.16 | async-start | bytes 4915200 | tf_op jit(solution)/shard_map/reduce_scatter | solution.py:498
  676.2 25.0 %collective-permute-start.57 = (bf16[128,2048]{1,0:T(8,128)(2,1)}, bf16[128,2048]{1,0:T(8,128)(2,1)}, u32[]{:S(2)}, u32[]{:S(2)}) collective-permute-start(bf16[128,2048]{1,0:T(8,128)(2,1)} %pad_maximum_fusion.14), channel_id=1, source_target_pairs={{8,0},{16,8},{24,16},{28,24},{20,28},{12,20},{4,12},{0,4},{9,1},{1... | collective-permute-start | bytes 1572872 | tf_op jit(solution)/shard_map/ppermute | solution.py:141
  677.6 23.6 %collective-permute-start.53 = (bf16[128,2048]{1,0:T(8,128)(2,1)}, bf16[128,2048]{1,0:T(8,128)(2,1)}, u32[]{:S(2)}, u32[]{:S(2)}) collective-permute-start(bf16[128,2048]{1,0:T(8,128)(2,1)} %pad_maximum_fusion.13), channel_id=1, source_target_pairs={{0,8},{8,16},{16,24},{24,28},{28,20},{20,12},{12,4},{4,0},{1,9},{9... | collective-permute-start | bytes 1572872 | tf_op jit(solution)/shard_map/ppermute | solution.py:140
  692.9 36.8 %collective-permute-start.46 = (bf16[128,2048]{1,0:T(8,128)(2,1)}, bf16[128,2048]{1,0:T(8,128)(2,1)}, u32[]{:S(2)}, u32[]{:S(2)}) collective-permute-start(bf16[128,2048]{1,0:T(8,128)(2,1)} %get-tuple-element.165), channel_id=1, source_target_pairs={{0,8},{8,16},{16,24},{24,28},{28,20},{20,12},{12,4},{4,0},{1,9},{9... | collective-permute-start | bytes 1572872 | tf_op jit(solution)/shard_map/ppermute | solution.py:140
  694.4 35.3 %collective-permute-start.50 = (bf16[128,2048]{1,0:T(8,128)(2,1)}, bf16[128,2048]{1,0:T(8,128)(2,1)}, u32[]{:S(2)}, u32[]{:S(2)}) collective-permute-start(bf16[128,2048]{1,0:T(8,128)(2,1)} %get-tuple-element.166), channel_id=1, source_target_pairs={{8,0},{16,8},{24,16},{28,24},{20,28},{12,20},{4,12},{0,4},{9,1},{1... | collective-permute-start | bytes 1572872 | tf_op jit(solution)/shard_map/ppermute | solution.py:141
  703.2 15.2 %collective-permute-start.54 = (bf16[128,2048]{1,0:T(8,128)(2,1)S(1)}, bf16[128,2048]{1,0:T(8,128)(2,1)S(1)}, u32[]{:S(2)}, u32[]{:S(2)}) collective-permute-start(bf16[128,2048]{1,0:T(8,128)(2,1)S(1)} %get-tuple-element.155), channel_id=1, source_target_pairs={{0,8},{8,16},{16,24},{24,28},{28,20},{20,12},{12,4},{4,0},{1,9},{9... | collective-permute-start | bytes 1572872 | tf_op jit(solution)/shard_map/ppermute | solution.py:140
  704.7 15.8 %collective-permute-start.58 = (bf16[128,2048]{1,0:T(8,128)(2,1)S(1)}, bf16[128,2048]{1,0:T(8,128)(2,1)S(1)}, u32[]{:S(2)}, u32[]{:S(2)}) collective-permute-start(bf16[128,2048]{1,0:T(8,128)(2,1)S(1)} %get-tuple-element.156), channel_id=1, source_target_pairs={{8,0},{16,8},{24,16},{28,24},{20,28},{12,20},{4,12},{0,4},{9,1},{1... | collective-permute-start | bytes 1572872 | tf_op jit(solution)/shard_map/ppermute | solution.py:141
  723.0 20.2 %collective-permute-start.55 = (bf16[128,2048]{1,0:T(8,128)(2,1)}, bf16[128,2048]{1,0:T(8,128)(2,1)}, u32[]{:S(2)}, u32[]{:S(2)}) collective-permute-start(bf16[128,2048]{1,0:T(8,128)(2,1)} %get-tuple-element.153), channel_id=1, source_target_pairs={{0,8},{8,16},{16,24},{24,28},{28,20},{20,12},{12,4},{4,0},{1,9},{9... | collective-permute-start | bytes 1572872 | tf_op jit(solution)/shard_map/ppermute | solution.py:140
  724.5 21.1 %collective-permute-start.59 = (bf16[128,2048]{1,0:T(8,128)(2,1)}, bf16[128,2048]{1,0:T(8,128)(2,1)}, u32[]{:S(2)}, u32[]{:S(2)}) collective-permute-start(bf16[128,2048]{1,0:T(8,128)(2,1)} %get-tuple-element.154), channel_id=1, source_target_pairs={{8,0},{16,8},{24,16},{28,24},{20,28},{12,20},{4,12},{0,4},{9,1},{1... | collective-permute-start | bytes 1572872 | tf_op jit(solution)/shard_map/ppermute | solution.py:141
  725.0 46.8 %all-to-all-start.4 = ((bf16[8,80,768]{2,1,0:T(8,128)(2,1)}), bf16[8,80,768]{2,1,0:T(8,128)(2,1)}, u32[]{:S(2)}, u32[]{:S(2)}) async-start(bf16[8,80,768]{2,1,0:T(8,128)(2,1)} %bitcast.434), calls=%async_computation.9 | async-start | bytes 1966080 | tf_op jit(solution)/shard_map/all_to_all | solution.py:500
  732.7 32.8 %collective-permute-start.47 = (bf16[128,2048]{1,0:T(8,128)(2,1)}, bf16[128,2048]{1,0:T(8,128)(2,1)}, u32[]{:S(2)}, u32[]{:S(2)}) collective-permute-start(bf16[128,2048]{1,0:T(8,128)(2,1)} %get-tuple-element.163), channel_id=1, source_target_pairs={{0,8},{8,16},{16,24},{24,28},{28,20},{20,12},{12,4},{4,0},{1,9},{9... | collective-permute-start | bytes 1572872 | tf_op jit(solution)/shard_map/ppermute | solution.py:140
  734.2 33.5 %collective-permute-start.51 = (bf16[128,2048]{1,0:T(8,128)(2,1)}, bf16[128,2048]{1,0:T(8,128)(2,1)}, u32[]{:S(2)}, u32[]{:S(2)}) collective-permute-start(bf16[128,2048]{1,0:T(8,128)(2,1)} %get-tuple-element.164), channel_id=1, source_target_pairs={{8,0},{16,8},{24,16},{28,24},{20,28},{12,20},{4,12},{0,4},{9,1},{1... | collective-permute-start | bytes 1572872 | tf_op jit(solution)/shard_map/ppermute | solution.py:141
  (137 other events, 1696.2 us)
Sparse Core Ops, SparseCore 0:
  9.6 44.5 all-gather.11
  55.7 47.8 all-gather.13
  105.8 86.7 all-gather.9
  194.0 76.3 all-gather.15
  273.4 44.0 all-gather.17
  359.7 93.3 reduce-scatter.6
  471.8 35.7 reduce-scatter.10
  510.3 54.8 reduce-scatter.8
  567.8 54.8 reduce-scatter.12
  625.8 24.8 reduce-scatter.16
  654.5 42.9 reduce-scatter.14

commit v9 on v8

--- a/solution.py
+++ b/solution.py
@@ -86,8 +86,17 @@
     return [row[k] for k in range(size)]
 
 
-def ring_walk(block, size, ctx_index, out, put):
-    rows = block.shape[0]
+def after(value, *deps):
+    return lax.optimization_barrier((value,) + deps)
+
+
+def ring_gather(block, size, ctx_index, rider=None):
+    rows, width = block.shape
+
+    def put(out, piece, peer, offset):
+        return lax.dynamic_update_slice(out, piece, (peer * rows + offset, jnp.zeros_like(peer)))
+
+    out = jnp.zeros((size * rows, width), block.dtype)
     ahead, back = ring_steps(size)
     peers = ring_peers(size, ctx_index)
     half = size // 2
@@ -96,21 +105,15 @@
     for k in range(1, half):
         fore = lax.ppermute(fore, "ctx", ahead)
         rear = lax.ppermute(rear, "ctx", back)
+        if rider is not None and k == 2:
+            fore, rider = after(fore, rider)
         out = put(out, fore, peers[size - k], 0)
         out = put(out, rear, peers[k], 0)
     fore = lax.ppermute(fore[: rows // 2], "ctx", ahead)
     rear = lax.ppermute(rear[rows // 2 :], "ctx", back)
     out = put(out, fore, peers[half], 0)
-    return put(out, rear, peers[half], rows // 2)
-
-
-def ring_gather(block, size, ctx_index):
-    rows, width = block.shape
-
-    def put(out, piece, peer, offset):
-        return lax.dynamic_update_slice(out, piece, (peer * rows + offset, jnp.zeros_like(peer)))
-
-    return ring_walk(block, size, ctx_index, jnp.zeros((size * rows, width), block.dtype), put)
+    out = put(out, rear, peers[half], rows // 2)
+    return out if rider is None else (out, rider)
 
 
 def ring_sums(parts, size, ctx_index):
@@ -158,10 +161,6 @@
 
 def other_chip(size):
     return [(i, i ^ 2) for i in range(size)]
-
-
-def after(value, *deps):
-    return lax.optimization_barrier((value,) + deps)
 
 
 def fsdp_gather(shard, size, hold):
@@ -197,6 +196,9 @@
 
 def merge_columns(pieces, groups, size):
     width = pieces.shape[2] // groups
+    if width % 128 == 0:
+        pieces = pieces.reshape(size, -1, groups, width).transpose(1, 2, 0, 3)
+        return pieces.reshape(-1, groups * size * width).astype(jnp.float32)
     columns = [
         pieces[peer, :, group * width : (group + 1) * width]
         for group in range(groups)
@@ -261,10 +263,11 @@
     small_size = sum(piece.shape[0] for piece in small)
     small = jnp.concatenate(small + [routes.astype(bf16).reshape(-1)], axis=0)
     small_count = small.shape[0]
-    token_rows = ring_gather(tokens.reshape(token_count, width), ctx_size, ctx_index)
+    own_tokens = tokens.reshape(token_count, width).astype(f32)
+    own_scaled, inv_one = rms_norm(own_tokens, 1.0)
+    scaled_rows = ring_gather(own_scaled.astype(bf16), ctx_size, ctx_index)
     expert_out = lax.all_gather(w_expert_out[0], "fsdp", axis=0, tiled=True)
     pieces = column_pieces(w_qkv, 3, ctx_size, small)
-    pieces, expert_out = after(pieces, expert_out)
     pieces = lax.all_gather(pieces, "fsdp", axis=0, tiled=False).transpose(1, 0, 2, 3)
     qkv_weight = pieces[:, :, :shard].reshape(width, 3 * own_width)
     small = pieces[:, :, shard:].reshape(device_count, -1)[:, :small_count]
@@ -281,9 +284,6 @@
     ).reshape(ctx_size, token_count, top_count)
 
     expert_in = lax.all_gather(w_expert_in[0], "fsdp", axis=0, tiled=True)
-    grad_rows = lax.all_gather(
-        cotangent.reshape(token_count, width), "ctx", axis=0, tiled=True
-    )
 
     block_ids = jnp.arange(ctx_size, dtype=i32)[:, None]
     local_index = jnp.arange(block_len, dtype=i32)[None, :]
@@ -299,9 +299,7 @@
     )
     cos_tab, sine_tab = rope_tables(positions, HD)
 
-    inputs = token_rows.astype(f32)
-    normed, inv_one_all = rms_norm(inputs, attn_gain)
-    normed_low = normed.astype(bf16)
+    normed_low = (scaled_rows.astype(f32) * attn_gain).astype(bf16)
     projected = dot(normed_low, qkv_weight) + bias
     head_shape = (seq_len, own_heads, HD)
     queries = rotate(projected[:, :own_width].reshape(head_shape), cos_tab, sine_tab).astype(bf16)
@@ -322,15 +320,16 @@
     attended = jnp.einsum("hqk,khd->qhd", weights_low, values, preferred_element_type=f32)
     attn_own = attended.astype(bf16).reshape(seq_len, own_width)
     shared_out, attn_own = fsdp_gather(w_shared_out, fsdp_size, attn_own)
-    attn_parts = dot(attn_own, out_weight).astype(bf16)
-    own_tokens = tokens.reshape(token_count, width).astype(f32)
+    attn_parts, shared_in = after(dot(attn_own, out_weight).astype(bf16), shared_in)
+    shared_in = lax.all_gather(shared_in, "fsdp", axis=0, tiled=False)
     own_residual = own_tokens + ring_scatter(attn_parts, ctx_size, ctx_index)
 
     normed_two, inv_two = rms_norm(own_residual, ffn_gain)
     own_low = normed_two.astype(bf16)
-    shared_in, own_low = after(shared_in, own_low)
-    shared_in = lax.all_gather(shared_in, "fsdp", axis=0, tiled=False)
-    low_two = ring_gather(own_low, ctx_size, ctx_index)
+    low_two, grad_rows = ring_gather(
+        own_low, ctx_size, ctx_index, cotangent.reshape(token_count, width)
+    )
+    grad_rows = lax.all_gather(grad_rows, "ctx", axis=0, tiled=True)
     mixed_weight = jnp.concatenate([router_weight, gate_vector[:, None]], axis=1)
     logits = dot(low_two, mixed_weight)
     probs_all = jax.nn.softmax(logits[:, :expert_count], axis=-1)
@@ -360,11 +359,18 @@
         return spread.reshape(seq_len, width)
 
     buffer = to_slots(blocks_two).astype(bf16)
-    buffer, grad_rows = after(buffer, grad_rows)
     expert_pre = dot(buffer, expert_in)
     expert_hid = swiglu(expert_pre, FE).astype(bf16)
     expert_res = dot(expert_hid, expert_out).astype(bf16)
     routed = gate_all[:, None] * to_tokens(expert_res)
+
+    shared_in, expert_res = after(shared_in, expert_res)
+    shared_in = shared_in.transpose(1, 0, 2, 3).reshape(width, 2 * fs_own)
+    shared_pre = dot(low_two, shared_in)
+    shared_hid = swiglu(shared_pre, fs_own).astype(bf16)
+    shared_res = dot(shared_hid, shared_out)
+    grad_rows, shared_res = after(grad_rows, shared_res)
+    out_parts = (scale_all[:, None] * shared_res + routed).astype(bf16)
 
     grad_slots = to_slots(grad_rows.reshape(ctx_size, token_count, width))
     gate_slots = jnp.sum(jnp.where(slot_mask, gate_blocks[:, None, :], 0.0), axis=-1).reshape(-1, 1)
@@ -373,22 +379,16 @@
     grad_gates = jnp.sum(jnp.where(slot_mask, slot_dots, 0.0), axis=1)
     grad_hid = dot_t(grad_res, expert_out)
     grad_pre = swiglu_back(expert_pre, FE, grad_hid).astype(bf16)
-    grad_pre, shared_in = after(grad_pre, shared_in)
     grad_expert_in = t_dot(buffer, grad_pre)
     grad_buffer = dot_t(grad_pre, expert_in).astype(bf16)
 
-    grad_expert_in, low_shared = after(grad_expert_in.astype(bf16), low_two)
+    grad_f32 = grad_rows.astype(f32)
+    grad_expert_in, grad_shared_res = after(
+        grad_expert_in.astype(bf16), (scale_all[:, None] * grad_f32).astype(bf16)
+    )
     sum_expert_in = sum_rows(grad_expert_in)
 
-    shared_in = shared_in.transpose(1, 0, 2, 3).reshape(width, 2 * fs_own)
-    shared_pre = dot(low_shared, shared_in)
-    shared_hid = swiglu(shared_pre, fs_own).astype(bf16)
-    shared_res = dot(shared_hid, shared_out)
-    out_parts = (scale_all[:, None] * shared_res + routed).astype(bf16)
-
-    grad_f32 = grad_rows.astype(f32)
     gate_dots = jnp.sum(grad_f32 * shared_res, axis=-1).reshape(ctx_size, token_count)
-    grad_shared_res = (scale_all[:, None] * grad_f32).astype(bf16)
     grad_shared_hid = dot_t(grad_shared_res, shared_out)
     grad_shared_pre = swiglu_back(shared_pre, fs_own, grad_shared_hid).astype(bf16)
     two_parts = (dot_t(grad_shared_pre, shared_in) + to_tokens(grad_buffer)).astype(bf16)
@@ -399,8 +399,10 @@
     grad_shared_out = t_dot(shared_hid, grad_shared_res).astype(bf16)
     grad_shared_in = t_dot(low_two, grad_shared_pre).astype(bf16)
     grad_two = ring_scatter(two_parts, ctx_size, ctx_index)
-    grad_two, grad_shared_in, grad_shared_out, grad_expert_out = after(
-        grad_two, grad_shared_in, grad_shared_out, grad_expert_out
+    dots = jnp.stack([grad_gates, gate_dots], axis=1)
+    dots = lax.all_to_all(dots, "ctx", split_axis=0, concat_axis=0, tiled=True)
+    grad_two, grad_shared_in, grad_shared_out, grad_expert_out, dots = after(
+        grad_two, grad_shared_in, grad_shared_out, grad_expert_out, dots
     )
     sum_shared_in = grad_shared_in.reshape(ctx_size, fsdp_size, shard, 2 * fs_own)
     sum_shared_in = lax.psum_scatter(
@@ -411,8 +413,6 @@
     ).reshape(ctx_size, shard, 2 * fs_own)
     sum_shared_out = sum_rows(grad_shared_out)
     sum_expert_out = sum_rows(grad_expert_out)
-    dots = jnp.stack([grad_gates, gate_dots], axis=1)
-    dots = lax.all_to_all(dots, "ctx", split_axis=0, concat_axis=0, tiled=True)
     own_probs = own_rows(probs_all)
     own_scale = own_rows(scale_all)
     own_chosen = routes.reshape(token_count, top_count)
@@ -460,7 +460,7 @@
         grad_projected, sum_expert_out, sum_shared_in
     )
     one_sums = dot_t(grad_projected, qkv_weight)
-    grad_gain_one = jnp.sum(one_sums * inputs * inv_one_all, axis=0)
+    grad_gain_one = jnp.sum(one_sums * scaled_rows.astype(f32), axis=0)
     one_parts = one_sums.astype(bf16)
     one_kept, grad_projected = after(one_parts, grad_projected)
     one_kept, out_parts = after(one_kept, out_parts)
@@ -469,7 +469,7 @@
     grad_normed = ring_scatter(one_parts, ctx_size, ctx_index, one_kept)
     grad_inputs_norm, unused = rms_back(
         own_tokens,
-        own_rows(inv_one_all),
+        inv_one,
         attn_gain,
         grad_normed,
     )

time: 812 us -> 789 us (0.972)
  waiting for transfers between devices: 270 us -> 243 us
  other arithmetic: 82.4 us -> 100 us
  local copies, waits for them, and re-layouts: 122 us -> 107 us
    reduce_scatter x1, waiting for transfers between devices: 7.72 us -> 35.1 us  [local_split(): lax.psum_scatter(sum_shared_in.transpose(1, 0, 2, 3).reshape(width, 2 * f...]
    unnamed x218 -> x176, local copies, waits for them, and re-layouts: 51.1 us -> 27 us
    ppermute x12, waiting for transfers between devices: 49.3 us -> 27.5 us  [ring_sums(): rear = lax.ppermute(rear, 'ctx', back)]
    ppermute x12, waiting for transfers between devices: 78.2 us -> 58 us  [ring_sums(): fore = lax.ppermute(fore, 'ctx', ahead)]
    all_to_all x1, waiting for transfers between devices: 0.01 us -> 17.6 us  [column_pieces(): lax.all_to_all(pieces, 'ctx', split_axis=0, concat_axis=0, tiled=True)]
    all_gather x1, waiting for transfers between devices: 0.02 us -> 16.4 us  [local_split(): grad_rows = lax.all_gather(grad_rows, 'ctx', axis=0, tiled=True)]
    ppermute x4, waiting for transfers between devices: 28.4 us -> 12.5 us  [ring_sums(): fore = lax.ppermute(low(own(half, 0, cut)), 'ctx', ahead)]
    convert_element_type x1 -> x3, other arithmetic: 0.15 us -> 15.2 us  [the longest x1 11.9 us: local_split(): out_parts = (scale_all[:, None] * shared_res + routed).astype(bf16)]
  transfers between devices with their start and end apart: 75 -> 75, of which waited for: 43 -> 42; matrix products, arithmetic and copies ran while one was open for 42% -> 42% of each run, Pallas kernels for 0% -> 0%
where the time goes in v9:
time: 789 us; the launch traced here: 782 us
  waiting for transfers between devices  243 us (31%)
  matrix products  199 us (25%)
  local copies, waits for them, and re-layouts  107 us (14%)
  other arithmetic  100 us (13%)
  starting transfers between devices  81.5 us (10%)
  blocking collectives  29.9 us (4%)
  between operations  20.4 us (3%)
    ppermute x12, waiting for transfers between devices, ring_sums(): fore = lax.ppermute(fore, 'ctx', ahead)  58 us
    dot_general x7, matrix products, dot_t(): lax.dot_general(a, b, (((1,), (1,)), ((), ())), preferred_element_type=f32)  48.5 us
    dot_general x8, matrix products, dot(): return jnp.dot(a, b, preferred_element_type=f32)  46.6 us
    dot_general x8, matrix products, t_dot(): lax.dot_general(a, b, (((0,), (0,)), ((), ())), preferred_element_type=f32)  39.8 us
    reduce_scatter x1, waiting for transfers between devices, local_split(): lax.psum_scatter(sum_shared_in.transpose(1, 0, 2, 3).reshape(width, 2 * f...  35.1 us
    ppermute x9, waiting for transfers between devices, ring_gather(): rear = lax.ppermute(rear, 'ctx', back)  32 us
    all_to_all x1, blocking collectives, column_pieces(): lax.all_to_all(pieces, 'ctx', split_axis=0, concat_axis=0, tiled=True)  29.9 us
    ppermute x12, waiting for transfers between devices, ring_sums(): rear = lax.ppermute(rear, 'ctx', back)  27.5 us
  transfers between devices with their start and end apart: 75, of which 42 were waited for; matrix products, arithmetic and copies ran while one was open for 42% of the time, Pallas kernels for 0%

profile of v9, /device:TPU:8, one launch (start us, length us, event | category | flops | bytes accessed | tf_op | source)
XLA Modules:
  0.0 781.7 jit_solution(12668574290946890899)
XLA Ops:
  14.6 29.9 %all_to_all.25 = bf16[8,80,768]{2,1,0:T(8,128)(2,1)} all-to-all(bf16[8,80,768]{2,1,0:T(8,128)(2,1)S(1)} %pad_maximum_fusion.6), channel_id=1, replica_groups=mesh['ctx'=8,'fsdp'=4] {'ctx'}, dimensions={0} | all-to-all | bytes 1966080 | tf_op jit(solution)/shard_map/all_to_all | solution.py:194
  67.4 7.2 collective-permute-done.3
  79.2 7.3 collective-permute-done.5
  102.4 6.9 fusion.60
  140.3 17.6 %all-to-all-done.1 = bf16[8,64,1408]{2,1,0:T(8,128)(2,1)S(1)} async-done(((bf16[8,64,1408]{2,1,0:T(8,128)(2,1)}), bf16[8,64,1408]{2,1,0:T(8,128)(2,1)S(1)}, u32[]{:S(2)}, u32[]{:S(2)}) %all-to-all-start.1) | async-done | bytes 1441824 | tf_op jit(solution)/shard_map/all_to_all | solution.py:194
  173.8 11.0 %collective-permute-done.16 = bf16[128,2048]{1,0:T(8,128)(2,1)S(1)} collective-permute-done((bf16[128,2048]{1,0:T(8,128)(2,1)S(1)}, bf16[128,2048]{1,0:T(8,128)(2,1)S(1)}, u32[]{:S(2)}, u32[]{:S(2)}) %collective-permute-start.16) | collective-permute-done | bytes 524320 | tf_op jit(solution)/shard_map/ppermute | solution.py:144
  188.9 10.0 %collective-permute-done.13 = bf16[128,2048]{1,0:T(8,128)(2,1)S(1)} collective-permute-done((bf16[128,2048]{1,0:T(8,128)(2,1)S(1)}, bf16[128,2048]{1,0:T(8,128)(2,1)S(1)}, u32[]{:S(2)}, u32[]{:S(2)}) %collective-permute-start.13) | collective-permute-done | bytes 524320 | tf_op jit(solution)/shard_map/ppermute | solution.py:143
  237.0 8.2 %collective-permute-done.21 = bf16[128,2048]{1,0:T(8,128)(2,1)} collective-permute-done((bf16[128,2048]{1,0:T(8,128)(2,1)}, bf16[128,2048]{1,0:T(8,128)(2,1)}, u32[]{:S(2)}, u32[]{:S(2)}) %collective-permute-start.21) | collective-permute-done | bytes 524320 | tf_op jit(solution)/shard_map/ppermute | solution.py:106
  273.5 10.4 %fusion.3 = f32[512,2816]{1,0:T(8,128)S(1)} fusion(bf16[512,2048]{1,0:T(8,128)(2,1)S(1)} %bitcast.344, bf16[1,2048,2816]{2,1,0:T(8,128)(2,1)} %all-gather.16.cloned.1.call-done), kind=kOutput, calls=%fused_computation.3 | convolution fusion | flops 5905580032 | bytes 19398656 | tf_op jit(solution)/shard_map/dot_general | solution.py:245
  287.4 6.8 fusion.57
  302.4 10.0 %fusion.150 = f32[1024,1408]{1,0:T(8,128)S(1)} fusion(bf16[1024,2048]{1,0:T(8,128)(2,1)} %constant_dynamic-update-slice_fusion.4, bf16[2048,1408]{1,0:T(8,128)(2,1)S(1)} %bitcast.317), kind=kOutput, calls=%fused_computation.328 | convolution fusion | flops 5905580032 | bytes 15728640 | tf_op jit(solution)/shard_map/dot_general | solution.py:245
  322.6 16.4 %all-gather.10.cloned.1.call-done = bf16[1024,2048]{1,0:T(8,128)(2,1)} async-done(((bf16[128,2048]{1,0:T(8,128)(2,1)}), bf16[1024,2048]{1,0:T(8,128)(2,1)}) %all-gather.10.cloned.1.call-update) | async-done | bytes 4194320 | tf_op jit(solution)/shard_map/all_gather | solution.py:332
  347.2 8.9 %multiply_convert_fusion.4 = (bf16[512,1408]{1,0:T(8,128)(2,1)S(1)}, bf16[512,1408]{1,0:T(8,128)(2,1)S(1)}) fusion(f32[512,2816]{1,0:T(8,128)} %copy-done.9, bf16[512,2048]{1,0:T(8,128)(2,1)S(1)} %fusion.27, bf16[1,1408,2048]{2,1,0:T(8,128)(2,1)} %all-gather.18.cloned.1.call-done), kind=kOutput, calls=%fused_computation.68 | convolution fusion | flops 2962161664 | bytes 16515072 | tf_op jit(solution)/shard_map/dot_general | solution.py:248
  357.8 8.9 %convolution_convert_fusion = bf16[2048,2816]{1,0:T(8,128)(2,1)} fusion(bf16[512,2048]{1,0:T(8,128)(2,1)S(1)} %bitcast.345, bf16[512,1408]{1,0:T(8,128)(2,1)S(1)} %get-tuple-element.164, bf16[512,1408]{1,0:T(8,128)(2,1)S(1)} %get-tuple-element.163), kind=kOutput, calls=%fused_computation.5 | convolution fusion | flops 5917114368 | bytes 16515072 | tf_op jit(solution)/shard_map/dot_general | solution.py:251
  366.6 11.9 %fusion.10 = (bf16[1024,2048]{1,0:T(8,128)(2,1)}, f32[1024]{0:T(1024)S(1)}, bf16[1024,2048]{1,0:T(8,128)(2,1)}) fusion(f32[8,128,2048]{2,1,0:T(8,128)} %fusion.93, f32[1024,2048]{1,0:T(8,128)} %fusion.151, f32[1024]{0:T(1024)S(1)} %bitcast.369, f32[1024]{0:T(1024)S(1)} %bitcast.371, bf16[1024,2048]{1,0:T(8,128)(2,1)} %all-gather.10.cloned.1.call-done), kind=kLoop, calls=%fused_computation.16 | loop fusion | flops 18873344 | bytes 29372416 | tf_op jit(solution)/shard_map/convert_element_type | solution.py:373
  380.3 9.2 %multiply_convert_fusion.1 = (bf16[1024,704]{1,0:T(8,128)(2,1)S(1)}, bf16[1024,704]{1,0:T(8,128)(2,1)S(1)}) fusion(f32[1024,1408]{1,0:T(8,128)} %copy-done.6, bf16[1024,2048]{1,0:T(8,128)(2,1)} %get-tuple-element.62, bf16[704,2048]{1,0:T(8,128)(2,1)S(1)} %bitcast.339), kind=kOutput, calls=%fused_computation.58 | convolution fusion | flops 2962161664 | bytes 15728640 | tf_op jit(solution)/shard_map/dot_general | solution.py:248
  392.0 11.2 %fusion.54 = bf16[512,2048]{1,0:T(8,128)(2,1)S(1)} fusion(bf16[1,2048,2816]{2,1,0:T(8,128)(2,1)} %all-gather.16.cloned.1.call-done, bf16[512,1408]{1,0:T(8,128)(2,1)S(1)} %copy-done.81, bf16[512,1408]{1,0:T(8,128)(2,1)S(1)} %copy-done.79), kind=kOutput, calls=%fused_computation.61 | convolution fusion | flops 5912395776 | bytes 16515072 | tf_op jit(solution)/shard_map/dot_general | solution.py:248
  404.6 7.5 fusion.11
  427.3 10.8 %convolution_convert_fusion.2 = bf16[2048,1408]{1,0:T(8,128)(2,1)} fusion(bf16[1024,2048]{1,0:T(8,128)(2,1)} %constant_dynamic-update-slice_fusion.4, bf16[1024,1408]{1,0:T(8,128)(2,1)S(1)} %pad_maximum_fusion.2), kind=kOutput, calls=%fused_computation.26 | convolution fusion | flops 5908463616 | bytes 12845056 | tf_op jit(solution)/shard_map/dot_general | solution.py:251
  485.9 8.9 %collective-permute-done.37 = bf16[128,2048]{1,0:T(8,128)(2,1)} collective-permute-done((bf16[128,2048]{1,0:T(8,128)(2,1)}, bf16[128,2048]{1,0:T(8,128)(2,1)}, u32[]{:S(2)}, u32[]{:S(2)}) %collective-permute-start.37) | collective-permute-done | bytes 524320 | tf_op jit(solution)/shard_map/ppermute | solution.py:107
  512.9 6.6 collective-permute-done.41
  531.8 35.1 %reduce-scatter.9.cloned.1.call-done = bf16[512,1408]{1,0:T(8,128)(2,1)} async-done(((bf16[2048,1408]{1,0:T(8,128)(2,1)}), bf16[512,1408]{1,0:T(8,128)(2,1)}) %reduce-scatter.9.cloned.1.call-update) | async-done | bytes 1441808 | tf_op jit(solution)/shard_map/reduce_scatter | solution.py:408
  566.9 6.0 all-to-all-start.3
  573.0 6.7 fusion.153
  582.1 16.6 %fusion.67 = f32[1024,2,128]{0,2,1:T(8,128)} fusion(bf16[1024,2,128]{0,2,1:T(8,128)(2,1)} %get-tuple-element.51, f32[2,1024,1024]{1,2,0:T(8,128)} %fusion.153, f32[2,1024,1024]{1,2,0:T(8,128)} %copy-done.5, f32[2,1024]{1,0:T(2,128)S(1)} %copy-done.69, pred[1024,1024]{0,1:T(8,128)(4,1)} %compare_and_fusion), kind=kOutput, calls=%fused_computation.82 | convolution fusion | flops 559942656 | bytes 19406848 | tf_op jit(solution)/shard_map/hqk,qhd->khd/dot_general | solution.py:448
  598.7 16.5 %broadcast_multiply_fusion.1 = (f32[1024,2,128]{0,2,1:T(8,128)}, f32[1024,2,128]{0,2,1:T(8,128)}, f32[1024,2,128]{0,2,1:T(8,128)}) fusion(f32[1024,128]{0,1:T(8,128)} %get-tuple-element.252, f32[1024,2,128]{0,2,1:T(8,128)} %fusion.67, bf16[1024,2,128]{0,2,1:T(8,128)(2,1)S(1)} %copy-done.54, f32[2,1024,1024]{1,2,0:T(8,128)} %fusion.153, ...), kind=kOutput, calls=%fused_computation.169 | convolution fusion | flops 560466944 | bytes 23076864 | tf_op jit(solution)/shard_map/hqk,khd->qhd/dot_general | solution.py:446
  618.9 5.9 convolution_convert_fusion.8
  626.1 9.2 %fusion.6 = (bf16[2048]{0:T(1024)(128)(2,1)S(1)}, bf16[1024,2048]{1,0:T(8,128)(2,1)}) fusion(bf16[1024,2048]{1,0:T(8,128)(2,1)} %constant_dynamic-update-slice_fusion.18, bf16[1024,768]{0,1:T(8,128)(2,1)} %pad_maximum_fusion.5, bf16[2048,768]{1,0:T(8,128)(2,1)} %bitcast.333), kind=kOutput, calls=%fused_computation.11 | convolution fusion | flops 3229612032 | bytes 13111296 | tf_op jit(solution)/shard_map/dot_general | solution.py:248
  636.2 6.3 fusion.51
  686.5 6.3 collective-permute-done.57
  698.8 11.6 %collective-permute-done.54 = bf16[128,2048]{1,0:T(8,128)(2,1)S(1)} collective-permute-done((bf16[128,2048]{1,0:T(8,128)(2,1)S(1)}, bf16[128,2048]{1,0:T(8,128)(2,1)S(1)}, u32[]{:S(2)}, u32[]{:S(2)}) %collective-permute-start.54) | collective-permute-done | bytes 524320 | tf_op jit(solution)/shard_map/ppermute | solution.py:143
  737.8 19.9 %collective-permute-done.47 = bf16[128,2048]{1,0:T(8,128)(2,1)} collective-permute-done((bf16[128,2048]{1,0:T(8,128)(2,1)}, bf16[128,2048]{1,0:T(8,128)(2,1)}, u32[]{:S(2)}, u32[]{:S(2)}) %collective-permute-start.47) | collective-permute-done | bytes 524320 | tf_op jit(solution)/shard_map/ppermute | solution.py:143
  (538 shorter events, 395.5 us)
Async XLA Ops:
  7.2 88.6 %all-gather.12.cloned.1.call-start = ((), (), s32[]{:S(2)}) async-start(), calls=%async_computation.18 | async-start | bytes 4915200 | tf_op jit(solution)/shard_map/all_gather | solution.py:271
  44.5 229.0 %all-gather.16.cloned.1.call-start = ((), (), s32[]{:S(2)}) async-start(), calls=%async_computation.20 | async-start | bytes 14417920 | tf_op jit(solution)/shard_map/all_gather | solution.py:286
  45.3 242.1 %all-gather.18.cloned.1.call-start = ((), (), s32[]{:S(2)}) async-start(), calls=%async_computation.21 | async-start | bytes 7208960 | tf_op jit(solution)/shard_map/all_gather | solution.py:269
  51.3 60.9 %collective-permute-start.9 = (bf16[64,2048]{1,0:T(8,128)(2,1)S(1)}, bf16[64,2048]{1,0:T(8,128)(2,1)S(1)}, u32[]{:S(2)}, u32[]{:S(2)}) collective-permute-start(bf16[64,2048]{1,0:T(8,128)(2,1)S(1)} %copy-done.44), channel_id=1, source_target_pairs={{0,2},{1,3},{2,0},{3,1},{4,6},{5,7},{6,4},{7,5},{8,10},{9,11},{10,... | collective-permute-start | bytes 786440 | tf_op jit(solution)/shard_map/ppermute | solution.py:169
  52.8 82.8 %collective-permute-start = (bf16[176,2048]{1,0:T(8,128)(2,1)}, bf16[176,2048]{1,0:T(8,128)(2,1)}, u32[]{:S(2)}, u32[]{:S(2)}) collective-permute-start(bf16[176,2048]{1,0:T(8,128)(2,1)} %param.34), channel_id=1, source_target_pairs={{0,2},{1,3},{2,0},{3,1},{4,6},{5,7},{6,4},{7,5},{8,10},{9,11},{10,... | collective-permute-start | bytes 2162696 | tf_op jit(solution)/shard_map/ppermute | solution.py:169
  113.1 22.8 %collective-permute-start.10 = (bf16[2,64,2048]{2,1,0:T(8,128)(2,1)}, bf16[2,64,2048]{2,1,0:T(8,128)(2,1)}, u32[]{:S(2)}, u32[]{:S(2)}) collective-permute-start(bf16[2,64,2048]{2,1,0:T(8,128)(2,1)} %maximum_select_fusion.3), channel_id=1, source_target_pairs={{0,1},{1,0},{2,3},{3,2},{4,5},{5,4},{6,7},{7,6},{8,9},{9,8},{10,11... | collective-permute-start | bytes 1572872 | tf_op jit(solution)/shard_map/ppermute | solution.py:174
  120.8 37.1 %all-to-all-start.1 = ((bf16[8,64,1408]{2,1,0:T(8,128)(2,1)}), bf16[8,64,1408]{2,1,0:T(8,128)(2,1)S(1)}, u32[]{:S(2)}, u32[]{:S(2)}) async-start(bf16[8,64,1408]{2,1,0:T(8,128)(2,1)} %reshape.809), calls=%async_computation.1 | async-start | bytes 2883584 | tf_op jit(solution)/shard_map/all_to_all | solution.py:194
  125.8 172.9 %all-gather.14.cloned.1.call-start = ((), (), s32[]{:S(2)}) async-start(), calls=%async_computation.19 | async-start | bytes 7208960 | tf_op jit(solution)/shard_map/all_gather | solution.py:324
  159.0 180.0 %all-gather.10.cloned.1.call-start = ((), (), s32[]{:S(2)}) async-start(), calls=%async_computation.11 | async-start | bytes 4718592 | tf_op jit(solution)/shard_map/all_gather | solution.py:332
  208.7 24.6 %collective-permute-start.27 = (bf16[2,176,2048]{2,1,0:T(8,128)(2,1)}, bf16[2,176,2048]{2,1,0:T(8,128)(2,1)S(1)}, u32[]{:S(2)}, u32[]{:S(2)}) collective-permute-start(bf16[2,176,2048]{2,1,0:T(8,128)(2,1)} %maximum_select_fusion.1), channel_id=1, source_target_pairs={{0,1},{1,0},{2,3},{3,2},{4,5},{5,4},{6,7},{7,6},{8,9},{9,8},{10,11... | collective-permute-start | bytes 4325384 | tf_op jit(solution)/shard_map/ppermute | solution.py:174
  230.8 15.5 %collective-permute-start.22 = (bf16[128,2048]{1,0:T(8,128)(2,1)S(1)}, bf16[128,2048]{1,0:T(8,128)(2,1)}, u32[]{:S(2)}, u32[]{:S(2)}) collective-permute-start(bf16[128,2048]{1,0:T(8,128)(2,1)S(1)} %collective-permute-done.20), channel_id=1, source_target_pairs={{8,0},{16,8},{24,16},{28,24},{20,28},{12,20},{4,12},{0,4},{9,1},{1... | collective-permute-start | bytes 1572872 | tf_op jit(solution)/shard_map/ppermute | solution.py:107
  248.1 234.6 %reduce-scatter.7.cloned.1.call-start = ((), (), s32[]{:S(2)}) async-start(), calls=%async_computation.12 | async-start | bytes 14417920 | tf_op jit(solution)/shard_map/reduce_scatter | solution.py:259
  417.6 54.0 %all-to-all-start.2 = ((f32[8,2,128]{2,1,0:T(2,128)}), f32[8,2,128]{2,1,0:T(2,128)S(1)}, u32[]{:S(2)}, u32[]{:S(2)}) async-start(f32[8,2,128]{2,1,0:T(2,128)} %pad_maximum_fusion.17), calls=%async_computation.2 | async-start | bytes 16384 | tf_op jit(solution)/shard_map/all_to_all | solution.py:403
  421.8 109.9 %reduce-scatter.11.cloned.1.call-start = ((), (), s32[]{:S(2)}) async-start(), calls=%async_computation.14 | async-start | bytes 3604480 | tf_op jit(solution)/shard_map/reduce_scatter | solution.py:259
  471.6 95.3 %reduce-scatter.9.cloned.1.call-start = ((), (), s32[]{:S(2)}) async-start(), calls=%async_computation.13 | async-start | bytes 7208960 | tf_op jit(solution)/shard_map/reduce_scatter | solution.py:408
  477.4 148.7 %reduce-scatter.13.cloned.1.call-start = ((), (), s32[]{:S(2)}) async-start(), calls=%async_computation.15 | async-start | bytes 7208960 | tf_op jit(solution)/shard_map/reduce_scatter | solution.py:259
  566.9 59.2 %all-to-all-start.3 = ((bf16[8,64,1408]{2,1,0:T(8,128)(2,1)}), bf16[8,64,1408]{2,1,0:T(8,128)(2,1)}, u32[]{:S(2)}, u32[]{:S(2)}) async-start(bf16[8,64,1408]{2,1,0:T(8,128)(2,1)} %bitcast.349), calls=%async_computation.7 | async-start | bytes 2883584 | tf_op jit(solution)/shard_map/all_to_all | solution.py:440
  572.9 102.0 %reduce-scatter.17.cloned.1.call-start = ((), (), s32[]{:S(2)}) async-start(), calls=%async_computation.17 | async-start | bytes 1310720 | tf_op jit(solution)/shard_map/reduce_scatter | solution.py:259
  582.0 135.0 %reduce-scatter.15.cloned.1.call-start = ((), (), s32[]{:S(2)}) async-start(), calls=%async_computation.16 | async-start | bytes 4915200 | tf_op jit(solution)/shard_map/reduce_scatter | solution.py:498
  664.1 15.2 %collective-permute-start.45 = (bf16[128,2048]{1,0:T(8,128)(2,1)}, bf16[128,2048]{1,0:T(8,128)(2,1)}, u32[]{:S(2)}, u32[]{:S(2)}) collective-permute-start(bf16[128,2048]{1,0:T(8,128)(2,1)} %pad_maximum_fusion.13), channel_id=1, source_target_pairs={{0,8},{8,16},{16,24},{24,28},{28,20},{20,12},{12,4},{4,0},{1,9},{9... | collective-permute-start | bytes 1572872 | tf_op jit(solution)/shard_map/ppermute | solution.py:143
  666.4 15.2 %collective-permute-start.49 = (bf16[128,2048]{1,0:T(8,128)(2,1)}, bf16[128,2048]{1,0:T(8,128)(2,1)}, u32[]{:S(2)}, u32[]{:S(2)}) collective-permute-start(bf16[128,2048]{1,0:T(8,128)(2,1)} %pad_maximum_fusion.14), channel_id=1, source_target_pairs={{8,0},{16,8},{24,16},{28,24},{20,28},{12,20},{4,12},{0,4},{9,1},{1... | collective-permute-start | bytes 1572872 | tf_op jit(solution)/shard_map/ppermute | solution.py:144
  667.8 25.0 %collective-permute-start.57 = (bf16[128,2048]{1,0:T(8,128)(2,1)}, bf16[128,2048]{1,0:T(8,128)(2,1)}, u32[]{:S(2)}, u32[]{:S(2)}) collective-permute-start(bf16[128,2048]{1,0:T(8,128)(2,1)} %pad_maximum_fusion.16), channel_id=1, source_target_pairs={{8,0},{16,8},{24,16},{28,24},{20,28},{12,20},{4,12},{0,4},{9,1},{1... | collective-permute-start | bytes 1572872 | tf_op jit(solution)/shard_map/ppermute | solution.py:144
  669.2 23.6 %collective-permute-start.53 = (bf16[128,2048]{1,0:T(8,128)(2,1)}, bf16[128,2048]{1,0:T(8,128)(2,1)}, u32[]{:S(2)}, u32[]{:S(2)}) collective-permute-start(bf16[128,2048]{1,0:T(8,128)(2,1)} %pad_maximum_fusion.15), channel_id=1, source_target_pairs={{0,8},{8,16},{16,24},{24,28},{28,20},{20,12},{12,4},{4,0},{1,9},{9... | collective-permute-start | bytes 1572872 | tf_op jit(solution)/shard_map/ppermute | solution.py:143
  684.5 37.1 %collective-permute-start.46 = (bf16[128,2048]{1,0:T(8,128)(2,1)}, bf16[128,2048]{1,0:T(8,128)(2,1)S(1)}, u32[]{:S(2)}, u32[]{:S(2)}) collective-permute-start(bf16[128,2048]{1,0:T(8,128)(2,1)} %get-tuple-element.182), channel_id=1, source_target_pairs={{0,8},{8,16},{16,24},{24,28},{28,20},{20,12},{12,4},{4,0},{1,9},{9... | collective-permute-start | bytes 1572872 | tf_op jit(solution)/shard_map/ppermute | solution.py:143
  685.9 35.7 %collective-permute-start.50 = (bf16[128,2048]{1,0:T(8,128)(2,1)}, bf16[128,2048]{1,0:T(8,128)(2,1)}, u32[]{:S(2)}, u32[]{:S(2)}) collective-permute-start(bf16[128,2048]{1,0:T(8,128)(2,1)} %get-tuple-element.183), channel_id=1, source_target_pairs={{8,0},{16,8},{24,16},{28,24},{20,28},{12,20},{4,12},{0,4},{9,1},{1... | collective-permute-start | bytes 1572872 | tf_op jit(solution)/shard_map/ppermute | solution.py:144
  694.8 15.6 %collective-permute-start.54 = (bf16[128,2048]{1,0:T(8,128)(2,1)S(1)}, bf16[128,2048]{1,0:T(8,128)(2,1)S(1)}, u32[]{:S(2)}, u32[]{:S(2)}) collective-permute-start(bf16[128,2048]{1,0:T(8,128)(2,1)S(1)} %get-tuple-element.172), channel_id=1, source_target_pairs={{0,8},{8,16},{16,24},{24,28},{28,20},{20,12},{12,4},{4,0},{1,9},{9... | collective-permute-start | bytes 1572872 | tf_op jit(solution)/shard_map/ppermute | solution.py:143
  696.3 16.1 %collective-permute-start.58 = (bf16[128,2048]{1,0:T(8,128)(2,1)S(1)}, bf16[128,2048]{1,0:T(8,128)(2,1)S(1)}, u32[]{:S(2)}, u32[]{:S(2)}) collective-permute-start(bf16[128,2048]{1,0:T(8,128)(2,1)S(1)} %get-tuple-element.173), channel_id=1, source_target_pairs={{8,0},{16,8},{24,16},{28,24},{20,28},{12,20},{4,12},{0,4},{9,1},{1... | collective-permute-start | bytes 1572872 | tf_op jit(solution)/shard_map/ppermute | solution.py:144
  715.0 21.1 %collective-permute-start.55 = (bf16[128,2048]{1,0:T(8,128)(2,1)}, bf16[128,2048]{1,0:T(8,128)(2,1)}, u32[]{:S(2)}, u32[]{:S(2)}) collective-permute-start(bf16[128,2048]{1,0:T(8,128)(2,1)} %get-tuple-element.170), channel_id=1, source_target_pairs={{0,8},{8,16},{16,24},{24,28},{28,20},{20,12},{12,4},{4,0},{1,9},{9... | collective-permute-start | bytes 1572872 | tf_op jit(solution)/shard_map/ppermute | solution.py:143
  716.4 19.6 %collective-permute-start.59 = (bf16[128,2048]{1,0:T(8,128)(2,1)}, bf16[128,2048]{1,0:T(8,128)(2,1)}, u32[]{:S(2)}, u32[]{:S(2)}) collective-permute-start(bf16[128,2048]{1,0:T(8,128)(2,1)} %get-tuple-element.171), channel_id=1, source_target_pairs={{8,0},{16,8},{24,16},{28,24},{20,28},{12,20},{4,12},{0,4},{9,1},{1... | collective-permute-start | bytes 1572872 | tf_op jit(solution)/shard_map/ppermute | solution.py:144
  717.0 47.1 %all-to-all-start.4 = ((bf16[8,80,768]{2,1,0:T(8,128)(2,1)}), bf16[8,80,768]{2,1,0:T(8,128)(2,1)}, u32[]{:S(2)}, u32[]{:S(2)}) async-start(bf16[8,80,768]{2,1,0:T(8,128)(2,1)} %bitcast.360), calls=%async_computation.9 | async-start | bytes 1966080 | tf_op jit(solution)/shard_map/all_to_all | solution.py:500
  724.3 33.4 %collective-permute-start.47 = (bf16[128,2048]{1,0:T(8,128)(2,1)}, bf16[128,2048]{1,0:T(8,128)(2,1)}, u32[]{:S(2)}, u32[]{:S(2)}) collective-permute-start(bf16[128,2048]{1,0:T(8,128)(2,1)} %get-tuple-element.180), channel_id=1, source_target_pairs={{0,8},{8,16},{16,24},{24,28},{28,20},{20,12},{12,4},{4,0},{1,9},{9... | collective-permute-start | bytes 1572872 | tf_op jit(solution)/shard_map/ppermute | solution.py:143
  725.8 34.1 %collective-permute-start.51 = (bf16[128,2048]{1,0:T(8,128)(2,1)}, bf16[128,2048]{1,0:T(8,128)(2,1)}, u32[]{:S(2)}, u32[]{:S(2)}) collective-permute-start(bf16[128,2048]{1,0:T(8,128)(2,1)} %get-tuple-element.181), channel_id=1, source_target_pairs={{8,0},{16,8},{24,16},{28,24},{20,28},{12,20},{4,12},{0,4},{9,1},{1... | collective-permute-start | bytes 1572872 | tf_op jit(solution)/shard_map/ppermute | solution.py:144
  (127 other events, 1249.0 us)
Sparse Core Ops, SparseCore 0:
  44.6 51.0 all-gather.11
  97.3 76.3 all-gather.15
  175.2 43.3 all-gather.17
  220.7 43.4 all-gather.13
  266.1 72.8 all-gather.9
  378.7 91.0 reduce-scatter.6
  472.9 36.3 reduce-scatter.10
  512.0 54.8 reduce-scatter.8
  569.4 54.8 reduce-scatter.12
  626.9 24.8 reduce-scatter.16
  654.3 42.8 reduce-scatter.14

commit v10 on v9

--- a/solution.py
+++ b/solution.py
@@ -191,7 +191,7 @@
             extra.reshape(1, more, groups * width), (size, more, groups * width)
         )
         pieces = jnp.concatenate([pieces, extra], axis=1)
-    return lax.all_to_all(pieces, "ctx", split_axis=0, concat_axis=0, tiled=True)
+    return pieces
 
 
 def merge_columns(pieces, groups, size):
@@ -266,8 +266,11 @@
     own_tokens = tokens.reshape(token_count, width).astype(f32)
     own_scaled, inv_one = rms_norm(own_tokens, 1.0)
     scaled_rows = ring_gather(own_scaled.astype(bf16), ctx_size, ctx_index)
-    expert_out = lax.all_gather(w_expert_out[0], "fsdp", axis=0, tiled=True)
     pieces = column_pieces(w_qkv, 3, ctx_size, small)
+    pieces = lax.all_to_all(pieces, "ctx", split_axis=0, concat_axis=0, tiled=True)
+    shared_in = column_pieces(w_shared_in, 2, ctx_size, None)
+    shared_in, scaled_rows = after(shared_in, scaled_rows)
+    shared_in = lax.all_to_all(shared_in, "ctx", split_axis=0, concat_axis=0, tiled=True)
     pieces = lax.all_gather(pieces, "fsdp", axis=0, tiled=False).transpose(1, 0, 2, 3)
     qkv_weight = pieces[:, :, :shard].reshape(width, 3 * own_width)
     small = pieces[:, :, shard:].reshape(device_count, -1)[:, :small_count]
@@ -307,8 +310,6 @@
         projected[:, own_width : 2 * own_width].reshape(head_shape), cos_tab, sine_tab
     ).astype(bf16)
     values = projected[:, 2 * own_width :].reshape(head_shape).astype(bf16)
-    queries, in_shard = after(queries, w_shared_in)
-    shared_in = column_pieces(in_shard, 2, ctx_size, None)
     out_weight, queries = fsdp_gather(w_out, fsdp_size, queries)
     allowed = (positions[None, :] <= positions[:, None]) & (seg_rows[None, :] == seg_rows[:, None])
     scores = jnp.einsum("qhd,khd->hqk", queries, keys, preferred_element_type=f32) * score_scale
@@ -320,6 +321,7 @@
     attended = jnp.einsum("hqk,khd->qhd", weights_low, values, preferred_element_type=f32)
     attn_own = attended.astype(bf16).reshape(seq_len, own_width)
     shared_out, attn_own = fsdp_gather(w_shared_out, fsdp_size, attn_own)
+    expert_out, attn_own = fsdp_gather(w_expert_out[0], fsdp_size, attn_own)
     attn_parts, shared_in = after(dot(attn_own, out_weight).astype(bf16), shared_in)
     shared_in = lax.all_gather(shared_in, "fsdp", axis=0, tiled=False)
     own_residual = own_tokens + ring_scatter(attn_parts, ctx_size, ctx_index)
@@ -369,15 +371,17 @@
     shared_pre = dot(low_two, shared_in)
     shared_hid = swiglu(shared_pre, fs_own).astype(bf16)
     shared_res = dot(shared_hid, shared_out)
-    grad_rows, shared_res = after(grad_rows, shared_res)
     out_parts = (scale_all[:, None] * shared_res + routed).astype(bf16)
+    grad_rows, out_parts = after(grad_rows, out_parts)
+    out_sum = lax.psum_scatter(out_parts, "ctx", scatter_dimension=0, tiled=True)
 
     grad_slots = to_slots(grad_rows.reshape(ctx_size, token_count, width))
     gate_slots = jnp.sum(jnp.where(slot_mask, gate_blocks[:, None, :], 0.0), axis=-1).reshape(-1, 1)
     grad_res = (gate_slots * grad_slots).astype(bf16)
-    slot_dots = jnp.sum(grad_slots * expert_res.astype(f32), axis=-1).reshape(ctx_size, capacity, 1)
-    grad_gates = jnp.sum(jnp.where(slot_mask, slot_dots, 0.0), axis=1)
     grad_hid = dot_t(grad_res, expert_out)
+    slot_terms = jnp.sum(expert_hid.astype(f32) * grad_hid, axis=-1)
+    slot_terms = slot_terms.reshape(ctx_size, capacity, 1)
+    gate_terms = jnp.sum(jnp.where(slot_mask, slot_terms, 0.0), axis=1)
     grad_pre = swiglu_back(expert_pre, FE, grad_hid).astype(bf16)
     grad_expert_in = t_dot(buffer, grad_pre)
     grad_buffer = dot_t(grad_pre, expert_in).astype(bf16)
@@ -388,8 +392,8 @@
     )
     sum_expert_in = sum_rows(grad_expert_in)
 
-    gate_dots = jnp.sum(grad_f32 * shared_res, axis=-1).reshape(ctx_size, token_count)
     grad_shared_hid = dot_t(grad_shared_res, shared_out)
+    scale_terms = jnp.sum(shared_hid.astype(f32) * grad_shared_hid, axis=-1)
     grad_shared_pre = swiglu_back(shared_pre, fs_own, grad_shared_hid).astype(bf16)
     two_parts = (dot_t(grad_shared_pre, shared_in) + to_tokens(grad_buffer)).astype(bf16)
     two_parts, expert_hid, shared_hid, grad_shared_pre = after(
@@ -399,11 +403,12 @@
     grad_shared_out = t_dot(shared_hid, grad_shared_res).astype(bf16)
     grad_shared_in = t_dot(low_two, grad_shared_pre).astype(bf16)
     grad_two = ring_scatter(two_parts, ctx_size, ctx_index)
-    dots = jnp.stack([grad_gates, gate_dots], axis=1)
+    dots = jnp.stack([gate_terms, scale_terms.reshape(ctx_size, token_count)], axis=1)
     dots = lax.all_to_all(dots, "ctx", split_axis=0, concat_axis=0, tiled=True)
-    grad_two, grad_shared_in, grad_shared_out, grad_expert_out, dots = after(
-        grad_two, grad_shared_in, grad_shared_out, grad_expert_out, dots
-    )
+    grad_two, grad_shared_in, grad_shared_out, grad_expert_out, dots, out_sum = after(
+        grad_two, grad_shared_in, grad_shared_out, grad_expert_out, dots, out_sum
+    )
+    output = (own_residual + out_sum.astype(f32)).astype(bf16).reshape(tokens.shape)
     sum_shared_in = grad_shared_in.reshape(ctx_size, fsdp_size, shard, 2 * fs_own)
     sum_shared_in = lax.psum_scatter(
         sum_shared_in.transpose(1, 0, 2, 3).reshape(width, 2 * fs_own),
@@ -419,11 +424,11 @@
     chosen_mask = jnp.any(
         own_chosen[..., None] == jnp.arange(expert_count, dtype=i32), axis=1
     )
-    grad_probs = jnp.where(chosen_mask, dots[:, 0].T, 0.0)
+    prob_terms = jnp.where(chosen_mask, dots[:, 0].T, 0.0)
     grad_logits = (
-        own_probs * (grad_probs - jnp.sum(own_probs * grad_probs, axis=-1, keepdims=True))
+        prob_terms - own_probs * jnp.sum(prob_terms, axis=-1, keepdims=True)
     ).astype(bf16)
-    grad_gate_pre = (jnp.sum(dots[:, 1], axis=0) * own_scale * (1.0 - own_scale)).astype(bf16)
+    grad_gate_pre = (jnp.sum(dots[:, 1], axis=0) * (1.0 - own_scale)).astype(bf16)
     grad_router = t_dot(own_low, grad_logits)
     grad_gate_vector = t_dot(own_low, grad_gate_pre[:, None])
     grad_two = grad_two + dot_t(grad_logits, router_weight)
@@ -436,13 +441,13 @@
     grad_mixed, sum_expert_in = after(grad_resid.astype(bf16), sum_expert_in)
     mixed_all = ring_gather(grad_mixed, ctx_size, ctx_index)
     grad_attn = dot_t(mixed_all, out_weight).astype(bf16).reshape(head_shape)
-    grad_attn, sum_shared_in, sum_shared_out = after(grad_attn, sum_shared_in, sum_shared_out)
-    sum_shared_in = lax.all_to_all(
-        sum_shared_in, "ctx", split_axis=0, concat_axis=0, tiled=True
-    )
     grad_weights = jnp.einsum("qhd,khd->hqk", grad_attn, values, preferred_element_type=f32)
     delta = jnp.sum(weights * grad_weights, axis=-1, keepdims=True)
     grad_scores = jnp.where(allowed[None], weights * (grad_weights - delta), 0.0).astype(bf16)
+    grad_scores, sum_shared_in = after(grad_scores, sum_shared_in)
+    sum_shared_in = lax.all_to_all(
+        sum_shared_in, "ctx", split_axis=0, concat_axis=0, tiled=True
+    )
     grad_q = jnp.einsum("hqk,khd->qhd", grad_scores, keys, preferred_element_type=f32) * score_scale
     grad_k = (
         jnp.einsum("hqk,qhd->khd", grad_scores, queries, preferred_element_type=f32) * score_scale
@@ -456,16 +461,14 @@
         ],
         axis=-1,
     ).astype(bf16)
-    grad_projected, sum_expert_out, sum_shared_in = after(
-        grad_projected, sum_expert_out, sum_shared_in
+    grad_projected, sum_shared_out, sum_shared_in = after(
+        grad_projected, sum_shared_out, sum_shared_in
     )
     one_sums = dot_t(grad_projected, qkv_weight)
     grad_gain_one = jnp.sum(one_sums * scaled_rows.astype(f32), axis=0)
     one_parts = one_sums.astype(bf16)
     one_kept, grad_projected = after(one_parts, grad_projected)
-    one_kept, out_parts = after(one_kept, out_parts)
-    output = own_residual + ring_scatter(out_parts, ctx_size, ctx_index)
-    output = output.astype(bf16).reshape(tokens.shape)
+    one_kept, sum_expert_out = after(one_kept, sum_expert_out)
     grad_normed = ring_scatter(one_parts, ctx_size, ctx_index, one_kept)
     grad_inputs_norm, unused = rms_back(
         own_tokens,

time: 789 us -> 802 us (1.016)
  waiting for transfers between devices: 243 us -> 289 us
  matrix products: 199 us -> 171 us
  other arithmetic: 100 us -> 88.6 us
  local copies, waits for them, and re-layouts: 107 us -> 116 us
    reduce_scatter x4, waiting for transfers between devices: 0.01 us -> 58.6 us  [sum_rows(): lax.psum_scatter(grad.astype(bf16), 'fsdp', scatter_dimension=0, tiled=True)]
    reduce_scatter x1, waiting for transfers between devices: 0.01 us -> 43.2 us  [local_split(): pieces = lax.psum_scatter(pieces, 'fsdp', scatter_dimension=0, tiled=True)]
    ppermute x9, waiting for transfers between devices: 23.2 us -> 61.7 us  [ring_gather(): fore = lax.ppermute(fore, 'ctx', ahead)]
    reduce_scatter x1, waiting for transfers between devices: 35.1 us -> 0.01 us  [local_split(): lax.psum_scatter(sum_shared_in.transpose(1, 0, 2, 3).reshape(width, 2 * f...]
    ppermute x9, waiting for transfers between devices: 32 us -> 0.02 us  [ring_gather(): rear = lax.ppermute(rear, 'ctx', back)]
    ppermute x12 -> x9, waiting for transfers between devices: 58 us -> 39.9 us  [ring_sums(): fore = lax.ppermute(fore, 'ctx', ahead)]
    all_to_all x1, waiting for transfers between devices: 17.6 us -> 0.01 us  [local_split(): lax.all_to_all(shared_in, 'ctx', split_axis=0, concat_axis=0, tiled=True)]
    all_gather x1, waiting for transfers between devices: 16.4 us -> 0.01 us  [local_split(): grad_rows = lax.all_gather(grad_rows, 'ctx', axis=0, tiled=True)]
  transfers between devices with their start and end apart: 75 -> 69, of which waited for: 42 -> 38; matrix products, arithmetic and copies ran while one was open for 42% -> 43% of each run, Pallas kernels for 0% -> 0%
where the time goes in v10:
time: 802 us; the launch traced here: 793 us
  waiting for transfers between devices  289 us (36%)
  matrix products  171 us (21%)
  local copies, waits for them, and re-layouts  116 us (14%)
  other arithmetic  88.6 us (11%)
  starting transfers between devices  77.8 us (10%)
  blocking collectives  29.7 us (4%)
  between operations  20.7 us (3%)
    ppermute x9, waiting for transfers between devices, ring_gather(): fore = lax.ppermute(fore, 'ctx', ahead)  61.7 us
    reduce_scatter x4, waiting for transfers between devices, sum_rows(): lax.psum_scatter(grad.astype(bf16), 'fsdp', scatter_dimension=0, tiled=True)  58.6 us
    dot_general x7, matrix products, dot_t(): lax.dot_general(a, b, (((1,), (1,)), ((), ())), preferred_element_type=f32)  49.9 us
    reduce_scatter x1, waiting for transfers between devices, local_split(): pieces = lax.psum_scatter(pieces, 'fsdp', scatter_dimension=0, tiled=True)  43.2 us
    dot_general x8, matrix products, dot(): return jnp.dot(a, b, preferred_element_type=f32)  42.4 us
    dot_general x8, matrix products, t_dot(): lax.dot_general(a, b, (((0,), (0,)), ((), ())), preferred_element_type=f32)  40 us
    ppermute x9, waiting for transfers between devices, ring_sums(): fore = lax.ppermute(fore, 'ctx', ahead)  39.9 us
    all_to_all x1, blocking collectives, local_split(): lax.all_to_all(pieces, 'ctx', split_axis=0, concat_axis=0, tiled=True)  29.7 us
  transfers between devices with their start and end apart: 69, of which 38 were waited for; matrix products, arithmetic and copies ran while one was open for 43% of the time, Pallas kernels for 0%

profile of v10, /device:TPU:8, one launch (start us, length us, event | category | flops | bytes accessed | tf_op | source)
XLA Modules:
  0.0 792.9 jit_solution(17527423366735802153)
XLA Ops:
  10.7 29.7 %all_to_all.25 = bf16[8,80,768]{2,1,0:T(8,128)(2,1)} all-to-all(bf16[8,80,768]{2,1,0:T(8,128)(2,1)S(1)} %pad_maximum_fusion.6), channel_id=1, replica_groups=mesh['ctx'=8,'fsdp'=4] {'ctx'}, dimensions={0} | all-to-all | bytes 1966080 | tf_op jit(solution)/shard_map/all_to_all | solution.py:270
  72.9 6.7 collective-permute-done.4
  85.3 6.3 collective-permute-done.6
  118.6 6.4 fusion.31
  146.3 6.6 collective-permute-done.12
  177.9 6.2 collective-permute-done.14
  233.4 7.2 collective-permute-done.24
  245.0 11.0 %collective-permute-done.26 = bf16[64,2048]{1,0:T(8,128)(2,1)S(1)} collective-permute-done((bf16[64,2048]{1,0:T(8,128)(2,1)S(1)}, bf16[64,2048]{1,0:T(8,128)(2,1)S(1)}, u32[]{:S(2)}, u32[]{:S(2)}) %collective-permute-start.26) | collective-permute-done | bytes 262176 | tf_op jit(solution)/shard_map/ppermute | solution.py:112
  269.9 10.3 %fusion.3 = f32[512,2816]{1,0:T(8,128)S(1)} fusion(bf16[512,2048]{1,0:T(8,128)(2,1)} %bitcast.344, bf16[1,2048,2816]{2,1,0:T(8,128)(2,1)} %all-gather.14.cloned.1.call-done), kind=kOutput, calls=%fused_computation.3 | convolution fusion | flops 5905580032 | bytes 19398656 | tf_op jit(solution)/shard_map/dot_general | solution.py:245
  294.0 8.6 %fusion.104 = f32[1024,1408]{1,0:T(8,128)S(1)} fusion(bf16[1024,2048]{1,0:T(8,128)(2,1)} %constant_dynamic-update-slice_fusion.6, bf16[2048,1408]{1,0:T(8,128)(2,1)S(1)} %bitcast.312), kind=kOutput, calls=%fused_computation.296 | convolution fusion | flops 5905580032 | bytes 15728640 | tf_op jit(solution)/shard_map/dot_general | solution.py:245
  307.2 5.6 fusion.9
  321.2 7.3 multiply_convert_fusion.6
  330.1 9.0 %convolution_convert_fusion = bf16[2048,2816]{1,0:T(8,128)(2,1)} fusion(bf16[512,2048]{1,0:T(8,128)(2,1)S(1)} %bitcast.345, bf16[512,1408]{1,0:T(8,128)(2,1)S(1)} %get-tuple-element.164, bf16[512,1408]{1,0:T(8,128)(2,1)S(1)} %get-tuple-element.163), kind=kOutput, calls=%fused_computation.5 | convolution fusion | flops 5917114368 | bytes 16515072 | tf_op jit(solution)/shard_map/dot_general | solution.py:251
  340.9 10.5 %multiply_convert_fusion.3 = (bf16[1024,704]{1,0:T(8,128)(2,1)}, bf16[1024,704]{1,0:T(8,128)(2,1)}, f32[1024]{0:T(1024)S(1)}) fusion(f32[1024,1408]{1,0:T(8,128)} %copy-done.7, bf16[1024,704]{1,0:T(8,128)(2,1)} %copy-done.39, bf16[1024,2048]{1,0:T(8,128)(2,1)} %multiply_convert_fusion, bf16[704,2048]{1,0:T(8,128)(2,1)S(1)} %bitcast.340), kind=kOutput, calls=%fused_computation.43 | convolution fusion | flops 2964323328 | bytes 17174528 | tf_op jit(solution)/shard_map/dot_general | solution.py:248
  358.6 9.9 %fusion.27 = bf16[512,2048]{1,0:T(8,128)(2,1)S(1)} fusion(bf16[1,2048,2816]{2,1,0:T(8,128)(2,1)} %all-gather.14.cloned.1.call-done, bf16[512,1408]{1,0:T(8,128)(2,1)} %copy-done.85, bf16[512,1408]{1,0:T(8,128)(2,1)S(1)} %copy-done.84), kind=kOutput, calls=%fused_computation.46 | convolution fusion | flops 5912395776 | bytes 16515072 | tf_op jit(solution)/shard_map/dot_general | solution.py:248
  369.9 7.5 fusion.7
  379.6 11.2 %convolution_convert_fusion.2 = bf16[2048,1408]{1,0:T(8,128)(2,1)} fusion(bf16[1024,2048]{1,0:T(8,128)(2,1)} %constant_dynamic-update-slice_fusion.6, bf16[1024,1408]{1,0:T(8,128)(2,1)S(1)} %pad_maximum_fusion.2), kind=kOutput, calls=%fused_computation.23 | convolution fusion | flops 5908463616 | bytes 12845056 | tf_op jit(solution)/shard_map/dot_general | solution.py:251
  404.0 7.5 collective-permute-done.35
  419.1 5.4 collective-permute-done.32
  441.5 5.8 copy.191
  451.1 52.0 %reduce-scatter.10.cloned.1.call-done = bf16[512,2816]{1,0:T(8,128)(2,1)} async-done(((bf16[2048,2816]{1,0:T(8,128)(2,1)}), bf16[512,2816]{1,0:T(8,128)(2,1)}) %reduce-scatter.10.cloned.1.call-update) | async-done | bytes 2883600 | tf_op jit(solution)/shard_map/reduce_scatter | solution.py:259
  505.2 11.6 %collective-permute-done.38 = bf16[128,2048]{1,0:T(8,128)(2,1)S(1)} collective-permute-done((bf16[128,2048]{1,0:T(8,128)(2,1)S(1)}, bf16[128,2048]{1,0:T(8,128)(2,1)S(1)}, u32[]{:S(2)}, u32[]{:S(2)}) %collective-permute-start.38) | collective-permute-done | bytes 524320 | tf_op jit(solution)/shard_map/ppermute | solution.py:106
  519.5 10.1 %collective-permute-done.40 = bf16[128,2048]{1,0:T(8,128)(2,1)S(1)} collective-permute-done((bf16[128,2048]{1,0:T(8,128)(2,1)S(1)}, bf16[128,2048]{1,0:T(8,128)(2,1)S(1)}, u32[]{:S(2)}, u32[]{:S(2)}) %collective-permute-start.40) | collective-permute-done | bytes 524320 | tf_op jit(solution)/shard_map/ppermute | solution.py:106
  531.8 9.7 %collective-permute-done.42 = bf16[128,2048]{1,0:T(8,128)(2,1)S(1)} collective-permute-done((bf16[128,2048]{1,0:T(8,128)(2,1)S(1)}, bf16[128,2048]{1,0:T(8,128)(2,1)S(1)}, u32[]{:S(2)}, u32[]{:S(2)}) %collective-permute-start.42) | collective-permute-done | bytes 524320 | tf_op jit(solution)/shard_map/ppermute | solution.py:106
  566.9 14.1 %select_convert_fusion = bf16[2,1024,1024]{1,2,0:T(8,128)(2,1)} fusion(f32[2,1024,1024]{1,2,0:T(8,128)} %copy-done.6, f32[2,1024]{1,0:T(2,128)S(1)} %copy-done.68, pred[1024,1024]{0,1:T(8,128)(4,1)S(1)} %copy-done.21, bf16[1024,2,128]{0,2,1:T(8,128)(2,1)} %bitcast.374, bf16[1024,2,128]{0,2,1:T(8,128)(2,1)} %bitcast.361), kind=kOutput, calls=%fused_computation.15 | convolution fusion | flops 1096813568 | bytes 14688256 | tf_op jit(solution)/shard_map/sub | solution.py:446
  600.2 14.1 %all-to-all-done.3 = bf16[8,64,1408]{2,1,0:T(8,128)(2,1)S(1)} async-done(((bf16[8,64,1408]{2,1,0:T(8,128)(2,1)}), bf16[8,64,1408]{2,1,0:T(8,128)(2,1)S(1)}, u32[]{:S(2)}, u32[]{:S(2)}) %all-to-all-start.3) | async-done | bytes 1441824 | tf_op jit(solution)/shard_map/all_to_all | solution.py:448
  614.3 9.8 %fusion.6 = (bf16[2048]{0:T(1024)(128)(2,1)}, bf16[1024,2048]{1,0:T(8,128)(2,1)}) fusion(bf16[1024,2048]{1,0:T(8,128)(2,1)} %constant_dynamic-update-slice_fusion.18, bf16[1024,768]{0,1:T(8,128)(2,1)} %pad_maximum_fusion.5, bf16[2048,768]{1,0:T(8,128)(2,1)} %bitcast.334), kind=kOutput, calls=%fused_computation.9 | convolution fusion | flops 3229612032 | bytes 13111296 | tf_op jit(solution)/shard_map/dot_general | solution.py:248
  632.9 6.3 fusion.24
  655.8 9.0 %collective-permute-done.51 = bf16[128,2048]{1,0:T(8,128)(2,1)S(1)} collective-permute-done((bf16[128,2048]{1,0:T(8,128)(2,1)S(1)}, bf16[128,2048]{1,0:T(8,128)(2,1)S(1)}, u32[]{:S(2)}, u32[]{:S(2)}) %collective-permute-start.51) | collective-permute-done | bytes 524320 | tf_op jit(solution)/shard_map/ppermute | solution.py:144
  688.1 43.2 %reduce-scatter.18.cloned.1.call-done = bf16[640,768]{1,0:T(8,128)(2,1)} async-done(((bf16[2560,768]{1,0:T(8,128)(2,1)}), bf16[640,768]{1,0:T(8,128)(2,1)}) %reduce-scatter.18.cloned.1.call-update) | async-done | bytes 983056 | tf_op jit(solution)/shard_map/reduce_scatter | solution.py:501
  731.3 6.1 all-to-all-start.4
  744.9 24.5 %collective-permute-done.49 = bf16[128,2048]{1,0:T(8,128)(2,1)S(1)} collective-permute-done((bf16[128,2048]{1,0:T(8,128)(2,1)S(1)}, bf16[128,2048]{1,0:T(8,128)(2,1)S(1)}, u32[]{:S(2)}, u32[]{:S(2)}) %collective-permute-start.49) | collective-permute-done | bytes 524320 | tf_op jit(solution)/shard_map/ppermute | solution.py:143
  (547 shorter events, 382.9 us)
Async XLA Ops:
  7.2 97.3 %all-gather.10.cloned.1.call-start = ((), (), s32[]{:S(2)}) async-start(), calls=%async_computation.20 | async-start | bytes 4915200 | tf_op jit(solution)/shard_map/all_gather | solution.py:274
  40.5 229.4 %all-gather.14.cloned.1.call-start = ((), (), s32[]{:S(2)}) async-start(), calls=%async_computation.22 | async-start | bytes 14417920 | tf_op jit(solution)/shard_map/all_gather | solution.py:289
  45.2 22.3 %collective-permute-start.2 = (bf16[128,2048]{1,0:T(8,128)(2,1)}, bf16[128,2048]{1,0:T(8,128)(2,1)}, u32[]{:S(2)}, u32[]{:S(2)}) collective-permute-start(bf16[128,2048]{1,0:T(8,128)(2,1)} %get-tuple-element.256), channel_id=1, source_target_pairs={{0,8},{8,16},{16,24},{24,28},{28,20},{20,12},{12,4},{4,0},{1,9},{9... | collective-permute-start | bytes 1572872 | tf_op jit(solution)/shard_map/ppermute | solution.py:106
  45.7 22.3 %collective-permute-start.3 = (bf16[128,2048]{1,0:T(8,128)(2,1)}, bf16[128,2048]{1,0:T(8,128)(2,1)S(1)}, u32[]{:S(2)}, u32[]{:S(2)}) collective-permute-start(bf16[128,2048]{1,0:T(8,128)(2,1)} %get-tuple-element.256), channel_id=1, source_target_pairs={{8,0},{16,8},{24,16},{28,24},{20,28},{12,20},{4,12},{0,4},{9,1},{1... | collective-permute-start | bytes 1572872 | tf_op jit(solution)/shard_map/ppermute | solution.py:107
  47.2 79.9 %collective-permute-start.10 = (bf16[64,2048]{1,0:T(8,128)(2,1)}, bf16[64,2048]{1,0:T(8,128)(2,1)}, u32[]{:S(2)}, u32[]{:S(2)}) collective-permute-start(bf16[64,2048]{1,0:T(8,128)(2,1)} %param.27), channel_id=1, source_target_pairs={{0,2},{1,3},{2,0},{3,1},{4,6},{5,7},{6,4},{7,5},{8,10},{9,11},{10,... | collective-permute-start | bytes 786440 | tf_op jit(solution)/shard_map/ppermute | solution.py:169
  48.7 88.1 %collective-permute-start.1 = (bf16[176,2048]{1,0:T(8,128)(2,1)}, bf16[176,2048]{1,0:T(8,128)(2,1)}, u32[]{:S(2)}, u32[]{:S(2)}) collective-permute-start(bf16[176,2048]{1,0:T(8,128)(2,1)} %param.33), channel_id=1, source_target_pairs={{0,2},{1,3},{2,0},{3,1},{4,6},{5,7},{6,4},{7,5},{8,10},{9,11},{10,... | collective-permute-start | bytes 2162696 | tf_op jit(solution)/shard_map/ppermute | solution.py:169
  49.2 87.6 %collective-permute-start = (bf16[352,2048]{1,0:T(8,128)(2,1)}, bf16[352,2048]{1,0:T(8,128)(2,1)}, u32[]{:S(2)}, u32[]{:S(2)}) collective-permute-start(bf16[352,2048]{1,0:T(8,128)(2,1)} %bitcast.1), channel_id=1, source_target_pairs={{0,2},{1,3},{2,0},{3,1},{4,6},{5,7},{6,4},{7,5},{8,10},{9,11},{10,... | collective-permute-start | bytes 4325384 | tf_op jit(solution)/shard_map/ppermute | solution.py:169
  99.5 42.3 %all-to-all-start.1 = ((bf16[8,64,1408]{2,1,0:T(8,128)(2,1)}), bf16[8,64,1408]{2,1,0:T(8,128)(2,1)S(1)}, u32[]{:S(2)}, u32[]{:S(2)}) async-start(bf16[8,64,1408]{2,1,0:T(8,128)(2,1)} %reshape.829), calls=%async_computation.1 | async-start | bytes 2883584 | tf_op jit(solution)/shard_map/all_to_all | solution.py:273
  104.4 183.8 %all-gather.12.cloned.1.call-start = ((), (), s32[]{:S(2)}) async-start(), calls=%async_computation.21 | async-start | bytes 7208960 | tf_op jit(solution)/shard_map/all_gather | solution.py:326
  142.9 169.9 %all-gather.8.cloned.1.call-start = ((), (), s32[]{:S(2)}) async-start(), calls=%async_computation.12 | async-start | bytes 4718592 | tf_op jit(solution)/shard_map/all_gather | solution.py:334
  162.2 56.5 %collective-permute-start.28 = (bf16[2,352,2048]{2,1,0:T(8,128)(2,1)}, bf16[2,352,2048]{2,1,0:T(8,128)(2,1)}, u32[]{:S(2)}, u32[]{:S(2)}) collective-permute-start(bf16[2,352,2048]{2,1,0:T(8,128)(2,1)} %maximum_select_fusion.1), channel_id=1, source_target_pairs={{0,1},{1,0},{2,3},{3,2},{4,5},{5,4},{6,7},{7,6},{8,9},{9,8},{10,11... | collective-permute-start | bytes 8650760 | tf_op jit(solution)/shard_map/ppermute | solution.py:174
  177.8 31.4 %collective-permute-start.29 = (bf16[2,176,2048]{2,1,0:T(8,128)(2,1)S(1)}, bf16[2,176,2048]{2,1,0:T(8,128)(2,1)}, u32[]{:S(2)}, u32[]{:S(2)}) collective-permute-start(bf16[2,176,2048]{2,1,0:T(8,128)(2,1)S(1)} %maximum_select_fusion.3), channel_id=1, source_target_pairs={{0,1},{1,0},{2,3},{3,2},{4,5},{5,4},{6,7},{7,6},{8,9},{9,8},{10,11... | collective-permute-start | bytes 4325384 | tf_op jit(solution)/shard_map/ppermute | solution.py:174
  231.7 209.7 %reduce-scatter.8.cloned.1.call-start = ((), (), s32[]{:S(2)}) async-start(), calls=%async_computation.13 | async-start | bytes 4718592 | tf_op jit(solution)/shard_map/reduce_scatter | solution.py:376
  240.7 15.3 %collective-permute-start.26 = (bf16[64,2048]{1,0:T(8,128)(2,1)S(1)}, bf16[64,2048]{1,0:T(8,128)(2,1)S(1)}, u32[]{:S(2)}, u32[]{:S(2)}) collective-permute-start(bf16[64,2048]{1,0:T(8,128)(2,1)S(1)} %slice.465), channel_id=1, source_target_pairs={{0,8},{8,16},{16,24},{24,28},{28,20},{20,12},{12,4},{4,0},{1,9},{9... | collective-permute-start | bytes 786440 | tf_op jit(solution)/shard_map/ppermute | solution.py:112
  242.3 18.4 %collective-permute-start.27 = (bf16[64,2048]{1,0:T(8,128)(2,1)S(1)}, bf16[64,2048]{1,0:T(8,128)(2,1)S(1)}, u32[]{:S(2)}, u32[]{:S(2)}) collective-permute-start(bf16[64,2048]{1,0:T(8,128)(2,1)S(1)} %slice.466), channel_id=1, source_target_pairs={{8,0},{16,8},{24,16},{28,24},{20,28},{12,20},{4,12},{0,4},{9,1},{1... | collective-permute-start | bytes 786440 | tf_op jit(solution)/shard_map/ppermute | solution.py:113
  312.8 190.3 %reduce-scatter.10.cloned.1.call-start = ((), (), s32[]{:S(2)}) async-start(), calls=%async_computation.14 | async-start | bytes 14417920 | tf_op jit(solution)/shard_map/reduce_scatter | solution.py:259
  352.0 89.4 %all-to-all-start.2 = ((f32[8,2,128]{2,1,0:T(2,128)}), f32[8,2,128]{2,1,0:T(2,128)S(1)}, u32[]{:S(2)}, u32[]{:S(2)}) async-start(f32[8,2,128]{2,1,0:T(2,128)} %pad_maximum_fusion.15), calls=%async_computation.2 | async-start | bytes 16384 | tf_op jit(solution)/shard_map/all_to_all | solution.py:407
  355.7 225.3 %reduce-scatter.12.cloned.1.call-start = ((), (), s32[]{:S(2)}) async-start(), calls=%async_computation.15 | async-start | bytes 7208960 | tf_op jit(solution)/shard_map/reduce_scatter | solution.py:413
  377.5 16.0 %collective-permute-start.30 = (bf16[64,2048]{1,0:T(8,128)(2,1)S(1)}, bf16[64,2048]{1,0:T(8,128)(2,1)S(1)}, u32[]{:S(2)}, u32[]{:S(2)}) collective-permute-start(bf16[64,2048]{1,0:T(8,128)(2,1)S(1)} %get-tuple-element.183), channel_id=1, source_target_pairs={{0,8},{8,16},{16,24},{24,28},{28,20},{20,12},{12,4},{4,0},{1,9},{9... | collective-permute-start | bytes 786440 | tf_op jit(solution)/shard_map/ppermute | solution.py:134
  379.0 17.7 %collective-permute-start.34 = (bf16[64,2048]{1,0:T(8,128)(2,1)S(1)}, bf16[64,2048]{1,0:T(8,128)(2,1)S(1)}, u32[]{:S(2)}, u32[]{:S(2)}) collective-permute-start(bf16[64,2048]{1,0:T(8,128)(2,1)S(1)} %get-tuple-element.184), channel_id=1, source_target_pairs={{8,0},{16,8},{24,16},{28,24},{20,28},{12,20},{4,12},{0,4},{9,1},{1... | collective-permute-start | bytes 786440 | tf_op jit(solution)/shard_map/ppermute | solution.py:135
  396.9 14.6 %collective-permute-start.35 = (bf16[128,2048]{1,0:T(8,128)(2,1)S(1)}, bf16[128,2048]{1,0:T(8,128)(2,1)S(1)}, u32[]{:S(2)}, u32[]{:S(2)}) collective-permute-start(bf16[128,2048]{1,0:T(8,128)(2,1)S(1)} %pad_maximum_fusion.12), channel_id=1, source_target_pairs={{8,0},{16,8},{24,16},{28,24},{20,28},{12,20},{4,12},{0,4},{9,1},{1... | collective-permute-start | bytes 1572872 | tf_op jit(solution)/shard_map/ppermute | solution.py:144
  447.3 152.9 %reduce-scatter.14.cloned.1.call-start = ((), (), s32[]{:S(2)}) async-start(), calls=%async_computation.16 | async-start | bytes 3604480 | tf_op jit(solution)/shard_map/reduce_scatter | solution.py:259
  448.1 225.0 %reduce-scatter.20.cloned.1.call-start = ((), (), s32[]{:S(2)}) async-start(), calls=%async_computation.19 | async-start | bytes 1310720 | tf_op jit(solution)/shard_map/reduce_scatter | solution.py:259
  504.6 13.7 %collective-permute-start.39 = (bf16[128,2048]{1,0:T(8,128)(2,1)S(1)}, bf16[128,2048]{1,0:T(8,128)(2,1)S(1)}, u32[]{:S(2)}, u32[]{:S(2)}) collective-permute-start(bf16[128,2048]{1,0:T(8,128)(2,1)S(1)} %fusion.96), channel_id=1, source_target_pairs={{8,0},{16,8},{24,16},{28,24},{20,28},{12,20},{4,12},{0,4},{9,1},{1... | collective-permute-start | bytes 1572872 | tf_op jit(solution)/shard_map/ppermute | solution.py:107
  553.9 131.9 %reduce-scatter.16.cloned.1.call-start = ((), (), s32[]{:S(2)}) async-start(), calls=%async_computation.17 | async-start | bytes 7208960 | tf_op jit(solution)/shard_map/reduce_scatter | solution.py:259
  581.0 33.3 %all-to-all-start.3 = ((bf16[8,64,1408]{2,1,0:T(8,128)(2,1)}), bf16[8,64,1408]{2,1,0:T(8,128)(2,1)S(1)}, u32[]{:S(2)}, u32[]{:S(2)}) async-start(bf16[8,64,1408]{2,1,0:T(8,128)(2,1)} %bitcast.350), calls=%async_computation.7 | async-start | bytes 2883584 | tf_op jit(solution)/shard_map/all_to_all | solution.py:448
  586.2 145.2 %reduce-scatter.18.cloned.1.call-start = ((), (), s32[]{:S(2)}) async-start(), calls=%async_computation.18 | async-start | bytes 4915200 | tf_op jit(solution)/shard_map/reduce_scatter | solution.py:501
  667.7 69.7 %collective-permute-start.48 = (bf16[128,2048]{1,0:T(8,128)(2,1)}, bf16[128,2048]{1,0:T(8,128)(2,1)}, u32[]{:S(2)}, u32[]{:S(2)}) collective-permute-start(bf16[128,2048]{1,0:T(8,128)(2,1)} %get-tuple-element.169), channel_id=1, source_target_pairs={{0,8},{8,16},{16,24},{24,28},{28,20},{20,12},{12,4},{4,0},{1,9},{9... | collective-permute-start | bytes 1572872 | tf_op jit(solution)/shard_map/ppermute | solution.py:143
  669.9 67.6 %collective-permute-start.52 = (bf16[128,2048]{1,0:T(8,128)(2,1)}, bf16[128,2048]{1,0:T(8,128)(2,1)}, u32[]{:S(2)}, u32[]{:S(2)}) collective-permute-start(bf16[128,2048]{1,0:T(8,128)(2,1)} %get-tuple-element.170), channel_id=1, source_target_pairs={{8,0},{16,8},{24,16},{28,24},{20,28},{12,20},{4,12},{0,4},{9,1},{1... | collective-permute-start | bytes 1572872 | tf_op jit(solution)/shard_map/ppermute | solution.py:144
  731.3 45.0 %all-to-all-start.4 = ((bf16[8,80,768]{2,1,0:T(8,128)(2,1)}), bf16[8,80,768]{2,1,0:T(8,128)(2,1)S(1)}, u32[]{:S(2)}, u32[]{:S(2)}) async-start(bf16[8,80,768]{2,1,0:T(8,128)(2,1)} %bitcast.357), calls=%async_computation.10 | async-start | bytes 1966080 | tf_op jit(solution)/shard_map/all_to_all | solution.py:503
  739.5 29.8 %collective-permute-start.49 = (bf16[128,2048]{1,0:T(8,128)(2,1)S(1)}, bf16[128,2048]{1,0:T(8,128)(2,1)S(1)}, u32[]{:S(2)}, u32[]{:S(2)}) collective-permute-start(bf16[128,2048]{1,0:T(8,128)(2,1)S(1)} %get-tuple-element.167), channel_id=1, source_target_pairs={{0,8},{8,16},{16,24},{24,28},{28,20},{20,12},{12,4},{4,0},{1,9},{9... | collective-permute-start | bytes 1572872 | tf_op jit(solution)/shard_map/ppermute | solution.py:143
  741.0 30.6 %collective-permute-start.53 = (bf16[128,2048]{1,0:T(8,128)(2,1)S(1)}, bf16[128,2048]{1,0:T(8,128)(2,1)S(1)}, u32[]{:S(2)}, u32[]{:S(2)}) collective-permute-start(bf16[128,2048]{1,0:T(8,128)(2,1)S(1)} %get-tuple-element.168), channel_id=1, source_target_pairs={{8,0},{16,8},{24,16},{28,24},{20,28},{12,20},{4,12},{0,4},{9,1},{1... | collective-permute-start | bytes 1572872 | tf_op jit(solution)/shard_map/ppermute | solution.py:144
  (132 other events, 1423.8 us)
Sparse Core Ops, SparseCore 0:
  40.6 53.4 all-gather.9
  95.6 89.2 all-gather.13
  187.0 43.5 all-gather.11
  232.6 75.5 all-gather.7
  313.0 95.8 reduce-scatter.7
  411.4 91.6 reduce-scatter.9
  505.8 54.8 reduce-scatter.11
  563.9 36.3 reduce-scatter.13
  603.5 24.8 reduce-scatter.19
  630.8 54.8 reduce-scatter.15
  688.4 42.8 reduce-scatter.17

commit v11 on v10

--- a/solution.py
+++ b/solution.py
@@ -176,6 +176,20 @@
     out = lax.dynamic_update_index_in_dim(out, pair, index % 2, 1)
     out = lax.dynamic_update_index_in_dim(out, near, 1 - index % 2, 1)
     return (out.reshape(size * rows, width), hold)
+
+
+def fsdp_scatter(grad, size):
+    index = lax.axis_index("fsdp")
+    core, chip = index % 2, index // 2
+    grad = grad.reshape((2, 2) + grad.shape[1:])
+
+    def pick(array, at, axis):
+        return lax.dynamic_index_in_dim(array, at, axis, keepdims=False)
+
+    near = lax.ppermute(pick(grad, 1 - core, 1), "fsdp", other_core(size))
+    mine = (pick(grad, core, 1).astype(jnp.float32) + near.astype(jnp.float32)).astype(grad.dtype)
+    far = lax.ppermute(pick(mine, 1 - chip, 0), "fsdp", other_chip(size))
+    return pick(mine, chip, 0).astype(jnp.float32) + far.astype(jnp.float32)
 
 
 def column_pieces(weight, groups, size, extra):
@@ -405,10 +419,9 @@
     grad_two = ring_scatter(two_parts, ctx_size, ctx_index)
     dots = jnp.stack([gate_terms, scale_terms.reshape(ctx_size, token_count)], axis=1)
     dots = lax.all_to_all(dots, "ctx", split_axis=0, concat_axis=0, tiled=True)
-    grad_two, grad_shared_in, grad_shared_out, grad_expert_out, dots, out_sum = after(
-        grad_two, grad_shared_in, grad_shared_out, grad_expert_out, dots, out_sum
-    )
-    output = (own_residual + out_sum.astype(f32)).astype(bf16).reshape(tokens.shape)
+    grad_two, grad_shared_in, grad_shared_out, grad_expert_out, dots = after(
+        grad_two, grad_shared_in, grad_shared_out, grad_expert_out, dots
+    )
     sum_shared_in = grad_shared_in.reshape(ctx_size, fsdp_size, shard, 2 * fs_own)
     sum_shared_in = lax.psum_scatter(
         sum_shared_in.transpose(1, 0, 2, 3).reshape(width, 2 * fs_own),
@@ -416,8 +429,7 @@
         scatter_dimension=0,
         tiled=True,
     ).reshape(ctx_size, shard, 2 * fs_own)
-    sum_shared_out = sum_rows(grad_shared_out)
-    sum_expert_out = sum_rows(grad_expert_out)
+    sum_expert_out = fsdp_scatter(grad_expert_out.reshape(fsdp_size, -1, width), fsdp_size)
     own_probs = own_rows(probs_all)
     own_scale = own_rows(scale_all)
     own_chosen = routes.reshape(token_count, top_count)
@@ -441,13 +453,13 @@
     grad_mixed, sum_expert_in = after(grad_resid.astype(bf16), sum_expert_in)
     mixed_all = ring_gather(grad_mixed, ctx_size, ctx_index)
     grad_attn = dot_t(mixed_all, out_weight).astype(bf16).reshape(head_shape)
+    grad_attn, sum_shared_in = after(grad_attn, sum_shared_in)
+    sum_shared_in = lax.all_to_all(
+        sum_shared_in, "ctx", split_axis=0, concat_axis=0, tiled=True
+    )
     grad_weights = jnp.einsum("qhd,khd->hqk", grad_attn, values, preferred_element_type=f32)
     delta = jnp.sum(weights * grad_weights, axis=-1, keepdims=True)
     grad_scores = jnp.where(allowed[None], weights * (grad_weights - delta), 0.0).astype(bf16)
-    grad_scores, sum_shared_in = after(grad_scores, sum_shared_in)
-    sum_shared_in = lax.all_to_all(
-        sum_shared_in, "ctx", split_axis=0, concat_axis=0, tiled=True
-    )
     grad_q = jnp.einsum("hqk,khd->qhd", grad_scores, keys, preferred_element_type=f32) * score_scale
     grad_k = (
         jnp.einsum("hqk,qhd->khd", grad_scores, queries, preferred_element_type=f32) * score_scale
@@ -461,14 +473,13 @@
         ],
         axis=-1,
     ).astype(bf16)
-    grad_projected, sum_shared_out, sum_shared_in = after(
-        grad_projected, sum_shared_out, sum_shared_in
-    )
+    grad_projected, out_sum, sum_expert_out = after(grad_projected, out_sum, sum_expert_out)
+    output = (own_residual + out_sum.astype(f32)).astype(bf16).reshape(tokens.shape)
     one_sums = dot_t(grad_projected, qkv_weight)
     grad_gain_one = jnp.sum(one_sums * scaled_rows.astype(f32), axis=0)
     one_parts = one_sums.astype(bf16)
     one_kept, grad_projected = after(one_parts, grad_projected)
-    one_kept, sum_expert_out = after(one_kept, sum_expert_out)
+    one_kept, sum_shared_in = after(one_kept, sum_shared_in)
     grad_normed = ring_scatter(one_parts, ctx_size, ctx_index, one_kept)
     grad_inputs_norm, unused = rms_back(
         own_tokens,
@@ -499,6 +510,8 @@
     )
     pieces = pieces.transpose(1, 0, 2, 3).reshape(-1, 3 * own_width)
     pieces = lax.psum_scatter(pieces, "fsdp", scatter_dimension=0, tiled=True)
+    pieces, grad_shared_out = after(pieces, grad_shared_out)
+    sum_shared_out = sum_rows(grad_shared_out)
     pieces = pieces.reshape(ctx_size, shard + more, 3 * own_width)
     pieces = lax.all_to_all(pieces, "ctx", split_axis=0, concat_axis=0, tiled=True)
     small_grads = jnp.sum(pieces[:, shard:].reshape(ctx_size, -1).astype(f32), axis=0)
@@ -515,7 +528,7 @@
         merge_columns(sum_shared_in, 2, ctx_size),
         sum_shared_out.astype(f32),
         sum_expert_in.astype(f32)[None],
-        sum_expert_out.astype(f32)[None],
+        sum_expert_out[None],
     )
 
 

time: 802 us -> 793 us (0.989)
  waiting for transfers between devices: 289 us -> 239 us
  matrix products: 171 us -> 194 us
  other arithmetic: 88.6 us -> 102 us
    reduce_scatter x4 -> x3, waiting for transfers between devices: 58.6 us -> 0.01 us  [sum_rows(): lax.psum_scatter(grad.astype(bf16), 'fsdp', scatter_dimension=0, tiled=True)]
    ppermute x0 -> x2, waiting for transfers between devices: none -> 52.1 us  [the longest x1 45.2 us: fsdp_scatter(): far = lax.ppermute(pick(mine, 1 - chip, 0), 'fsdp', other_chip(size))]
    reduce_scatter x1, waiting for transfers between devices: 43.2 us -> 24.7 us  [local_split(): pieces = lax.psum_scatter(pieces, 'fsdp', scatter_dimension=0, tiled=True)]
    dot_general x1, matrix products: 0.83 us -> 17 us  [local_split(): jnp.einsum('hqk,khd->qhd', grad_scores, keys, preferred_element_type=f32)]
    sub x1 -> x0, matrix products: 14.1 us -> none  [local_split(): grad_weights - delta]
    all_to_all x1, waiting for transfers between devices: 14.1 us -> 0.01 us  [local_split(): lax.all_to_all(sum_shared_in, 'ctx', split_axis=0, concat_axis=0, tiled=T...]
    ppermute x9, waiting for transfers between devices: 39.9 us -> 28.1 us  [ring_sums(): fore = lax.ppermute(fore, 'ctx', ahead)]
    dot_general x1, matrix products: 4.02 us -> 15.8 us  [local_split(): jnp.einsum('hqk,qhd->khd', grad_scores, queries, preferred_element_type=f32)]
  transfers between devices with their start and end apart: 69 -> 70, of which waited for: 38 -> 34; matrix products, arithmetic and copies ran while one was open for 43% -> 43% of each run, Pallas kernels for 0% -> 0%
where the time goes in v11:
time: 793 us; the launch traced here: 782 us
  waiting for transfers between devices  239 us (30%)
  matrix products  194 us (24%)
  local copies, waits for them, and re-layouts  115 us (15%)
  other arithmetic  102 us (13%)
  starting transfers between devices  81.2 us (10%)
  blocking collectives  29.7 us (4%)
  between operations  21.1 us (3%)
    ppermute x9, waiting for transfers between devices, ring_gather(): fore = lax.ppermute(fore, 'ctx', ahead)  59 us
    dot_general x7, matrix products, dot_t(): lax.dot_general(a, b, (((1,), (1,)), ((), ())), preferred_element_type=f32)  47.7 us
    ppermute x1, waiting for transfers between devices, fsdp_scatter(): far = lax.ppermute(pick(mine, 1 - chip, 0), 'fsdp', other_chip(size))  45.2 us
    dot_general x8, matrix products, t_dot(): lax.dot_general(a, b, (((0,), (0,)), ((), ())), preferred_element_type=f32)  44.1 us
    dot_general x8, matrix products, dot(): return jnp.dot(a, b, preferred_element_type=f32)  43.2 us
    all_to_all x1, blocking collectives, local_split(): lax.all_to_all(pieces, 'ctx', split_axis=0, concat_axis=0, tiled=True)  29.7 us
    ppermute x9, waiting for transfers between devices, ring_sums(): fore = lax.ppermute(fore, 'ctx', ahead)  28.1 us
    ppermute x9, waiting for transfers between devices, ring_sums(): rear = lax.ppermute(rear, 'ctx', back)  25.7 us
  transfers between devices with their start and end apart: 70, of which 34 were waited for; matrix products, arithmetic and copies ran while one was open for 43% of the time, Pallas kernels for 0%

profile of v11, /device:TPU:8, one launch (start us, length us, event | category | flops | bytes accessed | tf_op | source)
XLA Modules:
  0.0 781.7 jit_solution(14702783600834693603)
XLA Ops:
  10.7 29.7 %all_to_all.25 = bf16[8,80,768]{2,1,0:T(8,128)(2,1)} all-to-all(bf16[8,80,768]{2,1,0:T(8,128)(2,1)S(1)} %pad_maximum_fusion.6), channel_id=1, replica_groups=mesh['ctx'=8,'fsdp'=4] {'ctx'}, dimensions={0} | all-to-all | bytes 1966080 | tf_op jit(solution)/shard_map/all_to_all | solution.py:284
  72.9 6.7 collective-permute-done.4
  85.3 6.2 collective-permute-done.6
  118.6 6.4 fusion.52
  146.3 6.6 collective-permute-done.12
  177.9 6.1 collective-permute-done.14
  233.5 7.1 collective-permute-done.24
  244.7 11.2 %collective-permute-done.26 = bf16[64,2048]{1,0:T(8,128)(2,1)S(1)} collective-permute-done((bf16[64,2048]{1,0:T(8,128)(2,1)S(1)}, bf16[64,2048]{1,0:T(8,128)(2,1)S(1)}, u32[]{:S(2)}, u32[]{:S(2)}) %collective-permute-start.26) | collective-permute-done | bytes 262176 | tf_op jit(solution)/shard_map/ppermute | solution.py:112
  269.1 11.1 %fusion.3 = f32[512,2816]{1,0:T(8,128)S(1)} fusion(bf16[512,2048]{1,0:T(8,128)(2,1)} %bitcast.354, bf16[1,2048,2816]{2,1,0:T(8,128)(2,1)} %all-gather.14.cloned.1.call-done), kind=kOutput, calls=%fused_computation.3 | convolution fusion | flops 5905580032 | bytes 19398656 | tf_op jit(solution)/shard_map/dot_general | solution.py:259
  295.0 8.5 %fusion.140 = f32[1024,1408]{1,0:T(8,128)S(1)} fusion(bf16[1024,2048]{1,0:T(8,128)(2,1)} %constant_dynamic-update-slice_fusion.3, bf16[2048,1408]{1,0:T(8,128)(2,1)S(1)} %bitcast.319), kind=kOutput, calls=%fused_computation.312 | convolution fusion | flops 5905580032 | bytes 15728640 | tf_op jit(solution)/shard_map/dot_general | solution.py:259
  321.8 7.4 multiply_convert_fusion.6
  330.8 9.1 %convolution_convert_fusion = bf16[2048,2816]{1,0:T(8,128)(2,1)} fusion(bf16[512,2048]{1,0:T(8,128)(2,1)S(1)} %bitcast.355, bf16[512,1408]{1,0:T(8,128)(2,1)S(1)} %get-tuple-element.166, bf16[512,1408]{1,0:T(8,128)(2,1)S(1)} %get-tuple-element.165), kind=kOutput, calls=%fused_computation.5 | convolution fusion | flops 5917114368 | bytes 16515072 | tf_op jit(solution)/shard_map/dot_general | solution.py:265
  340.2 11.6 %multiply_convert_fusion.3 = (bf16[1024,704]{1,0:T(8,128)(2,1)}, bf16[1024,704]{1,0:T(8,128)(2,1)}, f32[1024]{0:T(1024)S(1)}) fusion(f32[1024,1408]{1,0:T(8,128)} %copy-done.7, bf16[1024,704]{1,0:T(8,128)(2,1)} %copy-done.36, bf16[1024,2048]{1,0:T(8,128)(2,1)} %multiply_convert_fusion, bf16[704,2048]{1,0:T(8,128)(2,1)S(1)} %bitcast.348), kind=kOutput, calls=%fused_computation.53 | convolution fusion | flops 2964323328 | bytes 17174528 | tf_op jit(solution)/shard_map/dot_general | solution.py:262
  359.5 9.6 %fusion.48 = bf16[512,2048]{1,0:T(8,128)(2,1)S(1)} fusion(bf16[1,2048,2816]{2,1,0:T(8,128)(2,1)} %all-gather.14.cloned.1.call-done, bf16[512,1408]{1,0:T(8,128)(2,1)} %copy-done.87, bf16[512,1408]{1,0:T(8,128)(2,1)S(1)} %copy-done.86), kind=kOutput, calls=%fused_computation.56 | convolution fusion | flops 5912395776 | bytes 16515072 | tf_op jit(solution)/shard_map/dot_general | solution.py:262
  370.4 7.5 fusion.7
  380.1 11.7 %convolution_convert_fusion.2 = bf16[2048,1408]{1,0:T(8,128)(2,1)} fusion(bf16[1024,2048]{1,0:T(8,128)(2,1)} %constant_dynamic-update-slice_fusion.3, bf16[1024,1408]{1,0:T(8,128)(2,1)S(1)} %pad_maximum_fusion.2), kind=kOutput, calls=%fused_computation.23 | convolution fusion | flops 5908463616 | bytes 12845056 | tf_op jit(solution)/shard_map/dot_general | solution.py:265
  409.7 6.9 collective-permute-done.32
  444.3 6.9 collective-permute-done.46
  466.0 8.9 %collective-permute-done.38 = bf16[128,2048]{1,0:T(8,128)(2,1)} collective-permute-done((bf16[128,2048]{1,0:T(8,128)(2,1)}, bf16[128,2048]{1,0:T(8,128)(2,1)}, u32[]{:S(2)}, u32[]{:S(2)}) %collective-permute-start.38) | collective-permute-done | bytes 524320 | tf_op jit(solution)/shard_map/ppermute | solution.py:106
  476.9 45.2 %collective-permute-done.47 = bf16[352,2048]{1,0:T(8,128)(2,1)} collective-permute-done((bf16[352,2048]{1,0:T(8,128)(2,1)}, bf16[352,2048]{1,0:T(8,128)(2,1)}, u32[]{:S(2)}, u32[]{:S(2)}) %collective-permute-start.47) | collective-permute-done | bytes 1441824 | tf_op jit(solution)/shard_map/ppermute | solution.py:191
  532.5 20.0 %collective-permute-done.42 = bf16[128,2048]{1,0:T(8,128)(2,1)S(1)} collective-permute-done((bf16[128,2048]{1,0:T(8,128)(2,1)S(1)}, bf16[128,2048]{1,0:T(8,128)(2,1)S(1)}, u32[]{:S(2)}, u32[]{:S(2)}) %collective-permute-start.42) | collective-permute-done | bytes 524320 | tf_op jit(solution)/shard_map/ppermute | solution.py:106
  553.0 7.3 collective-permute-done.43
  564.8 13.8 %collective-permute-done.45 = bf16[64,2048]{1,0:T(8,128)(2,1)S(1)} collective-permute-done((bf16[64,2048]{1,0:T(8,128)(2,1)S(1)}, bf16[64,2048]{1,0:T(8,128)(2,1)S(1)}, u32[]{:S(2)}, u32[]{:S(2)}) %collective-permute-start.45) | collective-permute-done | bytes 262176 | tf_op jit(solution)/shard_map/ppermute | solution.py:113
  588.4 15.8 %fusion.59 = f32[1024,2,128]{0,2,1:T(8,128)} fusion(bf16[1024,2,128]{0,2,1:T(8,128)(2,1)} %copy-done.51, f32[2,1024,1024]{1,2,0:T(8,128)} %fusion.142, f32[2,1024,1024]{1,2,0:T(8,128)} %copy-done.6, f32[2,1024]{1,0:T(2,128)S(1)} %copy-done.71, pred[1024,1024]{0,1:T(8,128)(4,1)} %copy-done.18), kind=kOutput, calls=%fused_computation.84 | convolution fusion | flops 559942656 | bytes 19406848 | tf_op jit(solution)/shard_map/hqk,qhd->khd/dot_general | solution.py:465
  604.2 17.0 %broadcast_multiply_fusion.1 = (f32[1024,2,128]{0,2,1:T(8,128)}, f32[1024,2,128]{0,2,1:T(8,128)}, f32[1024,2,128]{0,2,1:T(8,128)}) fusion(f32[1024,128]{0,1:T(8,128)} %get-tuple-element.243, f32[1024,2,128]{0,2,1:T(8,128)} %fusion.59, bf16[1024,2,128]{0,2,1:T(8,128)(2,1)S(1)} %copy-done.50, f32[2,1024,1024]{1,2,0:T(8,128)} %fusion.142, ...), kind=kOutput, calls=%fused_computation.160 | convolution fusion | flops 560466944 | bytes 23076864 | tf_op jit(solution)/shard_map/hqk,khd->qhd/dot_general | solution.py:463
  632.1 9.2 %fusion.6 = (bf16[2048]{0:T(1024)(128)(2,1)S(1)}, bf16[1024,2048]{1,0:T(8,128)(2,1)}) fusion(bf16[1024,2048]{1,0:T(8,128)(2,1)} %constant_dynamic-update-slice_fusion.18, bf16[1024,768]{0,1:T(8,128)(2,1)} %pad_maximum_fusion.5, bf16[2048,768]{1,0:T(8,128)(2,1)} %bitcast.341), kind=kOutput, calls=%fused_computation.9 | convolution fusion | flops 3229612032 | bytes 13111296 | tf_op jit(solution)/shard_map/dot_general | solution.py:262
  641.4 7.5 fusion.45
  664.6 6.2 all-to-all-start.3
  670.8 24.7 %reduce-scatter.13.cloned.1.call-done = bf16[640,768]{1,0:T(8,128)(2,1)} async-done(((bf16[2560,768]{1,0:T(8,128)(2,1)}), bf16[640,768]{1,0:T(8,128)(2,1)}) %reduce-scatter.13.cloned.1.call-update) | async-done | bytes 983056 | tf_op jit(solution)/shard_map/reduce_scatter | solution.py:512
  699.1 11.6 %collective-permute-done.53 = bf16[128,2048]{1,0:T(8,128)(2,1)S(1)} collective-permute-done((bf16[128,2048]{1,0:T(8,128)(2,1)S(1)}, bf16[128,2048]{1,0:T(8,128)(2,1)S(1)}, u32[]{:S(2)}, u32[]{:S(2)}) %collective-permute-start.53) | collective-permute-done | bytes 524320 | tf_op jit(solution)/shard_map/ppermute | solution.py:144
  714.6 10.5 %collective-permute-done.50 = bf16[128,2048]{1,0:T(8,128)(2,1)S(1)} collective-permute-done((bf16[128,2048]{1,0:T(8,128)(2,1)S(1)}, bf16[128,2048]{1,0:T(8,128)(2,1)S(1)}, u32[]{:S(2)}, u32[]{:S(2)}) %collective-permute-start.50) | collective-permute-done | bytes 524320 | tf_op jit(solution)/shard_map/ppermute | solution.py:143
  730.9 6.0 all-to-all-start.4
  (549 shorter events, 386.4 us)
Async XLA Ops:
  7.2 97.3 %all-gather.10.cloned.1.call-start = ((), (), s32[]{:S(2)}) async-start(), calls=%async_computation.18 | async-start | bytes 4915200 | tf_op jit(solution)/shard_map/all_gather | solution.py:288
  40.5 228.6 %all-gather.14.cloned.1.call-start = ((), (), s32[]{:S(2)}) async-start(), calls=%async_computation.20 | async-start | bytes 14417920 | tf_op jit(solution)/shard_map/all_gather | solution.py:303
  45.2 22.3 %collective-permute-start.2 = (bf16[128,2048]{1,0:T(8,128)(2,1)}, bf16[128,2048]{1,0:T(8,128)(2,1)}, u32[]{:S(2)}, u32[]{:S(2)}) collective-permute-start(bf16[128,2048]{1,0:T(8,128)(2,1)} %get-tuple-element.258), channel_id=1, source_target_pairs={{0,8},{8,16},{16,24},{24,28},{28,20},{20,12},{12,4},{4,0},{1,9},{9... | collective-permute-start | bytes 1572872 | tf_op jit(solution)/shard_map/ppermute | solution.py:106
  45.7 22.3 %collective-permute-start.3 = (bf16[128,2048]{1,0:T(8,128)(2,1)}, bf16[128,2048]{1,0:T(8,128)(2,1)S(1)}, u32[]{:S(2)}, u32[]{:S(2)}) collective-permute-start(bf16[128,2048]{1,0:T(8,128)(2,1)} %get-tuple-element.258), channel_id=1, source_target_pairs={{8,0},{16,8},{24,16},{28,24},{20,28},{12,20},{4,12},{0,4},{9,1},{1... | collective-permute-start | bytes 1572872 | tf_op jit(solution)/shard_map/ppermute | solution.py:107
  47.2 79.9 %collective-permute-start.10 = (bf16[64,2048]{1,0:T(8,128)(2,1)}, bf16[64,2048]{1,0:T(8,128)(2,1)}, u32[]{:S(2)}, u32[]{:S(2)}) collective-permute-start(bf16[64,2048]{1,0:T(8,128)(2,1)} %param.27), channel_id=1, source_target_pairs={{0,2},{1,3},{2,0},{3,1},{4,6},{5,7},{6,4},{7,5},{8,10},{9,11},{10,... | collective-permute-start | bytes 786440 | tf_op jit(solution)/shard_map/ppermute | solution.py:169
  48.7 88.1 %collective-permute-start.1 = (bf16[176,2048]{1,0:T(8,128)(2,1)}, bf16[176,2048]{1,0:T(8,128)(2,1)}, u32[]{:S(2)}, u32[]{:S(2)}) collective-permute-start(bf16[176,2048]{1,0:T(8,128)(2,1)} %param.33), channel_id=1, source_target_pairs={{0,2},{1,3},{2,0},{3,1},{4,6},{5,7},{6,4},{7,5},{8,10},{9,11},{10,... | collective-permute-start | bytes 2162696 | tf_op jit(solution)/shard_map/ppermute | solution.py:169
  49.2 87.6 %collective-permute-start = (bf16[352,2048]{1,0:T(8,128)(2,1)}, bf16[352,2048]{1,0:T(8,128)(2,1)}, u32[]{:S(2)}, u32[]{:S(2)}) collective-permute-start(bf16[352,2048]{1,0:T(8,128)(2,1)} %bitcast.1), channel_id=1, source_target_pairs={{0,2},{1,3},{2,0},{3,1},{4,6},{5,7},{6,4},{7,5},{8,10},{9,11},{10,... | collective-permute-start | bytes 4325384 | tf_op jit(solution)/shard_map/ppermute | solution.py:169
  99.5 42.3 %all-to-all-start.1 = ((bf16[8,64,1408]{2,1,0:T(8,128)(2,1)}), bf16[8,64,1408]{2,1,0:T(8,128)(2,1)S(1)}, u32[]{:S(2)}, u32[]{:S(2)}) async-start(bf16[8,64,1408]{2,1,0:T(8,128)(2,1)} %reshape.833), calls=%async_computation.1 | async-start | bytes 2883584 | tf_op jit(solution)/shard_map/all_to_all | solution.py:287
  104.3 184.8 %all-gather.12.cloned.1.call-start = ((), (), s32[]{:S(2)}) async-start(), calls=%async_computation.19 | async-start | bytes 7208960 | tf_op jit(solution)/shard_map/all_gather | solution.py:340
  142.9 170.9 %all-gather.8.cloned.1.call-start = ((), (), s32[]{:S(2)}) async-start(), calls=%async_computation.11 | async-start | bytes 4718592 | tf_op jit(solution)/shard_map/all_gather | solution.py:348
  162.2 56.6 %collective-permute-start.28 = (bf16[2,352,2048]{2,1,0:T(8,128)(2,1)}, bf16[2,352,2048]{2,1,0:T(8,128)(2,1)}, u32[]{:S(2)}, u32[]{:S(2)}) collective-permute-start(bf16[2,352,2048]{2,1,0:T(8,128)(2,1)} %maximum_select_fusion.1), channel_id=1, source_target_pairs={{0,1},{1,0},{2,3},{3,2},{4,5},{5,4},{6,7},{7,6},{8,9},{9,8},{10,11... | collective-permute-start | bytes 8650760 | tf_op jit(solution)/shard_map/ppermute | solution.py:174
  177.9 31.4 %collective-permute-start.29 = (bf16[2,176,2048]{2,1,0:T(8,128)(2,1)S(1)}, bf16[2,176,2048]{2,1,0:T(8,128)(2,1)}, u32[]{:S(2)}, u32[]{:S(2)}) collective-permute-start(bf16[2,176,2048]{2,1,0:T(8,128)(2,1)S(1)} %maximum_select_fusion.3), channel_id=1, source_target_pairs={{0,1},{1,0},{2,3},{3,2},{4,5},{5,4},{6,7},{7,6},{8,9},{9,8},{10,11... | collective-permute-start | bytes 4325384 | tf_op jit(solution)/shard_map/ppermute | solution.py:174
  231.8 228.3 %reduce-scatter.7.cloned.1.call-start = ((), (), s32[]{:S(2)}) async-start(), calls=%async_computation.12 | async-start | bytes 14417920 | tf_op jit(solution)/shard_map/reduce_scatter | solution.py:273
  242.3 17.5 %collective-permute-start.27 = (bf16[64,2048]{1,0:T(8,128)(2,1)S(1)}, bf16[64,2048]{1,0:T(8,128)(2,1)S(1)}, u32[]{:S(2)}, u32[]{:S(2)}) collective-permute-start(bf16[64,2048]{1,0:T(8,128)(2,1)S(1)} %slice.466), channel_id=1, source_target_pairs={{8,0},{16,8},{24,16},{28,24},{20,28},{12,20},{4,12},{0,4},{9,1},{1... | collective-permute-start | bytes 786440 | tf_op jit(solution)/shard_map/ppermute | solution.py:113
  352.4 81.5 %all-to-all-start.2 = ((f32[8,2,128]{2,1,0:T(2,128)}), f32[8,2,128]{2,1,0:T(2,128)S(1)}, u32[]{:S(2)}, u32[]{:S(2)}) async-start(f32[8,2,128]{2,1,0:T(2,128)} %pad_maximum_fusion.15), calls=%async_computation.2 | async-start | bytes 16384 | tf_op jit(solution)/shard_map/all_to_all | solution.py:421
  356.3 226.3 %reduce-scatter.9.cloned.1.call-start = ((), (), s32[]{:S(2)}) async-start(), calls=%async_computation.13 | async-start | bytes 7208960 | tf_op jit(solution)/shard_map/reduce_scatter | solution.py:426
  439.6 192.5 %reduce-scatter.11.cloned.1.call-start = ((), (), s32[]{:S(2)}) async-start(), calls=%async_computation.14 | async-start | bytes 4718592 | tf_op jit(solution)/shard_map/reduce_scatter | solution.py:390
  443.8 251.7 %reduce-scatter.13.cloned.1.call-start = ((), (), s32[]{:S(2)}) async-start(), calls=%async_computation.15 | async-start | bytes 4915200 | tf_op jit(solution)/shard_map/reduce_scatter | solution.py:512
  458.4 63.7 %collective-permute-start.47 = (bf16[352,2048]{1,0:T(8,128)(2,1)}, bf16[352,2048]{1,0:T(8,128)(2,1)}, u32[]{:S(2)}, u32[]{:S(2)}) collective-permute-start(bf16[352,2048]{1,0:T(8,128)(2,1)} %dynamic-slice_bitcast_fusion.1), channel_id=1, source_target_pairs={{0,2},{1,3},{2,0},{3,1},{4,6},{5,7},{6,4},{7,5},{8,10},{9,11},{10,... | collective-permute-start | bytes 4325384 | tf_op jit(solution)/shard_map/ppermute | solution.py:191
  474.9 52.9 %collective-permute-start.40 = (bf16[128,2048]{1,0:T(8,128)(2,1)}, bf16[128,2048]{1,0:T(8,128)(2,1)S(1)}, u32[]{:S(2)}, u32[]{:S(2)}) collective-permute-start(bf16[128,2048]{1,0:T(8,128)(2,1)} %collective-permute-done.38), channel_id=1, source_target_pairs={{0,8},{8,16},{16,24},{24,28},{28,20},{20,12},{12,4},{4,0},{1,9},{9... | collective-permute-start | bytes 1572872 | tf_op jit(solution)/shard_map/ppermute | solution.py:106
  475.2 52.7 %collective-permute-start.41 = (bf16[128,2048]{1,0:T(8,128)(2,1)}, bf16[128,2048]{1,0:T(8,128)(2,1)S(1)}, u32[]{:S(2)}, u32[]{:S(2)}) collective-permute-start(bf16[128,2048]{1,0:T(8,128)(2,1)} %collective-permute-done.39), channel_id=1, source_target_pairs={{8,0},{16,8},{24,16},{28,24},{20,28},{12,20},{4,12},{0,4},{9,1},{1... | collective-permute-start | bytes 1572872 | tf_op jit(solution)/shard_map/ppermute | solution.py:107
  527.8 24.7 %collective-permute-start.42 = (bf16[128,2048]{1,0:T(8,128)(2,1)S(1)}, bf16[128,2048]{1,0:T(8,128)(2,1)S(1)}, u32[]{:S(2)}, u32[]{:S(2)}) collective-permute-start(bf16[128,2048]{1,0:T(8,128)(2,1)S(1)} %collective-permute-done.40), channel_id=1, source_target_pairs={{0,8},{8,16},{16,24},{24,28},{28,20},{20,12},{12,4},{4,0},{1,9},{9... | collective-permute-start | bytes 1572872 | tf_op jit(solution)/shard_map/ppermute | solution.py:106
  527.9 32.4 %collective-permute-start.43 = (bf16[128,2048]{1,0:T(8,128)(2,1)S(1)}, bf16[128,2048]{1,0:T(8,128)(2,1)S(1)}, u32[]{:S(2)}, u32[]{:S(2)}) collective-permute-start(bf16[128,2048]{1,0:T(8,128)(2,1)S(1)} %collective-permute-done.41), channel_id=1, source_target_pairs={{8,0},{16,8},{24,16},{28,24},{20,28},{12,20},{4,12},{0,4},{9,1},{1... | collective-permute-start | bytes 1572872 | tf_op jit(solution)/shard_map/ppermute | solution.py:107
  560.3 18.3 %collective-permute-start.45 = (bf16[64,2048]{1,0:T(8,128)(2,1)S(1)}, bf16[64,2048]{1,0:T(8,128)(2,1)S(1)}, u32[]{:S(2)}, u32[]{:S(2)}) collective-permute-start(bf16[64,2048]{1,0:T(8,128)(2,1)S(1)} %slice.477), channel_id=1, source_target_pairs={{8,0},{16,8},{24,16},{28,24},{20,28},{12,20},{4,12},{0,4},{9,1},{1... | collective-permute-start | bytes 786440 | tf_op jit(solution)/shard_map/ppermute | solution.py:113
  654.2 87.4 %reduce-scatter.15.cloned.1.call-start = ((), (), s32[]{:S(2)}) async-start(), calls=%async_computation.16 | async-start | bytes 1310720 | tf_op jit(solution)/shard_map/reduce_scatter | solution.py:273
  661.0 34.5 %collective-permute-start.48 = (bf16[64,2048]{1,0:T(8,128)(2,1)}, bf16[64,2048]{1,0:T(8,128)(2,1)}, u32[]{:S(2)}, u32[]{:S(2)}) collective-permute-start(bf16[64,2048]{1,0:T(8,128)(2,1)} %get-tuple-element.175), channel_id=1, source_target_pairs={{0,8},{8,16},{16,24},{24,28},{28,20},{20,12},{12,4},{4,0},{1,9},{9... | collective-permute-start | bytes 786440 | tf_op jit(solution)/shard_map/ppermute | solution.py:134
  661.0 34.5 %collective-permute-start.52 = (bf16[64,2048]{1,0:T(8,128)(2,1)S(1)}, bf16[64,2048]{1,0:T(8,128)(2,1)}, u32[]{:S(2)}, u32[]{:S(2)}) collective-permute-start(bf16[64,2048]{1,0:T(8,128)(2,1)S(1)} %get-tuple-element.176), channel_id=1, source_target_pairs={{8,0},{16,8},{24,16},{28,24},{20,28},{12,20},{4,12},{0,4},{9,1},{1... | collective-permute-start | bytes 786440 | tf_op jit(solution)/shard_map/ppermute | solution.py:135
  664.6 66.3 %all-to-all-start.3 = ((bf16[8,64,1408]{2,1,0:T(8,128)(2,1)}), bf16[8,64,1408]{2,1,0:T(8,128)(2,1)}, u32[]{:S(2)}, u32[]{:S(2)}) async-start(bf16[8,64,1408]{2,1,0:T(8,128)(2,1)} %bitcast.360), calls=%async_computation.6 | async-start | bytes 2883584 | tf_op jit(solution)/shard_map/all_to_all | solution.py:457
  670.8 101.2 %reduce-scatter.17.cloned.1.call-start = ((), (), s32[]{:S(2)}) async-start(), calls=%async_computation.17 | async-start | bytes 3604480 | tf_op jit(solution)/shard_map/reduce_scatter | solution.py:273
  728.8 24.8 %collective-permute-start.51 = (bf16[128,2048]{1,0:T(8,128)(2,1)}, bf16[128,2048]{1,0:T(8,128)(2,1)}, u32[]{:S(2)}, u32[]{:S(2)}) collective-permute-start(bf16[128,2048]{1,0:T(8,128)(2,1)} %get-tuple-element.169), channel_id=1, source_target_pairs={{0,8},{8,16},{16,24},{24,28},{28,20},{20,12},{12,4},{4,0},{1,9},{9... | collective-permute-start | bytes 1572872 | tf_op jit(solution)/shard_map/ppermute | solution.py:143
  730.3 23.3 %collective-permute-start.55 = (bf16[128,2048]{1,0:T(8,128)(2,1)}, bf16[128,2048]{1,0:T(8,128)(2,1)}, u32[]{:S(2)}, u32[]{:S(2)}) collective-permute-start(bf16[128,2048]{1,0:T(8,128)(2,1)} %get-tuple-element.170), channel_id=1, source_target_pairs={{8,0},{16,8},{24,16},{28,24},{20,28},{12,20},{4,12},{0,4},{9,1},{1... | collective-permute-start | bytes 1572872 | tf_op jit(solution)/shard_map/ppermute | solution.py:144
  730.9 30.3 %all-to-all-start.4 = ((bf16[8,80,768]{2,1,0:T(8,128)(2,1)}), bf16[8,80,768]{2,1,0:T(8,128)(2,1)}, u32[]{:S(2)}, u32[]{:S(2)}) async-start(bf16[8,80,768]{2,1,0:T(8,128)(2,1)} %bitcast.367), calls=%async_computation.8 | async-start | bytes 1966080 | tf_op jit(solution)/shard_map/all_to_all | solution.py:516
  (132 other events, 1265.2 us)
Sparse Core Ops, SparseCore 0:
  40.6 53.4 all-gather.9
  95.6 89.2 all-gather.13
  187.0 43.5 all-gather.11
  232.6 75.5 all-gather.7
  340.1 90.3 reduce-scatter.6
  439.7 85.5 reduce-scatter.8
  529.3 95.6 reduce-scatter.10
  654.4 41.0 reduce-scatter.12
  698.7 24.8 reduce-scatter.14
  726.1 36.3 reduce-scatter.16

commit v12 on v11

--- a/solution.py
+++ b/solution.py
@@ -176,20 +176,6 @@
     out = lax.dynamic_update_index_in_dim(out, pair, index % 2, 1)
     out = lax.dynamic_update_index_in_dim(out, near, 1 - index % 2, 1)
     return (out.reshape(size * rows, width), hold)
-
-
-def fsdp_scatter(grad, size):
-    index = lax.axis_index("fsdp")
-    core, chip = index % 2, index // 2
-    grad = grad.reshape((2, 2) + grad.shape[1:])
-
-    def pick(array, at, axis):
-        return lax.dynamic_index_in_dim(array, at, axis, keepdims=False)
-
-    near = lax.ppermute(pick(grad, 1 - core, 1), "fsdp", other_core(size))
-    mine = (pick(grad, core, 1).astype(jnp.float32) + near.astype(jnp.float32)).astype(grad.dtype)
-    far = lax.ppermute(pick(mine, 1 - chip, 0), "fsdp", other_chip(size))
-    return pick(mine, chip, 0).astype(jnp.float32) + far.astype(jnp.float32)
 
 
 def column_pieces(weight, groups, size, extra):
@@ -387,7 +373,6 @@
     shared_res = dot(shared_hid, shared_out)
     out_parts = (scale_all[:, None] * shared_res + routed).astype(bf16)
     grad_rows, out_parts = after(grad_rows, out_parts)
-    out_sum = lax.psum_scatter(out_parts, "ctx", scatter_dimension=0, tiled=True)
 
     grad_slots = to_slots(grad_rows.reshape(ctx_size, token_count, width))
     gate_slots = jnp.sum(jnp.where(slot_mask, gate_blocks[:, None, :], 0.0), axis=-1).reshape(-1, 1)
@@ -429,7 +414,7 @@
         scatter_dimension=0,
         tiled=True,
     ).reshape(ctx_size, shard, 2 * fs_own)
-    sum_expert_out = fsdp_scatter(grad_expert_out.reshape(fsdp_size, -1, width), fsdp_size)
+    sum_expert_out = sum_rows(grad_expert_out)
     own_probs = own_rows(probs_all)
     own_scale = own_rows(scale_all)
     own_chosen = routes.reshape(token_count, top_count)
@@ -473,21 +458,16 @@
         ],
         axis=-1,
     ).astype(bf16)
-    grad_projected, out_sum, sum_expert_out = after(grad_projected, out_sum, sum_expert_out)
-    output = (own_residual + out_sum.astype(f32)).astype(bf16).reshape(tokens.shape)
+    grad_projected, sum_expert_out, sum_shared_in = after(
+        grad_projected, sum_expert_out, sum_shared_in
+    )
     one_sums = dot_t(grad_projected, qkv_weight)
     grad_gain_one = jnp.sum(one_sums * scaled_rows.astype(f32), axis=0)
     one_parts = one_sums.astype(bf16)
     one_kept, grad_projected = after(one_parts, grad_projected)
-    one_kept, sum_shared_in = after(one_kept, sum_shared_in)
-    grad_normed = ring_scatter(one_parts, ctx_size, ctx_index, one_kept)
-    grad_inputs_norm, unused = rms_back(
-        own_tokens,
-        inv_one,
-        attn_gain,
-        grad_normed,
-    )
-    grad_tokens = (grad_resid + grad_inputs_norm).reshape(tokens.shape)
+    one_kept, out_parts = after(one_kept, out_parts)
+    output = own_residual + ring_scatter(out_parts, ctx_size, ctx_index)
+    output = output.astype(bf16).reshape(tokens.shape)
     grad_qkv_weight = t_dot(normed_low, grad_projected)
     grad_bias = jnp.sum(grad_projected.astype(f32), axis=0).reshape(3, 1, own_width)
     grad_bias = jnp.where(
@@ -514,6 +494,15 @@
     sum_shared_out = sum_rows(grad_shared_out)
     pieces = pieces.reshape(ctx_size, shard + more, 3 * own_width)
     pieces = lax.all_to_all(pieces, "ctx", split_axis=0, concat_axis=0, tiled=True)
+    one_kept, pieces = after(one_kept, pieces)
+    grad_normed = ring_scatter(one_parts, ctx_size, ctx_index, one_kept)
+    grad_inputs_norm, unused = rms_back(
+        own_tokens,
+        inv_one,
+        attn_gain,
+        grad_normed,
+    )
+    grad_tokens = (grad_resid + grad_inputs_norm).reshape(tokens.shape)
     small_grads = jnp.sum(pieces[:, shard:].reshape(ctx_size, -1).astype(f32), axis=0)
     return (
         output,
@@ -528,7 +517,7 @@
         merge_columns(sum_shared_in, 2, ctx_size),
         sum_shared_out.astype(f32),
         sum_expert_in.astype(f32)[None],
-        sum_expert_out[None],
+        sum_expert_out.astype(f32)[None],
     )
 
 

time: 793 us -> 761 us (0.960)
  waiting for transfers between devices: 239 us -> 194 us
    ppermute x2 -> x0, waiting for transfers between devices: 52.1 us -> none  [the longest x1 45.2 us: fsdp_scatter(): far = lax.ppermute(pick(mine, 1 - chip, 0), 'fsdp', other_chip(size))]
    reduce_scatter x3 -> x4, waiting for transfers between devices: 0.01 us -> 23.8 us  [sum_rows(): lax.psum_scatter(grad.astype(bf16), 'fsdp', scatter_dimension=0, tiled=True)]
    ppermute x9 -> x12, waiting for transfers between devices: 28.1 us -> 46.3 us  [ring_sums(): fore = lax.ppermute(fore, 'ctx', ahead)]
    ppermute x9 -> x12, waiting for transfers between devices: 25.7 us -> 13.3 us  [ring_sums(): rear = lax.ppermute(rear, 'ctx', back)]
    ppermute x3, waiting for transfers between devices: 17 us -> 4.99 us  [ring_gather(): rear = lax.ppermute(rear[rows // 2:], 'ctx', back)]
    ppermute x9, waiting for transfers between devices: 59 us -> 49.2 us  [ring_gather(): fore = lax.ppermute(fore, 'ctx', ahead)]
    convert_element_type x9 -> x11, other arithmetic: 14 us -> 22.3 us  [low(): return values.astype(jnp.bfloat16)]
    reduce_scatter x1, waiting for transfers between devices: 24.7 us -> 16.4 us  [local_split(): pieces = lax.psum_scatter(pieces, 'fsdp', scatter_dimension=0, tiled=True)]
  transfers between devices with their start and end apart: 70 -> 76, of which waited for: 34 -> 38; matrix products, arithmetic and copies ran while one was open for 43% -> 47% of each run, Pallas kernels for 0% -> 0%
where the time goes in v12:
time: 761 us; the launch traced here: 749 us
  matrix products  196 us (26%)
  waiting for transfers between devices  194 us (25%)
  local copies, waits for them, and re-layouts  114 us (15%)
  other arithmetic  109 us (14%)
  starting transfers between devices  85.1 us (11%)
  blocking collectives  29.7 us (4%)
  between operations  21 us (3%)
    ppermute x9, waiting for transfers between devices, ring_gather(): fore = lax.ppermute(fore, 'ctx', ahead)  49.2 us
    dot_general x7, matrix products, dot_t(): lax.dot_general(a, b, (((1,), (1,)), ((), ())), preferred_element_type=f32)  47.7 us
    ppermute x12, waiting for transfers between devices, ring_sums(): fore = lax.ppermute(fore, 'ctx', ahead)  46.3 us
    dot_general x8, matrix products, t_dot(): lax.dot_general(a, b, (((0,), (0,)), ((), ())), preferred_element_type=f32)  44.1 us
    dot_general x8, matrix products, dot(): return jnp.dot(a, b, preferred_element_type=f32)  43.2 us
    all_to_all x1, blocking collectives, local_split(): lax.all_to_all(pieces, 'ctx', split_axis=0, concat_axis=0, tiled=True)  29.7 us
    reduce_scatter x4, waiting for transfers between devices, sum_rows(): lax.psum_scatter(grad.astype(bf16), 'fsdp', scatter_dimension=0, tiled=True)  23.8 us
    ppermute x12, starting transfers between devices, ring_sums(): fore = lax.ppermute(fore, 'ctx', ahead)  22.3 us
  transfers between devices with their start and end apart: 76, of which 38 were waited for; matrix products, arithmetic and copies ran while one was open for 47% of the time, Pallas kernels for 0%

profile of v12, /device:TPU:8, one launch (start us, length us, event | category | flops | bytes accessed | tf_op | source)
XLA Modules:
  0.0 749.4 jit_solution(5990862910783582621)
XLA Ops:
  10.7 29.7 %all_to_all.25 = bf16[8,80,768]{2,1,0:T(8,128)(2,1)} all-to-all(bf16[8,80,768]{2,1,0:T(8,128)(2,1)S(1)} %pad_maximum_fusion.6), channel_id=1, replica_groups=mesh['ctx'=8,'fsdp'=4] {'ctx'}, dimensions={0} | all-to-all | bytes 1966080 | tf_op jit(solution)/shard_map/all_to_all | solution.py:270
  73.0 6.7 collective-permute-done.4
  85.4 6.2 collective-permute-done.6
  118.7 6.4 fusion.51
  146.4 6.6 collective-permute-done.12
  178.0 6.2 collective-permute-done.14
  233.2 7.4 collective-permute-done.24
  244.4 11.5 %collective-permute-done.26 = bf16[64,2048]{1,0:T(8,128)(2,1)S(1)} collective-permute-done((bf16[64,2048]{1,0:T(8,128)(2,1)S(1)}, bf16[64,2048]{1,0:T(8,128)(2,1)S(1)}, u32[]{:S(2)}, u32[]{:S(2)}) %collective-permute-start.26) | collective-permute-done | bytes 262176 | tf_op jit(solution)/shard_map/ppermute | solution.py:112
  269.1 11.1 %fusion.3 = f32[512,2816]{1,0:T(8,128)S(1)} fusion(bf16[512,2048]{1,0:T(8,128)(2,1)} %bitcast.345, bf16[1,2048,2816]{2,1,0:T(8,128)(2,1)} %all-gather.14.cloned.1.call-done), kind=kOutput, calls=%fused_computation.3 | convolution fusion | flops 5905580032 | bytes 19398656 | tf_op jit(solution)/shard_map/dot_general | solution.py:245
  295.0 8.5 %fusion.142 = f32[1024,1408]{1,0:T(8,128)S(1)} fusion(bf16[1024,2048]{1,0:T(8,128)(2,1)} %constant_dynamic-update-slice_fusion.4, bf16[2048,1408]{1,0:T(8,128)(2,1)S(1)} %bitcast.310), kind=kOutput, calls=%fused_computation.323 | convolution fusion | flops 5905580032 | bytes 15728640 | tf_op jit(solution)/shard_map/dot_general | solution.py:245
  308.1 5.8 fusion.9
  321.8 7.4 multiply_convert_fusion.6
  330.8 9.2 %convolution_convert_fusion = bf16[2048,2816]{1,0:T(8,128)(2,1)} fusion(bf16[512,2048]{1,0:T(8,128)(2,1)S(1)} %bitcast.346, bf16[512,1408]{1,0:T(8,128)(2,1)S(1)} %get-tuple-element.170, bf16[512,1408]{1,0:T(8,128)(2,1)S(1)} %get-tuple-element.169), kind=kOutput, calls=%fused_computation.5 | convolution fusion | flops 5917114368 | bytes 16515072 | tf_op jit(solution)/shard_map/dot_general | solution.py:251
  340.3 11.6 %multiply_convert_fusion.3 = (bf16[1024,704]{1,0:T(8,128)(2,1)}, bf16[1024,704]{1,0:T(8,128)(2,1)}, f32[1024]{0:T(1024)S(1)}) fusion(f32[1024,1408]{1,0:T(8,128)} %copy-done.6, bf16[1024,704]{1,0:T(8,128)(2,1)} %copy-done.34, bf16[1024,2048]{1,0:T(8,128)(2,1)} %multiply_convert_fusion, bf16[704,2048]{1,0:T(8,128)(2,1)S(1)} %bitcast.339), kind=kOutput, calls=%fused_computation.51 | convolution fusion | flops 2964323328 | bytes 17174528 | tf_op jit(solution)/shard_map/dot_general | solution.py:248
  359.4 9.6 %fusion.47 = bf16[512,2048]{1,0:T(8,128)(2,1)S(1)} fusion(bf16[1,2048,2816]{2,1,0:T(8,128)(2,1)} %all-gather.14.cloned.1.call-done, bf16[512,1408]{1,0:T(8,128)(2,1)} %copy-done.85, bf16[512,1408]{1,0:T(8,128)(2,1)S(1)} %copy-done.84), kind=kOutput, calls=%fused_computation.54 | convolution fusion | flops 5912395776 | bytes 16515072 | tf_op jit(solution)/shard_map/dot_general | solution.py:248
  370.3 7.5 %fusion.7 = bf16[1024,2048]{1,0:T(8,128)(2,1)S(1)} fusion(f32[8,128,2048]{2,1,0:T(8,128)S(1)} %fusion.84, bf16[1024,1408]{1,0:T(8,128)(2,1)S(1)} %pad_maximum_fusion.2, bf16[2048,1408]{1,0:T(8,128)(2,1)S(1)} %bitcast.313), kind=kOutput, calls=%fused_computation.11 | convolution fusion | flops 5909774336 | bytes 21233664 | tf_op jit(solution)/shard_map/dot_general | solution.py:248
  380.0 11.7 %convolution_convert_fusion.2 = bf16[2048,1408]{1,0:T(8,128)(2,1)} fusion(bf16[1024,2048]{1,0:T(8,128)(2,1)} %constant_dynamic-update-slice_fusion.4, bf16[1024,1408]{1,0:T(8,128)(2,1)S(1)} %pad_maximum_fusion.2), kind=kOutput, calls=%fused_computation.23 | convolution fusion | flops 5908463616 | bytes 12845056 | tf_op jit(solution)/shard_map/dot_general | solution.py:251
  409.6 6.9 collective-permute-done.32
  447.3 9.7 %collective-permute-done.38 = bf16[128,2048]{1,0:T(8,128)(2,1)} collective-permute-done((bf16[128,2048]{1,0:T(8,128)(2,1)}, bf16[128,2048]{1,0:T(8,128)(2,1)}, u32[]{:S(2)}, u32[]{:S(2)}) %collective-permute-start.38) | collective-permute-done | bytes 524320 | tf_op jit(solution)/shard_map/ppermute | solution.py:106
  494.1 6.0 all-to-all-start.3
  500.1 6.5 fusion.144
  506.6 17.2 %fusion.58 = f32[1024,2,128]{0,2,1:T(8,128)} fusion(bf16[1024,2,128]{0,2,1:T(8,128)(2,1)} %copy-done.50, f32[2,1024,1024]{1,2,0:T(8,128)} %fusion.144, f32[2,1024,1024]{1,2,0:T(8,128)} %copy-done.5, f32[2,1024]{1,0:T(2,128)S(1)} %copy-done.69, pred[1024,1024]{0,1:T(8,128)(4,1)} %copy-done.17), kind=kOutput, calls=%fused_computation.80 | convolution fusion | flops 559942656 | bytes 19406848 | tf_op jit(solution)/shard_map/hqk,qhd->khd/dot_general | solution.py:450
  523.8 16.7 %broadcast_multiply_fusion.1 = (f32[1024,2,128]{0,2,1:T(8,128)}, f32[1024,2,128]{0,2,1:T(8,128)}, f32[1024,2,128]{0,2,1:T(8,128)}) fusion(f32[1024,128]{0,1:T(8,128)} %get-tuple-element.257, f32[1024,2,128]{0,2,1:T(8,128)} %fusion.58, bf16[1024,2,128]{0,2,1:T(8,128)(2,1)S(1)} %copy-done.49, f32[2,1024,1024]{1,2,0:T(8,128)} %fusion.144, ...), kind=kOutput, calls=%fused_computation.167 | convolution fusion | flops 560466944 | bytes 23076864 | tf_op jit(solution)/shard_map/hqk,khd->qhd/dot_general | solution.py:448
  544.1 5.9 convolution_convert_fusion.9
  551.7 9.2 %fusion.6 = (bf16[2048]{0:T(1024)(128)(2,1)S(1)}, bf16[1024,2048]{1,0:T(8,128)(2,1)}) fusion(bf16[1024,2048]{1,0:T(8,128)(2,1)} %constant_dynamic-update-slice_fusion.18, bf16[1024,768]{0,1:T(8,128)(2,1)} %pad_maximum_fusion.5, bf16[2048,768]{1,0:T(8,128)(2,1)} %bitcast.333), kind=kOutput, calls=%fused_computation.9 | convolution fusion | flops 3229612032 | bytes 13111296 | tf_op jit(solution)/shard_map/dot_general | solution.py:248
  560.9 7.4 fusion.44
  600.6 16.4 %reduce-scatter.13.cloned.1.call-done = bf16[640,768]{1,0:T(8,128)(2,1)} async-done(((bf16[2560,768]{1,0:T(8,128)(2,1)}), bf16[640,768]{1,0:T(8,128)(2,1)}) %reduce-scatter.13.cloned.1.call-update) | async-done | bytes 983056 | tf_op jit(solution)/shard_map/reduce_scatter | solution.py:492
  621.8 23.4 %reduce-scatter.15.cloned.1.call-done = bf16[64,2048]{1,0:T(8,128)(2,1)} async-done(((bf16[256,2048]{1,0:T(8,128)(2,1)}), bf16[64,2048]{1,0:T(8,128)(2,1)}) %reduce-scatter.15.cloned.1.call-update) | async-done | bytes 262160 | tf_op jit(solution)/shard_map/reduce_scatter | solution.py:259
  658.7 6.0 all-to-all-start.4
  670.5 7.4 collective-permute-done.56
  693.2 14.9 %collective-permute-done.48 = bf16[128,2048]{1,0:T(8,128)(2,1)} collective-permute-done((bf16[128,2048]{1,0:T(8,128)(2,1)}, bf16[128,2048]{1,0:T(8,128)(2,1)}, u32[]{:S(2)}, u32[]{:S(2)}) %collective-permute-start.48) | collective-permute-done | bytes 524320 | tf_op jit(solution)/shard_map/ppermute | solution.py:143
  713.4 5.9 collective-permute-done.57
  (562 shorter events, 405.6 us)
Async XLA Ops:
  7.2 97.4 %all-gather.10.cloned.1.call-start = ((), (), s32[]{:S(2)}) async-start(), calls=%async_computation.18 | async-start | bytes 4915200 | tf_op jit(solution)/shard_map/all_gather | solution.py:274
  40.5 228.6 %all-gather.14.cloned.1.call-start = ((), (), s32[]{:S(2)}) async-start(), calls=%async_computation.20 | async-start | bytes 14417920 | tf_op jit(solution)/shard_map/all_gather | solution.py:289
  45.2 22.4 %collective-permute-start.2 = (bf16[128,2048]{1,0:T(8,128)(2,1)}, bf16[128,2048]{1,0:T(8,128)(2,1)}, u32[]{:S(2)}, u32[]{:S(2)}) collective-permute-start(bf16[128,2048]{1,0:T(8,128)(2,1)} %get-tuple-element.272), channel_id=1, source_target_pairs={{0,8},{8,16},{16,24},{24,28},{28,20},{20,12},{12,4},{4,0},{1,9},{9... | collective-permute-start | bytes 1572872 | tf_op jit(solution)/shard_map/ppermute | solution.py:106
  45.7 22.4 %collective-permute-start.3 = (bf16[128,2048]{1,0:T(8,128)(2,1)}, bf16[128,2048]{1,0:T(8,128)(2,1)S(1)}, u32[]{:S(2)}, u32[]{:S(2)}) collective-permute-start(bf16[128,2048]{1,0:T(8,128)(2,1)} %get-tuple-element.272), channel_id=1, source_target_pairs={{8,0},{16,8},{24,16},{28,24},{20,28},{12,20},{4,12},{0,4},{9,1},{1... | collective-permute-start | bytes 1572872 | tf_op jit(solution)/shard_map/ppermute | solution.py:107
  47.2 80.0 %collective-permute-start.10 = (bf16[64,2048]{1,0:T(8,128)(2,1)}, bf16[64,2048]{1,0:T(8,128)(2,1)}, u32[]{:S(2)}, u32[]{:S(2)}) collective-permute-start(bf16[64,2048]{1,0:T(8,128)(2,1)} %param.28), channel_id=1, source_target_pairs={{0,2},{1,3},{2,0},{3,1},{4,6},{5,7},{6,4},{7,5},{8,10},{9,11},{10,... | collective-permute-start | bytes 786440 | tf_op jit(solution)/shard_map/ppermute | solution.py:169
  48.7 88.2 %collective-permute-start.1 = (bf16[176,2048]{1,0:T(8,128)(2,1)}, bf16[176,2048]{1,0:T(8,128)(2,1)}, u32[]{:S(2)}, u32[]{:S(2)}) collective-permute-start(bf16[176,2048]{1,0:T(8,128)(2,1)} %param.34), channel_id=1, source_target_pairs={{0,2},{1,3},{2,0},{3,1},{4,6},{5,7},{6,4},{7,5},{8,10},{9,11},{10,... | collective-permute-start | bytes 2162696 | tf_op jit(solution)/shard_map/ppermute | solution.py:169
  49.2 87.7 %collective-permute-start = (bf16[352,2048]{1,0:T(8,128)(2,1)}, bf16[352,2048]{1,0:T(8,128)(2,1)}, u32[]{:S(2)}, u32[]{:S(2)}) collective-permute-start(bf16[352,2048]{1,0:T(8,128)(2,1)} %bitcast.1), channel_id=1, source_target_pairs={{0,2},{1,3},{2,0},{3,1},{4,6},{5,7},{6,4},{7,5},{8,10},{9,11},{10,... | collective-permute-start | bytes 4325384 | tf_op jit(solution)/shard_map/ppermute | solution.py:169
  99.5 42.4 %all-to-all-start.1 = ((bf16[8,64,1408]{2,1,0:T(8,128)(2,1)}), bf16[8,64,1408]{2,1,0:T(8,128)(2,1)S(1)}, u32[]{:S(2)}, u32[]{:S(2)}) async-start(bf16[8,64,1408]{2,1,0:T(8,128)(2,1)} %reshape.862), calls=%async_computation.1 | async-start | bytes 2883584 | tf_op jit(solution)/shard_map/all_to_all | solution.py:273
  104.5 184.8 %all-gather.12.cloned.1.call-start = ((), (), s32[]{:S(2)}) async-start(), calls=%async_computation.19 | async-start | bytes 7208960 | tf_op jit(solution)/shard_map/all_gather | solution.py:326
  143.0 170.8 %all-gather.8.cloned.1.call-start = ((), (), s32[]{:S(2)}) async-start(), calls=%async_computation.11 | async-start | bytes 4718592 | tf_op jit(solution)/shard_map/all_gather | solution.py:334
  162.2 56.5 %collective-permute-start.28 = (bf16[2,352,2048]{2,1,0:T(8,128)(2,1)}, bf16[2,352,2048]{2,1,0:T(8,128)(2,1)}, u32[]{:S(2)}, u32[]{:S(2)}) collective-permute-start(bf16[2,352,2048]{2,1,0:T(8,128)(2,1)} %maximum_select_fusion.1), channel_id=1, source_target_pairs={{0,1},{1,0},{2,3},{3,2},{4,5},{5,4},{6,7},{7,6},{8,9},{9,8},{10,11... | collective-permute-start | bytes 8650760 | tf_op jit(solution)/shard_map/ppermute | solution.py:174
  177.9 31.2 %collective-permute-start.29 = (bf16[2,176,2048]{2,1,0:T(8,128)(2,1)S(1)}, bf16[2,176,2048]{2,1,0:T(8,128)(2,1)}, u32[]{:S(2)}, u32[]{:S(2)}) collective-permute-start(bf16[2,176,2048]{2,1,0:T(8,128)(2,1)S(1)} %maximum_select_fusion.3), channel_id=1, source_target_pairs={{0,1},{1,0},{2,3},{3,2},{4,5},{5,4},{6,7},{7,6},{8,9},{9,8},{10,11... | collective-permute-start | bytes 4325384 | tf_op jit(solution)/shard_map/ppermute | solution.py:174
  231.5 212.5 %reduce-scatter.7.cloned.1.call-start = ((), (), s32[]{:S(2)}) async-start(), calls=%async_computation.12 | async-start | bytes 14417920 | tf_op jit(solution)/shard_map/reduce_scatter | solution.py:259
  242.2 17.5 %collective-permute-start.27 = (bf16[64,2048]{1,0:T(8,128)(2,1)S(1)}, bf16[64,2048]{1,0:T(8,128)(2,1)S(1)}, u32[]{:S(2)}, u32[]{:S(2)}) collective-permute-start(bf16[64,2048]{1,0:T(8,128)(2,1)S(1)} %slice.501), channel_id=1, source_target_pairs={{8,0},{16,8},{24,16},{28,24},{20,28},{12,20},{4,12},{0,4},{9,1},{1... | collective-permute-start | bytes 786440 | tf_op jit(solution)/shard_map/ppermute | solution.py:113
  352.5 81.3 %all-to-all-start.2 = ((f32[8,2,128]{2,1,0:T(2,128)}), f32[8,2,128]{2,1,0:T(2,128)S(1)}, u32[]{:S(2)}, u32[]{:S(2)}) async-start(f32[8,2,128]{2,1,0:T(2,128)} %pad_maximum_fusion.17), calls=%async_computation.2 | async-start | bytes 16384 | tf_op jit(solution)/shard_map/all_to_all | solution.py:406
  356.3 137.8 %reduce-scatter.9.cloned.1.call-start = ((), (), s32[]{:S(2)}) async-start(), calls=%async_computation.13 | async-start | bytes 7208960 | tf_op jit(solution)/shard_map/reduce_scatter | solution.py:411
  439.6 112.1 %reduce-scatter.11.cloned.1.call-start = ((), (), s32[]{:S(2)}) async-start(), calls=%async_computation.14 | async-start | bytes 7208960 | tf_op jit(solution)/shard_map/reduce_scatter | solution.py:259
  494.1 57.6 %all-to-all-start.3 = ((bf16[8,64,1408]{2,1,0:T(8,128)(2,1)}), bf16[8,64,1408]{2,1,0:T(8,128)(2,1)}, u32[]{:S(2)}, u32[]{:S(2)}) async-start(bf16[8,64,1408]{2,1,0:T(8,128)(2,1)} %bitcast.351), calls=%async_computation.6 | async-start | bytes 2883584 | tf_op jit(solution)/shard_map/all_to_all | solution.py:442
  500.1 116.9 %reduce-scatter.13.cloned.1.call-start = ((), (), s32[]{:S(2)}) async-start(), calls=%async_computation.15 | async-start | bytes 4915200 | tf_op jit(solution)/shard_map/reduce_scatter | solution.py:492
  573.7 71.5 %reduce-scatter.15.cloned.1.call-start = ((), (), s32[]{:S(2)}) async-start(), calls=%async_computation.16 | async-start | bytes 1310720 | tf_op jit(solution)/shard_map/reduce_scatter | solution.py:259
  578.5 161.3 %reduce-scatter.17.cloned.1.call-start = ((), (), s32[]{:S(2)}) async-start(), calls=%async_computation.17 | async-start | bytes 3604480 | tf_op jit(solution)/shard_map/reduce_scatter | solution.py:259
  597.7 54.1 %collective-permute-start.59 = (bf16[128,2048]{1,0:T(8,128)(2,1)}, bf16[128,2048]{1,0:T(8,128)(2,1)}, u32[]{:S(2)}, u32[]{:S(2)}) collective-permute-start(bf16[128,2048]{1,0:T(8,128)(2,1)} %pad_maximum_fusion.16), channel_id=1, source_target_pairs={{8,0},{16,8},{24,16},{28,24},{20,28},{12,20},{4,12},{0,4},{9,1},{1... | collective-permute-start | bytes 1572872 | tf_op jit(solution)/shard_map/ppermute | solution.py:144
  599.2 52.6 %collective-permute-start.55 = (bf16[128,2048]{1,0:T(8,128)(2,1)}, bf16[128,2048]{1,0:T(8,128)(2,1)}, u32[]{:S(2)}, u32[]{:S(2)}) collective-permute-start(bf16[128,2048]{1,0:T(8,128)(2,1)} %pad_maximum_fusion.15), channel_id=1, source_target_pairs={{0,8},{8,16},{16,24},{24,28},{28,20},{20,12},{12,4},{4,0},{1,9},{9... | collective-permute-start | bytes 1572872 | tf_op jit(solution)/shard_map/ppermute | solution.py:143
  654.7 23.2 %collective-permute-start.56 = (bf16[128,2048]{1,0:T(8,128)(2,1)}, bf16[128,2048]{1,0:T(8,128)(2,1)S(1)}, u32[]{:S(2)}, u32[]{:S(2)}) collective-permute-start(bf16[128,2048]{1,0:T(8,128)(2,1)} %get-tuple-element.175), channel_id=1, source_target_pairs={{0,8},{8,16},{16,24},{24,28},{28,20},{20,12},{12,4},{4,0},{1,9},{9... | collective-permute-start | bytes 1572872 | tf_op jit(solution)/shard_map/ppermute | solution.py:143
  656.2 21.7 %collective-permute-start.60 = (bf16[128,2048]{1,0:T(8,128)(2,1)}, bf16[128,2048]{1,0:T(8,128)(2,1)}, u32[]{:S(2)}, u32[]{:S(2)}) collective-permute-start(bf16[128,2048]{1,0:T(8,128)(2,1)} %get-tuple-element.176), channel_id=1, source_target_pairs={{8,0},{16,8},{24,16},{28,24},{20,28},{12,20},{4,12},{0,4},{9,1},{1... | collective-permute-start | bytes 1572872 | tf_op jit(solution)/shard_map/ppermute | solution.py:144
  658.7 54.8 %all-to-all-start.4 = ((bf16[8,80,768]{2,1,0:T(8,128)(2,1)}), bf16[8,80,768]{2,1,0:T(8,128)(2,1)}, u32[]{:S(2)}, u32[]{:S(2)}) async-start(bf16[8,80,768]{2,1,0:T(8,128)(2,1)} %bitcast.358), calls=%async_computation.8 | async-start | bytes 1966080 | tf_op jit(solution)/shard_map/all_to_all | solution.py:496
  668.5 39.6 %collective-permute-start.48 = (bf16[128,2048]{1,0:T(8,128)(2,1)}, bf16[128,2048]{1,0:T(8,128)(2,1)}, u32[]{:S(2)}, u32[]{:S(2)}) collective-permute-start(bf16[128,2048]{1,0:T(8,128)(2,1)} %get-tuple-element.185), channel_id=1, source_target_pairs={{0,8},{8,16},{16,24},{24,28},{28,20},{20,12},{12,4},{4,0},{1,9},{9... | collective-permute-start | bytes 1572872 | tf_op jit(solution)/shard_map/ppermute | solution.py:143
  670.0 38.1 %collective-permute-start.52 = (bf16[128,2048]{1,0:T(8,128)(2,1)}, bf16[128,2048]{1,0:T(8,128)(2,1)}, u32[]{:S(2)}, u32[]{:S(2)}) collective-permute-start(bf16[128,2048]{1,0:T(8,128)(2,1)} %get-tuple-element.186), channel_id=1, source_target_pairs={{8,0},{16,8},{24,16},{28,24},{20,28},{12,20},{4,12},{0,4},{9,1},{1... | collective-permute-start | bytes 1572872 | tf_op jit(solution)/shard_map/ppermute | solution.py:144
  680.6 38.7 %collective-permute-start.57 = (bf16[128,2048]{1,0:T(8,128)(2,1)}, bf16[128,2048]{1,0:T(8,128)(2,1)}, u32[]{:S(2)}, u32[]{:S(2)}) collective-permute-start(bf16[128,2048]{1,0:T(8,128)(2,1)} %get-tuple-element.173), channel_id=1, source_target_pairs={{0,8},{8,16},{16,24},{24,28},{28,20},{20,12},{12,4},{4,0},{1,9},{9... | collective-permute-start | bytes 1572872 | tf_op jit(solution)/shard_map/ppermute | solution.py:143
  683.8 35.5 %collective-permute-start.61 = (bf16[128,2048]{1,0:T(8,128)(2,1)}, bf16[128,2048]{1,0:T(8,128)(2,1)}, u32[]{:S(2)}, u32[]{:S(2)}) collective-permute-start(bf16[128,2048]{1,0:T(8,128)(2,1)} %get-tuple-element.174), channel_id=1, source_target_pairs={{8,0},{16,8},{24,16},{28,24},{20,28},{12,20},{4,12},{0,4},{9,1},{1... | collective-permute-start | bytes 1572872 | tf_op jit(solution)/shard_map/ppermute | solution.py:144
  710.9 24.6 %collective-permute-start.49 = (bf16[128,2048]{1,0:T(8,128)(2,1)}, bf16[128,2048]{1,0:T(8,128)(2,1)}, u32[]{:S(2)}, u32[]{:S(2)}) collective-permute-start(bf16[128,2048]{1,0:T(8,128)(2,1)} %get-tuple-element.183), channel_id=1, source_target_pairs={{0,8},{8,16},{16,24},{24,28},{28,20},{20,12},{12,4},{4,0},{1,9},{9... | collective-permute-start | bytes 1572872 | tf_op jit(solution)/shard_map/ppermute | solution.py:143
  713.4 22.1 %collective-permute-start.53 = (bf16[128,2048]{1,0:T(8,128)(2,1)}, bf16[128,2048]{1,0:T(8,128)(2,1)}, u32[]{:S(2)}, u32[]{:S(2)}) collective-permute-start(bf16[128,2048]{1,0:T(8,128)(2,1)} %get-tuple-element.184), channel_id=1, source_target_pairs={{8,0},{16,8},{24,16},{28,24},{20,28},{12,20},{4,12},{0,4},{9,1},{1... | collective-permute-start | bytes 1572872 | tf_op jit(solution)/shard_map/ppermute | solution.py:144
  (137 other events, 1202.6 us)
Sparse Core Ops, SparseCore 0:
  40.6 53.3 all-gather.9
  95.6 89.2 all-gather.13
  187.0 43.5 all-gather.11
  232.6 75.5 all-gather.7
  340.1 90.1 reduce-scatter.6
  439.6 54.4 reduce-scatter.8
  496.8 54.8 reduce-scatter.10
  573.8 43.1 reduce-scatter.12
  620.3 24.8 reduce-scatter.14
  647.6 36.3 reduce-scatter.16

commit v13 on v12

--- a/solution.py
+++ b/solution.py
@@ -465,9 +465,8 @@
     grad_gain_one = jnp.sum(one_sums * scaled_rows.astype(f32), axis=0)
     one_parts = one_sums.astype(bf16)
     one_kept, grad_projected = after(one_parts, grad_projected)
-    one_kept, out_parts = after(one_kept, out_parts)
-    output = own_residual + ring_scatter(out_parts, ctx_size, ctx_index)
-    output = output.astype(bf16).reshape(tokens.shape)
+    one_kept, attn_own = after(one_kept, attn_own)
+    grad_normed = ring_scatter(one_parts, ctx_size, ctx_index, one_kept)
     grad_qkv_weight = t_dot(normed_low, grad_projected)
     grad_bias = jnp.sum(grad_projected.astype(f32), axis=0).reshape(3, 1, own_width)
     grad_bias = jnp.where(
@@ -490,12 +489,15 @@
     )
     pieces = pieces.transpose(1, 0, 2, 3).reshape(-1, 3 * own_width)
     pieces = lax.psum_scatter(pieces, "fsdp", scatter_dimension=0, tiled=True)
-    pieces, grad_shared_out = after(pieces, grad_shared_out)
+    grad_normed, pieces, out_parts, grad_shared_out, grad_out_weight = after(
+        grad_normed, pieces, out_parts, grad_shared_out, grad_out_weight.astype(bf16)
+    )
     sum_shared_out = sum_rows(grad_shared_out)
+    sum_out_weight = sum_rows(grad_out_weight)
+    output = own_residual + ring_scatter(out_parts, ctx_size, ctx_index)
+    output = output.astype(bf16).reshape(tokens.shape)
     pieces = pieces.reshape(ctx_size, shard + more, 3 * own_width)
     pieces = lax.all_to_all(pieces, "ctx", split_axis=0, concat_axis=0, tiled=True)
-    one_kept, pieces = after(one_kept, pieces)
-    grad_normed = ring_scatter(one_parts, ctx_size, ctx_index, one_kept)
     grad_inputs_norm, unused = rms_back(
         own_tokens,
         inv_one,
@@ -509,7 +511,7 @@
         grad_tokens,
         merge_columns(pieces[:, :shard], 3, ctx_size),
         small_grads[router_end:small_size],
-        sum_rows(grad_out_weight).astype(f32),
+        sum_out_weight.astype(f32),
         small_grads[:shard],
         small_grads[shard : 2 * shard],
         small_grads[3 * shard : router_end].reshape(shard, expert_count),

time: 761 us -> 730 us (0.959)
  waiting for transfers between devices: 194 us -> 178 us
  other arithmetic: 109 us -> 101 us
    ppermute x12, waiting for transfers between devices: 13.3 us -> 50.6 us  [ring_sums(): rear = lax.ppermute(rear, 'ctx', back)]
    reduce_scatter x4, waiting for transfers between devices: 23.8 us -> 0.13 us  [sum_rows(): lax.psum_scatter(grad.astype(bf16), 'fsdp', scatter_dimension=0, tiled=True)]
    reduce_scatter x1, waiting for transfers between devices: 16.4 us -> 0.02 us  [local_split(): pieces = lax.psum_scatter(pieces, 'fsdp', scatter_dimension=0, tiled=True)]
    ppermute x12, waiting for transfers between devices: 46.3 us -> 33.3 us  [ring_sums(): fore = lax.ppermute(fore, 'ctx', ahead)]
    convert_element_type x11 -> x12, other arithmetic: 22.3 us -> 18.5 us  [low(): return values.astype(jnp.bfloat16)]
    unnamed x192 -> x198, local copies, waits for them, and re-layouts: 21.4 us -> 21.9 us
where the time goes in v13:
time: 730 us; the launch traced here: 719 us
  matrix products  193 us (26%)
  waiting for transfers between devices  178 us (24%)
  local copies, waits for them, and re-layouts  114 us (16%)
  other arithmetic  101 us (14%)
  starting transfers between devices  83.5 us (11%)
  blocking collectives  29.7 us (4%)
  between operations  21.1 us (3%)
    ppermute x9, waiting for transfers between devices, ring_gather(): fore = lax.ppermute(fore, 'ctx', ahead)  51.2 us
    ppermute x12, waiting for transfers between devices, ring_sums(): rear = lax.ppermute(rear, 'ctx', back)  50.6 us
    dot_general x7, matrix products, dot_t(): lax.dot_general(a, b, (((1,), (1,)), ((), ())), preferred_element_type=f32)  48.1 us
    dot_general x8, matrix products, dot(): return jnp.dot(a, b, preferred_element_type=f32)  43.2 us
    dot_general x8, matrix products, t_dot(): lax.dot_general(a, b, (((0,), (0,)), ((), ())), preferred_element_type=f32)  40.8 us
    ppermute x12, waiting for transfers between devices, ring_sums(): fore = lax.ppermute(fore, 'ctx', ahead)  33.3 us
    all_to_all x1, blocking collectives, local_split(): lax.all_to_all(pieces, 'ctx', split_axis=0, concat_axis=0, tiled=True)  29.7 us
    unnamed x198, local copies, waits for them, and re-layouts  21.9 us
  transfers between devices with their start and end apart: 76, of which 38 were waited for; matrix products, arithmetic and copies ran while one was open for 47% of the time, Pallas kernels for 0%

profile of v13, /device:TPU:8, one launch (start us, length us, event | category | flops | bytes accessed | tf_op | source)
XLA Modules:
  0.0 719.2 jit_solution(5408773703548129928)
XLA Ops:
  10.7 29.7 %all_to_all.25 = bf16[8,80,768]{2,1,0:T(8,128)(2,1)} all-to-all(bf16[8,80,768]{2,1,0:T(8,128)(2,1)S(1)} %pad_maximum_fusion.6), channel_id=1, replica_groups=mesh['ctx'=8,'fsdp'=4] {'ctx'}, dimensions={0} | all-to-all | bytes 1966080 | tf_op jit(solution)/shard_map/all_to_all | solution.py:270
  72.9 6.7 collective-permute-done.4
  85.3 6.3 collective-permute-done.6
  118.6 6.4 fusion.51
  146.4 6.6 collective-permute-done.12
  177.9 6.1 collective-permute-done.14
  233.4 7.2 collective-permute-done.24
  244.6 11.3 %collective-permute-done.26 = bf16[64,2048]{1,0:T(8,128)(2,1)S(1)} collective-permute-done((bf16[64,2048]{1,0:T(8,128)(2,1)S(1)}, bf16[64,2048]{1,0:T(8,128)(2,1)S(1)}, u32[]{:S(2)}, u32[]{:S(2)}) %collective-permute-start.26) | collective-permute-done | bytes 262176 | tf_op jit(solution)/shard_map/ppermute | solution.py:112
  269.1 11.1 %fusion.3 = f32[512,2816]{1,0:T(8,128)S(1)} fusion(bf16[512,2048]{1,0:T(8,128)(2,1)} %bitcast.343, bf16[1,2048,2816]{2,1,0:T(8,128)(2,1)} %all-gather.14.cloned.1.call-done), kind=kOutput, calls=%fused_computation.3 | convolution fusion | flops 5905580032 | bytes 19398656 | tf_op jit(solution)/shard_map/dot_general | solution.py:245
  294.9 8.5 %fusion.141 = f32[1024,1408]{1,0:T(8,128)S(1)} fusion(bf16[1024,2048]{1,0:T(8,128)(2,1)} %constant_dynamic-update-slice_fusion.4, bf16[2048,1408]{1,0:T(8,128)(2,1)S(1)} %bitcast.309), kind=kOutput, calls=%fused_computation.322 | convolution fusion | flops 5905580032 | bytes 15728640 | tf_op jit(solution)/shard_map/dot_general | solution.py:245
  308.0 5.8 fusion.9
  321.8 7.4 %multiply_convert_fusion.6 = (bf16[512,1408]{1,0:T(8,128)(2,1)S(1)}, bf16[512,1408]{1,0:T(8,128)(2,1)S(1)}, f32[512]{0:T(512)S(1)}) fusion(f32[512,2816]{1,0:T(8,128)S(1)} %bitcast.314, bf16[512,1408]{1,0:T(8,128)(2,1)S(1)} %copy-done.40, bf16[512,2048]{1,0:T(8,128)(2,1)S(1)} %bitcast.345, bf16[1408,2048]{1,0:T(8,128)(2,1)} %bitcast.315), kind=kOutput, calls=%fused_computation.66 | convolution fusion | flops 2964323840 | bytes 17958912 | tf_op jit(solution)/shard_map/dot_general | solution.py:248
  330.7 9.2 %convolution_convert_fusion = bf16[2048,2816]{1,0:T(8,128)(2,1)} fusion(bf16[512,2048]{1,0:T(8,128)(2,1)S(1)} %bitcast.344, bf16[512,1408]{1,0:T(8,128)(2,1)S(1)} %get-tuple-element.172, bf16[512,1408]{1,0:T(8,128)(2,1)S(1)} %get-tuple-element.171), kind=kOutput, calls=%fused_computation.5 | convolution fusion | flops 5917114368 | bytes 16515072 | tf_op jit(solution)/shard_map/dot_general | solution.py:251
  340.2 11.5 %multiply_convert_fusion.3 = (bf16[1024,704]{1,0:T(8,128)(2,1)}, bf16[1024,704]{1,0:T(8,128)(2,1)}, f32[1024]{0:T(1024)S(1)}) fusion(f32[1024,1408]{1,0:T(8,128)} %copy-done.7, bf16[1024,704]{1,0:T(8,128)(2,1)} %copy-done.37, bf16[1024,2048]{1,0:T(8,128)(2,1)} %multiply_convert_fusion, bf16[704,2048]{1,0:T(8,128)(2,1)S(1)} %bitcast.337), kind=kOutput, calls=%fused_computation.51 | convolution fusion | flops 2964323328 | bytes 17174528 | tf_op jit(solution)/shard_map/dot_general | solution.py:248
  359.5 9.6 %fusion.47 = bf16[512,2048]{1,0:T(8,128)(2,1)S(1)} fusion(bf16[1,2048,2816]{2,1,0:T(8,128)(2,1)} %all-gather.14.cloned.1.call-done, bf16[512,1408]{1,0:T(8,128)(2,1)} %copy-done.88, bf16[512,1408]{1,0:T(8,128)(2,1)S(1)} %copy-done.87), kind=kOutput, calls=%fused_computation.54 | convolution fusion | flops 5912395776 | bytes 16515072 | tf_op jit(solution)/shard_map/dot_general | solution.py:248
  370.4 7.5 %fusion.7 = bf16[1024,2048]{1,0:T(8,128)(2,1)S(1)} fusion(f32[8,128,2048]{2,1,0:T(8,128)S(1)} %fusion.83, bf16[1024,1408]{1,0:T(8,128)(2,1)S(1)} %pad_maximum_fusion.2, bf16[2048,1408]{1,0:T(8,128)(2,1)S(1)} %bitcast.312), kind=kOutput, calls=%fused_computation.11 | convolution fusion | flops 5909774336 | bytes 21233664 | tf_op jit(solution)/shard_map/dot_general | solution.py:248
  380.1 11.7 %convolution_convert_fusion.2 = bf16[2048,1408]{1,0:T(8,128)(2,1)} fusion(bf16[1024,2048]{1,0:T(8,128)(2,1)} %constant_dynamic-update-slice_fusion.4, bf16[1024,1408]{1,0:T(8,128)(2,1)S(1)} %pad_maximum_fusion.2), kind=kOutput, calls=%fused_computation.23 | convolution fusion | flops 5908463616 | bytes 12845056 | tf_op jit(solution)/shard_map/dot_general | solution.py:251
  409.7 6.9 collective-permute-done.32
  446.8 10.3 %collective-permute-done.38 = bf16[128,2048]{1,0:T(8,128)(2,1)} collective-permute-done((bf16[128,2048]{1,0:T(8,128)(2,1)S(1)}, bf16[128,2048]{1,0:T(8,128)(2,1)}, u32[]{:S(2)}, u32[]{:S(2)}) %collective-permute-start.38) | collective-permute-done | bytes 524320 | tf_op jit(solution)/shard_map/ppermute | solution.py:106
  462.6 6.6 collective-permute-done.40
  493.2 6.1 all-to-all-start.3
  499.3 6.6 fusion.143
  505.9 17.1 %fusion.58 = f32[1024,2,128]{0,2,1:T(8,128)} fusion(bf16[1024,2,128]{0,2,1:T(8,128)(2,1)} %copy-done.52, f32[2,1024,1024]{1,2,0:T(8,128)} %fusion.143, f32[2,1024,1024]{1,2,0:T(8,128)} %copy-done.6, f32[2,1024]{1,0:T(2,128)S(1)} %copy-done.72, pred[1024,1024]{0,1:T(8,128)(4,1)} %copy-done.20), kind=kOutput, calls=%fused_computation.80 | convolution fusion | flops 559942656 | bytes 19406848 | tf_op jit(solution)/shard_map/hqk,qhd->khd/dot_general | solution.py:450
  523.0 16.9 %broadcast_multiply_fusion.1 = (f32[1024,2,128]{0,2,1:T(8,128)}, f32[1024,2,128]{0,2,1:T(8,128)}, f32[1024,2,128]{0,2,1:T(8,128)}) fusion(f32[1024,128]{0,1:T(8,128)} %get-tuple-element.259, f32[1024,2,128]{0,2,1:T(8,128)} %fusion.58, bf16[1024,2,128]{0,2,1:T(8,128)(2,1)} %copy-done.51, f32[2,1024,1024]{1,2,0:T(8,128)} %fusion.143, ...), kind=kOutput, calls=%fused_computation.166 | convolution fusion | flops 560466944 | bytes 23076864 | tf_op jit(solution)/shard_map/hqk,khd->qhd/dot_general | solution.py:448
  543.5 5.9 convolution_convert_fusion.9
  550.8 9.7 %fusion.6 = (bf16[2048]{0:T(1024)(128)(2,1)S(1)}, bf16[1024,2048]{1,0:T(8,128)(2,1)}) fusion(bf16[1024,2048]{1,0:T(8,128)(2,1)} %constant_dynamic-update-slice_fusion.18, bf16[1024,768]{0,1:T(8,128)(2,1)} %pad_maximum_fusion.5, bf16[2048,768]{1,0:T(8,128)(2,1)} %bitcast.331), kind=kOutput, calls=%fused_computation.9 | convolution fusion | flops 3229612032 | bytes 13111296 | tf_op jit(solution)/shard_map/dot_general | solution.py:248
  560.5 7.4 %fusion.44 = bf16[2048,768]{1,0:T(8,128)(2,1)} fusion(bf16[1024,768]{0,1:T(8,128)(2,1)S(1)} %copy-done.10, bf16[1024,2048]{1,0:T(8,128)(2,1)} %constant_dynamic-update-slice_fusion.18, f32[2048]{0:T(1024)S(1)} %copy-done.60), kind=kOutput, calls=%fused_computation.46 | convolution fusion | flops 3229089792 | bytes 8921088 | tf_op jit(solution)/shard_map/dot_general | solution.py:251
  577.1 5.9 collective-permute-done.46
  587.8 10.4 %collective-permute-done.51 = bf16[128,2048]{1,0:T(8,128)(2,1)S(1)} collective-permute-done((bf16[128,2048]{1,0:T(8,128)(2,1)S(1)}, bf16[128,2048]{1,0:T(8,128)(2,1)S(1)}, u32[]{:S(2)}, u32[]{:S(2)}) %collective-permute-start.51) | collective-permute-done | bytes 524320 | tf_op jit(solution)/shard_map/ppermute | solution.py:144
  601.1 9.4 %collective-permute-done.48 = bf16[128,2048]{1,0:T(8,128)(2,1)S(1)} collective-permute-done((bf16[128,2048]{1,0:T(8,128)(2,1)S(1)}, bf16[128,2048]{1,0:T(8,128)(2,1)S(1)}, u32[]{:S(2)}, u32[]{:S(2)}) %collective-permute-start.48) | collective-permute-done | bytes 524320 | tf_op jit(solution)/shard_map/ppermute | solution.py:143
  617.2 6.2 collective-permute-done.49
  646.7 24.0 %collective-permute-done.59 = bf16[128,2048]{1,0:T(8,128)(2,1)S(1)} collective-permute-done((bf16[128,2048]{1,0:T(8,128)(2,1)S(1)}, bf16[128,2048]{1,0:T(8,128)(2,1)S(1)}, u32[]{:S(2)}, u32[]{:S(2)}) %collective-permute-start.59) | collective-permute-done | bytes 524320 | tf_op jit(solution)/shard_map/ppermute | solution.py:144
  (568 shorter events, 386.2 us)
Async XLA Ops:
  7.2 97.3 %all-gather.10.cloned.1.call-start = ((), (), s32[]{:S(2)}) async-start(), calls=%async_computation.18 | async-start | bytes 4915200 | tf_op jit(solution)/shard_map/all_gather | solution.py:274
  40.5 228.6 %all-gather.14.cloned.1.call-start = ((), (), s32[]{:S(2)}) async-start(), calls=%async_computation.20 | async-start | bytes 14417920 | tf_op jit(solution)/shard_map/all_gather | solution.py:289
  45.1 22.3 %collective-permute-start.2 = (bf16[128,2048]{1,0:T(8,128)(2,1)}, bf16[128,2048]{1,0:T(8,128)(2,1)}, u32[]{:S(2)}, u32[]{:S(2)}) collective-permute-start(bf16[128,2048]{1,0:T(8,128)(2,1)} %get-tuple-element.274), channel_id=1, source_target_pairs={{0,8},{8,16},{16,24},{24,28},{28,20},{20,12},{12,4},{4,0},{1,9},{9... | collective-permute-start | bytes 1572872 | tf_op jit(solution)/shard_map/ppermute | solution.py:106
  45.7 22.3 %collective-permute-start.3 = (bf16[128,2048]{1,0:T(8,128)(2,1)}, bf16[128,2048]{1,0:T(8,128)(2,1)S(1)}, u32[]{:S(2)}, u32[]{:S(2)}) collective-permute-start(bf16[128,2048]{1,0:T(8,128)(2,1)} %get-tuple-element.274), channel_id=1, source_target_pairs={{8,0},{16,8},{24,16},{28,24},{20,28},{12,20},{4,12},{0,4},{9,1},{1... | collective-permute-start | bytes 1572872 | tf_op jit(solution)/shard_map/ppermute | solution.py:107
  47.2 79.9 %collective-permute-start.10 = (bf16[64,2048]{1,0:T(8,128)(2,1)}, bf16[64,2048]{1,0:T(8,128)(2,1)}, u32[]{:S(2)}, u32[]{:S(2)}) collective-permute-start(bf16[64,2048]{1,0:T(8,128)(2,1)} %param.28), channel_id=1, source_target_pairs={{0,2},{1,3},{2,0},{3,1},{4,6},{5,7},{6,4},{7,5},{8,10},{9,11},{10,... | collective-permute-start | bytes 786440 | tf_op jit(solution)/shard_map/ppermute | solution.py:169
  48.7 88.1 %collective-permute-start.1 = (bf16[176,2048]{1,0:T(8,128)(2,1)}, bf16[176,2048]{1,0:T(8,128)(2,1)}, u32[]{:S(2)}, u32[]{:S(2)}) collective-permute-start(bf16[176,2048]{1,0:T(8,128)(2,1)} %param.34), channel_id=1, source_target_pairs={{0,2},{1,3},{2,0},{3,1},{4,6},{5,7},{6,4},{7,5},{8,10},{9,11},{10,... | collective-permute-start | bytes 2162696 | tf_op jit(solution)/shard_map/ppermute | solution.py:169
  49.2 87.6 %collective-permute-start = (bf16[352,2048]{1,0:T(8,128)(2,1)}, bf16[352,2048]{1,0:T(8,128)(2,1)}, u32[]{:S(2)}, u32[]{:S(2)}) collective-permute-start(bf16[352,2048]{1,0:T(8,128)(2,1)} %bitcast.1), channel_id=1, source_target_pairs={{0,2},{1,3},{2,0},{3,1},{4,6},{5,7},{6,4},{7,5},{8,10},{9,11},{10,... | collective-permute-start | bytes 4325384 | tf_op jit(solution)/shard_map/ppermute | solution.py:169
  99.5 42.4 %all-to-all-start.1 = ((bf16[8,64,1408]{2,1,0:T(8,128)(2,1)}), bf16[8,64,1408]{2,1,0:T(8,128)(2,1)S(1)}, u32[]{:S(2)}, u32[]{:S(2)}) async-start(bf16[8,64,1408]{2,1,0:T(8,128)(2,1)} %reshape.862), calls=%async_computation.1 | async-start | bytes 2883584 | tf_op jit(solution)/shard_map/all_to_all | solution.py:273
  104.4 184.8 %all-gather.12.cloned.1.call-start = ((), (), s32[]{:S(2)}) async-start(), calls=%async_computation.19 | async-start | bytes 7208960 | tf_op jit(solution)/shard_map/all_gather | solution.py:326
  142.9 170.9 %all-gather.8.cloned.1.call-start = ((), (), s32[]{:S(2)}) async-start(), calls=%async_computation.11 | async-start | bytes 4718592 | tf_op jit(solution)/shard_map/all_gather | solution.py:334
  155.3 13.3 %collective-permute-start.17 = (bf16[128,2048]{1,0:T(8,128)(2,1)S(1)}, bf16[128,2048]{1,0:T(8,128)(2,1)S(1)}, u32[]{:S(2)}, u32[]{:S(2)}) collective-permute-start(bf16[128,2048]{1,0:T(8,128)(2,1)S(1)} %pad_maximum_fusion.10), channel_id=1, source_target_pairs={{8,0},{16,8},{24,16},{28,24},{20,28},{12,20},{4,12},{0,4},{9,1},{1... | collective-permute-start | bytes 1572872 | tf_op jit(solution)/shard_map/ppermute | solution.py:144
  156.0 13.2 %collective-permute-start.13 = (bf16[128,2048]{1,0:T(8,128)(2,1)S(1)}, bf16[128,2048]{1,0:T(8,128)(2,1)S(1)}, u32[]{:S(2)}, u32[]{:S(2)}) collective-permute-start(bf16[128,2048]{1,0:T(8,128)(2,1)S(1)} %pad_maximum_fusion.9), channel_id=1, source_target_pairs={{0,8},{8,16},{16,24},{24,28},{28,20},{20,12},{12,4},{4,0},{1,9},{9... | collective-permute-start | bytes 1572872 | tf_op jit(solution)/shard_map/ppermute | solution.py:143
  162.1 56.5 %collective-permute-start.28 = (bf16[2,352,2048]{2,1,0:T(8,128)(2,1)}, bf16[2,352,2048]{2,1,0:T(8,128)(2,1)}, u32[]{:S(2)}, u32[]{:S(2)}) collective-permute-start(bf16[2,352,2048]{2,1,0:T(8,128)(2,1)} %maximum_select_fusion.1), channel_id=1, source_target_pairs={{0,1},{1,0},{2,3},{3,2},{4,5},{5,4},{6,7},{7,6},{8,9},{9,8},{10,11... | collective-permute-start | bytes 8650760 | tf_op jit(solution)/shard_map/ppermute | solution.py:174
  177.9 31.3 %collective-permute-start.29 = (bf16[2,176,2048]{2,1,0:T(8,128)(2,1)S(1)}, bf16[2,176,2048]{2,1,0:T(8,128)(2,1)}, u32[]{:S(2)}, u32[]{:S(2)}) collective-permute-start(bf16[2,176,2048]{2,1,0:T(8,128)(2,1)S(1)} %maximum_select_fusion.3), channel_id=1, source_target_pairs={{0,1},{1,0},{2,3},{3,2},{4,5},{5,4},{6,7},{7,6},{8,9},{9,8},{10,11... | collective-permute-start | bytes 4325384 | tf_op jit(solution)/shard_map/ppermute | solution.py:174
  231.7 212.5 %reduce-scatter.7.cloned.1.call-start = ((), (), s32[]{:S(2)}) async-start(), calls=%async_computation.12 | async-start | bytes 14417920 | tf_op jit(solution)/shard_map/reduce_scatter | solution.py:259
  240.6 15.3 %collective-permute-start.26 = (bf16[64,2048]{1,0:T(8,128)(2,1)S(1)}, bf16[64,2048]{1,0:T(8,128)(2,1)S(1)}, u32[]{:S(2)}, u32[]{:S(2)}) collective-permute-start(bf16[64,2048]{1,0:T(8,128)(2,1)S(1)} %slice.500), channel_id=1, source_target_pairs={{0,8},{8,16},{16,24},{24,28},{28,20},{20,12},{12,4},{4,0},{1,9},{9... | collective-permute-start | bytes 786440 | tf_op jit(solution)/shard_map/ppermute | solution.py:112
  242.2 17.5 %collective-permute-start.27 = (bf16[64,2048]{1,0:T(8,128)(2,1)S(1)}, bf16[64,2048]{1,0:T(8,128)(2,1)S(1)}, u32[]{:S(2)}, u32[]{:S(2)}) collective-permute-start(bf16[64,2048]{1,0:T(8,128)(2,1)S(1)} %slice.501), channel_id=1, source_target_pairs={{8,0},{16,8},{24,16},{28,24},{20,28},{12,20},{4,12},{0,4},{9,1},{1... | collective-permute-start | bytes 786440 | tf_op jit(solution)/shard_map/ppermute | solution.py:113
  352.4 81.4 %all-to-all-start.2 = ((f32[8,2,128]{2,1,0:T(2,128)}), f32[8,2,128]{2,1,0:T(2,128)S(1)}, u32[]{:S(2)}, u32[]{:S(2)}) async-start(f32[8,2,128]{2,1,0:T(2,128)} %pad_maximum_fusion.17), calls=%async_computation.2 | async-start | bytes 16384 | tf_op jit(solution)/shard_map/all_to_all | solution.py:406
  356.3 136.9 %reduce-scatter.9.cloned.1.call-start = ((), (), s32[]{:S(2)}) async-start(), calls=%async_computation.13 | async-start | bytes 7208960 | tf_op jit(solution)/shard_map/reduce_scatter | solution.py:411
  378.0 13.8 %collective-permute-start.30 = (bf16[64,2048]{1,0:T(8,128)(2,1)S(1)}, bf16[64,2048]{1,0:T(8,128)(2,1)S(1)}, u32[]{:S(2)}, u32[]{:S(2)}) collective-permute-start(bf16[64,2048]{1,0:T(8,128)(2,1)S(1)} %get-tuple-element.201), channel_id=1, source_target_pairs={{0,8},{8,16},{16,24},{24,28},{28,20},{20,12},{12,4},{4,0},{1,9},{9... | collective-permute-start | bytes 786440 | tf_op jit(solution)/shard_map/ppermute | solution.py:134
  439.6 111.3 %reduce-scatter.11.cloned.1.call-start = ((), (), s32[]{:S(2)}) async-start(), calls=%async_computation.14 | async-start | bytes 7208960 | tf_op jit(solution)/shard_map/reduce_scatter | solution.py:259
  444.2 12.9 %collective-permute-start.38 = (bf16[128,2048]{1,0:T(8,128)(2,1)S(1)}, bf16[128,2048]{1,0:T(8,128)(2,1)}, u32[]{:S(2)}, u32[]{:S(2)}) collective-permute-start(bf16[128,2048]{1,0:T(8,128)(2,1)S(1)} %fusion.130), channel_id=1, source_target_pairs={{0,8},{8,16},{16,24},{24,28},{28,20},{20,12},{12,4},{4,0},{1,9},{9... | collective-permute-start | bytes 1572872 | tf_op jit(solution)/shard_map/ppermute | solution.py:106
  445.4 13.2 %collective-permute-start.39 = (bf16[128,2048]{1,0:T(8,128)(2,1)S(1)}, bf16[128,2048]{1,0:T(8,128)(2,1)}, u32[]{:S(2)}, u32[]{:S(2)}) collective-permute-start(bf16[128,2048]{1,0:T(8,128)(2,1)S(1)} %fusion.130), channel_id=1, source_target_pairs={{8,0},{16,8},{24,16},{28,24},{20,28},{12,20},{4,12},{0,4},{9,1},{1... | collective-permute-start | bytes 1572872 | tf_op jit(solution)/shard_map/ppermute | solution.py:107
  493.2 57.6 %all-to-all-start.3 = ((bf16[8,64,1408]{2,1,0:T(8,128)(2,1)}), bf16[8,64,1408]{2,1,0:T(8,128)(2,1)S(1)}, u32[]{:S(2)}, u32[]{:S(2)}) async-start(bf16[8,64,1408]{2,1,0:T(8,128)(2,1)} %bitcast.349), calls=%async_computation.6 | async-start | bytes 2883584 | tf_op jit(solution)/shard_map/all_to_all | solution.py:442
  499.3 126.9 %reduce-scatter.13.cloned.1.call-start = ((), (), s32[]{:S(2)}) async-start(), calls=%async_computation.15 | async-start | bytes 4915200 | tf_op jit(solution)/shard_map/reduce_scatter | solution.py:491
  573.3 134.5 %reduce-scatter.15.cloned.1.call-start = ((), (), s32[]{:S(2)}) async-start(), calls=%async_computation.16 | async-start | bytes 1310720 | tf_op jit(solution)/shard_map/reduce_scatter | solution.py:259
  626.2 83.4 %reduce-scatter.17.cloned.1.call-start = ((), (), s32[]{:S(2)}) async-start(), calls=%async_computation.17 | async-start | bytes 3604480 | tf_op jit(solution)/shard_map/reduce_scatter | solution.py:259
  635.6 53.9 %all-to-all-start.4 = ((bf16[8,80,768]{2,1,0:T(8,128)(2,1)}), bf16[8,80,768]{2,1,0:T(8,128)(2,1)}, u32[]{:S(2)}, u32[]{:S(2)}) async-start(bf16[8,80,768]{2,1,0:T(8,128)(2,1)} %bitcast.356), calls=%async_computation.8 | async-start | bytes 1966080 | tf_op jit(solution)/shard_map/all_to_all | solution.py:500
  642.6 28.1 %collective-permute-start.59 = (bf16[128,2048]{1,0:T(8,128)(2,1)S(1)}, bf16[128,2048]{1,0:T(8,128)(2,1)S(1)}, u32[]{:S(2)}, u32[]{:S(2)}) collective-permute-start(bf16[128,2048]{1,0:T(8,128)(2,1)S(1)} %pad_maximum_fusion.16), channel_id=1, source_target_pairs={{8,0},{16,8},{24,16},{28,24},{20,28},{12,20},{4,12},{0,4},{9,1},{1... | collective-permute-start | bytes 1572872 | tf_op jit(solution)/shard_map/ppermute | solution.py:144
  642.7 28.0 %collective-permute-start.55 = (bf16[128,2048]{1,0:T(8,128)(2,1)S(1)}, bf16[128,2048]{1,0:T(8,128)(2,1)S(1)}, u32[]{:S(2)}, u32[]{:S(2)}) collective-permute-start(bf16[128,2048]{1,0:T(8,128)(2,1)S(1)} %pad_maximum_fusion.15), channel_id=1, source_target_pairs={{0,8},{8,16},{16,24},{24,28},{28,20},{20,12},{12,4},{4,0},{1,9},{9... | collective-permute-start | bytes 1572872 | tf_op jit(solution)/shard_map/ppermute | solution.py:143
  687.5 16.5 %collective-permute-start.57 = (bf16[128,2048]{1,0:T(8,128)(2,1)}, bf16[128,2048]{1,0:T(8,128)(2,1)}, u32[]{:S(2)}, u32[]{:S(2)}) collective-permute-start(bf16[128,2048]{1,0:T(8,128)(2,1)} %get-tuple-element.175), channel_id=1, source_target_pairs={{0,8},{8,16},{16,24},{24,28},{28,20},{20,12},{12,4},{4,0},{1,9},{9... | collective-permute-start | bytes 1572872 | tf_op jit(solution)/shard_map/ppermute | solution.py:143
  687.8 16.2 %collective-permute-start.61 = (bf16[128,2048]{1,0:T(8,128)(2,1)}, bf16[128,2048]{1,0:T(8,128)(2,1)}, u32[]{:S(2)}, u32[]{:S(2)}) collective-permute-start(bf16[128,2048]{1,0:T(8,128)(2,1)} %get-tuple-element.176), channel_id=1, source_target_pairs={{8,0},{16,8},{24,16},{28,24},{20,28},{12,20},{4,12},{0,4},{9,1},{1... | collective-permute-start | bytes 1572872 | tf_op jit(solution)/shard_map/ppermute | solution.py:144
  (140 other events, 1250.1 us)
Sparse Core Ops, SparseCore 0:
  40.6 53.4 all-gather.9
  95.6 89.2 all-gather.13
  187.0 43.5 all-gather.11
  232.6 75.5 all-gather.7
  340.1 90.3 reduce-scatter.6
  439.6 53.6 reduce-scatter.8
  495.9 54.8 reduce-scatter.10
  573.4 43.5 reduce-scatter.12
  626.4 24.0 reduce-scatter.14
  652.9 36.3 reduce-scatter.16

commit v14 on v13

--- a/solution.py
+++ b/solution.py
@@ -1,6 +1,10 @@
+import functools
+
 import jax
 import jax.numpy as jnp
 from jax import lax
+from jax.experimental import pallas as pl
+from jax.experimental.pallas import tpu as pltpu
 from jax.sharding import PartitionSpec as P
 
 HD = 128
@@ -205,6 +209,62 @@
         for peer in range(size)
     ]
     return jnp.concatenate(columns, axis=1).astype(jnp.float32)
+
+
+def attention_back_kernel(
+    q_ref, k_ref, v_ref, do_ref, lse_ref, key_ref, query_ref, dq_ref, dk_ref, dv_ref, *, rows
+):
+    f32, bf16 = jnp.float32, jnp.bfloat16
+    scale = HD ** (-0.5)
+    keys, values = k_ref[...], v_ref[...]
+    key_pos, key_seg = key_ref[:, 0:1], key_ref[:, 1:2]
+
+    def pair(a, b, dims):
+        return lax.dot_general(a, b, (dims, ((), ())), preferred_element_type=f32)
+
+    for start in range(0, q_ref.shape[0], rows):
+        here = slice(start, start + rows)
+        queries, upstream = q_ref[here, :], do_ref[here, :]
+        allowed = (key_pos <= query_ref[0:1, here]) & (key_seg == query_ref[1:2, here])
+        scores = jnp.where(allowed, pair(keys, queries, ((1,), (1,))) * scale, MASK_FILL)
+        weights = jnp.exp(scores - lse_ref[0, :, here])
+        grads = pair(values, upstream, ((1,), (1,)))
+        delta = jnp.sum(weights * grads, axis=0, keepdims=True)
+        grads = jnp.where(allowed, weights * (grads - delta), 0.0).astype(bf16)
+        part_v = pair(weights.astype(bf16), upstream, ((1,), (0,)))
+        part_k = pair(grads, queries, ((1,), (0,))) * scale
+        if start == 0:
+            dv_ref[...] = part_v
+            dk_ref[...] = part_k
+        else:
+            dv_ref[...] += part_v
+            dk_ref[...] += part_k
+        dq_ref[here, :] = pair(grads, keys, ((0,), (0,))) * scale
+
+
+def attention_back(queries, keys, values, upstream, log_total, positions, seg_rows):
+    tokens, width = queries.shape
+    heads = width // HD
+    marks = jnp.stack([positions, seg_rows], axis=0)
+    by_head = pl.BlockSpec((tokens, HD), lambda h: (0, h))
+    return pl.pallas_call(
+        functools.partial(attention_back_kernel, rows=min(256, tokens)),
+        grid=(heads,),
+        in_specs=[by_head] * 4
+        + [
+            pl.BlockSpec((1, 1, tokens), lambda h: (h, 0, 0)),
+            pl.BlockSpec((tokens, 2), lambda h: (0, 0)),
+            pl.BlockSpec((2, tokens), lambda h: (0, 0)),
+        ],
+        out_specs=[by_head] * 3,
+        out_shape=[jax.ShapeDtypeStruct((tokens, width), jnp.float32)] * 3,
+        compiler_params=pltpu.CompilerParams(vmem_limit_bytes=40 * 1024 * 1024),
+        cost_estimate=pl.CostEstimate(
+            flops=10 * tokens * tokens * width,
+            bytes_accessed=20 * tokens * width,
+            transcendentals=tokens * tokens * heads,
+        ),
+    )(queries, keys, values, upstream, log_total.reshape(heads, 1, tokens), marks.T, marks)
 
 
 def local_split(
@@ -437,33 +497,33 @@
 
     grad_mixed, sum_expert_in = after(grad_resid.astype(bf16), sum_expert_in)
     mixed_all = ring_gather(grad_mixed, ctx_size, ctx_index)
-    grad_attn = dot_t(mixed_all, out_weight).astype(bf16).reshape(head_shape)
+    grad_attn = dot_t(mixed_all, out_weight).astype(bf16)
     grad_attn, sum_shared_in = after(grad_attn, sum_shared_in)
     sum_shared_in = lax.all_to_all(
         sum_shared_in, "ctx", split_axis=0, concat_axis=0, tiled=True
     )
-    grad_weights = jnp.einsum("qhd,khd->hqk", grad_attn, values, preferred_element_type=f32)
-    delta = jnp.sum(weights * grad_weights, axis=-1, keepdims=True)
-    grad_scores = jnp.where(allowed[None], weights * (grad_weights - delta), 0.0).astype(bf16)
-    grad_q = jnp.einsum("hqk,khd->qhd", grad_scores, keys, preferred_element_type=f32) * score_scale
-    grad_k = (
-        jnp.einsum("hqk,qhd->khd", grad_scores, queries, preferred_element_type=f32) * score_scale
-    )
-    grad_v = jnp.einsum("hqk,qhd->khd", weights_low, grad_attn, preferred_element_type=f32)
+    grad_q, grad_k, grad_v = attention_back(
+        queries.reshape(seq_len, own_width),
+        keys.reshape(seq_len, own_width),
+        values.reshape(seq_len, own_width),
+        grad_attn,
+        log_total,
+        positions,
+        seg_rows,
+    )
     grad_projected = jnp.concatenate(
         [
-            rotate_back(grad_q, cos_tab, sine_tab).reshape(seq_len, own_width),
-            rotate_back(grad_k, cos_tab, sine_tab).reshape(seq_len, own_width),
-            grad_v.reshape(seq_len, own_width),
+            rotate_back(grad_q.reshape(head_shape), cos_tab, sine_tab).reshape(seq_len, own_width),
+            rotate_back(grad_k.reshape(head_shape), cos_tab, sine_tab).reshape(seq_len, own_width),
+            grad_v,
         ],
         axis=-1,
     ).astype(bf16)
-    grad_projected, sum_expert_out, sum_shared_in = after(
-        grad_projected, sum_expert_out, sum_shared_in
-    )
     one_sums = dot_t(grad_projected, qkv_weight)
     grad_gain_one = jnp.sum(one_sums * scaled_rows.astype(f32), axis=0)
-    one_parts = one_sums.astype(bf16)
+    one_parts, sum_expert_out, sum_shared_in = after(
+        one_sums.astype(bf16), sum_expert_out, sum_shared_in
+    )
     one_kept, grad_projected = after(one_parts, grad_projected)
     one_kept, attn_own = after(one_kept, attn_own)
     grad_normed = ring_scatter(one_parts, ctx_size, ctx_index, one_kept)

time: 730 us -> 723 us (level)
  matrix products: 193 us -> 145 us
  waiting for transfers between devices: 178 us -> 209 us
  Pallas kernels: 0 us -> 9.56 us
    dot_general x4 -> x0, matrix products: 46.5 us -> none  [the longest x1 17.1 us: local_split(): jnp.einsum('hqk,qhd->khd', grad_scores, queries, preferred_element_type=f32)]
    reduce_scatter x4, waiting for transfers between devices: 0.13 us -> 31.4 us  [sum_rows(): lax.psum_scatter(grad.astype(bf16), 'fsdp', scatter_dimension=0, tiled=True)]
    pallas_call x0 -> x1, Pallas kernels: none -> 9.56 us  [attention_back(): pl.pallas_call(functools.partial(attention_back_kernel, rows=min(256, tok...]
  transfers between devices with their start and end apart: 76 -> 76, of which waited for: 38 -> 37; matrix products, arithmetic and copies ran while one was open for 47% -> 42% of each run, Pallas kernels for 0% -> 1%
where the time goes in v14:
time: 723 us; the launch traced here: 712 us
  waiting for transfers between devices  209 us (29%)
  matrix products  145 us (20%)
  local copies, waits for them, and re-layouts  115 us (16%)
  other arithmetic  98.7 us (14%)
  starting transfers between devices  84.2 us (12%)
  blocking collectives  29.7 us (4%)
  between operations  21 us (3%)
  Pallas kernels  9.56 us (1%)
    ppermute x12, waiting for transfers between devices, ring_sums(): rear = lax.ppermute(rear, 'ctx', back)  49.7 us
    ppermute x9, waiting for transfers between devices, ring_gather(): fore = lax.ppermute(fore, 'ctx', ahead)  48.5 us
    dot_general x7, matrix products, dot_t(): lax.dot_general(a, b, (((1,), (1,)), ((), ())), preferred_element_type=f32)  45.4 us
    dot_general x8, matrix products, dot(): return jnp.dot(a, b, preferred_element_type=f32)  44.1 us
    dot_general x8, matrix products, t_dot(): lax.dot_general(a, b, (((0,), (0,)), ((), ())), preferred_element_type=f32)  41.2 us
    ppermute x12, waiting for transfers between devices, ring_sums(): fore = lax.ppermute(fore, 'ctx', ahead)  35.8 us
    reduce_scatter x4, waiting for transfers between devices, sum_rows(): lax.psum_scatter(grad.astype(bf16), 'fsdp', scatter_dimension=0, tiled=True)  31.4 us
    all_to_all x1, blocking collectives, local_split(): lax.all_to_all(pieces, 'ctx', split_axis=0, concat_axis=0, tiled=True)  29.7 us
  transfers between devices with their start and end apart: 76, of which 37 were waited for; matrix products, arithmetic and copies ran while one was open for 42% of the time, Pallas kernels for 1%

profile of v14, /device:TPU:8, one launch (start us, length us, event | category | flops | bytes accessed | tf_op | source)
XLA Modules:
  0.0 712.2 jit_solution(17308062691129863323)
XLA Ops:
  10.7 29.7 %all_to_all.25 = bf16[8,80,768]{2,1,0:T(8,128)(2,1)} all-to-all(bf16[8,80,768]{2,1,0:T(8,128)(2,1)S(1)} %pad_maximum_fusion.6), channel_id=1, replica_groups=mesh['ctx'=8,'fsdp'=4] {'ctx'}, dimensions={0} | all-to-all | bytes 1966080 | tf_op jit(solution)/shard_map/all_to_all | solution.py:330
  72.0 7.1 collective-permute-done.4
  83.6 7.4 %collective-permute-done.6 = bf16[128,2048]{1,0:T(8,128)(2,1)S(1)} collective-permute-done((bf16[128,2048]{1,0:T(8,128)(2,1)S(1)}, bf16[128,2048]{1,0:T(8,128)(2,1)S(1)}, u32[]{:S(2)}, u32[]{:S(2)}) %collective-permute-start.6) | collective-permute-done | bytes 524320 | tf_op jit(solution)/shard_map/ppermute | solution.py:110
  115.5 6.4 fusion.24
  148.4 6.7 collective-permute-done.12
  179.8 7.2 %collective-permute-done.14 = bf16[128,2048]{1,0:T(8,128)(2,1)} collective-permute-done((bf16[128,2048]{1,0:T(8,128)(2,1)}, bf16[128,2048]{1,0:T(8,128)(2,1)}, u32[]{:S(2)}, u32[]{:S(2)}) %collective-permute-start.14) | collective-permute-done | bytes 524320 | tf_op jit(solution)/shard_map/ppermute | solution.py:147
  237.5 6.3 collective-permute-done.24
  247.7 11.6 %collective-permute-done.26 = bf16[64,2048]{1,0:T(8,128)(2,1)S(1)} collective-permute-done((bf16[64,2048]{1,0:T(8,128)(2,1)S(1)}, bf16[64,2048]{1,0:T(8,128)(2,1)S(1)}, u32[]{:S(2)}, u32[]{:S(2)}) %collective-permute-start.26) | collective-permute-done | bytes 262176 | tf_op jit(solution)/shard_map/ppermute | solution.py:116
  271.1 10.3 %fusion.2 = f32[512,2816]{1,0:T(8,128)S(1)} fusion(bf16[512,2048]{1,0:T(8,128)(2,1)S(1)} %bitcast.387, bf16[1,2048,2816]{2,1,0:T(8,128)(2,1)} %all-gather.14.cloned.1.call-done), kind=kOutput, calls=%fused_computation.2 | convolution fusion | flops 5905580032 | bytes 19398656 | tf_op jit(solution)/shard_map/dot_general | solution.py:305
  285.9 6.2 convolution_convert_fusion.6
  297.8 8.5 %fusion.104 = f32[1024,1408]{1,0:T(8,128)S(1)} fusion(bf16[1024,2048]{1,0:T(8,128)(2,1)} %constant_dynamic-update-slice_fusion.4, bf16[2048,1408]{1,0:T(8,128)(2,1)S(1)} %bitcast.357), kind=kOutput, calls=%fused_computation.315 | convolution fusion | flops 5905580032 | bytes 15728640 | tf_op jit(solution)/shard_map/dot_general | solution.py:305
  310.9 5.8 fusion.8
  324.7 7.4 %multiply_convert_fusion.6 = (bf16[512,1408]{1,0:T(8,128)(2,1)S(1)}, bf16[512,1408]{1,0:T(8,128)(2,1)S(1)}, f32[512]{0:T(512)S(1)}) fusion(f32[512,2816]{1,0:T(8,128)S(1)} %bitcast.362, bf16[512,1408]{1,0:T(8,128)(2,1)S(1)} %copy-done.43, bf16[512,2048]{1,0:T(8,128)(2,1)S(1)} %bitcast.389, bf16[1408,2048]{1,0:T(8,128)(2,1)} %bitcast.364), kind=kOutput, calls=%fused_computation.51 | convolution fusion | flops 2964323840 | bytes 17958912 | tf_op jit(solution)/shard_map/dot_general | solution.py:308
  333.2 9.4 %convolution_convert_fusion = bf16[2048,2816]{1,0:T(8,128)(2,1)} fusion(bf16[512,2048]{1,0:T(8,128)(2,1)S(1)} %bitcast.388, bf16[512,1408]{1,0:T(8,128)(2,1)S(1)} %get-tuple-element.178, bf16[512,1408]{1,0:T(8,128)(2,1)S(1)} %get-tuple-element.177), kind=kOutput, calls=%fused_computation.4 | convolution fusion | flops 5917114368 | bytes 16515072 | tf_op jit(solution)/shard_map/dot_general | solution.py:311
  342.9 11.8 %multiply_convert_fusion.3 = (bf16[1024,704]{1,0:T(8,128)(2,1)S(1)}, bf16[1024,704]{1,0:T(8,128)(2,1)}, f32[1024]{0:T(1024)S(1)}) fusion(f32[1024,1408]{1,0:T(8,128)} %copy-done.16, bf16[1024,704]{1,0:T(8,128)(2,1)} %copy-done.40, bf16[1024,2048]{1,0:T(8,128)(2,1)} %multiply_convert_fusion, bf16[704,2048]{1,0:T(8,128)(2,1)} %bitcast.382), kind=kOutput, calls=%fused_computation.36 | convolution fusion | flops 2964323328 | bytes 17174528 | tf_op jit(solution)/shard_map/dot_general | solution.py:308
  363.4 9.1 %fusion.20 = bf16[512,2048]{1,0:T(8,128)(2,1)S(1)} fusion(bf16[1,2048,2816]{2,1,0:T(8,128)(2,1)} %all-gather.14.cloned.1.call-done, bf16[512,1408]{1,0:T(8,128)(2,1)S(1)} %copy-done.90, bf16[512,1408]{1,0:T(8,128)(2,1)S(1)} %copy-done.88), kind=kOutput, calls=%fused_computation.39 | convolution fusion | flops 5912395776 | bytes 16515072 | tf_op jit(solution)/shard_map/dot_general | solution.py:308
  373.9 8.4 %fusion.6 = bf16[1024,2048]{1,0:T(8,128)(2,1)S(1)} fusion(f32[8,128,2048]{2,1,0:T(8,128)S(1)} %fusion.55, bf16[1024,1408]{1,0:T(8,128)(2,1)} %pad_maximum_fusion.2, bf16[2048,1408]{1,0:T(8,128)(2,1)S(1)} %bitcast.360), kind=kOutput, calls=%fused_computation.10 | convolution fusion | flops 5909774336 | bytes 21233664 | tf_op jit(solution)/shard_map/dot_general | solution.py:308
  384.5 11.8 %convolution_convert_fusion.2 = bf16[2048,1408]{1,0:T(8,128)(2,1)} fusion(bf16[1024,2048]{1,0:T(8,128)(2,1)} %constant_dynamic-update-slice_fusion.4, bf16[1024,1408]{1,0:T(8,128)(2,1)} %pad_maximum_fusion.2), kind=kOutput, calls=%fused_computation.19 | convolution fusion | flops 5908463616 | bytes 12845056 | tf_op jit(solution)/shard_map/dot_general | solution.py:311
  415.6 7.9 %collective-permute-done.32 = bf16[128,2048]{1,0:T(8,128)(2,1)S(1)} collective-permute-done((bf16[128,2048]{1,0:T(8,128)(2,1)S(1)}, bf16[128,2048]{1,0:T(8,128)(2,1)S(1)}, u32[]{:S(2)}, u32[]{:S(2)}) %collective-permute-start.32) | collective-permute-done | bytes 524320 | tf_op jit(solution)/shard_map/ppermute | solution.py:147
  440.4 5.7 copy.245
  456.0 9.3 %collective-permute-done.38 = bf16[128,2048]{1,0:T(8,128)(2,1)} collective-permute-done((bf16[128,2048]{1,0:T(8,128)(2,1)}, bf16[128,2048]{1,0:T(8,128)(2,1)}, u32[]{:S(2)}, u32[]{:S(2)}) %collective-permute-start.38) | collective-permute-done | bytes 524320 | tf_op jit(solution)/shard_map/ppermute | solution.py:110
  470.9 5.6 collective-permute-done.40
  500.8 6.1 all-to-all-start.3
  506.8 9.6 %shard_map.309 = (f32[1024,256]{1,0:T(8,128)S(1)}, f32[1024,256]{1,0:T(8,128)S(1)}, f32[1024,256]{1,0:T(8,128)S(1)}) custom-call(bf16[1024,256]{1,0:T(8,128)(2,1)S(1)} %copy_bitcast_fusion.4.q_ref, bf16[1024,256]{1,0:T(8,128)(2,1)S(1)} %get-tuple-element.222.k_ref, bf16[1024,256]{1,0:T(8,128)(2,1)S(1)} %slice.585.v_ref, ...), custom_call_target="tpu_custom_call" | custom-call | flops 2684354560 | bytes 5242880 | tf_op jit(solution)/shard_map/pallas_call | solution.py:250
  519.8 7.0 fusion.5
  527.0 31.4 %reduce-scatter.11.cloned.1.call-done = bf16[352,2048]{1,0:T(8,128)(2,1)} async-done(((bf16[1408,2048]{1,0:T(8,128)(2,1)}), bf16[352,2048]{1,0:T(8,128)(2,1)}) %reduce-scatter.11.cloned.1.call-update) | async-done | bytes 1441808 | tf_op jit(solution)/shard_map/reduce_scatter | solution.py:319
  558.4 7.5 %fusion.17 = bf16[2048,768]{1,0:T(8,128)(2,1)} fusion(bf16[1024,768]{1,0:T(8,128)(2,1)S(1)} %pad_maximum_fusion.5, bf16[1024,2048]{1,0:T(8,128)(2,1)} %constant_dynamic-update-slice_fusion.18, f32[2048]{0:T(1024)S(1)} %copy-done.61), kind=kOutput, calls=%fused_computation.31 | convolution fusion | flops 3229089792 | bytes 8921088 | tf_op jit(solution)/shard_map/dot_general | solution.py:311
  574.8 6.0 collective-permute-done.46
  585.4 10.4 %collective-permute-done.51 = bf16[128,2048]{1,0:T(8,128)(2,1)S(1)} collective-permute-done((bf16[128,2048]{1,0:T(8,128)(2,1)S(1)}, bf16[128,2048]{1,0:T(8,128)(2,1)S(1)}, u32[]{:S(2)}, u32[]{:S(2)}) %collective-permute-start.51) | collective-permute-done | bytes 524320 | tf_op jit(solution)/shard_map/ppermute | solution.py:148
  598.6 9.4 %collective-permute-done.48 = bf16[128,2048]{1,0:T(8,128)(2,1)S(1)} collective-permute-done((bf16[128,2048]{1,0:T(8,128)(2,1)S(1)}, bf16[128,2048]{1,0:T(8,128)(2,1)S(1)}, u32[]{:S(2)}, u32[]{:S(2)}) %collective-permute-start.48) | collective-permute-done | bytes 524320 | tf_op jit(solution)/shard_map/ppermute | solution.py:147
  614.0 6.0 collective-permute-done.49
  642.6 22.5 %collective-permute-done.59 = bf16[128,2048]{1,0:T(8,128)(2,1)S(1)} collective-permute-done((bf16[128,2048]{1,0:T(8,128)(2,1)S(1)}, bf16[128,2048]{1,0:T(8,128)(2,1)S(1)}, u32[]{:S(2)}, u32[]{:S(2)}) %collective-permute-start.59) | collective-permute-done | bytes 524320 | tf_op jit(solution)/shard_map/ppermute | solution.py:148
  (577 shorter events, 375.7 us)
Async XLA Ops:
  7.2 97.5 %all-gather.10.cloned.1.call-start = ((), (), s32[]{:S(2)}) async-start(), calls=%async_computation.18 | async-start | bytes 4915200 | tf_op jit(solution)/shard_map/all_gather | solution.py:334
  40.5 230.6 %all-gather.14.cloned.1.call-start = ((), (), s32[]{:S(2)}) async-start(), calls=%async_computation.20 | async-start | bytes 14417920 | tf_op jit(solution)/shard_map/all_gather | solution.py:349
  45.2 21.6 %collective-permute-start.2 = (bf16[128,2048]{1,0:T(8,128)(2,1)}, bf16[128,2048]{1,0:T(8,128)(2,1)}, u32[]{:S(2)}, u32[]{:S(2)}) collective-permute-start(bf16[128,2048]{1,0:T(8,128)(2,1)} %get-tuple-element.276), channel_id=1, source_target_pairs={{0,8},{8,16},{16,24},{24,28},{28,20},{20,12},{12,4},{4,0},{1,9},{9... | collective-permute-start | bytes 1572872 | tf_op jit(solution)/shard_map/ppermute | solution.py:110
  45.7 21.7 %collective-permute-start.3 = (bf16[128,2048]{1,0:T(8,128)(2,1)}, bf16[128,2048]{1,0:T(8,128)(2,1)S(1)}, u32[]{:S(2)}, u32[]{:S(2)}) collective-permute-start(bf16[128,2048]{1,0:T(8,128)(2,1)} %get-tuple-element.276), channel_id=1, source_target_pairs={{8,0},{16,8},{24,16},{28,24},{20,28},{12,20},{4,12},{0,4},{9,1},{1... | collective-permute-start | bytes 1572872 | tf_op jit(solution)/shard_map/ppermute | solution.py:111
  47.2 79.3 %collective-permute-start.10 = (bf16[64,2048]{1,0:T(8,128)(2,1)S(1)}, bf16[64,2048]{1,0:T(8,128)(2,1)}, u32[]{:S(2)}, u32[]{:S(2)}) collective-permute-start(bf16[64,2048]{1,0:T(8,128)(2,1)S(1)} %copy-done.48), channel_id=1, source_target_pairs={{0,2},{1,3},{2,0},{3,1},{4,6},{5,7},{6,4},{7,5},{8,10},{9,11},{10,... | collective-permute-start | bytes 786440 | tf_op jit(solution)/shard_map/ppermute | solution.py:173
  48.7 89.5 %collective-permute-start.1 = (bf16[176,2048]{1,0:T(8,128)(2,1)}, bf16[176,2048]{1,0:T(8,128)(2,1)}, u32[]{:S(2)}, u32[]{:S(2)}) collective-permute-start(bf16[176,2048]{1,0:T(8,128)(2,1)} %param.34), channel_id=1, source_target_pairs={{0,2},{1,3},{2,0},{3,1},{4,6},{5,7},{6,4},{7,5},{8,10},{9,11},{10,... | collective-permute-start | bytes 2162696 | tf_op jit(solution)/shard_map/ppermute | solution.py:173
  49.2 89.0 %collective-permute-start = (bf16[352,2048]{1,0:T(8,128)(2,1)}, bf16[352,2048]{1,0:T(8,128)(2,1)}, u32[]{:S(2)}, u32[]{:S(2)}) collective-permute-start(bf16[352,2048]{1,0:T(8,128)(2,1)} %bitcast.1), channel_id=1, source_target_pairs={{0,2},{1,3},{2,0},{3,1},{4,6},{5,7},{6,4},{7,5},{8,10},{9,11},{10,... | collective-permute-start | bytes 4325384 | tf_op jit(solution)/shard_map/ppermute | solution.py:173
  98.9 46.1 %all-to-all-start.1 = ((bf16[8,64,1408]{2,1,0:T(8,128)(2,1)}), bf16[8,64,1408]{2,1,0:T(8,128)(2,1)}, u32[]{:S(2)}, u32[]{:S(2)}) async-start(bf16[8,64,1408]{2,1,0:T(8,128)(2,1)} %reshape.884), calls=%async_computation.1 | async-start | bytes 2883584 | tf_op jit(solution)/shard_map/all_to_all | solution.py:333
  104.5 187.7 %all-gather.12.cloned.1.call-start = ((), (), s32[]{:S(2)}) async-start(), calls=%async_computation.19 | async-start | bytes 7208960 | tf_op jit(solution)/shard_map/all_gather | solution.py:386
  145.0 171.7 %all-gather.8.cloned.1.call-start = ((), (), s32[]{:S(2)}) async-start(), calls=%async_computation.11 | async-start | bytes 4718592 | tf_op jit(solution)/shard_map/all_gather | solution.py:394
  157.5 13.5 %collective-permute-start.17 = (bf16[128,2048]{1,0:T(8,128)(2,1)S(1)}, bf16[128,2048]{1,0:T(8,128)(2,1)}, u32[]{:S(2)}, u32[]{:S(2)}) collective-permute-start(bf16[128,2048]{1,0:T(8,128)(2,1)S(1)} %pad_maximum_fusion.10), channel_id=1, source_target_pairs={{8,0},{16,8},{24,16},{28,24},{20,28},{12,20},{4,12},{0,4},{9,1},{1... | collective-permute-start | bytes 1572872 | tf_op jit(solution)/shard_map/ppermute | solution.py:148
  158.1 13.6 %collective-permute-start.13 = (bf16[128,2048]{1,0:T(8,128)(2,1)S(1)}, bf16[128,2048]{1,0:T(8,128)(2,1)S(1)}, u32[]{:S(2)}, u32[]{:S(2)}) collective-permute-start(bf16[128,2048]{1,0:T(8,128)(2,1)S(1)} %pad_maximum_fusion.9), channel_id=1, source_target_pairs={{0,8},{8,16},{16,24},{24,28},{28,20},{20,12},{12,4},{4,0},{1,9},{9... | collective-permute-start | bytes 1572872 | tf_op jit(solution)/shard_map/ppermute | solution.py:147
  164.7 56.9 %collective-permute-start.28 = (bf16[2,352,2048]{2,1,0:T(8,128)(2,1)}, bf16[2,352,2048]{2,1,0:T(8,128)(2,1)}, u32[]{:S(2)}, u32[]{:S(2)}) collective-permute-start(bf16[2,352,2048]{2,1,0:T(8,128)(2,1)} %maximum_select_fusion.1), channel_id=1, source_target_pairs={{0,1},{1,0},{2,3},{3,2},{4,5},{5,4},{6,7},{7,6},{8,9},{9,8},{10,11... | collective-permute-start | bytes 8650760 | tf_op jit(solution)/shard_map/ppermute | solution.py:178
  179.8 32.5 %collective-permute-start.29 = (bf16[2,176,2048]{2,1,0:T(8,128)(2,1)S(1)}, bf16[2,176,2048]{2,1,0:T(8,128)(2,1)}, u32[]{:S(2)}, u32[]{:S(2)}) collective-permute-start(bf16[2,176,2048]{2,1,0:T(8,128)(2,1)S(1)} %maximum_select_fusion.3), channel_id=1, source_target_pairs={{0,1},{1,0},{2,3},{3,2},{4,5},{5,4},{6,7},{7,6},{8,9},{9,8},{10,11... | collective-permute-start | bytes 4325384 | tf_op jit(solution)/shard_map/ppermute | solution.py:178
  235.8 217.4 %reduce-scatter.7.cloned.1.call-start = ((), (), s32[]{:S(2)}) async-start(), calls=%async_computation.12 | async-start | bytes 14417920 | tf_op jit(solution)/shard_map/reduce_scatter | solution.py:319
  243.8 15.5 %collective-permute-start.26 = (bf16[64,2048]{1,0:T(8,128)(2,1)S(1)}, bf16[64,2048]{1,0:T(8,128)(2,1)S(1)}, u32[]{:S(2)}, u32[]{:S(2)}) collective-permute-start(bf16[64,2048]{1,0:T(8,128)(2,1)S(1)} %slice.499), channel_id=1, source_target_pairs={{0,8},{8,16},{16,24},{24,28},{28,20},{20,12},{12,4},{4,0},{1,9},{9... | collective-permute-start | bytes 786440 | tf_op jit(solution)/shard_map/ppermute | solution.py:116
  245.2 18.0 %collective-permute-start.27 = (bf16[64,2048]{1,0:T(8,128)(2,1)S(1)}, bf16[64,2048]{1,0:T(8,128)(2,1)S(1)}, u32[]{:S(2)}, u32[]{:S(2)}) collective-permute-start(bf16[64,2048]{1,0:T(8,128)(2,1)S(1)} %slice.500), channel_id=1, source_target_pairs={{8,0},{16,8},{24,16},{28,24},{20,28},{12,20},{4,12},{0,4},{9,1},{1... | collective-permute-start | bytes 786440 | tf_op jit(solution)/shard_map/ppermute | solution.py:117
  355.4 85.0 %all-to-all-start.2 = ((f32[8,2,128]{2,1,0:T(2,128)}), f32[8,2,128]{2,1,0:T(2,128)S(1)}, u32[]{:S(2)}, u32[]{:S(2)}) async-start(f32[8,2,128]{2,1,0:T(2,128)} %pad_maximum_fusion.17), calls=%async_computation.2 | async-start | bytes 16384 | tf_op jit(solution)/shard_map/all_to_all | solution.py:466
  359.3 141.5 %reduce-scatter.9.cloned.1.call-start = ((), (), s32[]{:S(2)}) async-start(), calls=%async_computation.13 | async-start | bytes 7208960 | tf_op jit(solution)/shard_map/reduce_scatter | solution.py:471
  382.4 13.9 %collective-permute-start.30 = (bf16[64,2048]{1,0:T(8,128)(2,1)S(1)}, bf16[64,2048]{1,0:T(8,128)(2,1)S(1)}, u32[]{:S(2)}, u32[]{:S(2)}) collective-permute-start(bf16[64,2048]{1,0:T(8,128)(2,1)S(1)} %get-tuple-element.207), channel_id=1, source_target_pairs={{0,8},{8,16},{16,24},{24,28},{28,20},{20,12},{12,4},{4,0},{1,9},{9... | collective-permute-start | bytes 786440 | tf_op jit(solution)/shard_map/ppermute | solution.py:138
  410.7 12.9 %collective-permute-start.32 = (bf16[128,2048]{1,0:T(8,128)(2,1)S(1)}, bf16[128,2048]{1,0:T(8,128)(2,1)S(1)}, u32[]{:S(2)}, u32[]{:S(2)}) collective-permute-start(bf16[128,2048]{1,0:T(8,128)(2,1)S(1)} %get-tuple-element.203), channel_id=1, source_target_pairs={{0,8},{8,16},{16,24},{24,28},{28,20},{20,12},{12,4},{4,0},{1,9},{9... | collective-permute-start | bytes 1572872 | tf_op jit(solution)/shard_map/ppermute | solution.py:147
  412.6 13.2 %collective-permute-start.36 = (bf16[128,2048]{1,0:T(8,128)(2,1)S(1)}, bf16[128,2048]{1,0:T(8,128)(2,1)S(1)}, u32[]{:S(2)}, u32[]{:S(2)}) collective-permute-start(bf16[128,2048]{1,0:T(8,128)(2,1)S(1)} %get-tuple-element.204), channel_id=1, source_target_pairs={{8,0},{16,8},{24,16},{28,24},{20,28},{12,20},{4,12},{0,4},{9,1},{1... | collective-permute-start | bytes 1572872 | tf_op jit(solution)/shard_map/ppermute | solution.py:148
  446.3 112.1 %reduce-scatter.11.cloned.1.call-start = ((), (), s32[]{:S(2)}) async-start(), calls=%async_computation.14 | async-start | bytes 7208960 | tf_op jit(solution)/shard_map/reduce_scatter | solution.py:319
  500.8 57.6 %all-to-all-start.3 = ((bf16[8,64,1408]{2,1,0:T(8,128)(2,1)}), bf16[8,64,1408]{2,1,0:T(8,128)(2,1)}, u32[]{:S(2)}, u32[]{:S(2)}) async-start(bf16[8,64,1408]{2,1,0:T(8,128)(2,1)} %bitcast.391), calls=%async_computation.6 | async-start | bytes 2883584 | tf_op jit(solution)/shard_map/all_to_all | solution.py:502
  506.8 115.7 %reduce-scatter.13.cloned.1.call-start = ((), (), s32[]{:S(2)}) async-start(), calls=%async_computation.15 | async-start | bytes 4915200 | tf_op jit(solution)/shard_map/reduce_scatter | solution.py:551
  571.2 129.8 %reduce-scatter.15.cloned.1.call-start = ((), (), s32[]{:S(2)}) async-start(), calls=%async_computation.16 | async-start | bytes 1310720 | tf_op jit(solution)/shard_map/reduce_scatter | solution.py:319
  622.6 80.2 %reduce-scatter.17.cloned.1.call-start = ((), (), s32[]{:S(2)}) async-start(), calls=%async_computation.17 | async-start | bytes 3604480 | tf_op jit(solution)/shard_map/reduce_scatter | solution.py:319
  631.3 53.4 %all-to-all-start.4 = ((bf16[8,80,768]{2,1,0:T(8,128)(2,1)}), bf16[8,80,768]{2,1,0:T(8,128)(2,1)S(1)}, u32[]{:S(2)}, u32[]{:S(2)}) async-start(bf16[8,80,768]{2,1,0:T(8,128)(2,1)} %bitcast.400), calls=%async_computation.8 | async-start | bytes 1966080 | tf_op jit(solution)/shard_map/all_to_all | solution.py:560
  637.2 28.0 %collective-permute-start.59 = (bf16[128,2048]{1,0:T(8,128)(2,1)S(1)}, bf16[128,2048]{1,0:T(8,128)(2,1)S(1)}, u32[]{:S(2)}, u32[]{:S(2)}) collective-permute-start(bf16[128,2048]{1,0:T(8,128)(2,1)S(1)} %pad_maximum_fusion.16), channel_id=1, source_target_pairs={{8,0},{16,8},{24,16},{28,24},{20,28},{12,20},{4,12},{0,4},{9,1},{1... | collective-permute-start | bytes 1572872 | tf_op jit(solution)/shard_map/ppermute | solution.py:148
  637.3 27.9 %collective-permute-start.55 = (bf16[128,2048]{1,0:T(8,128)(2,1)S(1)}, bf16[128,2048]{1,0:T(8,128)(2,1)S(1)}, u32[]{:S(2)}, u32[]{:S(2)}) collective-permute-start(bf16[128,2048]{1,0:T(8,128)(2,1)S(1)} %pad_maximum_fusion.15), channel_id=1, source_target_pairs={{0,8},{8,16},{16,24},{24,28},{28,20},{20,12},{12,4},{4,0},{1,9},{9... | collective-permute-start | bytes 1572872 | tf_op jit(solution)/shard_map/ppermute | solution.py:147
  682.5 14.7 %collective-permute-start.57 = (bf16[128,2048]{1,0:T(8,128)(2,1)}, bf16[128,2048]{1,0:T(8,128)(2,1)}, u32[]{:S(2)}, u32[]{:S(2)}) collective-permute-start(bf16[128,2048]{1,0:T(8,128)(2,1)} %get-tuple-element.181), channel_id=1, source_target_pairs={{0,8},{8,16},{16,24},{24,28},{28,20},{20,12},{12,4},{4,0},{1,9},{9... | collective-permute-start | bytes 1572872 | tf_op jit(solution)/shard_map/ppermute | solution.py:147
  682.7 14.4 %collective-permute-start.61 = (bf16[128,2048]{1,0:T(8,128)(2,1)}, bf16[128,2048]{1,0:T(8,128)(2,1)}, u32[]{:S(2)}, u32[]{:S(2)}) collective-permute-start(bf16[128,2048]{1,0:T(8,128)(2,1)} %get-tuple-element.182), channel_id=1, source_target_pairs={{8,0},{16,8},{24,16},{28,24},{20,28},{12,20},{4,12},{0,4},{9,1},{1... | collective-permute-start | bytes 1572872 | tf_op jit(solution)/shard_map/ppermute | solution.py:148
  (140 other events, 1290.1 us)
Sparse Core Ops, SparseCore 0:
  40.6 53.4 all-gather.9
  95.6 88.9 all-gather.13
  186.3 43.5 all-gather.11
  235.9 74.3 all-gather.7
  342.8 90.0 reduce-scatter.6
  446.3 54.4 reduce-scatter.8
  503.5 54.8 reduce-scatter.10
  571.3 42.8 reduce-scatter.12
  622.7 23.2 reduce-scatter.14
  648.4 36.3 reduce-scatter.16

commit v15 on v14

--- a/solution.py
+++ b/solution.py
@@ -120,7 +120,7 @@
     return out if rider is None else (out, rider)
 
 
-def ring_sums(parts, size, ctx_index):
+def ring_sums(parts, size, ctx_index, riders):
     f32 = jnp.float32
     rows = parts.shape[0] // size
     ahead, back = ring_steps(size)
@@ -146,17 +146,20 @@
     for k in range(half - 1, 0, -1):
         fore = lax.ppermute(fore, "ctx", ahead)
         rear = lax.ppermute(rear, "ctx", back)
+        if riders and k == half - 1:
+            fore, *riders = after(fore, *riders)
         if k > 1:
             fore = low(fore.astype(f32) + own(k - 1, 0, rows))
             rear = low(rear.astype(f32) + own(1 - k, 0, rows))
-    return (fore, rear)
-
-
-def ring_scatter(parts, size, ctx_index, kept=None):
-    fore, rear = ring_sums(parts, size, ctx_index)
+    return (fore, rear, riders)
+
+
+def ring_scatter(parts, size, ctx_index, kept=None, riders=()):
+    fore, rear, riders = ring_sums(parts, size, ctx_index, riders)
     kept = (parts if kept is None else kept).reshape(size, -1, parts.shape[1])
     kept = lax.dynamic_index_in_dim(kept, ctx_index, 0, keepdims=False)
-    return kept.astype(jnp.float32) + fore.astype(jnp.float32) + rear.astype(jnp.float32)
+    total = kept.astype(jnp.float32) + fore.astype(jnp.float32) + rear.astype(jnp.float32)
+    return (total, *riders) if riders else total
 
 
 def other_core(size):
@@ -180,6 +183,20 @@
     out = lax.dynamic_update_index_in_dim(out, pair, index % 2, 1)
     out = lax.dynamic_update_index_in_dim(out, near, 1 - index % 2, 1)
     return (out.reshape(size * rows, width), hold)
+
+
+def fsdp_scatter(grad, size):
+    index = lax.axis_index("fsdp")
+    core, chip = index % 2, index // 2
+    grad = grad.reshape((2, 2) + grad.shape[1:])
+
+    def pick(array, at, axis):
+        return lax.dynamic_index_in_dim(array, at, axis, keepdims=False)
+
+    near = lax.ppermute(pick(grad, 1 - core, 1), "fsdp", other_core(size))
+    mine = (pick(grad, core, 1).astype(jnp.float32) + near.astype(jnp.float32)).astype(grad.dtype)
+    far = lax.ppermute(pick(mine, 1 - chip, 0), "fsdp", other_chip(size))
+    return pick(mine, chip, 0).astype(jnp.float32) + far.astype(jnp.float32)
 
 
 def column_pieces(weight, groups, size, extra):
@@ -521,12 +538,12 @@
     ).astype(bf16)
     one_sums = dot_t(grad_projected, qkv_weight)
     grad_gain_one = jnp.sum(one_sums * scaled_rows.astype(f32), axis=0)
-    one_parts, sum_expert_out, sum_shared_in = after(
-        one_sums.astype(bf16), sum_expert_out, sum_shared_in
-    )
+    one_parts = one_sums.astype(bf16)
     one_kept, grad_projected = after(one_parts, grad_projected)
     one_kept, attn_own = after(one_kept, attn_own)
-    grad_normed = ring_scatter(one_parts, ctx_size, ctx_index, one_kept)
+    grad_normed, sum_expert_out, sum_shared_in = ring_scatter(
+        one_parts, ctx_size, ctx_index, one_kept, (sum_expert_out, sum_shared_in)
+    )
     grad_qkv_weight = t_dot(normed_low, grad_projected)
     grad_bias = jnp.sum(grad_projected.astype(f32), axis=0).reshape(3, 1, own_width)
     grad_bias = jnp.where(
@@ -552,9 +569,12 @@
     grad_normed, pieces, out_parts, grad_shared_out, grad_out_weight = after(
         grad_normed, pieces, out_parts, grad_shared_out, grad_out_weight.astype(bf16)
     )
-    sum_shared_out = sum_rows(grad_shared_out)
+    sum_shared_out = fsdp_scatter(grad_shared_out.reshape(fsdp_size, -1, width), fsdp_size)
     sum_out_weight = sum_rows(grad_out_weight)
-    output = own_residual + ring_scatter(out_parts, ctx_size, ctx_index)
+    out_sum, sum_shared_out, sum_out_weight = ring_scatter(
+        out_parts, ctx_size, ctx_index, riders=(sum_shared_out, sum_out_weight)
+    )
+    output = own_residual + out_sum
     output = output.astype(bf16).reshape(tokens.shape)
     pieces = pieces.reshape(ctx_size, shard + more, 3 * own_width)
     pieces = lax.all_to_all(pieces, "ctx", split_axis=0, concat_axis=0, tiled=True)
@@ -577,7 +597,7 @@
         small_grads[3 * shard : router_end].reshape(shard, expert_count),
         small_grads[2 * shard : 3 * shard],
         merge_columns(sum_shared_in, 2, ctx_size),
-        sum_shared_out.astype(f32),
+        sum_shared_out,
         sum_expert_in.astype(f32)[None],
         sum_expert_out.astype(f32)[None],
     )

time: 723 us -> 726 us (level)
    ppermute x12, waiting for transfers between devices: 49.7 us -> 18.2 us  [ring_sums(): rear = lax.ppermute(rear, 'ctx', back)]
    reduce_scatter x4 -> x3, waiting for transfers between devices: 31.4 us -> 0.01 us  [sum_rows(): lax.psum_scatter(grad.astype(bf16), 'fsdp', scatter_dimension=0, tiled=True)]
    ppermute x4, waiting for transfers between devices: 12.7 us -> 39.2 us  [ring_sums(): fore = lax.ppermute(low(own(half, 0, cut)), 'ctx', ahead)]
    ppermute x12, waiting for transfers between devices: 35.8 us -> 55.2 us  [ring_sums(): fore = lax.ppermute(fore, 'ctx', ahead)]
    ppermute x0 -> x2, waiting for transfers between devices: none -> 15.5 us  [the longest x1 15.5 us: fsdp_scatter(): far = lax.ppermute(pick(mine, 1 - chip, 0), 'fsdp', other_chip(size))]
    unnamed x198 -> x204, local copies, waits for them, and re-layouts: 22.8 us -> 24.2 us
  transfers between devices with their start and end apart: 76 -> 77, of which waited for: 37 -> 38; matrix products, arithmetic and copies ran while one was open for 42% -> 43% of each run, Pallas kernels for 1% -> 1%
where the time goes in v15:
time: 726 us; the launch traced here: 715 us
  waiting for transfers between devices  209 us (29%)
  matrix products  146 us (20%)
  local copies, waits for them, and re-layouts  119 us (16%)
  other arithmetic  96.9 us (13%)
  starting transfers between devices  84.3 us (12%)
  blocking collectives  29.9 us (4%)
  between operations  20.7 us (3%)
  Pallas kernels  9.55 us (1%)
    ppermute x12, waiting for transfers between devices, ring_sums(): fore = lax.ppermute(fore, 'ctx', ahead)  55.2 us
    ppermute x9, waiting for transfers between devices, ring_gather(): fore = lax.ppermute(fore, 'ctx', ahead)  49.9 us
    dot_general x7, matrix products, dot_t(): lax.dot_general(a, b, (((1,), (1,)), ((), ())), preferred_element_type=f32)  45.3 us
    dot_general x8, matrix products, dot(): return jnp.dot(a, b, preferred_element_type=f32)  44.1 us
    dot_general x8, matrix products, t_dot(): lax.dot_general(a, b, (((0,), (0,)), ((), ())), preferred_element_type=f32)  42.2 us
    ppermute x4, waiting for transfers between devices, ring_sums(): fore = lax.ppermute(low(own(half, 0, cut)), 'ctx', ahead)  39.2 us
    all_to_all x1, blocking collectives, local_split(): lax.all_to_all(pieces, 'ctx', split_axis=0, concat_axis=0, tiled=True)  29.9 us
    unnamed x204, local copies, waits for them, and re-layouts  24.2 us
  transfers between devices with their start and end apart: 77, of which 38 were waited for; matrix products, arithmetic and copies ran while one was open for 43% of the time, Pallas kernels for 1%

profile of v15, /device:TPU:8, one launch (start us, length us, event | category | flops | bytes accessed | tf_op | source)
XLA Modules:
  0.0 715.4 jit_solution(17369861657895464019)
XLA Ops:
  10.7 29.9 %all_to_all.25 = bf16[8,80,768]{2,1,0:T(8,128)(2,1)} all-to-all(bf16[8,80,768]{2,1,0:T(8,128)(2,1)S(1)} %pad_maximum_fusion.6), channel_id=1, replica_groups=mesh['ctx'=8,'fsdp'=4] {'ctx'}, dimensions={0} | all-to-all | bytes 1966080 | tf_op jit(solution)/shard_map/all_to_all | solution.py:347
  72.1 7.1 collective-permute-done.4
  83.8 7.4 %collective-permute-done.6 = bf16[128,2048]{1,0:T(8,128)(2,1)S(1)} collective-permute-done((bf16[128,2048]{1,0:T(8,128)(2,1)S(1)}, bf16[128,2048]{1,0:T(8,128)(2,1)S(1)}, u32[]{:S(2)}, u32[]{:S(2)}) %collective-permute-start.6) | collective-permute-done | bytes 524320 | tf_op jit(solution)/shard_map/ppermute | solution.py:110
  99.1 5.6 all-to-all-start.1
  115.6 6.4 fusion.25
  148.6 6.7 collective-permute-done.12
  180.0 7.2 %collective-permute-done.14 = bf16[128,2048]{1,0:T(8,128)(2,1)} collective-permute-done((bf16[128,2048]{1,0:T(8,128)(2,1)}, bf16[128,2048]{1,0:T(8,128)(2,1)}, u32[]{:S(2)}, u32[]{:S(2)}) %collective-permute-start.14) | collective-permute-done | bytes 524320 | tf_op jit(solution)/shard_map/ppermute | solution.py:147
  237.5 6.3 collective-permute-done.24
  247.7 11.7 %collective-permute-done.26 = bf16[64,2048]{1,0:T(8,128)(2,1)S(1)} collective-permute-done((bf16[64,2048]{1,0:T(8,128)(2,1)S(1)}, bf16[64,2048]{1,0:T(8,128)(2,1)S(1)}, u32[]{:S(2)}, u32[]{:S(2)}) %collective-permute-start.26) | collective-permute-done | bytes 262176 | tf_op jit(solution)/shard_map/ppermute | solution.py:116
  271.0 10.3 %fusion.2 = f32[512,2816]{1,0:T(8,128)S(1)} fusion(bf16[512,2048]{1,0:T(8,128)(2,1)S(1)} %bitcast.402, bf16[1,2048,2816]{2,1,0:T(8,128)(2,1)} %all-gather.14.cloned.1.call-done), kind=kOutput, calls=%fused_computation.2 | convolution fusion | flops 5905580032 | bytes 19398656 | tf_op jit(solution)/shard_map/dot_general | solution.py:322
  285.8 6.2 convolution_convert_fusion.6
  297.8 8.5 %fusion.105 = f32[1024,1408]{1,0:T(8,128)S(1)} fusion(bf16[1024,2048]{1,0:T(8,128)(2,1)} %constant_dynamic-update-slice_fusion.6, bf16[2048,1408]{1,0:T(8,128)(2,1)S(1)} %bitcast.370), kind=kOutput, calls=%fused_computation.320 | convolution fusion | flops 5905580032 | bytes 15728640 | tf_op jit(solution)/shard_map/dot_general | solution.py:322
  310.3 5.9 fusion.8
  324.1 7.4 %multiply_convert_fusion.6 = (bf16[512,1408]{1,0:T(8,128)(2,1)S(1)}, bf16[512,1408]{1,0:T(8,128)(2,1)S(1)}, f32[512]{0:T(512)S(1)}) fusion(f32[512,2816]{1,0:T(8,128)S(1)} %bitcast.375, bf16[512,1408]{1,0:T(8,128)(2,1)S(1)} %copy-done.44, bf16[512,2048]{1,0:T(8,128)(2,1)S(1)} %bitcast.404, bf16[1408,2048]{1,0:T(8,128)(2,1)} %bitcast.377), kind=kOutput, calls=%fused_computation.53 | convolution fusion | flops 2964323840 | bytes 17958912 | tf_op jit(solution)/shard_map/dot_general | solution.py:325
  332.6 9.4 %convolution_convert_fusion = bf16[2048,2816]{1,0:T(8,128)(2,1)} fusion(bf16[512,2048]{1,0:T(8,128)(2,1)S(1)} %bitcast.403, bf16[512,1408]{1,0:T(8,128)(2,1)S(1)} %get-tuple-element.184, bf16[512,1408]{1,0:T(8,128)(2,1)S(1)} %get-tuple-element.183), kind=kOutput, calls=%fused_computation.4 | convolution fusion | flops 5917114368 | bytes 16515072 | tf_op jit(solution)/shard_map/dot_general | solution.py:328
  342.4 11.7 %multiply_convert_fusion.3 = (bf16[1024,704]{1,0:T(8,128)(2,1)S(1)}, bf16[1024,704]{1,0:T(8,128)(2,1)}, f32[1024]{0:T(1024)S(1)}) fusion(f32[1024,1408]{1,0:T(8,128)} %copy-done.17, bf16[1024,704]{1,0:T(8,128)(2,1)} %copy-done.41, bf16[1024,2048]{1,0:T(8,128)(2,1)} %multiply_convert_fusion, bf16[704,2048]{1,0:T(8,128)(2,1)} %bitcast.397), kind=kOutput, calls=%fused_computation.36 | convolution fusion | flops 2964323328 | bytes 17174528 | tf_op jit(solution)/shard_map/dot_general | solution.py:325
  363.0 9.1 %fusion.20 = bf16[512,2048]{1,0:T(8,128)(2,1)S(1)} fusion(bf16[1,2048,2816]{2,1,0:T(8,128)(2,1)} %all-gather.14.cloned.1.call-done, bf16[512,1408]{1,0:T(8,128)(2,1)S(1)} %copy-done.93, bf16[512,1408]{1,0:T(8,128)(2,1)S(1)} %copy-done.91), kind=kOutput, calls=%fused_computation.39 | convolution fusion | flops 5912395776 | bytes 16515072 | tf_op jit(solution)/shard_map/dot_general | solution.py:325
  373.4 8.4 %fusion.6 = bf16[1024,2048]{1,0:T(8,128)(2,1)S(1)} fusion(f32[8,128,2048]{2,1,0:T(8,128)S(1)} %fusion.56, bf16[1024,1408]{1,0:T(8,128)(2,1)} %pad_maximum_fusion.2, bf16[2048,1408]{1,0:T(8,128)(2,1)S(1)} %bitcast.373), kind=kOutput, calls=%fused_computation.10 | convolution fusion | flops 5909774336 | bytes 21233664 | tf_op jit(solution)/shard_map/dot_general | solution.py:325
  384.0 11.7 %convolution_convert_fusion.2 = bf16[2048,1408]{1,0:T(8,128)(2,1)} fusion(bf16[1024,2048]{1,0:T(8,128)(2,1)} %constant_dynamic-update-slice_fusion.6, bf16[1024,1408]{1,0:T(8,128)(2,1)} %pad_maximum_fusion.2), kind=kOutput, calls=%fused_computation.19 | convolution fusion | flops 5908463616 | bytes 12845056 | tf_op jit(solution)/shard_map/dot_general | solution.py:328
  412.5 11.0 %collective-permute-done.32 = bf16[128,2048]{1,0:T(8,128)(2,1)S(1)} collective-permute-done((bf16[128,2048]{1,0:T(8,128)(2,1)S(1)}, bf16[128,2048]{1,0:T(8,128)(2,1)S(1)}, u32[]{:S(2)}, u32[]{:S(2)}) %collective-permute-start.32) | collective-permute-done | bytes 524320 | tf_op jit(solution)/shard_map/ppermute | solution.py:147
  438.6 5.7 copy.250
  454.2 9.7 %collective-permute-done.38 = bf16[128,2048]{1,0:T(8,128)(2,1)} collective-permute-done((bf16[128,2048]{1,0:T(8,128)(2,1)}, bf16[128,2048]{1,0:T(8,128)(2,1)}, u32[]{:S(2)}, u32[]{:S(2)}) %collective-permute-start.38) | collective-permute-done | bytes 524320 | tf_op jit(solution)/shard_map/ppermute | solution.py:110
  469.4 6.1 collective-permute-done.40
  499.4 9.6 %shard_map.309 = (f32[1024,256]{1,0:T(8,128)S(1)}, f32[1024,256]{1,0:T(8,128)S(1)}, f32[1024,256]{1,0:T(8,128)S(1)}) custom-call(bf16[1024,256]{1,0:T(8,128)(2,1)S(1)} %copy_bitcast_fusion.4.q_ref, bf16[1024,256]{1,0:T(8,128)(2,1)S(1)} %get-tuple-element.228.k_ref, bf16[1024,256]{1,0:T(8,128)(2,1)S(1)} %slice.585.v_ref, ...), custom_call_target="tpu_custom_call" | custom-call | flops 2684354560 | bytes 5242880 | tf_op jit(solution)/shard_map/pallas_call | solution.py:267
  513.2 7.1 fusion.5
  521.2 6.4 fusion.17
  530.2 6.1 all-to-all-start.3
  539.7 32.5 %collective-permute-done.46 = bf16[64,2048]{1,0:T(8,128)(2,1)S(1)} collective-permute-done((bf16[64,2048]{1,0:T(8,128)(2,1)S(1)}, bf16[64,2048]{1,0:T(8,128)(2,1)S(1)}, u32[]{:S(2)}, u32[]{:S(2)}) %collective-permute-start.46) | collective-permute-done | bytes 262176 | tf_op jit(solution)/shard_map/ppermute | solution.py:138
  577.7 10.0 %collective-permute-done.47 = bf16[128,2048]{1,0:T(8,128)(2,1)S(1)} collective-permute-done((bf16[128,2048]{1,0:T(8,128)(2,1)S(1)}, bf16[128,2048]{1,0:T(8,128)(2,1)S(1)}, u32[]{:S(2)}, u32[]{:S(2)}) %collective-permute-start.47) | collective-permute-done | bytes 524320 | tf_op jit(solution)/shard_map/ppermute | solution.py:147
  593.5 10.7 %collective-permute-done.48 = bf16[128,2048]{1,0:T(8,128)(2,1)S(1)} collective-permute-done((bf16[128,2048]{1,0:T(8,128)(2,1)S(1)}, bf16[128,2048]{1,0:T(8,128)(2,1)S(1)}, u32[]{:S(2)}, u32[]{:S(2)}) %collective-permute-start.48) | collective-permute-done | bytes 524320 | tf_op jit(solution)/shard_map/ppermute | solution.py:147
  613.4 5.6 collective-permute-done.49
  647.2 15.5 %collective-permute-done.57 = bf16[176,2048]{1,0:T(8,128)(2,1)} collective-permute-done((bf16[176,2048]{1,0:T(8,128)(2,1)}, bf16[176,2048]{1,0:T(8,128)(2,1)}, u32[]{:S(2)}, u32[]{:S(2)}) %collective-permute-start.57) | collective-permute-done | bytes 720928 | tf_op jit(solution)/shard_map/ppermute | solution.py:198
  (587 shorter events, 381.9 us)
Async XLA Ops:
  7.2 97.7 %all-gather.10.cloned.1.call-start = ((), (), s32[]{:S(2)}) async-start(), calls=%async_computation.16 | async-start | bytes 4915200 | tf_op jit(solution)/shard_map/all_gather | solution.py:351
  40.6 230.4 %all-gather.14.cloned.1.call-start = ((), (), s32[]{:S(2)}) async-start(), calls=%async_computation.18 | async-start | bytes 14417920 | tf_op jit(solution)/shard_map/all_gather | solution.py:366
  45.3 21.6 %collective-permute-start.2 = (bf16[128,2048]{1,0:T(8,128)(2,1)}, bf16[128,2048]{1,0:T(8,128)(2,1)}, u32[]{:S(2)}, u32[]{:S(2)}) collective-permute-start(bf16[128,2048]{1,0:T(8,128)(2,1)} %get-tuple-element.282), channel_id=1, source_target_pairs={{0,8},{8,16},{16,24},{24,28},{28,20},{20,12},{12,4},{4,0},{1,9},{9... | collective-permute-start | bytes 1572872 | tf_op jit(solution)/shard_map/ppermute | solution.py:110
  45.8 21.7 %collective-permute-start.3 = (bf16[128,2048]{1,0:T(8,128)(2,1)}, bf16[128,2048]{1,0:T(8,128)(2,1)S(1)}, u32[]{:S(2)}, u32[]{:S(2)}) collective-permute-start(bf16[128,2048]{1,0:T(8,128)(2,1)} %get-tuple-element.282), channel_id=1, source_target_pairs={{8,0},{16,8},{24,16},{28,24},{20,28},{12,20},{4,12},{0,4},{9,1},{1... | collective-permute-start | bytes 1572872 | tf_op jit(solution)/shard_map/ppermute | solution.py:111
  47.4 79.3 %collective-permute-start.10 = (bf16[64,2048]{1,0:T(8,128)(2,1)S(1)}, bf16[64,2048]{1,0:T(8,128)(2,1)}, u32[]{:S(2)}, u32[]{:S(2)}) collective-permute-start(bf16[64,2048]{1,0:T(8,128)(2,1)S(1)} %copy-done.50), channel_id=1, source_target_pairs={{0,2},{1,3},{2,0},{3,1},{4,6},{5,7},{6,4},{7,5},{8,10},{9,11},{10,... | collective-permute-start | bytes 786440 | tf_op jit(solution)/shard_map/ppermute | solution.py:176
  48.8 89.6 %collective-permute-start.1 = (bf16[176,2048]{1,0:T(8,128)(2,1)}, bf16[176,2048]{1,0:T(8,128)(2,1)}, u32[]{:S(2)}, u32[]{:S(2)}) collective-permute-start(bf16[176,2048]{1,0:T(8,128)(2,1)} %param.34), channel_id=1, source_target_pairs={{0,2},{1,3},{2,0},{3,1},{4,6},{5,7},{6,4},{7,5},{8,10},{9,11},{10,... | collective-permute-start | bytes 2162696 | tf_op jit(solution)/shard_map/ppermute | solution.py:176
  49.4 89.0 %collective-permute-start = (bf16[352,2048]{1,0:T(8,128)(2,1)}, bf16[352,2048]{1,0:T(8,128)(2,1)}, u32[]{:S(2)}, u32[]{:S(2)}) collective-permute-start(bf16[352,2048]{1,0:T(8,128)(2,1)} %bitcast.1), channel_id=1, source_target_pairs={{0,2},{1,3},{2,0},{3,1},{4,6},{5,7},{6,4},{7,5},{8,10},{9,11},{10,... | collective-permute-start | bytes 4325384 | tf_op jit(solution)/shard_map/ppermute | solution.py:176
  99.1 46.1 %all-to-all-start.1 = ((bf16[8,64,1408]{2,1,0:T(8,128)(2,1)}), bf16[8,64,1408]{2,1,0:T(8,128)(2,1)}, u32[]{:S(2)}, u32[]{:S(2)}) async-start(bf16[8,64,1408]{2,1,0:T(8,128)(2,1)} %reshape.888), calls=%async_computation.1 | async-start | bytes 2883584 | tf_op jit(solution)/shard_map/all_to_all | solution.py:350
  104.6 187.4 %all-gather.12.cloned.1.call-start = ((), (), s32[]{:S(2)}) async-start(), calls=%async_computation.17 | async-start | bytes 7208960 | tf_op jit(solution)/shard_map/all_gather | solution.py:403
  145.2 171.1 %all-gather.8.cloned.1.call-start = ((), (), s32[]{:S(2)}) async-start(), calls=%async_computation.10 | async-start | bytes 4718592 | tf_op jit(solution)/shard_map/all_gather | solution.py:411
  164.8 56.9 %collective-permute-start.28 = (bf16[2,352,2048]{2,1,0:T(8,128)(2,1)}, bf16[2,352,2048]{2,1,0:T(8,128)(2,1)}, u32[]{:S(2)}, u32[]{:S(2)}) collective-permute-start(bf16[2,352,2048]{2,1,0:T(8,128)(2,1)} %maximum_select_fusion.1), channel_id=1, source_target_pairs={{0,1},{1,0},{2,3},{3,2},{4,5},{5,4},{6,7},{7,6},{8,9},{9,8},{10,11... | collective-permute-start | bytes 8650760 | tf_op jit(solution)/shard_map/ppermute | solution.py:181
  179.9 32.3 %collective-permute-start.29 = (bf16[2,176,2048]{2,1,0:T(8,128)(2,1)S(1)}, bf16[2,176,2048]{2,1,0:T(8,128)(2,1)}, u32[]{:S(2)}, u32[]{:S(2)}) collective-permute-start(bf16[2,176,2048]{2,1,0:T(8,128)(2,1)S(1)} %maximum_select_fusion.3), channel_id=1, source_target_pairs={{0,1},{1,0},{2,3},{3,2},{4,5},{5,4},{6,7},{7,6},{8,9},{9,8},{10,11... | collective-permute-start | bytes 4325384 | tf_op jit(solution)/shard_map/ppermute | solution.py:181
  235.8 215.6 %reduce-scatter.6.cloned.1.call-start = ((), (), s32[]{:S(2)}) async-start(), calls=%async_computation.11 | async-start | bytes 14417920 | tf_op jit(solution)/shard_map/reduce_scatter | solution.py:336
  243.8 15.5 %collective-permute-start.26 = (bf16[64,2048]{1,0:T(8,128)(2,1)S(1)}, bf16[64,2048]{1,0:T(8,128)(2,1)S(1)}, u32[]{:S(2)}, u32[]{:S(2)}) collective-permute-start(bf16[64,2048]{1,0:T(8,128)(2,1)S(1)} %slice.499), channel_id=1, source_target_pairs={{0,8},{8,16},{16,24},{24,28},{28,20},{20,12},{12,4},{4,0},{1,9},{9... | collective-permute-start | bytes 786440 | tf_op jit(solution)/shard_map/ppermute | solution.py:116
  245.3 17.8 %collective-permute-start.27 = (bf16[64,2048]{1,0:T(8,128)(2,1)S(1)}, bf16[64,2048]{1,0:T(8,128)(2,1)S(1)}, u32[]{:S(2)}, u32[]{:S(2)}) collective-permute-start(bf16[64,2048]{1,0:T(8,128)(2,1)S(1)} %slice.500), channel_id=1, source_target_pairs={{8,0},{16,8},{24,16},{28,24},{20,28},{12,20},{4,12},{0,4},{9,1},{1... | collective-permute-start | bytes 786440 | tf_op jit(solution)/shard_map/ppermute | solution.py:117
  354.7 83.9 %all-to-all-start.2 = ((f32[8,2,128]{2,1,0:T(2,128)}), f32[8,2,128]{2,1,0:T(2,128)S(1)}, u32[]{:S(2)}, u32[]{:S(2)}) async-start(f32[8,2,128]{2,1,0:T(2,128)} %pad_maximum_fusion.17), calls=%async_computation.2 | async-start | bytes 16384 | tf_op jit(solution)/shard_map/all_to_all | solution.py:483
  358.9 140.5 %reduce-scatter.8.cloned.1.call-start = ((), (), s32[]{:S(2)}) async-start(), calls=%async_computation.12 | async-start | bytes 7208960 | tf_op jit(solution)/shard_map/reduce_scatter | solution.py:488
  411.5 14.0 %collective-permute-start.36 = (bf16[128,2048]{1,0:T(8,128)(2,1)S(1)}, bf16[128,2048]{1,0:T(8,128)(2,1)S(1)}, u32[]{:S(2)}, u32[]{:S(2)}) collective-permute-start(bf16[128,2048]{1,0:T(8,128)(2,1)S(1)} %get-tuple-element.210), channel_id=1, source_target_pairs={{8,0},{16,8},{24,16},{28,24},{20,28},{12,20},{4,12},{0,4},{9,1},{1... | collective-permute-start | bytes 1572872 | tf_op jit(solution)/shard_map/ppermute | solution.py:148
  444.5 133.2 %reduce-scatter.10.cloned.1.call-start = ((), (), s32[]{:S(2)}) async-start(), calls=%async_computation.13 | async-start | bytes 7208960 | tf_op jit(solution)/shard_map/reduce_scatter | solution.py:336
  445.2 176.4 %reduce-scatter.12.cloned.1.call-start = ((), (), s32[]{:S(2)}) async-start(), calls=%async_computation.14 | async-start | bytes 4915200 | tf_op jit(solution)/shard_map/reduce_scatter | solution.py:568
  530.2 57.5 %all-to-all-start.3 = ((bf16[8,64,1408]{2,1,0:T(8,128)(2,1)}), bf16[8,64,1408]{2,1,0:T(8,128)(2,1)S(1)}, u32[]{:S(2)}, u32[]{:S(2)}) async-start(bf16[8,64,1408]{2,1,0:T(8,128)(2,1)} %bitcast.70), calls=%async_computation.6 | async-start | bytes 2883584 | tf_op jit(solution)/shard_map/all_to_all | solution.py:519
  536.3 129.0 %reduce-scatter.14.cloned.1.call-start = ((), (), s32[]{:S(2)}) async-start(), calls=%async_computation.15 | async-start | bytes 1310720 | tf_op jit(solution)/shard_map/reduce_scatter | solution.py:336
  537.6 34.6 %collective-permute-start.46 = (bf16[64,2048]{1,0:T(8,128)(2,1)S(1)}, bf16[64,2048]{1,0:T(8,128)(2,1)S(1)}, u32[]{:S(2)}, u32[]{:S(2)}) collective-permute-start(bf16[64,2048]{1,0:T(8,128)(2,1)S(1)} %get-tuple-element.203), channel_id=1, source_target_pairs={{0,8},{8,16},{16,24},{24,28},{28,20},{20,12},{12,4},{4,0},{1,9},{9... | collective-permute-start | bytes 786440 | tf_op jit(solution)/shard_map/ppermute | solution.py:138
  539.1 35.2 %collective-permute-start.50 = (bf16[64,2048]{1,0:T(8,128)(2,1)S(1)}, bf16[64,2048]{1,0:T(8,128)(2,1)S(1)}, u32[]{:S(2)}, u32[]{:S(2)}) collective-permute-start(bf16[64,2048]{1,0:T(8,128)(2,1)S(1)} %get-tuple-element.204), channel_id=1, source_target_pairs={{8,0},{16,8},{24,16},{28,24},{20,28},{12,20},{4,12},{0,4},{9,1},{1... | collective-permute-start | bytes 786440 | tf_op jit(solution)/shard_map/ppermute | solution.py:139
  633.6 31.7 %collective-permute-start.61 = (bf16[128,2048]{1,0:T(8,128)(2,1)}, bf16[128,2048]{1,0:T(8,128)(2,1)}, u32[]{:S(2)}, u32[]{:S(2)}) collective-permute-start(bf16[128,2048]{1,0:T(8,128)(2,1)} %pad_maximum_fusion.16), channel_id=1, source_target_pairs={{8,0},{16,8},{24,16},{28,24},{20,28},{12,20},{4,12},{0,4},{9,1},{1... | collective-permute-start | bytes 1572872 | tf_op jit(solution)/shard_map/ppermute | solution.py:148
  639.0 23.7 %collective-permute-start.57 = (bf16[176,2048]{1,0:T(8,128)(2,1)}, bf16[176,2048]{1,0:T(8,128)(2,1)}, u32[]{:S(2)}, u32[]{:S(2)}) collective-permute-start(bf16[176,2048]{1,0:T(8,128)(2,1)} %dynamic-slice_bitcast_fusion.1), channel_id=1, source_target_pairs={{0,2},{1,3},{2,0},{3,1},{4,6},{5,7},{6,4},{7,5},{8,10},{9,11},{10,... | collective-permute-start | bytes 2162696 | tf_op jit(solution)/shard_map/ppermute | solution.py:198
  639.0 26.2 %collective-permute-start.55 = (bf16[128,2048]{1,0:T(8,128)(2,1)S(1)}, bf16[128,2048]{1,0:T(8,128)(2,1)}, u32[]{:S(2)}, u32[]{:S(2)}) collective-permute-start(bf16[128,2048]{1,0:T(8,128)(2,1)S(1)} %pad_maximum_fusion.15), channel_id=1, source_target_pairs={{0,8},{8,16},{16,24},{24,28},{28,20},{20,12},{12,4},{4,0},{1,9},{9... | collective-permute-start | bytes 1572872 | tf_op jit(solution)/shard_map/ppermute | solution.py:147
  642.2 47.2 %all-to-all-start.4 = ((bf16[8,80,768]{2,1,0:T(8,128)(2,1)}), bf16[8,80,768]{2,1,0:T(8,128)(2,1)}, u32[]{:S(2)}, u32[]{:S(2)}) async-start(bf16[8,80,768]{2,1,0:T(8,128)(2,1)} %bitcast.414), calls=%async_computation.9 | async-start | bytes 1966080 | tf_op jit(solution)/shard_map/all_to_all | solution.py:580
  668.2 16.1 %collective-permute-start.58 = (bf16[128,2048]{1,0:T(8,128)(2,1)}, bf16[128,2048]{1,0:T(8,128)(2,1)S(1)}, u32[]{:S(2)}, u32[]{:S(2)}) collective-permute-start(bf16[128,2048]{1,0:T(8,128)(2,1)} %get-tuple-element.189), channel_id=1, source_target_pairs={{0,8},{8,16},{16,24},{24,28},{28,20},{20,12},{12,4},{4,0},{1,9},{9... | collective-permute-start | bytes 1572872 | tf_op jit(solution)/shard_map/ppermute | solution.py:147
  669.9 14.4 %collective-permute-start.62 = (bf16[128,2048]{1,0:T(8,128)(2,1)}, bf16[128,2048]{1,0:T(8,128)(2,1)}, u32[]{:S(2)}, u32[]{:S(2)}) collective-permute-start(bf16[128,2048]{1,0:T(8,128)(2,1)} %get-tuple-element.190), channel_id=1, source_target_pairs={{8,0},{16,8},{24,16},{28,24},{20,28},{12,20},{4,12},{0,4},{9,1},{1... | collective-permute-start | bytes 1572872 | tf_op jit(solution)/shard_map/ppermute | solution.py:148
  687.0 17.8 %collective-permute-start.59 = (bf16[128,2048]{1,0:T(8,128)(2,1)}, bf16[128,2048]{1,0:T(8,128)(2,1)}, u32[]{:S(2)}, u32[]{:S(2)}) collective-permute-start(bf16[128,2048]{1,0:T(8,128)(2,1)} %get-tuple-element.187), channel_id=1, source_target_pairs={{0,8},{8,16},{16,24},{24,28},{28,20},{20,12},{12,4},{4,0},{1,9},{9... | collective-permute-start | bytes 1572872 | tf_op jit(solution)/shard_map/ppermute | solution.py:147
  689.4 15.5 %collective-permute-start.63 = (bf16[128,2048]{1,0:T(8,128)(2,1)}, bf16[128,2048]{1,0:T(8,128)(2,1)}, u32[]{:S(2)}, u32[]{:S(2)}) collective-permute-start(bf16[128,2048]{1,0:T(8,128)(2,1)} %get-tuple-element.188), channel_id=1, source_target_pairs={{8,0},{16,8},{24,16},{28,24},{20,28},{12,20},{4,12},{0,4},{9,1},{1... | collective-permute-start | bytes 1572872 | tf_op jit(solution)/shard_map/ppermute | solution.py:148
  (144 other events, 1286.4 us)
Sparse Core Ops, SparseCore 0:
  40.7 53.3 all-gather.9
  95.7 89.0 all-gather.13
  186.4 43.5 all-gather.11
  235.9 74.2 all-gather.7
  342.2 90.5 reduce-scatter.5
  444.5 54.8 reduce-scatter.7
  502.0 54.8 reduce-scatter.9
  559.5 42.8 reduce-scatter.11
  631.5 28.6 reduce-scatter.13

commit v16 on v14

--- a/solution.py
+++ b/solution.py
@@ -120,7 +120,7 @@
     return out if rider is None else (out, rider)
 
 
-def ring_sums(parts, size, ctx_index):
+def ring_sums(parts, size, ctx_index, riders):
     f32 = jnp.float32
     rows = parts.shape[0] // size
     ahead, back = ring_steps(size)
@@ -146,17 +146,20 @@
     for k in range(half - 1, 0, -1):
         fore = lax.ppermute(fore, "ctx", ahead)
         rear = lax.ppermute(rear, "ctx", back)
+        if riders and k == half - 1:
+            fore, *riders = after(fore, *riders)
         if k > 1:
             fore = low(fore.astype(f32) + own(k - 1, 0, rows))
             rear = low(rear.astype(f32) + own(1 - k, 0, rows))
-    return (fore, rear)
-
-
-def ring_scatter(parts, size, ctx_index, kept=None):
-    fore, rear = ring_sums(parts, size, ctx_index)
+    return (fore, rear, riders)
+
+
+def ring_scatter(parts, size, ctx_index, kept=None, riders=()):
+    fore, rear, riders = ring_sums(parts, size, ctx_index, riders)
     kept = (parts if kept is None else kept).reshape(size, -1, parts.shape[1])
     kept = lax.dynamic_index_in_dim(kept, ctx_index, 0, keepdims=False)
-    return kept.astype(jnp.float32) + fore.astype(jnp.float32) + rear.astype(jnp.float32)
+    total = kept.astype(jnp.float32) + fore.astype(jnp.float32) + rear.astype(jnp.float32)
+    return (total, *riders) if riders else total
 
 
 def other_core(size):
@@ -521,12 +524,13 @@
     ).astype(bf16)
     one_sums = dot_t(grad_projected, qkv_weight)
     grad_gain_one = jnp.sum(one_sums * scaled_rows.astype(f32), axis=0)
-    one_parts, sum_expert_out, sum_shared_in = after(
-        one_sums.astype(bf16), sum_expert_out, sum_shared_in
-    )
+    one_parts = one_sums.astype(bf16)
     one_kept, grad_projected = after(one_parts, grad_projected)
     one_kept, attn_own = after(one_kept, attn_own)
-    grad_normed = ring_scatter(one_parts, ctx_size, ctx_index, one_kept)
+    one_parts, sum_shared_in = after(one_parts, sum_shared_in)
+    grad_normed, sum_expert_out = ring_scatter(
+        one_parts, ctx_size, ctx_index, one_kept, (sum_expert_out,)
+    )
     grad_qkv_weight = t_dot(normed_low, grad_projected)
     grad_bias = jnp.sum(grad_projected.astype(f32), axis=0).reshape(3, 1, own_width)
     grad_bias = jnp.where(

time: 723 us -> 719 us (level)
  blocking collectives: 29.7 us -> 68.7 us
  waiting for transfers between devices: 209 us -> 175 us
    all_to_all x0 -> x1, blocking collectives: none -> 39 us  [local_split(): lax.all_to_all(sum_shared_in, 'ctx', split_axis=0, concat_axis=0, tiled=T...]
    ppermute x12, waiting for transfers between devices: 49.7 us -> 16.7 us  [ring_sums(): rear = lax.ppermute(rear, 'ctx', back)]
    reduce_scatter x4, waiting for transfers between devices: 31.4 us -> 0.01 us  [sum_rows(): lax.psum_scatter(grad.astype(bf16), 'fsdp', scatter_dimension=0, tiled=True)]
    ppermute x12, waiting for transfers between devices: 35.8 us -> 59.3 us  [ring_sums(): fore = lax.ppermute(fore, 'ctx', ahead)]
    unnamed x198 -> x200, local copies, waits for them, and re-layouts: 22.8 us -> 23.6 us
  transfers between devices with their start and end apart: 76 -> 75, of which waited for: 37 -> 38; matrix products, arithmetic and copies ran while one was open for 42% -> 43% of each run, Pallas kernels for 1% -> 1%
where the time goes in v16:
time: 719 us; the launch traced here: 709 us
  waiting for transfers between devices  175 us (24%)
  matrix products  144 us (20%)
  local copies, waits for them, and re-layouts  113 us (16%)
  other arithmetic  97 us (13%)
  starting transfers between devices  80.7 us (11%)
  blocking collectives  68.7 us (10%)
  between operations  21 us (3%)
  Pallas kernels  9.55 us (1%)
    ppermute x12, waiting for transfers between devices, ring_sums(): fore = lax.ppermute(fore, 'ctx', ahead)  59.3 us
    ppermute x9, waiting for transfers between devices, ring_gather(): fore = lax.ppermute(fore, 'ctx', ahead)  49.4 us
    dot_general x7, matrix products, dot_t(): lax.dot_general(a, b, (((1,), (1,)), ((), ())), preferred_element_type=f32)  45.4 us
    dot_general x8, matrix products, dot(): return jnp.dot(a, b, preferred_element_type=f32)  44.1 us
    dot_general x8, matrix products, t_dot(): lax.dot_general(a, b, (((0,), (0,)), ((), ())), preferred_element_type=f32)  40 us
    all_to_all x1, blocking collectives, local_split(): lax.all_to_all(sum_shared_in, 'ctx', split_axis=0, concat_axis=0, tiled=T...  39 us
    all_to_all x1, blocking collectives, local_split(): lax.all_to_all(pieces, 'ctx', split_axis=0, concat_axis=0, tiled=True)  29.7 us
    unnamed x200, local copies, waits for them, and re-layouts  23.6 us
  transfers between devices with their start and end apart: 75, of which 38 were waited for; matrix products, arithmetic and copies ran while one was open for 43% of the time, Pallas kernels for 1%

profile of v16, /device:TPU:8, one launch (start us, length us, event | category | flops | bytes accessed | tf_op | source)
XLA Modules:
  0.0 708.6 jit_solution(15167328483520545358)
XLA Ops:
  10.7 29.7 %all_to_all.25 = bf16[8,80,768]{2,1,0:T(8,128)(2,1)} all-to-all(bf16[8,80,768]{2,1,0:T(8,128)(2,1)S(1)} %pad_maximum_fusion.6), channel_id=1, replica_groups=mesh['ctx'=8,'fsdp'=4] {'ctx'}, dimensions={0} | all-to-all | bytes 1966080 | tf_op jit(solution)/shard_map/all_to_all | solution.py:333
  72.0 7.1 %collective-permute-done.4 = bf16[128,2048]{1,0:T(8,128)(2,1)S(1)} collective-permute-done((bf16[128,2048]{1,0:T(8,128)(2,1)}, bf16[128,2048]{1,0:T(8,128)(2,1)S(1)}, u32[]{:S(2)}, u32[]{:S(2)}) %collective-permute-start.4) | collective-permute-done | bytes 524320 | tf_op jit(solution)/shard_map/ppermute | solution.py:110
  83.6 7.4 %collective-permute-done.6 = bf16[128,2048]{1,0:T(8,128)(2,1)S(1)} collective-permute-done((bf16[128,2048]{1,0:T(8,128)(2,1)S(1)}, bf16[128,2048]{1,0:T(8,128)(2,1)S(1)}, u32[]{:S(2)}, u32[]{:S(2)}) %collective-permute-start.6) | collective-permute-done | bytes 524320 | tf_op jit(solution)/shard_map/ppermute | solution.py:110
  98.9 5.6 all-to-all-start.1
  115.5 6.4 fusion.24
  148.4 6.7 collective-permute-done.12
  179.9 7.1 %collective-permute-done.14 = bf16[128,2048]{1,0:T(8,128)(2,1)} collective-permute-done((bf16[128,2048]{1,0:T(8,128)(2,1)}, bf16[128,2048]{1,0:T(8,128)(2,1)}, u32[]{:S(2)}, u32[]{:S(2)}) %collective-permute-start.14) | collective-permute-done | bytes 524320 | tf_op jit(solution)/shard_map/ppermute | solution.py:147
  237.4 6.3 collective-permute-done.24
  247.6 11.7 %collective-permute-done.26 = bf16[64,2048]{1,0:T(8,128)(2,1)S(1)} collective-permute-done((bf16[64,2048]{1,0:T(8,128)(2,1)S(1)}, bf16[64,2048]{1,0:T(8,128)(2,1)S(1)}, u32[]{:S(2)}, u32[]{:S(2)}) %collective-permute-start.26) | collective-permute-done | bytes 262176 | tf_op jit(solution)/shard_map/ppermute | solution.py:116
  271.0 10.3 %fusion.2 = f32[512,2816]{1,0:T(8,128)S(1)} fusion(bf16[512,2048]{1,0:T(8,128)(2,1)S(1)} %bitcast.387, bf16[1,2048,2816]{2,1,0:T(8,128)(2,1)} %all-gather.14.cloned.1.call-done), kind=kOutput, calls=%fused_computation.2 | convolution fusion | flops 5905580032 | bytes 19398656 | tf_op jit(solution)/shard_map/dot_general | solution.py:308
  285.7 6.2 convolution_convert_fusion.6
  297.7 8.5 %fusion.104 = f32[1024,1408]{1,0:T(8,128)S(1)} fusion(bf16[1024,2048]{1,0:T(8,128)(2,1)} %constant_dynamic-update-slice_fusion.4, bf16[2048,1408]{1,0:T(8,128)(2,1)S(1)} %bitcast.357), kind=kOutput, calls=%fused_computation.315 | convolution fusion | flops 5905580032 | bytes 15728640 | tf_op jit(solution)/shard_map/dot_general | solution.py:308
  310.7 5.9 fusion.8
  316.7 5.2 multiply_convert_fusion
  324.6 7.4 %multiply_convert_fusion.6 = (bf16[512,1408]{1,0:T(8,128)(2,1)S(1)}, bf16[512,1408]{1,0:T(8,128)(2,1)S(1)}, f32[512]{0:T(512)S(1)}) fusion(f32[512,2816]{1,0:T(8,128)S(1)} %bitcast.362, bf16[512,1408]{1,0:T(8,128)(2,1)S(1)} %copy-done.43, bf16[512,2048]{1,0:T(8,128)(2,1)S(1)} %bitcast.389, bf16[1408,2048]{1,0:T(8,128)(2,1)} %bitcast.364), kind=kOutput, calls=%fused_computation.51 | convolution fusion | flops 2964323840 | bytes 17958912 | tf_op jit(solution)/shard_map/dot_general | solution.py:311
  333.1 9.4 %convolution_convert_fusion = bf16[2048,2816]{1,0:T(8,128)(2,1)} fusion(bf16[512,2048]{1,0:T(8,128)(2,1)S(1)} %bitcast.388, bf16[512,1408]{1,0:T(8,128)(2,1)S(1)} %get-tuple-element.180, bf16[512,1408]{1,0:T(8,128)(2,1)S(1)} %get-tuple-element.179), kind=kOutput, calls=%fused_computation.4 | convolution fusion | flops 5917114368 | bytes 16515072 | tf_op jit(solution)/shard_map/dot_general | solution.py:314
  342.8 11.7 %multiply_convert_fusion.3 = (bf16[1024,704]{1,0:T(8,128)(2,1)S(1)}, bf16[1024,704]{1,0:T(8,128)(2,1)}, f32[1024]{0:T(1024)S(1)}) fusion(f32[1024,1408]{1,0:T(8,128)} %copy-done.16, bf16[1024,704]{1,0:T(8,128)(2,1)} %copy-done.40, bf16[1024,2048]{1,0:T(8,128)(2,1)} %multiply_convert_fusion, bf16[704,2048]{1,0:T(8,128)(2,1)} %bitcast.382), kind=kOutput, calls=%fused_computation.36 | convolution fusion | flops 2964323328 | bytes 17174528 | tf_op jit(solution)/shard_map/dot_general | solution.py:311
  363.4 9.1 %fusion.20 = bf16[512,2048]{1,0:T(8,128)(2,1)S(1)} fusion(bf16[1,2048,2816]{2,1,0:T(8,128)(2,1)} %all-gather.14.cloned.1.call-done, bf16[512,1408]{1,0:T(8,128)(2,1)S(1)} %copy-done.91, bf16[512,1408]{1,0:T(8,128)(2,1)S(1)} %copy-done.89), kind=kOutput, calls=%fused_computation.39 | convolution fusion | flops 5912395776 | bytes 16515072 | tf_op jit(solution)/shard_map/dot_general | solution.py:311
  373.8 8.4 %fusion.6 = bf16[1024,2048]{1,0:T(8,128)(2,1)S(1)} fusion(f32[8,128,2048]{2,1,0:T(8,128)S(1)} %fusion.55, bf16[1024,1408]{1,0:T(8,128)(2,1)} %pad_maximum_fusion.2, bf16[2048,1408]{1,0:T(8,128)(2,1)S(1)} %bitcast.360), kind=kOutput, calls=%fused_computation.10 | convolution fusion | flops 5909774336 | bytes 21233664 | tf_op jit(solution)/shard_map/dot_general | solution.py:311
  384.4 11.7 %convolution_convert_fusion.2 = bf16[2048,1408]{1,0:T(8,128)(2,1)} fusion(bf16[1024,2048]{1,0:T(8,128)(2,1)} %constant_dynamic-update-slice_fusion.4, bf16[1024,1408]{1,0:T(8,128)(2,1)} %pad_maximum_fusion.2), kind=kOutput, calls=%fused_computation.19 | convolution fusion | flops 5908463616 | bytes 12845056 | tf_op jit(solution)/shard_map/dot_general | solution.py:314
  415.3 7.6 %collective-permute-done.32 = bf16[128,2048]{1,0:T(8,128)(2,1)S(1)} collective-permute-done((bf16[128,2048]{1,0:T(8,128)(2,1)S(1)}, bf16[128,2048]{1,0:T(8,128)(2,1)S(1)}, u32[]{:S(2)}, u32[]{:S(2)}) %collective-permute-start.32) | collective-permute-done | bytes 524320 | tf_op jit(solution)/shard_map/ppermute | solution.py:147
  439.2 5.7 copy.245
  454.9 9.5 %collective-permute-done.38 = bf16[128,2048]{1,0:T(8,128)(2,1)} collective-permute-done((bf16[128,2048]{1,0:T(8,128)(2,1)}, bf16[128,2048]{1,0:T(8,128)(2,1)}, u32[]{:S(2)}, u32[]{:S(2)}) %collective-permute-start.38) | collective-permute-done | bytes 524320 | tf_op jit(solution)/shard_map/ppermute | solution.py:110
  470.0 5.9 collective-permute-done.40
  499.9 9.6 %shard_map.309 = (f32[1024,256]{1,0:T(8,128)S(1)}, f32[1024,256]{1,0:T(8,128)S(1)}, f32[1024,256]{1,0:T(8,128)S(1)}) custom-call(bf16[1024,256]{1,0:T(8,128)(2,1)S(1)} %copy_bitcast_fusion.4.q_ref, bf16[1024,256]{1,0:T(8,128)(2,1)S(1)} %get-tuple-element.224.k_ref, bf16[1024,256]{1,0:T(8,128)(2,1)S(1)} %slice.585.v_ref, ...), custom_call_target="tpu_custom_call" | custom-call | flops 2684354560 | bytes 5242880 | tf_op jit(solution)/shard_map/pallas_call | solution.py:253
  513.8 7.1 %fusion.5 = (bf16[2048]{0:T(1024)(128)(2,1)S(1)}, bf16[1024,2048]{1,0:T(8,128)(2,1)}) fusion(bf16[1024,2048]{1,0:T(8,128)(2,1)} %constant_dynamic-update-slice_fusion.18, bf16[2048,768]{1,0:T(8,128)(2,1)S(1)} %bitcast.377, bf16[1024,256]{1,0:T(8,128)(2,1)S(1)} %convert.63, bf16[1024,256]{1,0:T(8,128)(2,1)S(1)} %get-tuple-element.246, ...), kind=kOutput, calls=%fused_computation.8 | convolution fusion | flops 3234330624 | bytes 13111296 | tf_op jit(solution)/shard_map/dot_general | solution.py:311
  521.7 6.5 fusion.17
  530.8 39.0 %all_to_all.26 = bf16[8,64,1408]{2,1,0:T(8,128)(2,1)S(1)} all-to-all(bf16[8,64,1408]{2,1,0:T(8,128)(2,1)S(1)} %bitcast.391), channel_id=1, replica_groups=mesh['ctx'=8,'fsdp'=4] {'ctx'}, dimensions={0} | all-to-all | bytes 2883584 | tf_op jit(solution)/shard_map/all_to_all | solution.py:505
  582.3 9.4 %collective-permute-done.47 = bf16[128,2048]{1,0:T(8,128)(2,1)S(1)} collective-permute-done((bf16[128,2048]{1,0:T(8,128)(2,1)S(1)}, bf16[128,2048]{1,0:T(8,128)(2,1)S(1)}, u32[]{:S(2)}, u32[]{:S(2)}) %collective-permute-start.47) | collective-permute-done | bytes 524320 | tf_op jit(solution)/shard_map/ppermute | solution.py:147
  596.5 8.6 %collective-permute-done.48 = bf16[128,2048]{1,0:T(8,128)(2,1)S(1)} collective-permute-done((bf16[128,2048]{1,0:T(8,128)(2,1)S(1)}, bf16[128,2048]{1,0:T(8,128)(2,1)S(1)}, u32[]{:S(2)}, u32[]{:S(2)}) %collective-permute-start.48) | collective-permute-done | bytes 524320 | tf_op jit(solution)/shard_map/ppermute | solution.py:147
  613.1 5.3 collective-permute-done.49
  659.7 16.0 %collective-permute-done.56 = bf16[128,2048]{1,0:T(8,128)(2,1)S(1)} collective-permute-done((bf16[128,2048]{1,0:T(8,128)(2,1)S(1)}, bf16[128,2048]{1,0:T(8,128)(2,1)S(1)}, u32[]{:S(2)}, u32[]{:S(2)}) %collective-permute-start.56) | collective-permute-done | bytes 524320 | tf_op jit(solution)/shard_map/ppermute | solution.py:147
  (578 shorter events, 375.6 us)
Async XLA Ops:
  7.2 97.5 %all-gather.10.cloned.1.call-start = ((), (), s32[]{:S(2)}) async-start(), calls=%async_computation.18 | async-start | bytes 4915200 | tf_op jit(solution)/shard_map/all_gather | solution.py:337
  40.5 230.5 %all-gather.14.cloned.1.call-start = ((), (), s32[]{:S(2)}) async-start(), calls=%async_computation.20 | async-start | bytes 14417920 | tf_op jit(solution)/shard_map/all_gather | solution.py:352
  45.2 21.6 %collective-permute-start.2 = (bf16[128,2048]{1,0:T(8,128)(2,1)}, bf16[128,2048]{1,0:T(8,128)(2,1)}, u32[]{:S(2)}, u32[]{:S(2)}) collective-permute-start(bf16[128,2048]{1,0:T(8,128)(2,1)} %get-tuple-element.278), channel_id=1, source_target_pairs={{0,8},{8,16},{16,24},{24,28},{28,20},{20,12},{12,4},{4,0},{1,9},{9... | collective-permute-start | bytes 1572872 | tf_op jit(solution)/shard_map/ppermute | solution.py:110
  45.7 21.7 %collective-permute-start.3 = (bf16[128,2048]{1,0:T(8,128)(2,1)}, bf16[128,2048]{1,0:T(8,128)(2,1)S(1)}, u32[]{:S(2)}, u32[]{:S(2)}) collective-permute-start(bf16[128,2048]{1,0:T(8,128)(2,1)} %get-tuple-element.278), channel_id=1, source_target_pairs={{8,0},{16,8},{24,16},{28,24},{20,28},{12,20},{4,12},{0,4},{9,1},{1... | collective-permute-start | bytes 1572872 | tf_op jit(solution)/shard_map/ppermute | solution.py:111
  47.2 79.3 %collective-permute-start.10 = (bf16[64,2048]{1,0:T(8,128)(2,1)S(1)}, bf16[64,2048]{1,0:T(8,128)(2,1)}, u32[]{:S(2)}, u32[]{:S(2)}) collective-permute-start(bf16[64,2048]{1,0:T(8,128)(2,1)S(1)} %copy-done.49), channel_id=1, source_target_pairs={{0,2},{1,3},{2,0},{3,1},{4,6},{5,7},{6,4},{7,5},{8,10},{9,11},{10,... | collective-permute-start | bytes 786440 | tf_op jit(solution)/shard_map/ppermute | solution.py:176
  48.7 89.5 %collective-permute-start.1 = (bf16[176,2048]{1,0:T(8,128)(2,1)}, bf16[176,2048]{1,0:T(8,128)(2,1)}, u32[]{:S(2)}, u32[]{:S(2)}) collective-permute-start(bf16[176,2048]{1,0:T(8,128)(2,1)} %param.34), channel_id=1, source_target_pairs={{0,2},{1,3},{2,0},{3,1},{4,6},{5,7},{6,4},{7,5},{8,10},{9,11},{10,... | collective-permute-start | bytes 2162696 | tf_op jit(solution)/shard_map/ppermute | solution.py:176
  49.2 89.0 %collective-permute-start = (bf16[352,2048]{1,0:T(8,128)(2,1)}, bf16[352,2048]{1,0:T(8,128)(2,1)}, u32[]{:S(2)}, u32[]{:S(2)}) collective-permute-start(bf16[352,2048]{1,0:T(8,128)(2,1)} %bitcast.1), channel_id=1, source_target_pairs={{0,2},{1,3},{2,0},{3,1},{4,6},{5,7},{6,4},{7,5},{8,10},{9,11},{10,... | collective-permute-start | bytes 4325384 | tf_op jit(solution)/shard_map/ppermute | solution.py:176
  98.9 46.0 %all-to-all-start.1 = ((bf16[8,64,1408]{2,1,0:T(8,128)(2,1)}), bf16[8,64,1408]{2,1,0:T(8,128)(2,1)}, u32[]{:S(2)}, u32[]{:S(2)}) async-start(bf16[8,64,1408]{2,1,0:T(8,128)(2,1)} %reshape.884), calls=%async_computation.1 | async-start | bytes 2883584 | tf_op jit(solution)/shard_map/all_to_all | solution.py:336
  104.5 187.5 %all-gather.12.cloned.1.call-start = ((), (), s32[]{:S(2)}) async-start(), calls=%async_computation.19 | async-start | bytes 7208960 | tf_op jit(solution)/shard_map/all_gather | solution.py:389
  145.0 171.7 %all-gather.8.cloned.1.call-start = ((), (), s32[]{:S(2)}) async-start(), calls=%async_computation.11 | async-start | bytes 4718592 | tf_op jit(solution)/shard_map/all_gather | solution.py:397
  157.5 13.5 %collective-permute-start.17 = (bf16[128,2048]{1,0:T(8,128)(2,1)S(1)}, bf16[128,2048]{1,0:T(8,128)(2,1)}, u32[]{:S(2)}, u32[]{:S(2)}) collective-permute-start(bf16[128,2048]{1,0:T(8,128)(2,1)S(1)} %pad_maximum_fusion.10), channel_id=1, source_target_pairs={{8,0},{16,8},{24,16},{28,24},{20,28},{12,20},{4,12},{0,4},{9,1},{1... | collective-permute-start | bytes 1572872 | tf_op jit(solution)/shard_map/ppermute | solution.py:148
  158.1 13.6 %collective-permute-start.13 = (bf16[128,2048]{1,0:T(8,128)(2,1)S(1)}, bf16[128,2048]{1,0:T(8,128)(2,1)S(1)}, u32[]{:S(2)}, u32[]{:S(2)}) collective-permute-start(bf16[128,2048]{1,0:T(8,128)(2,1)S(1)} %pad_maximum_fusion.9), channel_id=1, source_target_pairs={{0,8},{8,16},{16,24},{24,28},{28,20},{20,12},{12,4},{4,0},{1,9},{9... | collective-permute-start | bytes 1572872 | tf_op jit(solution)/shard_map/ppermute | solution.py:147
  164.7 56.9 %collective-permute-start.28 = (bf16[2,352,2048]{2,1,0:T(8,128)(2,1)}, bf16[2,352,2048]{2,1,0:T(8,128)(2,1)}, u32[]{:S(2)}, u32[]{:S(2)}) collective-permute-start(bf16[2,352,2048]{2,1,0:T(8,128)(2,1)} %maximum_select_fusion.1), channel_id=1, source_target_pairs={{0,1},{1,0},{2,3},{3,2},{4,5},{5,4},{6,7},{7,6},{8,9},{9,8},{10,11... | collective-permute-start | bytes 8650760 | tf_op jit(solution)/shard_map/ppermute | solution.py:181
  179.8 32.4 %collective-permute-start.29 = (bf16[2,176,2048]{2,1,0:T(8,128)(2,1)S(1)}, bf16[2,176,2048]{2,1,0:T(8,128)(2,1)}, u32[]{:S(2)}, u32[]{:S(2)}) collective-permute-start(bf16[2,176,2048]{2,1,0:T(8,128)(2,1)S(1)} %maximum_select_fusion.3), channel_id=1, source_target_pairs={{0,1},{1,0},{2,3},{3,2},{4,5},{5,4},{6,7},{7,6},{8,9},{9,8},{10,11... | collective-permute-start | bytes 4325384 | tf_op jit(solution)/shard_map/ppermute | solution.py:181
  235.7 216.3 %reduce-scatter.7.cloned.1.call-start = ((), (), s32[]{:S(2)}) async-start(), calls=%async_computation.12 | async-start | bytes 14417920 | tf_op jit(solution)/shard_map/reduce_scatter | solution.py:322
  243.8 15.5 %collective-permute-start.26 = (bf16[64,2048]{1,0:T(8,128)(2,1)S(1)}, bf16[64,2048]{1,0:T(8,128)(2,1)S(1)}, u32[]{:S(2)}, u32[]{:S(2)}) collective-permute-start(bf16[64,2048]{1,0:T(8,128)(2,1)S(1)} %slice.499), channel_id=1, source_target_pairs={{0,8},{8,16},{16,24},{24,28},{28,20},{20,12},{12,4},{4,0},{1,9},{9... | collective-permute-start | bytes 786440 | tf_op jit(solution)/shard_map/ppermute | solution.py:116
  245.2 17.8 %collective-permute-start.27 = (bf16[64,2048]{1,0:T(8,128)(2,1)S(1)}, bf16[64,2048]{1,0:T(8,128)(2,1)S(1)}, u32[]{:S(2)}, u32[]{:S(2)}) collective-permute-start(bf16[64,2048]{1,0:T(8,128)(2,1)S(1)} %slice.500), channel_id=1, source_target_pairs={{8,0},{16,8},{24,16},{28,24},{20,28},{12,20},{4,12},{0,4},{9,1},{1... | collective-permute-start | bytes 786440 | tf_op jit(solution)/shard_map/ppermute | solution.py:117
  355.2 84.1 %all-to-all-start.2 = ((f32[8,2,128]{2,1,0:T(2,128)}), f32[8,2,128]{2,1,0:T(2,128)S(1)}, u32[]{:S(2)}, u32[]{:S(2)}) async-start(f32[8,2,128]{2,1,0:T(2,128)} %pad_maximum_fusion.17), calls=%async_computation.2 | async-start | bytes 16384 | tf_op jit(solution)/shard_map/all_to_all | solution.py:469
  359.3 140.6 %reduce-scatter.9.cloned.1.call-start = ((), (), s32[]{:S(2)}) async-start(), calls=%async_computation.13 | async-start | bytes 7208960 | tf_op jit(solution)/shard_map/reduce_scatter | solution.py:474
  382.3 13.8 %collective-permute-start.30 = (bf16[64,2048]{1,0:T(8,128)(2,1)S(1)}, bf16[64,2048]{1,0:T(8,128)(2,1)S(1)}, u32[]{:S(2)}, u32[]{:S(2)}) collective-permute-start(bf16[64,2048]{1,0:T(8,128)(2,1)S(1)} %get-tuple-element.209), channel_id=1, source_target_pairs={{0,8},{8,16},{16,24},{24,28},{28,20},{20,12},{12,4},{4,0},{1,9},{9... | collective-permute-start | bytes 786440 | tf_op jit(solution)/shard_map/ppermute | solution.py:138
  411.9 12.8 %collective-permute-start.36 = (bf16[128,2048]{1,0:T(8,128)(2,1)S(1)}, bf16[128,2048]{1,0:T(8,128)(2,1)S(1)}, u32[]{:S(2)}, u32[]{:S(2)}) collective-permute-start(bf16[128,2048]{1,0:T(8,128)(2,1)S(1)} %get-tuple-element.206), channel_id=1, source_target_pairs={{8,0},{16,8},{24,16},{28,24},{20,28},{12,20},{4,12},{0,4},{9,1},{1... | collective-permute-start | bytes 1572872 | tf_op jit(solution)/shard_map/ppermute | solution.py:148
  445.1 137.1 %reduce-scatter.11.cloned.1.call-start = ((), (), s32[]{:S(2)}) async-start(), calls=%async_computation.14 | async-start | bytes 7208960 | tf_op jit(solution)/shard_map/reduce_scatter | solution.py:322
  445.9 175.0 %reduce-scatter.13.cloned.1.call-start = ((), (), s32[]{:S(2)}) async-start(), calls=%async_computation.15 | async-start | bytes 4915200 | tf_op jit(solution)/shard_map/reduce_scatter | solution.py:555
  530.8 166.6 %reduce-scatter.15.cloned.1.call-start = ((), (), s32[]{:S(2)}) async-start(), calls=%async_computation.16 | async-start | bytes 1310720 | tf_op jit(solution)/shard_map/reduce_scatter | solution.py:322
  620.9 78.3 %reduce-scatter.17.cloned.1.call-start = ((), (), s32[]{:S(2)}) async-start(), calls=%async_computation.17 | async-start | bytes 3604480 | tf_op jit(solution)/shard_map/reduce_scatter | solution.py:322
  633.7 16.6 %collective-permute-start.59 = (bf16[128,2048]{1,0:T(8,128)(2,1)S(1)}, bf16[128,2048]{1,0:T(8,128)(2,1)}, u32[]{:S(2)}, u32[]{:S(2)}) collective-permute-start(bf16[128,2048]{1,0:T(8,128)(2,1)S(1)} %pad_maximum_fusion.16), channel_id=1, source_target_pairs={{8,0},{16,8},{24,16},{28,24},{20,28},{12,20},{4,12},{0,4},{9,1},{1... | collective-permute-start | bytes 1572872 | tf_op jit(solution)/shard_map/ppermute | solution.py:148
  636.3 14.0 %collective-permute-start.55 = (bf16[128,2048]{1,0:T(8,128)(2,1)}, bf16[128,2048]{1,0:T(8,128)(2,1)}, u32[]{:S(2)}, u32[]{:S(2)}) collective-permute-start(bf16[128,2048]{1,0:T(8,128)(2,1)} %pad_maximum_fusion.15), channel_id=1, source_target_pairs={{0,8},{8,16},{16,24},{24,28},{28,20},{20,12},{12,4},{4,0},{1,9},{9... | collective-permute-start | bytes 1572872 | tf_op jit(solution)/shard_map/ppermute | solution.py:147
  645.1 35.9 %all-to-all-start.4 = ((bf16[8,80,768]{2,1,0:T(8,128)(2,1)}), bf16[8,80,768]{2,1,0:T(8,128)(2,1)S(1)}, u32[]{:S(2)}, u32[]{:S(2)}) async-start(bf16[8,80,768]{2,1,0:T(8,128)(2,1)} %bitcast.400), calls=%async_computation.8 | async-start | bytes 1966080 | tf_op jit(solution)/shard_map/all_to_all | solution.py:564
  652.2 23.5 %collective-permute-start.56 = (bf16[128,2048]{1,0:T(8,128)(2,1)S(1)}, bf16[128,2048]{1,0:T(8,128)(2,1)S(1)}, u32[]{:S(2)}, u32[]{:S(2)}) collective-permute-start(bf16[128,2048]{1,0:T(8,128)(2,1)S(1)} %get-tuple-element.185), channel_id=1, source_target_pairs={{0,8},{8,16},{16,24},{24,28},{28,20},{20,12},{12,4},{4,0},{1,9},{9... | collective-permute-start | bytes 1572872 | tf_op jit(solution)/shard_map/ppermute | solution.py:147
  653.8 22.0 %collective-permute-start.60 = (bf16[128,2048]{1,0:T(8,128)(2,1)S(1)}, bf16[128,2048]{1,0:T(8,128)(2,1)S(1)}, u32[]{:S(2)}, u32[]{:S(2)}) collective-permute-start(bf16[128,2048]{1,0:T(8,128)(2,1)S(1)} %get-tuple-element.186), channel_id=1, source_target_pairs={{8,0},{16,8},{24,16},{28,24},{20,28},{12,20},{4,12},{0,4},{9,1},{1... | collective-permute-start | bytes 1572872 | tf_op jit(solution)/shard_map/ppermute | solution.py:148
  678.3 15.2 %collective-permute-start.57 = (bf16[128,2048]{1,0:T(8,128)(2,1)}, bf16[128,2048]{1,0:T(8,128)(2,1)}, u32[]{:S(2)}, u32[]{:S(2)}) collective-permute-start(bf16[128,2048]{1,0:T(8,128)(2,1)} %get-tuple-element.183), channel_id=1, source_target_pairs={{0,8},{8,16},{16,24},{24,28},{28,20},{20,12},{12,4},{4,0},{1,9},{9... | collective-permute-start | bytes 1572872 | tf_op jit(solution)/shard_map/ppermute | solution.py:147
  680.8 12.7 %collective-permute-start.61 = (bf16[128,2048]{1,0:T(8,128)(2,1)}, bf16[128,2048]{1,0:T(8,128)(2,1)}, u32[]{:S(2)}, u32[]{:S(2)}) collective-permute-start(bf16[128,2048]{1,0:T(8,128)(2,1)} %get-tuple-element.184), channel_id=1, source_target_pairs={{8,0},{16,8},{24,16},{28,24},{20,28},{12,20},{4,12},{0,4},{9,1},{1... | collective-permute-start | bytes 1572872 | tf_op jit(solution)/shard_map/ppermute | solution.py:148
  (140 other events, 1233.0 us)
Sparse Core Ops, SparseCore 0:
  40.6 53.3 all-gather.9
  95.6 89.0 all-gather.13
  186.3 43.5 all-gather.11
  235.8 74.2 all-gather.7
  342.7 90.4 reduce-scatter.6
  445.1 54.7 reduce-scatter.8
  502.6 54.8 reduce-scatter.10
  560.0 42.9 reduce-scatter.12
  621.0 22.8 reduce-scatter.14
  646.3 36.3 reduce-scatter.16

commit v17 on v16

--- a/solution.py
+++ b/solution.py
@@ -524,10 +524,9 @@
     ).astype(bf16)
     one_sums = dot_t(grad_projected, qkv_weight)
     grad_gain_one = jnp.sum(one_sums * scaled_rows.astype(f32), axis=0)
-    one_parts = one_sums.astype(bf16)
+    one_parts, sum_shared_in = after(one_sums.astype(bf16), sum_shared_in)
     one_kept, grad_projected = after(one_parts, grad_projected)
     one_kept, attn_own = after(one_kept, attn_own)
-    one_parts, sum_shared_in = after(one_parts, sum_shared_in)
     grad_normed, sum_expert_out = ring_scatter(
         one_parts, ctx_size, ctx_index, one_kept, (sum_expert_out,)
     )

time: 719 us -> 709 us (0.986)
  blocking collectives: 68.7 us -> 29.7 us
  waiting for transfers between devices: 175 us -> 200 us
    all_to_all x1 -> x0, blocking collectives: 39 us -> none  [local_split(): lax.all_to_all(sum_shared_in, 'ctx', split_axis=0, concat_axis=0, tiled=T...]
    all_to_all x0 -> x1, waiting for transfers between devices: none -> 11.1 us  [local_split(): lax.all_to_all(sum_shared_in, 'ctx', split_axis=0, concat_axis=0, tiled=T...]
    ppermute x12, waiting for transfers between devices: 59.3 us -> 69.1 us  [ring_sums(): fore = lax.ppermute(fore, 'ctx', ahead)]
    unnamed x200 -> x198, local copies, waits for them, and re-layouts: 23.6 us -> 22.8 us
  transfers between devices with their start and end apart: 75 -> 76, of which waited for: 38 -> 41; matrix products, arithmetic and copies ran while one was open for 43% -> 44% of each run, Pallas kernels for 1% -> 1%
where the time goes in v17:
time: 709 us; the launch traced here: 698 us
  waiting for transfers between devices  200 us (28%)
  matrix products  143 us (20%)
  local copies, waits for them, and re-layouts  113 us (16%)
  other arithmetic  95.9 us (14%)
  starting transfers between devices  85.4 us (12%)
  blocking collectives  29.7 us (4%)
  between operations  21 us (3%)
  Pallas kernels  9.58 us (1%)
    ppermute x12, waiting for transfers between devices, ring_sums(): fore = lax.ppermute(fore, 'ctx', ahead)  69.1 us
    ppermute x9, waiting for transfers between devices, ring_gather(): fore = lax.ppermute(fore, 'ctx', ahead)  49.5 us
    dot_general x7, matrix products, dot_t(): lax.dot_general(a, b, (((1,), (1,)), ((), ())), preferred_element_type=f32)  45.3 us
    dot_general x8, matrix products, dot(): return jnp.dot(a, b, preferred_element_type=f32)  44.1 us
    dot_general x8, matrix products, t_dot(): lax.dot_general(a, b, (((0,), (0,)), ((), ())), preferred_element_type=f32)  39.3 us
    all_to_all x1, blocking collectives, local_split(): lax.all_to_all(pieces, 'ctx', split_axis=0, concat_axis=0, tiled=True)  29.7 us
    unnamed x198, local copies, waits for them, and re-layouts  22.8 us
    dynamic_update_slice x25, local copies, waits for them, and re-layouts, put(): lax.dynamic_update_slice(out, piece, (peer * rows + offset, jnp.zeros_lik...  20.7 us
  transfers between devices with their start and end apart: 76, of which 41 were waited for; matrix products, arithmetic and copies ran while one was open for 44% of the time, Pallas kernels for 1%

profile of v17, /device:TPU:8, one launch (start us, length us, event | category | flops | bytes accessed | tf_op | source)
XLA Modules:
  0.0 698.2 jit_solution(15041543654243250137)
XLA Ops:
  10.7 29.7 %all_to_all.25 = bf16[8,80,768]{2,1,0:T(8,128)(2,1)} all-to-all(bf16[8,80,768]{2,1,0:T(8,128)(2,1)S(1)} %pad_maximum_fusion.6), channel_id=1, replica_groups=mesh['ctx'=8,'fsdp'=4] {'ctx'}, dimensions={0} | all-to-all | bytes 1966080 | tf_op jit(solution)/shard_map/all_to_all | solution.py:333
  72.0 7.1 %collective-permute-done.4 = bf16[128,2048]{1,0:T(8,128)(2,1)S(1)} collective-permute-done((bf16[128,2048]{1,0:T(8,128)(2,1)}, bf16[128,2048]{1,0:T(8,128)(2,1)S(1)}, u32[]{:S(2)}, u32[]{:S(2)}) %collective-permute-start.4) | collective-permute-done | bytes 524320 | tf_op jit(solution)/shard_map/ppermute | solution.py:110
  83.6 7.4 %collective-permute-done.6 = bf16[128,2048]{1,0:T(8,128)(2,1)S(1)} collective-permute-done((bf16[128,2048]{1,0:T(8,128)(2,1)S(1)}, bf16[128,2048]{1,0:T(8,128)(2,1)S(1)}, u32[]{:S(2)}, u32[]{:S(2)}) %collective-permute-start.6) | collective-permute-done | bytes 524320 | tf_op jit(solution)/shard_map/ppermute | solution.py:110
  115.5 6.4 fusion.24
  148.4 6.7 collective-permute-done.12
  179.9 7.2 %collective-permute-done.14 = bf16[128,2048]{1,0:T(8,128)(2,1)} collective-permute-done((bf16[128,2048]{1,0:T(8,128)(2,1)}, bf16[128,2048]{1,0:T(8,128)(2,1)}, u32[]{:S(2)}, u32[]{:S(2)}) %collective-permute-start.14) | collective-permute-done | bytes 524320 | tf_op jit(solution)/shard_map/ppermute | solution.py:147
  237.5 6.3 collective-permute-done.24
  247.6 11.7 %collective-permute-done.26 = bf16[64,2048]{1,0:T(8,128)(2,1)S(1)} collective-permute-done((bf16[64,2048]{1,0:T(8,128)(2,1)S(1)}, bf16[64,2048]{1,0:T(8,128)(2,1)S(1)}, u32[]{:S(2)}, u32[]{:S(2)}) %collective-permute-start.26) | collective-permute-done | bytes 262176 | tf_op jit(solution)/shard_map/ppermute | solution.py:116
  271.1 10.3 %fusion.2 = f32[512,2816]{1,0:T(8,128)S(1)} fusion(bf16[512,2048]{1,0:T(8,128)(2,1)S(1)} %bitcast.387, bf16[1,2048,2816]{2,1,0:T(8,128)(2,1)} %all-gather.14.cloned.1.call-done), kind=kOutput, calls=%fused_computation.2 | convolution fusion | flops 5905580032 | bytes 19398656 | tf_op jit(solution)/shard_map/dot_general | solution.py:308
  285.8 6.2 convolution_convert_fusion.6
  297.8 8.5 %fusion.104 = f32[1024,1408]{1,0:T(8,128)S(1)} fusion(bf16[1024,2048]{1,0:T(8,128)(2,1)} %constant_dynamic-update-slice_fusion.4, bf16[2048,1408]{1,0:T(8,128)(2,1)S(1)} %bitcast.357), kind=kOutput, calls=%fused_computation.315 | convolution fusion | flops 5905580032 | bytes 15728640 | tf_op jit(solution)/shard_map/dot_general | solution.py:308
  310.8 5.8 fusion.8
  324.6 7.4 %multiply_convert_fusion.6 = (bf16[512,1408]{1,0:T(8,128)(2,1)S(1)}, bf16[512,1408]{1,0:T(8,128)(2,1)S(1)}, f32[512]{0:T(512)S(1)}) fusion(f32[512,2816]{1,0:T(8,128)S(1)} %bitcast.362, bf16[512,1408]{1,0:T(8,128)(2,1)S(1)} %copy-done.43, bf16[512,2048]{1,0:T(8,128)(2,1)S(1)} %bitcast.389, bf16[1408,2048]{1,0:T(8,128)(2,1)} %bitcast.364), kind=kOutput, calls=%fused_computation.51 | convolution fusion | flops 2964323840 | bytes 17958912 | tf_op jit(solution)/shard_map/dot_general | solution.py:311
  333.2 9.4 %convolution_convert_fusion = bf16[2048,2816]{1,0:T(8,128)(2,1)} fusion(bf16[512,2048]{1,0:T(8,128)(2,1)S(1)} %bitcast.388, bf16[512,1408]{1,0:T(8,128)(2,1)S(1)} %get-tuple-element.180, bf16[512,1408]{1,0:T(8,128)(2,1)S(1)} %get-tuple-element.179), kind=kOutput, calls=%fused_computation.4 | convolution fusion | flops 5917114368 | bytes 16515072 | tf_op jit(solution)/shard_map/dot_general | solution.py:314
  342.9 11.8 %multiply_convert_fusion.3 = (bf16[1024,704]{1,0:T(8,128)(2,1)S(1)}, bf16[1024,704]{1,0:T(8,128)(2,1)}, f32[1024]{0:T(1024)S(1)}) fusion(f32[1024,1408]{1,0:T(8,128)} %copy-done.16, bf16[1024,704]{1,0:T(8,128)(2,1)} %copy-done.40, bf16[1024,2048]{1,0:T(8,128)(2,1)} %multiply_convert_fusion, bf16[704,2048]{1,0:T(8,128)(2,1)} %bitcast.382), kind=kOutput, calls=%fused_computation.36 | convolution fusion | flops 2964323328 | bytes 17174528 | tf_op jit(solution)/shard_map/dot_general | solution.py:311
  363.2 9.1 %fusion.20 = bf16[512,2048]{1,0:T(8,128)(2,1)S(1)} fusion(bf16[1,2048,2816]{2,1,0:T(8,128)(2,1)} %all-gather.14.cloned.1.call-done, bf16[512,1408]{1,0:T(8,128)(2,1)S(1)} %copy-done.90, bf16[512,1408]{1,0:T(8,128)(2,1)S(1)} %copy-done.88), kind=kOutput, calls=%fused_computation.39 | convolution fusion | flops 5912395776 | bytes 16515072 | tf_op jit(solution)/shard_map/dot_general | solution.py:311
  373.6 8.4 %fusion.6 = bf16[1024,2048]{1,0:T(8,128)(2,1)S(1)} fusion(f32[8,128,2048]{2,1,0:T(8,128)S(1)} %fusion.55, bf16[1024,1408]{1,0:T(8,128)(2,1)} %pad_maximum_fusion.2, bf16[2048,1408]{1,0:T(8,128)(2,1)S(1)} %bitcast.360), kind=kOutput, calls=%fused_computation.10 | convolution fusion | flops 5909774336 | bytes 21233664 | tf_op jit(solution)/shard_map/dot_general | solution.py:311
  384.2 11.7 %convolution_convert_fusion.2 = bf16[2048,1408]{1,0:T(8,128)(2,1)} fusion(bf16[1024,2048]{1,0:T(8,128)(2,1)} %constant_dynamic-update-slice_fusion.4, bf16[1024,1408]{1,0:T(8,128)(2,1)} %pad_maximum_fusion.2), kind=kOutput, calls=%fused_computation.19 | convolution fusion | flops 5908463616 | bytes 12845056 | tf_op jit(solution)/shard_map/dot_general | solution.py:314
  415.0 7.6 %collective-permute-done.32 = bf16[128,2048]{1,0:T(8,128)(2,1)S(1)} collective-permute-done((bf16[128,2048]{1,0:T(8,128)(2,1)S(1)}, bf16[128,2048]{1,0:T(8,128)(2,1)S(1)}, u32[]{:S(2)}, u32[]{:S(2)}) %collective-permute-start.32) | collective-permute-done | bytes 524320 | tf_op jit(solution)/shard_map/ppermute | solution.py:147
  438.9 5.7 copy.245
  454.5 9.6 %collective-permute-done.38 = bf16[128,2048]{1,0:T(8,128)(2,1)} collective-permute-done((bf16[128,2048]{1,0:T(8,128)(2,1)}, bf16[128,2048]{1,0:T(8,128)(2,1)}, u32[]{:S(2)}, u32[]{:S(2)}) %collective-permute-start.38) | collective-permute-done | bytes 524320 | tf_op jit(solution)/shard_map/ppermute | solution.py:110
  469.6 5.9 collective-permute-done.40
  499.6 6.1 all-to-all-start.3
  505.6 9.6 %shard_map.309 = (f32[1024,256]{1,0:T(8,128)S(1)}, f32[1024,256]{1,0:T(8,128)S(1)}, f32[1024,256]{1,0:T(8,128)S(1)}) custom-call(bf16[1024,256]{1,0:T(8,128)(2,1)S(1)} %copy_bitcast_fusion.4.q_ref, bf16[1024,256]{1,0:T(8,128)(2,1)S(1)} %get-tuple-element.224.k_ref, bf16[1024,256]{1,0:T(8,128)(2,1)S(1)} %slice.585.v_ref, ...), custom_call_target="tpu_custom_call" | custom-call | flops 2684354560 | bytes 5242880 | tf_op jit(solution)/shard_map/pallas_call | solution.py:253
  518.6 7.0 fusion.5
  525.8 11.1 %all-to-all-done.3 = bf16[8,64,1408]{2,1,0:T(8,128)(2,1)} async-done(((bf16[8,64,1408]{2,1,0:T(8,128)(2,1)}), bf16[8,64,1408]{2,1,0:T(8,128)(2,1)}, u32[]{:S(2)}, u32[]{:S(2)}) %all-to-all-start.3) | async-done | bytes 1441824 | tf_op jit(solution)/shard_map/all_to_all | solution.py:505
  537.7 5.8 fusion.17
  561.0 10.9 %collective-permute-done.47 = bf16[128,2048]{1,0:T(8,128)(2,1)S(1)} collective-permute-done((bf16[128,2048]{1,0:T(8,128)(2,1)S(1)}, bf16[128,2048]{1,0:T(8,128)(2,1)S(1)}, u32[]{:S(2)}, u32[]{:S(2)}) %collective-permute-start.47) | collective-permute-done | bytes 524320 | tf_op jit(solution)/shard_map/ppermute | solution.py:147
  576.7 9.5 %collective-permute-done.48 = bf16[128,2048]{1,0:T(8,128)(2,1)S(1)} collective-permute-done((bf16[128,2048]{1,0:T(8,128)(2,1)S(1)}, bf16[128,2048]{1,0:T(8,128)(2,1)S(1)}, u32[]{:S(2)}, u32[]{:S(2)}) %collective-permute-start.48) | collective-permute-done | bytes 524320 | tf_op jit(solution)/shard_map/ppermute | solution.py:147
  593.1 6.2 collective-permute-done.49
  606.8 6.0 collective-permute-done.54
  641.4 22.4 %collective-permute-done.56 = bf16[128,2048]{1,0:T(8,128)(2,1)S(1)} collective-permute-done((bf16[128,2048]{1,0:T(8,128)(2,1)S(1)}, bf16[128,2048]{1,0:T(8,128)(2,1)S(1)}, u32[]{:S(2)}, u32[]{:S(2)}) %collective-permute-start.56) | collective-permute-done | bytes 524320 | tf_op jit(solution)/shard_map/ppermute | solution.py:147
  (577 shorter events, 382.8 us)
Async XLA Ops:
  7.2 97.5 %all-gather.10.cloned.1.call-start = ((), (), s32[]{:S(2)}) async-start(), calls=%async_computation.18 | async-start | bytes 4915200 | tf_op jit(solution)/shard_map/all_gather | solution.py:337
  40.5 230.6 %all-gather.14.cloned.1.call-start = ((), (), s32[]{:S(2)}) async-start(), calls=%async_computation.20 | async-start | bytes 14417920 | tf_op jit(solution)/shard_map/all_gather | solution.py:352
  45.2 21.6 %collective-permute-start.2 = (bf16[128,2048]{1,0:T(8,128)(2,1)}, bf16[128,2048]{1,0:T(8,128)(2,1)}, u32[]{:S(2)}, u32[]{:S(2)}) collective-permute-start(bf16[128,2048]{1,0:T(8,128)(2,1)} %get-tuple-element.278), channel_id=1, source_target_pairs={{0,8},{8,16},{16,24},{24,28},{28,20},{20,12},{12,4},{4,0},{1,9},{9... | collective-permute-start | bytes 1572872 | tf_op jit(solution)/shard_map/ppermute | solution.py:110
  45.7 21.7 %collective-permute-start.3 = (bf16[128,2048]{1,0:T(8,128)(2,1)}, bf16[128,2048]{1,0:T(8,128)(2,1)S(1)}, u32[]{:S(2)}, u32[]{:S(2)}) collective-permute-start(bf16[128,2048]{1,0:T(8,128)(2,1)} %get-tuple-element.278), channel_id=1, source_target_pairs={{8,0},{16,8},{24,16},{28,24},{20,28},{12,20},{4,12},{0,4},{9,1},{1... | collective-permute-start | bytes 1572872 | tf_op jit(solution)/shard_map/ppermute | solution.py:111
  47.2 79.3 %collective-permute-start.10 = (bf16[64,2048]{1,0:T(8,128)(2,1)S(1)}, bf16[64,2048]{1,0:T(8,128)(2,1)}, u32[]{:S(2)}, u32[]{:S(2)}) collective-permute-start(bf16[64,2048]{1,0:T(8,128)(2,1)S(1)} %copy-done.48), channel_id=1, source_target_pairs={{0,2},{1,3},{2,0},{3,1},{4,6},{5,7},{6,4},{7,5},{8,10},{9,11},{10,... | collective-permute-start | bytes 786440 | tf_op jit(solution)/shard_map/ppermute | solution.py:176
  48.7 89.5 %collective-permute-start.1 = (bf16[176,2048]{1,0:T(8,128)(2,1)}, bf16[176,2048]{1,0:T(8,128)(2,1)}, u32[]{:S(2)}, u32[]{:S(2)}) collective-permute-start(bf16[176,2048]{1,0:T(8,128)(2,1)} %param.34), channel_id=1, source_target_pairs={{0,2},{1,3},{2,0},{3,1},{4,6},{5,7},{6,4},{7,5},{8,10},{9,11},{10,... | collective-permute-start | bytes 2162696 | tf_op jit(solution)/shard_map/ppermute | solution.py:176
  49.2 89.0 %collective-permute-start = (bf16[352,2048]{1,0:T(8,128)(2,1)}, bf16[352,2048]{1,0:T(8,128)(2,1)}, u32[]{:S(2)}, u32[]{:S(2)}) collective-permute-start(bf16[352,2048]{1,0:T(8,128)(2,1)} %bitcast.1), channel_id=1, source_target_pairs={{0,2},{1,3},{2,0},{3,1},{4,6},{5,7},{6,4},{7,5},{8,10},{9,11},{10,... | collective-permute-start | bytes 4325384 | tf_op jit(solution)/shard_map/ppermute | solution.py:176
  98.9 46.0 %all-to-all-start.1 = ((bf16[8,64,1408]{2,1,0:T(8,128)(2,1)}), bf16[8,64,1408]{2,1,0:T(8,128)(2,1)}, u32[]{:S(2)}, u32[]{:S(2)}) async-start(bf16[8,64,1408]{2,1,0:T(8,128)(2,1)} %reshape.884), calls=%async_computation.1 | async-start | bytes 2883584 | tf_op jit(solution)/shard_map/all_to_all | solution.py:336
  104.5 187.6 %all-gather.12.cloned.1.call-start = ((), (), s32[]{:S(2)}) async-start(), calls=%async_computation.19 | async-start | bytes 7208960 | tf_op jit(solution)/shard_map/all_gather | solution.py:389
  145.0 171.7 %all-gather.8.cloned.1.call-start = ((), (), s32[]{:S(2)}) async-start(), calls=%async_computation.11 | async-start | bytes 4718592 | tf_op jit(solution)/shard_map/all_gather | solution.py:397
  157.5 13.5 %collective-permute-start.17 = (bf16[128,2048]{1,0:T(8,128)(2,1)S(1)}, bf16[128,2048]{1,0:T(8,128)(2,1)}, u32[]{:S(2)}, u32[]{:S(2)}) collective-permute-start(bf16[128,2048]{1,0:T(8,128)(2,1)S(1)} %pad_maximum_fusion.10), channel_id=1, source_target_pairs={{8,0},{16,8},{24,16},{28,24},{20,28},{12,20},{4,12},{0,4},{9,1},{1... | collective-permute-start | bytes 1572872 | tf_op jit(solution)/shard_map/ppermute | solution.py:148
  158.1 13.7 %collective-permute-start.13 = (bf16[128,2048]{1,0:T(8,128)(2,1)S(1)}, bf16[128,2048]{1,0:T(8,128)(2,1)S(1)}, u32[]{:S(2)}, u32[]{:S(2)}) collective-permute-start(bf16[128,2048]{1,0:T(8,128)(2,1)S(1)} %pad_maximum_fusion.9), channel_id=1, source_target_pairs={{0,8},{8,16},{16,24},{24,28},{28,20},{20,12},{12,4},{4,0},{1,9},{9... | collective-permute-start | bytes 1572872 | tf_op jit(solution)/shard_map/ppermute | solution.py:147
  164.7 56.9 %collective-permute-start.28 = (bf16[2,352,2048]{2,1,0:T(8,128)(2,1)}, bf16[2,352,2048]{2,1,0:T(8,128)(2,1)}, u32[]{:S(2)}, u32[]{:S(2)}) collective-permute-start(bf16[2,352,2048]{2,1,0:T(8,128)(2,1)} %maximum_select_fusion.1), channel_id=1, source_target_pairs={{0,1},{1,0},{2,3},{3,2},{4,5},{5,4},{6,7},{7,6},{8,9},{9,8},{10,11... | collective-permute-start | bytes 8650760 | tf_op jit(solution)/shard_map/ppermute | solution.py:181
  179.8 32.4 %collective-permute-start.29 = (bf16[2,176,2048]{2,1,0:T(8,128)(2,1)S(1)}, bf16[2,176,2048]{2,1,0:T(8,128)(2,1)}, u32[]{:S(2)}, u32[]{:S(2)}) collective-permute-start(bf16[2,176,2048]{2,1,0:T(8,128)(2,1)S(1)} %maximum_select_fusion.3), channel_id=1, source_target_pairs={{0,1},{1,0},{2,3},{3,2},{4,5},{5,4},{6,7},{7,6},{8,9},{9,8},{10,11... | collective-permute-start | bytes 4325384 | tf_op jit(solution)/shard_map/ppermute | solution.py:181
  235.8 215.9 %reduce-scatter.7.cloned.1.call-start = ((), (), s32[]{:S(2)}) async-start(), calls=%async_computation.12 | async-start | bytes 14417920 | tf_op jit(solution)/shard_map/reduce_scatter | solution.py:322
  243.8 15.6 %collective-permute-start.26 = (bf16[64,2048]{1,0:T(8,128)(2,1)S(1)}, bf16[64,2048]{1,0:T(8,128)(2,1)S(1)}, u32[]{:S(2)}, u32[]{:S(2)}) collective-permute-start(bf16[64,2048]{1,0:T(8,128)(2,1)S(1)} %slice.499), channel_id=1, source_target_pairs={{0,8},{8,16},{16,24},{24,28},{28,20},{20,12},{12,4},{4,0},{1,9},{9... | collective-permute-start | bytes 786440 | tf_op jit(solution)/shard_map/ppermute | solution.py:116
  245.3 17.8 %collective-permute-start.27 = (bf16[64,2048]{1,0:T(8,128)(2,1)S(1)}, bf16[64,2048]{1,0:T(8,128)(2,1)S(1)}, u32[]{:S(2)}, u32[]{:S(2)}) collective-permute-start(bf16[64,2048]{1,0:T(8,128)(2,1)S(1)} %slice.500), channel_id=1, source_target_pairs={{8,0},{16,8},{24,16},{28,24},{20,28},{12,20},{4,12},{0,4},{9,1},{1... | collective-permute-start | bytes 786440 | tf_op jit(solution)/shard_map/ppermute | solution.py:117
  355.3 83.7 %all-to-all-start.2 = ((f32[8,2,128]{2,1,0:T(2,128)}), f32[8,2,128]{2,1,0:T(2,128)S(1)}, u32[]{:S(2)}, u32[]{:S(2)}) async-start(f32[8,2,128]{2,1,0:T(2,128)} %pad_maximum_fusion.17), calls=%async_computation.2 | async-start | bytes 16384 | tf_op jit(solution)/shard_map/all_to_all | solution.py:469
  359.1 140.5 %reduce-scatter.9.cloned.1.call-start = ((), (), s32[]{:S(2)}) async-start(), calls=%async_computation.13 | async-start | bytes 7208960 | tf_op jit(solution)/shard_map/reduce_scatter | solution.py:474
  382.1 13.7 %collective-permute-start.30 = (bf16[64,2048]{1,0:T(8,128)(2,1)S(1)}, bf16[64,2048]{1,0:T(8,128)(2,1)S(1)}, u32[]{:S(2)}, u32[]{:S(2)}) collective-permute-start(bf16[64,2048]{1,0:T(8,128)(2,1)S(1)} %get-tuple-element.209), channel_id=1, source_target_pairs={{0,8},{8,16},{16,24},{24,28},{28,20},{20,12},{12,4},{4,0},{1,9},{9... | collective-permute-start | bytes 786440 | tf_op jit(solution)/shard_map/ppermute | solution.py:138
  444.8 116.1 %reduce-scatter.11.cloned.1.call-start = ((), (), s32[]{:S(2)}) async-start(), calls=%async_computation.14 | async-start | bytes 7208960 | tf_op jit(solution)/shard_map/reduce_scatter | solution.py:322
  499.6 37.3 %all-to-all-start.3 = ((bf16[8,64,1408]{2,1,0:T(8,128)(2,1)}), bf16[8,64,1408]{2,1,0:T(8,128)(2,1)}, u32[]{:S(2)}, u32[]{:S(2)}) async-start(bf16[8,64,1408]{2,1,0:T(8,128)(2,1)} %bitcast.391), calls=%async_computation.5 | async-start | bytes 2883584 | tf_op jit(solution)/shard_map/all_to_all | solution.py:505
  505.6 97.0 %reduce-scatter.13.cloned.1.call-start = ((), (), s32[]{:S(2)}) async-start(), calls=%async_computation.15 | async-start | bytes 4915200 | tf_op jit(solution)/shard_map/reduce_scatter | solution.py:554
  546.0 141.0 %reduce-scatter.15.cloned.1.call-start = ((), (), s32[]{:S(2)}) async-start(), calls=%async_computation.16 | async-start | bytes 1310720 | tf_op jit(solution)/shard_map/reduce_scatter | solution.py:322
  602.7 86.1 %reduce-scatter.17.cloned.1.call-start = ((), (), s32[]{:S(2)}) async-start(), calls=%async_computation.17 | async-start | bytes 3604480 | tf_op jit(solution)/shard_map/reduce_scatter | solution.py:322
  615.3 18.1 %collective-permute-start.59 = (bf16[128,2048]{1,0:T(8,128)(2,1)S(1)}, bf16[128,2048]{1,0:T(8,128)(2,1)}, u32[]{:S(2)}, u32[]{:S(2)}) collective-permute-start(bf16[128,2048]{1,0:T(8,128)(2,1)S(1)} %pad_maximum_fusion.16), channel_id=1, source_target_pairs={{8,0},{16,8},{24,16},{28,24},{20,28},{12,20},{4,12},{0,4},{9,1},{1... | collective-permute-start | bytes 1572872 | tf_op jit(solution)/shard_map/ppermute | solution.py:148
  616.7 16.7 %collective-permute-start.55 = (bf16[128,2048]{1,0:T(8,128)(2,1)}, bf16[128,2048]{1,0:T(8,128)(2,1)}, u32[]{:S(2)}, u32[]{:S(2)}) collective-permute-start(bf16[128,2048]{1,0:T(8,128)(2,1)} %pad_maximum_fusion.15), channel_id=1, source_target_pairs={{0,8},{8,16},{16,24},{24,28},{28,20},{20,12},{12,4},{4,0},{1,9},{9... | collective-permute-start | bytes 1572872 | tf_op jit(solution)/shard_map/ppermute | solution.py:147
  628.3 42.3 %all-to-all-start.4 = ((bf16[8,80,768]{2,1,0:T(8,128)(2,1)}), bf16[8,80,768]{2,1,0:T(8,128)(2,1)S(1)}, u32[]{:S(2)}, u32[]{:S(2)}) async-start(bf16[8,80,768]{2,1,0:T(8,128)(2,1)} %bitcast.400), calls=%async_computation.8 | async-start | bytes 1966080 | tf_op jit(solution)/shard_map/all_to_all | solution.py:563
  635.4 28.3 %collective-permute-start.56 = (bf16[128,2048]{1,0:T(8,128)(2,1)S(1)}, bf16[128,2048]{1,0:T(8,128)(2,1)S(1)}, u32[]{:S(2)}, u32[]{:S(2)}) collective-permute-start(bf16[128,2048]{1,0:T(8,128)(2,1)S(1)} %get-tuple-element.185), channel_id=1, source_target_pairs={{0,8},{8,16},{16,24},{24,28},{28,20},{20,12},{12,4},{4,0},{1,9},{9... | collective-permute-start | bytes 1572872 | tf_op jit(solution)/shard_map/ppermute | solution.py:147
  636.9 29.0 %collective-permute-start.60 = (bf16[128,2048]{1,0:T(8,128)(2,1)S(1)}, bf16[128,2048]{1,0:T(8,128)(2,1)S(1)}, u32[]{:S(2)}, u32[]{:S(2)}) collective-permute-start(bf16[128,2048]{1,0:T(8,128)(2,1)S(1)} %get-tuple-element.186), channel_id=1, source_target_pairs={{8,0},{16,8},{24,16},{28,24},{20,28},{12,20},{4,12},{0,4},{9,1},{1... | collective-permute-start | bytes 1572872 | tf_op jit(solution)/shard_map/ppermute | solution.py:148
  668.4 14.7 %collective-permute-start.57 = (bf16[128,2048]{1,0:T(8,128)(2,1)}, bf16[128,2048]{1,0:T(8,128)(2,1)}, u32[]{:S(2)}, u32[]{:S(2)}) collective-permute-start(bf16[128,2048]{1,0:T(8,128)(2,1)} %get-tuple-element.183), channel_id=1, source_target_pairs={{0,8},{8,16},{16,24},{24,28},{28,20},{20,12},{12,4},{4,0},{1,9},{9... | collective-permute-start | bytes 1572872 | tf_op jit(solution)/shard_map/ppermute | solution.py:147
  668.8 14.3 %collective-permute-start.61 = (bf16[128,2048]{1,0:T(8,128)(2,1)}, bf16[128,2048]{1,0:T(8,128)(2,1)}, u32[]{:S(2)}, u32[]{:S(2)}) collective-permute-start(bf16[128,2048]{1,0:T(8,128)(2,1)} %get-tuple-element.184), channel_id=1, source_target_pairs={{8,0},{16,8},{24,16},{28,24},{20,28},{12,20},{4,12},{0,4},{9,1},{1... | collective-permute-start | bytes 1572872 | tf_op jit(solution)/shard_map/ppermute | solution.py:148
  (140 other events, 1257.2 us)
Sparse Core Ops, SparseCore 0:
  40.6 53.4 all-gather.9
  95.6 88.9 all-gather.13
  186.2 43.5 all-gather.11
  235.9 74.3 all-gather.7
  342.7 90.3 reduce-scatter.6
  444.8 54.7 reduce-scatter.8
  502.3 54.8 reduce-scatter.10
  559.7 42.9 reduce-scatter.12
  605.4 24.8 reduce-scatter.14
  632.6 36.3 reduce-scatter.16

commit v18 on v17

--- a/solution.py
+++ b/solution.py
@@ -557,10 +557,10 @@
     )
     sum_shared_out = sum_rows(grad_shared_out)
     sum_out_weight = sum_rows(grad_out_weight)
-    output = own_residual + ring_scatter(out_parts, ctx_size, ctx_index)
-    output = output.astype(bf16).reshape(tokens.shape)
     pieces = pieces.reshape(ctx_size, shard + more, 3 * own_width)
     pieces = lax.all_to_all(pieces, "ctx", split_axis=0, concat_axis=0, tiled=True)
+    out_sum, pieces = ring_scatter(out_parts, ctx_size, ctx_index, riders=(pieces,))
+    output = (own_residual + out_sum).astype(bf16).reshape(tokens.shape)
     grad_inputs_norm, unused = rms_back(
         own_tokens,
         inv_one,

time: 709 us -> 708 us (level)
  transfers between devices with their start and end apart: 76 -> 76, of which waited for: 41 -> 42; matrix products, arithmetic and copies ran while one was open for 44% -> 44% of each run, Pallas kernels for 1% -> 1%
where the time goes in v18:
time: 708 us; the launch traced here: 696 us
  waiting for transfers between devices  195 us (28%)
  matrix products  143 us (20%)
  local copies, waits for them, and re-layouts  113 us (16%)
  other arithmetic  97.7 us (14%)
  starting transfers between devices  86.4 us (12%)
  blocking collectives  29.7 us (4%)
  between operations  21 us (3%)
  Pallas kernels  9.58 us (1%)
    ppermute x12, waiting for transfers between devices, ring_sums(): fore = lax.ppermute(fore, 'ctx', ahead)  69.2 us
    ppermute x9, waiting for transfers between devices, ring_gather(): fore = lax.ppermute(fore, 'ctx', ahead)  49.5 us
    dot_general x7, matrix products, dot_t(): lax.dot_general(a, b, (((1,), (1,)), ((), ())), preferred_element_type=f32)  45.3 us
    dot_general x8, matrix products, dot(): return jnp.dot(a, b, preferred_element_type=f32)  44.1 us
    dot_general x8, matrix products, t_dot(): lax.dot_general(a, b, (((0,), (0,)), ((), ())), preferred_element_type=f32)  39.3 us
    all_to_all x1, blocking collectives, local_split(): lax.all_to_all(pieces, 'ctx', split_axis=0, concat_axis=0, tiled=True)  29.7 us
    unnamed x198, local copies, waits for them, and re-layouts  22.8 us
    dynamic_update_slice x25, local copies, waits for them, and re-layouts, put(): lax.dynamic_update_slice(out, piece, (peer * rows + offset, jnp.zeros_lik...  20.7 us
  transfers between devices with their start and end apart: 76, of which 42 were waited for; matrix products, arithmetic and copies ran while one was open for 44% of the time, Pallas kernels for 1%

profile of v18, /device:TPU:8, one launch (start us, length us, event | category | flops | bytes accessed | tf_op | source)
XLA Modules:
  0.0 695.8 jit_solution(13960541887612708776)
XLA Ops:
  10.7 29.7 %all_to_all.25 = bf16[8,80,768]{2,1,0:T(8,128)(2,1)} all-to-all(bf16[8,80,768]{2,1,0:T(8,128)(2,1)S(1)} %pad_maximum_fusion.6), channel_id=1, replica_groups=mesh['ctx'=8,'fsdp'=4] {'ctx'}, dimensions={0} | all-to-all | bytes 1966080 | tf_op jit(solution)/shard_map/all_to_all | solution.py:333
  72.0 7.1 %collective-permute-done.4 = bf16[128,2048]{1,0:T(8,128)(2,1)S(1)} collective-permute-done((bf16[128,2048]{1,0:T(8,128)(2,1)}, bf16[128,2048]{1,0:T(8,128)(2,1)S(1)}, u32[]{:S(2)}, u32[]{:S(2)}) %collective-permute-start.4) | collective-permute-done | bytes 524320 | tf_op jit(solution)/shard_map/ppermute | solution.py:110
  83.6 7.4 %collective-permute-done.6 = bf16[128,2048]{1,0:T(8,128)(2,1)S(1)} collective-permute-done((bf16[128,2048]{1,0:T(8,128)(2,1)S(1)}, bf16[128,2048]{1,0:T(8,128)(2,1)S(1)}, u32[]{:S(2)}, u32[]{:S(2)}) %collective-permute-start.6) | collective-permute-done | bytes 524320 | tf_op jit(solution)/shard_map/ppermute | solution.py:110
  115.5 6.4 fusion.24
  148.4 6.7 collective-permute-done.12
  179.9 7.2 %collective-permute-done.14 = bf16[128,2048]{1,0:T(8,128)(2,1)} collective-permute-done((bf16[128,2048]{1,0:T(8,128)(2,1)}, bf16[128,2048]{1,0:T(8,128)(2,1)}, u32[]{:S(2)}, u32[]{:S(2)}) %collective-permute-start.14) | collective-permute-done | bytes 524320 | tf_op jit(solution)/shard_map/ppermute | solution.py:147
  237.5 6.3 collective-permute-done.24
  247.6 11.7 %collective-permute-done.26 = bf16[64,2048]{1,0:T(8,128)(2,1)S(1)} collective-permute-done((bf16[64,2048]{1,0:T(8,128)(2,1)S(1)}, bf16[64,2048]{1,0:T(8,128)(2,1)S(1)}, u32[]{:S(2)}, u32[]{:S(2)}) %collective-permute-start.26) | collective-permute-done | bytes 262176 | tf_op jit(solution)/shard_map/ppermute | solution.py:116
  271.1 10.3 %fusion.2 = f32[512,2816]{1,0:T(8,128)S(1)} fusion(bf16[512,2048]{1,0:T(8,128)(2,1)S(1)} %bitcast.387, bf16[1,2048,2816]{2,1,0:T(8,128)(2,1)} %all-gather.14.cloned.1.call-done), kind=kOutput, calls=%fused_computation.2 | convolution fusion | flops 5905580032 | bytes 19398656 | tf_op jit(solution)/shard_map/dot_general | solution.py:308
  285.8 6.2 convolution_convert_fusion.6
  297.8 8.5 %fusion.104 = f32[1024,1408]{1,0:T(8,128)S(1)} fusion(bf16[1024,2048]{1,0:T(8,128)(2,1)} %constant_dynamic-update-slice_fusion.4, bf16[2048,1408]{1,0:T(8,128)(2,1)S(1)} %bitcast.357), kind=kOutput, calls=%fused_computation.315 | convolution fusion | flops 5905580032 | bytes 15728640 | tf_op jit(solution)/shard_map/dot_general | solution.py:308
  310.8 5.8 fusion.8
  324.6 7.4 %multiply_convert_fusion.6 = (bf16[512,1408]{1,0:T(8,128)(2,1)S(1)}, bf16[512,1408]{1,0:T(8,128)(2,1)S(1)}, f32[512]{0:T(512)S(1)}) fusion(f32[512,2816]{1,0:T(8,128)S(1)} %bitcast.362, bf16[512,1408]{1,0:T(8,128)(2,1)S(1)} %copy-done.43, bf16[512,2048]{1,0:T(8,128)(2,1)S(1)} %bitcast.389, bf16[1408,2048]{1,0:T(8,128)(2,1)} %bitcast.364), kind=kOutput, calls=%fused_computation.51 | convolution fusion | flops 2964323840 | bytes 17958912 | tf_op jit(solution)/shard_map/dot_general | solution.py:311
  333.2 9.4 %convolution_convert_fusion = bf16[2048,2816]{1,0:T(8,128)(2,1)} fusion(bf16[512,2048]{1,0:T(8,128)(2,1)S(1)} %bitcast.388, bf16[512,1408]{1,0:T(8,128)(2,1)S(1)} %get-tuple-element.184, bf16[512,1408]{1,0:T(8,128)(2,1)S(1)} %get-tuple-element.183), kind=kOutput, calls=%fused_computation.4 | convolution fusion | flops 5917114368 | bytes 16515072 | tf_op jit(solution)/shard_map/dot_general | solution.py:314
  342.9 11.8 %multiply_convert_fusion.3 = (bf16[1024,704]{1,0:T(8,128)(2,1)S(1)}, bf16[1024,704]{1,0:T(8,128)(2,1)}, f32[1024]{0:T(1024)S(1)}) fusion(f32[1024,1408]{1,0:T(8,128)} %copy-done.16, bf16[1024,704]{1,0:T(8,128)(2,1)} %copy-done.40, bf16[1024,2048]{1,0:T(8,128)(2,1)} %multiply_convert_fusion, bf16[704,2048]{1,0:T(8,128)(2,1)} %bitcast.382), kind=kOutput, calls=%fused_computation.36 | convolution fusion | flops 2964323328 | bytes 17174528 | tf_op jit(solution)/shard_map/dot_general | solution.py:311
  363.2 9.1 %fusion.20 = bf16[512,2048]{1,0:T(8,128)(2,1)S(1)} fusion(bf16[1,2048,2816]{2,1,0:T(8,128)(2,1)} %all-gather.14.cloned.1.call-done, bf16[512,1408]{1,0:T(8,128)(2,1)S(1)} %copy-done.90, bf16[512,1408]{1,0:T(8,128)(2,1)S(1)} %copy-done.88), kind=kOutput, calls=%fused_computation.39 | convolution fusion | flops 5912395776 | bytes 16515072 | tf_op jit(solution)/shard_map/dot_general | solution.py:311
  373.6 8.4 %fusion.6 = bf16[1024,2048]{1,0:T(8,128)(2,1)S(1)} fusion(f32[8,128,2048]{2,1,0:T(8,128)S(1)} %fusion.55, bf16[1024,1408]{1,0:T(8,128)(2,1)} %pad_maximum_fusion.2, bf16[2048,1408]{1,0:T(8,128)(2,1)S(1)} %bitcast.360), kind=kOutput, calls=%fused_computation.10 | convolution fusion | flops 5909774336 | bytes 21233664 | tf_op jit(solution)/shard_map/dot_general | solution.py:311
  384.2 11.7 %convolution_convert_fusion.2 = bf16[2048,1408]{1,0:T(8,128)(2,1)} fusion(bf16[1024,2048]{1,0:T(8,128)(2,1)} %constant_dynamic-update-slice_fusion.4, bf16[1024,1408]{1,0:T(8,128)(2,1)} %pad_maximum_fusion.2), kind=kOutput, calls=%fused_computation.19 | convolution fusion | flops 5908463616 | bytes 12845056 | tf_op jit(solution)/shard_map/dot_general | solution.py:314
  415.0 7.6 %collective-permute-done.32 = bf16[128,2048]{1,0:T(8,128)(2,1)S(1)} collective-permute-done((bf16[128,2048]{1,0:T(8,128)(2,1)S(1)}, bf16[128,2048]{1,0:T(8,128)(2,1)S(1)}, u32[]{:S(2)}, u32[]{:S(2)}) %collective-permute-start.32) | collective-permute-done | bytes 524320 | tf_op jit(solution)/shard_map/ppermute | solution.py:147
  454.5 9.6 %collective-permute-done.38 = bf16[128,2048]{1,0:T(8,128)(2,1)} collective-permute-done((bf16[128,2048]{1,0:T(8,128)(2,1)}, bf16[128,2048]{1,0:T(8,128)(2,1)}, u32[]{:S(2)}, u32[]{:S(2)}) %collective-permute-start.38) | collective-permute-done | bytes 524320 | tf_op jit(solution)/shard_map/ppermute | solution.py:110
  469.6 5.9 collective-permute-done.40
  499.6 6.1 all-to-all-start.3
  505.6 9.6 %shard_map.309 = (f32[1024,256]{1,0:T(8,128)S(1)}, f32[1024,256]{1,0:T(8,128)S(1)}, f32[1024,256]{1,0:T(8,128)S(1)}) custom-call(bf16[1024,256]{1,0:T(8,128)(2,1)S(1)} %copy_bitcast_fusion.4.q_ref, bf16[1024,256]{1,0:T(8,128)(2,1)S(1)} %get-tuple-element.228.k_ref, bf16[1024,256]{1,0:T(8,128)(2,1)S(1)} %slice.583.v_ref, ...), custom_call_target="tpu_custom_call" | custom-call | flops 2684354560 | bytes 5242880 | tf_op jit(solution)/shard_map/pallas_call | solution.py:253
  518.6 7.0 %fusion.5 = (bf16[2048]{0:T(1024)(128)(2,1)S(1)}, bf16[1024,2048]{1,0:T(8,128)(2,1)}) fusion(bf16[1024,2048]{1,0:T(8,128)(2,1)} %constant_dynamic-update-slice_fusion.18, bf16[2048,768]{1,0:T(8,128)(2,1)S(1)} %bitcast.377, bf16[1024,256]{1,0:T(8,128)(2,1)S(1)} %convert.63, bf16[1024,256]{1,0:T(8,128)(2,1)S(1)} %get-tuple-element.250, ...), kind=kOutput, calls=%fused_computation.8 | convolution fusion | flops 3234330624 | bytes 13111296 | tf_op jit(solution)/shard_map/dot_general | solution.py:311
  525.8 11.1 %all-to-all-done.3 = bf16[8,64,1408]{2,1,0:T(8,128)(2,1)} async-done(((bf16[8,64,1408]{2,1,0:T(8,128)(2,1)}), bf16[8,64,1408]{2,1,0:T(8,128)(2,1)}, u32[]{:S(2)}, u32[]{:S(2)}) %all-to-all-start.3) | async-done | bytes 1441824 | tf_op jit(solution)/shard_map/all_to_all | solution.py:505
  537.7 5.8 fusion.17
  561.0 10.9 %collective-permute-done.47 = bf16[128,2048]{1,0:T(8,128)(2,1)S(1)} collective-permute-done((bf16[128,2048]{1,0:T(8,128)(2,1)S(1)}, bf16[128,2048]{1,0:T(8,128)(2,1)S(1)}, u32[]{:S(2)}, u32[]{:S(2)}) %collective-permute-start.47) | collective-permute-done | bytes 524320 | tf_op jit(solution)/shard_map/ppermute | solution.py:147
  576.7 9.5 %collective-permute-done.48 = bf16[128,2048]{1,0:T(8,128)(2,1)S(1)} collective-permute-done((bf16[128,2048]{1,0:T(8,128)(2,1)S(1)}, bf16[128,2048]{1,0:T(8,128)(2,1)S(1)}, u32[]{:S(2)}, u32[]{:S(2)}) %collective-permute-start.48) | collective-permute-done | bytes 524320 | tf_op jit(solution)/shard_map/ppermute | solution.py:147
  593.1 6.2 collective-permute-done.49
  606.6 6.1 all-to-all-start.4
  628.1 16.1 %collective-permute-done.55 = bf16[128,2048]{1,0:T(8,128)(2,1)} collective-permute-done((bf16[128,2048]{1,0:T(8,128)(2,1)}, bf16[128,2048]{1,0:T(8,128)(2,1)}, u32[]{:S(2)}, u32[]{:S(2)}) %collective-permute-start.55) | collective-permute-done | bytes 524320 | tf_op jit(solution)/shard_map/ppermute | solution.py:147
  654.2 6.5 collective-permute-done.56
  (577 shorter events, 386.0 us)
Async XLA Ops:
  7.2 97.5 %all-gather.10.cloned.1.call-start = ((), (), s32[]{:S(2)}) async-start(), calls=%async_computation.18 | async-start | bytes 4915200 | tf_op jit(solution)/shard_map/all_gather | solution.py:337
  40.5 230.6 %all-gather.14.cloned.1.call-start = ((), (), s32[]{:S(2)}) async-start(), calls=%async_computation.20 | async-start | bytes 14417920 | tf_op jit(solution)/shard_map/all_gather | solution.py:352
  45.2 21.6 %collective-permute-start.2 = (bf16[128,2048]{1,0:T(8,128)(2,1)}, bf16[128,2048]{1,0:T(8,128)(2,1)}, u32[]{:S(2)}, u32[]{:S(2)}) collective-permute-start(bf16[128,2048]{1,0:T(8,128)(2,1)} %get-tuple-element.282), channel_id=1, source_target_pairs={{0,8},{8,16},{16,24},{24,28},{28,20},{20,12},{12,4},{4,0},{1,9},{9... | collective-permute-start | bytes 1572872 | tf_op jit(solution)/shard_map/ppermute | solution.py:110
  45.7 21.7 %collective-permute-start.3 = (bf16[128,2048]{1,0:T(8,128)(2,1)}, bf16[128,2048]{1,0:T(8,128)(2,1)S(1)}, u32[]{:S(2)}, u32[]{:S(2)}) collective-permute-start(bf16[128,2048]{1,0:T(8,128)(2,1)} %get-tuple-element.282), channel_id=1, source_target_pairs={{8,0},{16,8},{24,16},{28,24},{20,28},{12,20},{4,12},{0,4},{9,1},{1... | collective-permute-start | bytes 1572872 | tf_op jit(solution)/shard_map/ppermute | solution.py:111
  47.2 79.3 %collective-permute-start.10 = (bf16[64,2048]{1,0:T(8,128)(2,1)S(1)}, bf16[64,2048]{1,0:T(8,128)(2,1)}, u32[]{:S(2)}, u32[]{:S(2)}) collective-permute-start(bf16[64,2048]{1,0:T(8,128)(2,1)S(1)} %copy-done.48), channel_id=1, source_target_pairs={{0,2},{1,3},{2,0},{3,1},{4,6},{5,7},{6,4},{7,5},{8,10},{9,11},{10,... | collective-permute-start | bytes 786440 | tf_op jit(solution)/shard_map/ppermute | solution.py:176
  48.7 89.5 %collective-permute-start.1 = (bf16[176,2048]{1,0:T(8,128)(2,1)}, bf16[176,2048]{1,0:T(8,128)(2,1)}, u32[]{:S(2)}, u32[]{:S(2)}) collective-permute-start(bf16[176,2048]{1,0:T(8,128)(2,1)} %param.34), channel_id=1, source_target_pairs={{0,2},{1,3},{2,0},{3,1},{4,6},{5,7},{6,4},{7,5},{8,10},{9,11},{10,... | collective-permute-start | bytes 2162696 | tf_op jit(solution)/shard_map/ppermute | solution.py:176
  49.2 89.0 %collective-permute-start = (bf16[352,2048]{1,0:T(8,128)(2,1)}, bf16[352,2048]{1,0:T(8,128)(2,1)}, u32[]{:S(2)}, u32[]{:S(2)}) collective-permute-start(bf16[352,2048]{1,0:T(8,128)(2,1)} %bitcast.1), channel_id=1, source_target_pairs={{0,2},{1,3},{2,0},{3,1},{4,6},{5,7},{6,4},{7,5},{8,10},{9,11},{10,... | collective-permute-start | bytes 4325384 | tf_op jit(solution)/shard_map/ppermute | solution.py:176
  98.9 46.0 %all-to-all-start.1 = ((bf16[8,64,1408]{2,1,0:T(8,128)(2,1)}), bf16[8,64,1408]{2,1,0:T(8,128)(2,1)}, u32[]{:S(2)}, u32[]{:S(2)}) async-start(bf16[8,64,1408]{2,1,0:T(8,128)(2,1)} %reshape.884), calls=%async_computation.1 | async-start | bytes 2883584 | tf_op jit(solution)/shard_map/all_to_all | solution.py:336
  104.5 187.6 %all-gather.12.cloned.1.call-start = ((), (), s32[]{:S(2)}) async-start(), calls=%async_computation.19 | async-start | bytes 7208960 | tf_op jit(solution)/shard_map/all_gather | solution.py:389
  145.0 171.7 %all-gather.8.cloned.1.call-start = ((), (), s32[]{:S(2)}) async-start(), calls=%async_computation.11 | async-start | bytes 4718592 | tf_op jit(solution)/shard_map/all_gather | solution.py:397
  157.5 13.5 %collective-permute-start.17 = (bf16[128,2048]{1,0:T(8,128)(2,1)S(1)}, bf16[128,2048]{1,0:T(8,128)(2,1)}, u32[]{:S(2)}, u32[]{:S(2)}) collective-permute-start(bf16[128,2048]{1,0:T(8,128)(2,1)S(1)} %pad_maximum_fusion.10), channel_id=1, source_target_pairs={{8,0},{16,8},{24,16},{28,24},{20,28},{12,20},{4,12},{0,4},{9,1},{1... | collective-permute-start | bytes 1572872 | tf_op jit(solution)/shard_map/ppermute | solution.py:148
  158.1 13.7 %collective-permute-start.13 = (bf16[128,2048]{1,0:T(8,128)(2,1)S(1)}, bf16[128,2048]{1,0:T(8,128)(2,1)S(1)}, u32[]{:S(2)}, u32[]{:S(2)}) collective-permute-start(bf16[128,2048]{1,0:T(8,128)(2,1)S(1)} %pad_maximum_fusion.9), channel_id=1, source_target_pairs={{0,8},{8,16},{16,24},{24,28},{28,20},{20,12},{12,4},{4,0},{1,9},{9... | collective-permute-start | bytes 1572872 | tf_op jit(solution)/shard_map/ppermute | solution.py:147
  164.7 56.9 %collective-permute-start.28 = (bf16[2,352,2048]{2,1,0:T(8,128)(2,1)}, bf16[2,352,2048]{2,1,0:T(8,128)(2,1)}, u32[]{:S(2)}, u32[]{:S(2)}) collective-permute-start(bf16[2,352,2048]{2,1,0:T(8,128)(2,1)} %maximum_select_fusion.1), channel_id=1, source_target_pairs={{0,1},{1,0},{2,3},{3,2},{4,5},{5,4},{6,7},{7,6},{8,9},{9,8},{10,11... | collective-permute-start | bytes 8650760 | tf_op jit(solution)/shard_map/ppermute | solution.py:181
  179.8 32.4 %collective-permute-start.29 = (bf16[2,176,2048]{2,1,0:T(8,128)(2,1)S(1)}, bf16[2,176,2048]{2,1,0:T(8,128)(2,1)}, u32[]{:S(2)}, u32[]{:S(2)}) collective-permute-start(bf16[2,176,2048]{2,1,0:T(8,128)(2,1)S(1)} %maximum_select_fusion.3), channel_id=1, source_target_pairs={{0,1},{1,0},{2,3},{3,2},{4,5},{5,4},{6,7},{7,6},{8,9},{9,8},{10,11... | collective-permute-start | bytes 4325384 | tf_op jit(solution)/shard_map/ppermute | solution.py:181
  235.8 215.9 %reduce-scatter.7.cloned.1.call-start = ((), (), s32[]{:S(2)}) async-start(), calls=%async_computation.12 | async-start | bytes 14417920 | tf_op jit(solution)/shard_map/reduce_scatter | solution.py:322
  243.8 15.6 %collective-permute-start.26 = (bf16[64,2048]{1,0:T(8,128)(2,1)S(1)}, bf16[64,2048]{1,0:T(8,128)(2,1)S(1)}, u32[]{:S(2)}, u32[]{:S(2)}) collective-permute-start(bf16[64,2048]{1,0:T(8,128)(2,1)S(1)} %slice.499), channel_id=1, source_target_pairs={{0,8},{8,16},{16,24},{24,28},{28,20},{20,12},{12,4},{4,0},{1,9},{9... | collective-permute-start | bytes 786440 | tf_op jit(solution)/shard_map/ppermute | solution.py:116
  245.3 17.8 %collective-permute-start.27 = (bf16[64,2048]{1,0:T(8,128)(2,1)S(1)}, bf16[64,2048]{1,0:T(8,128)(2,1)S(1)}, u32[]{:S(2)}, u32[]{:S(2)}) collective-permute-start(bf16[64,2048]{1,0:T(8,128)(2,1)S(1)} %slice.500), channel_id=1, source_target_pairs={{8,0},{16,8},{24,16},{28,24},{20,28},{12,20},{4,12},{0,4},{9,1},{1... | collective-permute-start | bytes 786440 | tf_op jit(solution)/shard_map/ppermute | solution.py:117
  355.3 83.7 %all-to-all-start.2 = ((f32[8,2,128]{2,1,0:T(2,128)}), f32[8,2,128]{2,1,0:T(2,128)S(1)}, u32[]{:S(2)}, u32[]{:S(2)}) async-start(f32[8,2,128]{2,1,0:T(2,128)} %pad_maximum_fusion.17), calls=%async_computation.2 | async-start | bytes 16384 | tf_op jit(solution)/shard_map/all_to_all | solution.py:469
  359.1 140.5 %reduce-scatter.9.cloned.1.call-start = ((), (), s32[]{:S(2)}) async-start(), calls=%async_computation.13 | async-start | bytes 7208960 | tf_op jit(solution)/shard_map/reduce_scatter | solution.py:474
  382.1 13.7 %collective-permute-start.30 = (bf16[64,2048]{1,0:T(8,128)(2,1)S(1)}, bf16[64,2048]{1,0:T(8,128)(2,1)S(1)}, u32[]{:S(2)}, u32[]{:S(2)}) collective-permute-start(bf16[64,2048]{1,0:T(8,128)(2,1)S(1)} %get-tuple-element.213), channel_id=1, source_target_pairs={{0,8},{8,16},{16,24},{24,28},{28,20},{20,12},{12,4},{4,0},{1,9},{9... | collective-permute-start | bytes 786440 | tf_op jit(solution)/shard_map/ppermute | solution.py:138
  444.8 116.1 %reduce-scatter.11.cloned.1.call-start = ((), (), s32[]{:S(2)}) async-start(), calls=%async_computation.14 | async-start | bytes 7208960 | tf_op jit(solution)/shard_map/reduce_scatter | solution.py:322
  499.6 37.3 %all-to-all-start.3 = ((bf16[8,64,1408]{2,1,0:T(8,128)(2,1)}), bf16[8,64,1408]{2,1,0:T(8,128)(2,1)}, u32[]{:S(2)}, u32[]{:S(2)}) async-start(bf16[8,64,1408]{2,1,0:T(8,128)(2,1)} %bitcast.391), calls=%async_computation.5 | async-start | bytes 2883584 | tf_op jit(solution)/shard_map/all_to_all | solution.py:505
  505.6 97.0 %reduce-scatter.13.cloned.1.call-start = ((), (), s32[]{:S(2)}) async-start(), calls=%async_computation.15 | async-start | bytes 4915200 | tf_op jit(solution)/shard_map/reduce_scatter | solution.py:554
  546.0 134.8 %reduce-scatter.15.cloned.1.call-start = ((), (), s32[]{:S(2)}) async-start(), calls=%async_computation.16 | async-start | bytes 1310720 | tf_op jit(solution)/shard_map/reduce_scatter | solution.py:322
  558.8 13.1 %collective-permute-start.47 = (bf16[128,2048]{1,0:T(8,128)(2,1)S(1)}, bf16[128,2048]{1,0:T(8,128)(2,1)S(1)}, u32[]{:S(2)}, u32[]{:S(2)}) collective-permute-start(bf16[128,2048]{1,0:T(8,128)(2,1)S(1)} %pad_maximum_fusion.13), channel_id=1, source_target_pairs={{0,8},{8,16},{16,24},{24,28},{28,20},{20,12},{12,4},{4,0},{1,9},{9... | collective-permute-start | bytes 1572872 | tf_op jit(solution)/shard_map/ppermute | solution.py:147
  602.7 83.7 %reduce-scatter.17.cloned.1.call-start = ((), (), s32[]{:S(2)}) async-start(), calls=%async_computation.17 | async-start | bytes 3604480 | tf_op jit(solution)/shard_map/reduce_scatter | solution.py:322
  606.6 37.5 %all-to-all-start.4 = ((bf16[8,80,768]{2,1,0:T(8,128)(2,1)}), bf16[8,80,768]{2,1,0:T(8,128)(2,1)}, u32[]{:S(2)}, u32[]{:S(2)}) async-start(bf16[8,80,768]{2,1,0:T(8,128)(2,1)} %bitcast.86), calls=%async_computation.8 | async-start | bytes 1966080 | tf_op jit(solution)/shard_map/all_to_all | solution.py:561
  615.1 31.5 %collective-permute-start.59 = (bf16[128,2048]{1,0:T(8,128)(2,1)S(1)}, bf16[128,2048]{1,0:T(8,128)(2,1)}, u32[]{:S(2)}, u32[]{:S(2)}) collective-permute-start(bf16[128,2048]{1,0:T(8,128)(2,1)S(1)} %pad_maximum_fusion.16), channel_id=1, source_target_pairs={{8,0},{16,8},{24,16},{28,24},{20,28},{12,20},{4,12},{0,4},{9,1},{1... | collective-permute-start | bytes 1572872 | tf_op jit(solution)/shard_map/ppermute | solution.py:148
  616.5 27.7 %collective-permute-start.55 = (bf16[128,2048]{1,0:T(8,128)(2,1)}, bf16[128,2048]{1,0:T(8,128)(2,1)}, u32[]{:S(2)}, u32[]{:S(2)}) collective-permute-start(bf16[128,2048]{1,0:T(8,128)(2,1)} %pad_maximum_fusion.15), channel_id=1, source_target_pairs={{0,8},{8,16},{16,24},{24,28},{28,20},{20,12},{12,4},{4,0},{1,9},{9... | collective-permute-start | bytes 1572872 | tf_op jit(solution)/shard_map/ppermute | solution.py:147
  648.6 12.9 %collective-permute-start.60 = (bf16[128,2048]{1,0:T(8,128)(2,1)S(1)}, bf16[128,2048]{1,0:T(8,128)(2,1)S(1)}, u32[]{:S(2)}, u32[]{:S(2)}) collective-permute-start(bf16[128,2048]{1,0:T(8,128)(2,1)S(1)} %get-tuple-element.190), channel_id=1, source_target_pairs={{8,0},{16,8},{24,16},{28,24},{20,28},{12,20},{4,12},{0,4},{9,1},{1... | collective-permute-start | bytes 1572872 | tf_op jit(solution)/shard_map/ppermute | solution.py:148
  664.0 18.5 %collective-permute-start.57 = (bf16[128,2048]{1,0:T(8,128)(2,1)}, bf16[128,2048]{1,0:T(8,128)(2,1)}, u32[]{:S(2)}, u32[]{:S(2)}) collective-permute-start(bf16[128,2048]{1,0:T(8,128)(2,1)} %get-tuple-element.187), channel_id=1, source_target_pairs={{0,8},{8,16},{16,24},{24,28},{28,20},{20,12},{12,4},{4,0},{1,9},{9... | collective-permute-start | bytes 1572872 | tf_op jit(solution)/shard_map/ppermute | solution.py:147
  664.4 18.2 %collective-permute-start.61 = (bf16[128,2048]{1,0:T(8,128)(2,1)}, bf16[128,2048]{1,0:T(8,128)(2,1)}, u32[]{:S(2)}, u32[]{:S(2)}) collective-permute-start(bf16[128,2048]{1,0:T(8,128)(2,1)} %get-tuple-element.188), channel_id=1, source_target_pairs={{8,0},{16,8},{24,16},{28,24},{20,28},{12,20},{4,12},{0,4},{9,1},{1... | collective-permute-start | bytes 1572872 | tf_op jit(solution)/shard_map/ppermute | solution.py:148
  (140 other events, 1273.9 us)
Sparse Core Ops, SparseCore 0:
  40.6 53.4 all-gather.9
  95.6 88.9 all-gather.13
  186.2 43.5 all-gather.11
  235.9 74.3 all-gather.7
  342.7 90.3 reduce-scatter.6
  444.8 54.7 reduce-scatter.8
  502.3 54.8 reduce-scatter.10
  559.7 42.9 reduce-scatter.12
  605.4 24.8 reduce-scatter.14
  632.6 36.3 reduce-scatter.16

commit v19 on v18

--- a/solution.py
+++ b/solution.py
@@ -527,8 +527,8 @@
     one_parts, sum_shared_in = after(one_sums.astype(bf16), sum_shared_in)
     one_kept, grad_projected = after(one_parts, grad_projected)
     one_kept, attn_own = after(one_kept, attn_own)
-    grad_normed, sum_expert_out = ring_scatter(
-        one_parts, ctx_size, ctx_index, one_kept, (sum_expert_out,)
+    grad_normed, sum_expert_out, out_parts = ring_scatter(
+        one_parts, ctx_size, ctx_index, one_kept, (sum_expert_out, out_parts)
     )
     grad_qkv_weight = t_dot(normed_low, grad_projected)
     grad_bias = jnp.sum(grad_projected.astype(f32), axis=0).reshape(3, 1, own_width)
@@ -552,8 +552,8 @@
     )
     pieces = pieces.transpose(1, 0, 2, 3).reshape(-1, 3 * own_width)
     pieces = lax.psum_scatter(pieces, "fsdp", scatter_dimension=0, tiled=True)
-    grad_normed, pieces, out_parts, grad_shared_out, grad_out_weight = after(
-        grad_normed, pieces, out_parts, grad_shared_out, grad_out_weight.astype(bf16)
+    grad_normed, pieces, grad_shared_out, grad_out_weight = after(
+        grad_normed, pieces, grad_shared_out, grad_out_weight.astype(bf16)
     )
     sum_shared_out = sum_rows(grad_shared_out)
     sum_out_weight = sum_rows(grad_out_weight)

time: 708 us -> 708 us (level)
  no operation moved by 1% of the time
where the time goes in v19:
time: 708 us; the launch traced here: 696 us
  waiting for transfers between devices  195 us (28%)
  matrix products  143 us (20%)
  local copies, waits for them, and re-layouts  113 us (16%)
  other arithmetic  97.7 us (14%)
  starting transfers between devices  86.4 us (12%)
  blocking collectives  29.7 us (4%)
  between operations  21 us (3%)
  Pallas kernels  9.58 us (1%)
    ppermute x12, waiting for transfers between devices, ring_sums(): fore = lax.ppermute(fore, 'ctx', ahead)  69.2 us
    ppermute x9, waiting for transfers between devices, ring_gather(): fore = lax.ppermute(fore, 'ctx', ahead)  49.5 us
    dot_general x7, matrix products, dot_t(): lax.dot_general(a, b, (((1,), (1,)), ((), ())), preferred_element_type=f32)  45.3 us
    dot_general x8, matrix products, dot(): return jnp.dot(a, b, preferred_element_type=f32)  44.1 us
    dot_general x8, matrix products, t_dot(): lax.dot_general(a, b, (((0,), (0,)), ((), ())), preferred_element_type=f32)  39.3 us
    all_to_all x1, blocking collectives, local_split(): lax.all_to_all(pieces, 'ctx', split_axis=0, concat_axis=0, tiled=True)  29.7 us
    unnamed x198, local copies, waits for them, and re-layouts  22.8 us
    dynamic_update_slice x25, local copies, waits for them, and re-layouts, put(): lax.dynamic_update_slice(out, piece, (peer * rows + offset, jnp.zeros_lik...  20.7 us
  transfers between devices with their start and end apart: 76, of which 42 were waited for; matrix products, arithmetic and copies ran while one was open for 44% of the time, Pallas kernels for 1%

profile of v19, /device:TPU:8, one launch (start us, length us, event | category | flops | bytes accessed | tf_op | source)
XLA Modules:
  0.0 695.8 jit_solution(10022067515764537021)
XLA Ops:
  10.7 29.7 %all_to_all.25 = bf16[8,80,768]{2,1,0:T(8,128)(2,1)} all-to-all(bf16[8,80,768]{2,1,0:T(8,128)(2,1)S(1)} %pad_maximum_fusion.6), channel_id=1, replica_groups=mesh['ctx'=8,'fsdp'=4] {'ctx'}, dimensions={0} | all-to-all | bytes 1966080 | tf_op jit(solution)/shard_map/all_to_all | solution.py:333
  72.0 7.1 %collective-permute-done.4 = bf16[128,2048]{1,0:T(8,128)(2,1)S(1)} collective-permute-done((bf16[128,2048]{1,0:T(8,128)(2,1)}, bf16[128,2048]{1,0:T(8,128)(2,1)S(1)}, u32[]{:S(2)}, u32[]{:S(2)}) %collective-permute-start.4) | collective-permute-done | bytes 524320 | tf_op jit(solution)/shard_map/ppermute | solution.py:110
  83.6 7.4 %collective-permute-done.6 = bf16[128,2048]{1,0:T(8,128)(2,1)S(1)} collective-permute-done((bf16[128,2048]{1,0:T(8,128)(2,1)S(1)}, bf16[128,2048]{1,0:T(8,128)(2,1)S(1)}, u32[]{:S(2)}, u32[]{:S(2)}) %collective-permute-start.6) | collective-permute-done | bytes 524320 | tf_op jit(solution)/shard_map/ppermute | solution.py:110
  115.5 6.4 fusion.24
  148.4 6.7 collective-permute-done.12
  179.9 7.2 %collective-permute-done.14 = bf16[128,2048]{1,0:T(8,128)(2,1)} collective-permute-done((bf16[128,2048]{1,0:T(8,128)(2,1)}, bf16[128,2048]{1,0:T(8,128)(2,1)}, u32[]{:S(2)}, u32[]{:S(2)}) %collective-permute-start.14) | collective-permute-done | bytes 524320 | tf_op jit(solution)/shard_map/ppermute | solution.py:147
  237.5 6.3 collective-permute-done.24
  247.6 11.7 %collective-permute-done.26 = bf16[64,2048]{1,0:T(8,128)(2,1)S(1)} collective-permute-done((bf16[64,2048]{1,0:T(8,128)(2,1)S(1)}, bf16[64,2048]{1,0:T(8,128)(2,1)S(1)}, u32[]{:S(2)}, u32[]{:S(2)}) %collective-permute-start.26) | collective-permute-done | bytes 262176 | tf_op jit(solution)/shard_map/ppermute | solution.py:116
  271.1 10.3 %fusion.2 = f32[512,2816]{1,0:T(8,128)S(1)} fusion(bf16[512,2048]{1,0:T(8,128)(2,1)S(1)} %bitcast.387, bf16[1,2048,2816]{2,1,0:T(8,128)(2,1)} %all-gather.14.cloned.1.call-done), kind=kOutput, calls=%fused_computation.2 | convolution fusion | flops 5905580032 | bytes 19398656 | tf_op jit(solution)/shard_map/dot_general | solution.py:308
  285.8 6.2 convolution_convert_fusion.6
  297.8 8.5 %fusion.104 = f32[1024,1408]{1,0:T(8,128)S(1)} fusion(bf16[1024,2048]{1,0:T(8,128)(2,1)} %constant_dynamic-update-slice_fusion.4, bf16[2048,1408]{1,0:T(8,128)(2,1)S(1)} %bitcast.357), kind=kOutput, calls=%fused_computation.315 | convolution fusion | flops 5905580032 | bytes 15728640 | tf_op jit(solution)/shard_map/dot_general | solution.py:308
  310.8 5.8 fusion.8
  324.6 7.4 %multiply_convert_fusion.6 = (bf16[512,1408]{1,0:T(8,128)(2,1)S(1)}, bf16[512,1408]{1,0:T(8,128)(2,1)S(1)}, f32[512]{0:T(512)S(1)}) fusion(f32[512,2816]{1,0:T(8,128)S(1)} %bitcast.362, bf16[512,1408]{1,0:T(8,128)(2,1)S(1)} %copy-done.43, bf16[512,2048]{1,0:T(8,128)(2,1)S(1)} %bitcast.389, bf16[1408,2048]{1,0:T(8,128)(2,1)} %bitcast.364), kind=kOutput, calls=%fused_computation.51 | convolution fusion | flops 2964323840 | bytes 17958912 | tf_op jit(solution)/shard_map/dot_general | solution.py:311
  333.2 9.4 %convolution_convert_fusion = bf16[2048,2816]{1,0:T(8,128)(2,1)} fusion(bf16[512,2048]{1,0:T(8,128)(2,1)S(1)} %bitcast.388, bf16[512,1408]{1,0:T(8,128)(2,1)S(1)} %get-tuple-element.184, bf16[512,1408]{1,0:T(8,128)(2,1)S(1)} %get-tuple-element.183), kind=kOutput, calls=%fused_computation.4 | convolution fusion | flops 5917114368 | bytes 16515072 | tf_op jit(solution)/shard_map/dot_general | solution.py:314
  342.9 11.8 %multiply_convert_fusion.3 = (bf16[1024,704]{1,0:T(8,128)(2,1)S(1)}, bf16[1024,704]{1,0:T(8,128)(2,1)}, f32[1024]{0:T(1024)S(1)}) fusion(f32[1024,1408]{1,0:T(8,128)} %copy-done.16, bf16[1024,704]{1,0:T(8,128)(2,1)} %copy-done.40, bf16[1024,2048]{1,0:T(8,128)(2,1)} %multiply_convert_fusion, bf16[704,2048]{1,0:T(8,128)(2,1)} %bitcast.382), kind=kOutput, calls=%fused_computation.36 | convolution fusion | flops 2964323328 | bytes 17174528 | tf_op jit(solution)/shard_map/dot_general | solution.py:311
  363.2 9.1 %fusion.20 = bf16[512,2048]{1,0:T(8,128)(2,1)S(1)} fusion(bf16[1,2048,2816]{2,1,0:T(8,128)(2,1)} %all-gather.14.cloned.1.call-done, bf16[512,1408]{1,0:T(8,128)(2,1)S(1)} %copy-done.90, bf16[512,1408]{1,0:T(8,128)(2,1)S(1)} %copy-done.88), kind=kOutput, calls=%fused_computation.39 | convolution fusion | flops 5912395776 | bytes 16515072 | tf_op jit(solution)/shard_map/dot_general | solution.py:311
  373.6 8.4 %fusion.6 = bf16[1024,2048]{1,0:T(8,128)(2,1)S(1)} fusion(f32[8,128,2048]{2,1,0:T(8,128)S(1)} %fusion.55, bf16[1024,1408]{1,0:T(8,128)(2,1)} %pad_maximum_fusion.2, bf16[2048,1408]{1,0:T(8,128)(2,1)S(1)} %bitcast.360), kind=kOutput, calls=%fused_computation.10 | convolution fusion | flops 5909774336 | bytes 21233664 | tf_op jit(solution)/shard_map/dot_general | solution.py:311
  384.2 11.7 %convolution_convert_fusion.2 = bf16[2048,1408]{1,0:T(8,128)(2,1)} fusion(bf16[1024,2048]{1,0:T(8,128)(2,1)} %constant_dynamic-update-slice_fusion.4, bf16[1024,1408]{1,0:T(8,128)(2,1)} %pad_maximum_fusion.2), kind=kOutput, calls=%fused_computation.19 | convolution fusion | flops 5908463616 | bytes 12845056 | tf_op jit(solution)/shard_map/dot_general | solution.py:314
  415.0 7.6 %collective-permute-done.32 = bf16[128,2048]{1,0:T(8,128)(2,1)S(1)} collective-permute-done((bf16[128,2048]{1,0:T(8,128)(2,1)S(1)}, bf16[128,2048]{1,0:T(8,128)(2,1)S(1)}, u32[]{:S(2)}, u32[]{:S(2)}) %collective-permute-start.32) | collective-permute-done | bytes 524320 | tf_op jit(solution)/shard_map/ppermute | solution.py:147
  454.5 9.6 %collective-permute-done.38 = bf16[128,2048]{1,0:T(8,128)(2,1)} collective-permute-done((bf16[128,2048]{1,0:T(8,128)(2,1)}, bf16[128,2048]{1,0:T(8,128)(2,1)}, u32[]{:S(2)}, u32[]{:S(2)}) %collective-permute-start.38) | collective-permute-done | bytes 524320 | tf_op jit(solution)/shard_map/ppermute | solution.py:110
  469.6 5.9 collective-permute-done.40
  499.6 6.1 all-to-all-start.3
  505.6 9.6 %shard_map.309 = (f32[1024,256]{1,0:T(8,128)S(1)}, f32[1024,256]{1,0:T(8,128)S(1)}, f32[1024,256]{1,0:T(8,128)S(1)}) custom-call(bf16[1024,256]{1,0:T(8,128)(2,1)S(1)} %copy_bitcast_fusion.4.q_ref, bf16[1024,256]{1,0:T(8,128)(2,1)S(1)} %get-tuple-element.228.k_ref, bf16[1024,256]{1,0:T(8,128)(2,1)S(1)} %slice.583.v_ref, ...), custom_call_target="tpu_custom_call" | custom-call | flops 2684354560 | bytes 5242880 | tf_op jit(solution)/shard_map/pallas_call | solution.py:253
  518.6 7.0 %fusion.5 = (bf16[2048]{0:T(1024)(128)(2,1)S(1)}, bf16[1024,2048]{1,0:T(8,128)(2,1)}) fusion(bf16[1024,2048]{1,0:T(8,128)(2,1)} %constant_dynamic-update-slice_fusion.18, bf16[2048,768]{1,0:T(8,128)(2,1)S(1)} %bitcast.377, bf16[1024,256]{1,0:T(8,128)(2,1)S(1)} %convert.63, bf16[1024,256]{1,0:T(8,128)(2,1)S(1)} %get-tuple-element.250, ...), kind=kOutput, calls=%fused_computation.8 | convolution fusion | flops 3234330624 | bytes 13111296 | tf_op jit(solution)/shard_map/dot_general | solution.py:311
  525.8 11.1 %all-to-all-done.3 = bf16[8,64,1408]{2,1,0:T(8,128)(2,1)} async-done(((bf16[8,64,1408]{2,1,0:T(8,128)(2,1)}), bf16[8,64,1408]{2,1,0:T(8,128)(2,1)}, u32[]{:S(2)}, u32[]{:S(2)}) %all-to-all-start.3) | async-done | bytes 1441824 | tf_op jit(solution)/shard_map/all_to_all | solution.py:505
  537.7 5.8 fusion.17
  561.0 10.9 %collective-permute-done.47 = bf16[128,2048]{1,0:T(8,128)(2,1)S(1)} collective-permute-done((bf16[128,2048]{1,0:T(8,128)(2,1)S(1)}, bf16[128,2048]{1,0:T(8,128)(2,1)S(1)}, u32[]{:S(2)}, u32[]{:S(2)}) %collective-permute-start.47) | collective-permute-done | bytes 524320 | tf_op jit(solution)/shard_map/ppermute | solution.py:147
  576.7 9.5 %collective-permute-done.50 = bf16[128,2048]{1,0:T(8,128)(2,1)S(1)} collective-permute-done((bf16[128,2048]{1,0:T(8,128)(2,1)S(1)}, bf16[128,2048]{1,0:T(8,128)(2,1)S(1)}, u32[]{:S(2)}, u32[]{:S(2)}) %collective-permute-start.50) | collective-permute-done | bytes 524320 | tf_op jit(solution)/shard_map/ppermute | solution.py:147
  593.1 6.2 collective-permute-done.51
  606.6 6.1 all-to-all-start.4
  628.1 16.1 %collective-permute-done.49 = bf16[128,2048]{1,0:T(8,128)(2,1)} collective-permute-done((bf16[128,2048]{1,0:T(8,128)(2,1)}, bf16[128,2048]{1,0:T(8,128)(2,1)}, u32[]{:S(2)}, u32[]{:S(2)}) %collective-permute-start.49) | collective-permute-done | bytes 524320 | tf_op jit(solution)/shard_map/ppermute | solution.py:147
  654.2 6.5 collective-permute-done.56
  (577 shorter events, 386.0 us)
Async XLA Ops:
  7.2 97.5 %all-gather.10.cloned.1.call-start = ((), (), s32[]{:S(2)}) async-start(), calls=%async_computation.18 | async-start | bytes 4915200 | tf_op jit(solution)/shard_map/all_gather | solution.py:337
  40.5 230.6 %all-gather.14.cloned.1.call-start = ((), (), s32[]{:S(2)}) async-start(), calls=%async_computation.20 | async-start | bytes 14417920 | tf_op jit(solution)/shard_map/all_gather | solution.py:352
  45.2 21.6 %collective-permute-start.2 = (bf16[128,2048]{1,0:T(8,128)(2,1)}, bf16[128,2048]{1,0:T(8,128)(2,1)}, u32[]{:S(2)}, u32[]{:S(2)}) collective-permute-start(bf16[128,2048]{1,0:T(8,128)(2,1)} %get-tuple-element.282), channel_id=1, source_target_pairs={{0,8},{8,16},{16,24},{24,28},{28,20},{20,12},{12,4},{4,0},{1,9},{9... | collective-permute-start | bytes 1572872 | tf_op jit(solution)/shard_map/ppermute | solution.py:110
  45.7 21.7 %collective-permute-start.3 = (bf16[128,2048]{1,0:T(8,128)(2,1)}, bf16[128,2048]{1,0:T(8,128)(2,1)S(1)}, u32[]{:S(2)}, u32[]{:S(2)}) collective-permute-start(bf16[128,2048]{1,0:T(8,128)(2,1)} %get-tuple-element.282), channel_id=1, source_target_pairs={{8,0},{16,8},{24,16},{28,24},{20,28},{12,20},{4,12},{0,4},{9,1},{1... | collective-permute-start | bytes 1572872 | tf_op jit(solution)/shard_map/ppermute | solution.py:111
  47.2 79.3 %collective-permute-start.10 = (bf16[64,2048]{1,0:T(8,128)(2,1)S(1)}, bf16[64,2048]{1,0:T(8,128)(2,1)}, u32[]{:S(2)}, u32[]{:S(2)}) collective-permute-start(bf16[64,2048]{1,0:T(8,128)(2,1)S(1)} %copy-done.48), channel_id=1, source_target_pairs={{0,2},{1,3},{2,0},{3,1},{4,6},{5,7},{6,4},{7,5},{8,10},{9,11},{10,... | collective-permute-start | bytes 786440 | tf_op jit(solution)/shard_map/ppermute | solution.py:176
  48.7 89.5 %collective-permute-start.1 = (bf16[176,2048]{1,0:T(8,128)(2,1)}, bf16[176,2048]{1,0:T(8,128)(2,1)}, u32[]{:S(2)}, u32[]{:S(2)}) collective-permute-start(bf16[176,2048]{1,0:T(8,128)(2,1)} %param.34), channel_id=1, source_target_pairs={{0,2},{1,3},{2,0},{3,1},{4,6},{5,7},{6,4},{7,5},{8,10},{9,11},{10,... | collective-permute-start | bytes 2162696 | tf_op jit(solution)/shard_map/ppermute | solution.py:176
  49.2 89.0 %collective-permute-start = (bf16[352,2048]{1,0:T(8,128)(2,1)}, bf16[352,2048]{1,0:T(8,128)(2,1)}, u32[]{:S(2)}, u32[]{:S(2)}) collective-permute-start(bf16[352,2048]{1,0:T(8,128)(2,1)} %bitcast.1), channel_id=1, source_target_pairs={{0,2},{1,3},{2,0},{3,1},{4,6},{5,7},{6,4},{7,5},{8,10},{9,11},{10,... | collective-permute-start | bytes 4325384 | tf_op jit(solution)/shard_map/ppermute | solution.py:176
  98.9 46.0 %all-to-all-start.1 = ((bf16[8,64,1408]{2,1,0:T(8,128)(2,1)}), bf16[8,64,1408]{2,1,0:T(8,128)(2,1)}, u32[]{:S(2)}, u32[]{:S(2)}) async-start(bf16[8,64,1408]{2,1,0:T(8,128)(2,1)} %reshape.884), calls=%async_computation.1 | async-start | bytes 2883584 | tf_op jit(solution)/shard_map/all_to_all | solution.py:336
  104.5 187.6 %all-gather.12.cloned.1.call-start = ((), (), s32[]{:S(2)}) async-start(), calls=%async_computation.19 | async-start | bytes 7208960 | tf_op jit(solution)/shard_map/all_gather | solution.py:389
  145.0 171.7 %all-gather.8.cloned.1.call-start = ((), (), s32[]{:S(2)}) async-start(), calls=%async_computation.11 | async-start | bytes 4718592 | tf_op jit(solution)/shard_map/all_gather | solution.py:397
  157.5 13.5 %collective-permute-start.17 = (bf16[128,2048]{1,0:T(8,128)(2,1)S(1)}, bf16[128,2048]{1,0:T(8,128)(2,1)}, u32[]{:S(2)}, u32[]{:S(2)}) collective-permute-start(bf16[128,2048]{1,0:T(8,128)(2,1)S(1)} %pad_maximum_fusion.10), channel_id=1, source_target_pairs={{8,0},{16,8},{24,16},{28,24},{20,28},{12,20},{4,12},{0,4},{9,1},{1... | collective-permute-start | bytes 1572872 | tf_op jit(solution)/shard_map/ppermute | solution.py:148
  158.1 13.7 %collective-permute-start.13 = (bf16[128,2048]{1,0:T(8,128)(2,1)S(1)}, bf16[128,2048]{1,0:T(8,128)(2,1)S(1)}, u32[]{:S(2)}, u32[]{:S(2)}) collective-permute-start(bf16[128,2048]{1,0:T(8,128)(2,1)S(1)} %pad_maximum_fusion.9), channel_id=1, source_target_pairs={{0,8},{8,16},{16,24},{24,28},{28,20},{20,12},{12,4},{4,0},{1,9},{9... | collective-permute-start | bytes 1572872 | tf_op jit(solution)/shard_map/ppermute | solution.py:147
  164.7 56.9 %collective-permute-start.28 = (bf16[2,352,2048]{2,1,0:T(8,128)(2,1)}, bf16[2,352,2048]{2,1,0:T(8,128)(2,1)}, u32[]{:S(2)}, u32[]{:S(2)}) collective-permute-start(bf16[2,352,2048]{2,1,0:T(8,128)(2,1)} %maximum_select_fusion.1), channel_id=1, source_target_pairs={{0,1},{1,0},{2,3},{3,2},{4,5},{5,4},{6,7},{7,6},{8,9},{9,8},{10,11... | collective-permute-start | bytes 8650760 | tf_op jit(solution)/shard_map/ppermute | solution.py:181
  179.8 32.4 %collective-permute-start.29 = (bf16[2,176,2048]{2,1,0:T(8,128)(2,1)S(1)}, bf16[2,176,2048]{2,1,0:T(8,128)(2,1)}, u32[]{:S(2)}, u32[]{:S(2)}) collective-permute-start(bf16[2,176,2048]{2,1,0:T(8,128)(2,1)S(1)} %maximum_select_fusion.3), channel_id=1, source_target_pairs={{0,1},{1,0},{2,3},{3,2},{4,5},{5,4},{6,7},{7,6},{8,9},{9,8},{10,11... | collective-permute-start | bytes 4325384 | tf_op jit(solution)/shard_map/ppermute | solution.py:181
  235.8 215.9 %reduce-scatter.7.cloned.1.call-start = ((), (), s32[]{:S(2)}) async-start(), calls=%async_computation.12 | async-start | bytes 14417920 | tf_op jit(solution)/shard_map/reduce_scatter | solution.py:322
  243.8 15.6 %collective-permute-start.26 = (bf16[64,2048]{1,0:T(8,128)(2,1)S(1)}, bf16[64,2048]{1,0:T(8,128)(2,1)S(1)}, u32[]{:S(2)}, u32[]{:S(2)}) collective-permute-start(bf16[64,2048]{1,0:T(8,128)(2,1)S(1)} %slice.499), channel_id=1, source_target_pairs={{0,8},{8,16},{16,24},{24,28},{28,20},{20,12},{12,4},{4,0},{1,9},{9... | collective-permute-start | bytes 786440 | tf_op jit(solution)/shard_map/ppermute | solution.py:116
  245.3 17.8 %collective-permute-start.27 = (bf16[64,2048]{1,0:T(8,128)(2,1)S(1)}, bf16[64,2048]{1,0:T(8,128)(2,1)S(1)}, u32[]{:S(2)}, u32[]{:S(2)}) collective-permute-start(bf16[64,2048]{1,0:T(8,128)(2,1)S(1)} %slice.500), channel_id=1, source_target_pairs={{8,0},{16,8},{24,16},{28,24},{20,28},{12,20},{4,12},{0,4},{9,1},{1... | collective-permute-start | bytes 786440 | tf_op jit(solution)/shard_map/ppermute | solution.py:117
  355.3 83.7 %all-to-all-start.2 = ((f32[8,2,128]{2,1,0:T(2,128)}), f32[8,2,128]{2,1,0:T(2,128)S(1)}, u32[]{:S(2)}, u32[]{:S(2)}) async-start(f32[8,2,128]{2,1,0:T(2,128)} %pad_maximum_fusion.17), calls=%async_computation.2 | async-start | bytes 16384 | tf_op jit(solution)/shard_map/all_to_all | solution.py:469
  359.1 140.5 %reduce-scatter.9.cloned.1.call-start = ((), (), s32[]{:S(2)}) async-start(), calls=%async_computation.13 | async-start | bytes 7208960 | tf_op jit(solution)/shard_map/reduce_scatter | solution.py:474
  382.1 13.7 %collective-permute-start.30 = (bf16[64,2048]{1,0:T(8,128)(2,1)S(1)}, bf16[64,2048]{1,0:T(8,128)(2,1)S(1)}, u32[]{:S(2)}, u32[]{:S(2)}) collective-permute-start(bf16[64,2048]{1,0:T(8,128)(2,1)S(1)} %get-tuple-element.213), channel_id=1, source_target_pairs={{0,8},{8,16},{16,24},{24,28},{28,20},{20,12},{12,4},{4,0},{1,9},{9... | collective-permute-start | bytes 786440 | tf_op jit(solution)/shard_map/ppermute | solution.py:138
  444.8 116.1 %reduce-scatter.11.cloned.1.call-start = ((), (), s32[]{:S(2)}) async-start(), calls=%async_computation.14 | async-start | bytes 7208960 | tf_op jit(solution)/shard_map/reduce_scatter | solution.py:322
  499.6 37.3 %all-to-all-start.3 = ((bf16[8,64,1408]{2,1,0:T(8,128)(2,1)}), bf16[8,64,1408]{2,1,0:T(8,128)(2,1)}, u32[]{:S(2)}, u32[]{:S(2)}) async-start(bf16[8,64,1408]{2,1,0:T(8,128)(2,1)} %bitcast.391), calls=%async_computation.5 | async-start | bytes 2883584 | tf_op jit(solution)/shard_map/all_to_all | solution.py:505
  505.6 97.0 %reduce-scatter.13.cloned.1.call-start = ((), (), s32[]{:S(2)}) async-start(), calls=%async_computation.15 | async-start | bytes 4915200 | tf_op jit(solution)/shard_map/reduce_scatter | solution.py:554
  546.0 134.8 %reduce-scatter.15.cloned.1.call-start = ((), (), s32[]{:S(2)}) async-start(), calls=%async_computation.16 | async-start | bytes 1310720 | tf_op jit(solution)/shard_map/reduce_scatter | solution.py:322
  558.8 13.1 %collective-permute-start.47 = (bf16[128,2048]{1,0:T(8,128)(2,1)S(1)}, bf16[128,2048]{1,0:T(8,128)(2,1)S(1)}, u32[]{:S(2)}, u32[]{:S(2)}) collective-permute-start(bf16[128,2048]{1,0:T(8,128)(2,1)S(1)} %pad_maximum_fusion.13), channel_id=1, source_target_pairs={{0,8},{8,16},{16,24},{24,28},{28,20},{20,12},{12,4},{4,0},{1,9},{9... | collective-permute-start | bytes 1572872 | tf_op jit(solution)/shard_map/ppermute | solution.py:147
  602.7 83.7 %reduce-scatter.17.cloned.1.call-start = ((), (), s32[]{:S(2)}) async-start(), calls=%async_computation.17 | async-start | bytes 3604480 | tf_op jit(solution)/shard_map/reduce_scatter | solution.py:322
  606.6 37.5 %all-to-all-start.4 = ((bf16[8,80,768]{2,1,0:T(8,128)(2,1)}), bf16[8,80,768]{2,1,0:T(8,128)(2,1)}, u32[]{:S(2)}, u32[]{:S(2)}) async-start(bf16[8,80,768]{2,1,0:T(8,128)(2,1)} %bitcast.86), calls=%async_computation.8 | async-start | bytes 1966080 | tf_op jit(solution)/shard_map/all_to_all | solution.py:561
  615.1 31.5 %collective-permute-start.59 = (bf16[128,2048]{1,0:T(8,128)(2,1)S(1)}, bf16[128,2048]{1,0:T(8,128)(2,1)}, u32[]{:S(2)}, u32[]{:S(2)}) collective-permute-start(bf16[128,2048]{1,0:T(8,128)(2,1)S(1)} %pad_maximum_fusion.16), channel_id=1, source_target_pairs={{8,0},{16,8},{24,16},{28,24},{20,28},{12,20},{4,12},{0,4},{9,1},{1... | collective-permute-start | bytes 1572872 | tf_op jit(solution)/shard_map/ppermute | solution.py:148
  616.5 27.7 %collective-permute-start.49 = (bf16[128,2048]{1,0:T(8,128)(2,1)}, bf16[128,2048]{1,0:T(8,128)(2,1)}, u32[]{:S(2)}, u32[]{:S(2)}) collective-permute-start(bf16[128,2048]{1,0:T(8,128)(2,1)} %pad_maximum_fusion.14), channel_id=1, source_target_pairs={{0,8},{8,16},{16,24},{24,28},{28,20},{20,12},{12,4},{4,0},{1,9},{9... | collective-permute-start | bytes 1572872 | tf_op jit(solution)/shard_map/ppermute | solution.py:147
  648.6 12.9 %collective-permute-start.60 = (bf16[128,2048]{1,0:T(8,128)(2,1)S(1)}, bf16[128,2048]{1,0:T(8,128)(2,1)S(1)}, u32[]{:S(2)}, u32[]{:S(2)}) collective-permute-start(bf16[128,2048]{1,0:T(8,128)(2,1)S(1)} %get-tuple-element.190), channel_id=1, source_target_pairs={{8,0},{16,8},{24,16},{28,24},{20,28},{12,20},{4,12},{0,4},{9,1},{1... | collective-permute-start | bytes 1572872 | tf_op jit(solution)/shard_map/ppermute | solution.py:148
  664.0 18.5 %collective-permute-start.57 = (bf16[128,2048]{1,0:T(8,128)(2,1)}, bf16[128,2048]{1,0:T(8,128)(2,1)}, u32[]{:S(2)}, u32[]{:S(2)}) collective-permute-start(bf16[128,2048]{1,0:T(8,128)(2,1)} %get-tuple-element.187), channel_id=1, source_target_pairs={{0,8},{8,16},{16,24},{24,28},{28,20},{20,12},{12,4},{4,0},{1,9},{9... | collective-permute-start | bytes 1572872 | tf_op jit(solution)/shard_map/ppermute | solution.py:147
  664.4 18.2 %collective-permute-start.61 = (bf16[128,2048]{1,0:T(8,128)(2,1)}, bf16[128,2048]{1,0:T(8,128)(2,1)}, u32[]{:S(2)}, u32[]{:S(2)}) collective-permute-start(bf16[128,2048]{1,0:T(8,128)(2,1)} %get-tuple-element.188), channel_id=1, source_target_pairs={{8,0},{16,8},{24,16},{28,24},{20,28},{12,20},{4,12},{0,4},{9,1},{1... | collective-permute-start | bytes 1572872 | tf_op jit(solution)/shard_map/ppermute | solution.py:148
  (140 other events, 1273.9 us)
Sparse Core Ops, SparseCore 0:
  40.6 53.4 all-gather.9
  95.6 88.9 all-gather.13
  186.2 43.5 all-gather.11
  235.9 74.3 all-gather.7
  342.7 90.3 reduce-scatter.6
  444.8 54.7 reduce-scatter.8
  502.3 54.8 reduce-scatter.10
  559.7 42.9 reduce-scatter.12
  605.4 24.8 reduce-scatter.14
  632.6 36.3 reduce-scatter.16
